TPU v7x, 32 devices: a whole 2x2x4 slice. The times are simulated.
32 devices in a mesh: shard: 2 (over core), context: 4 (over y, x), tensor: 4 (over z).
Axes of the slice: x: 2, y: 2, z: 4, core: 2. Of those that a mesh axis runs over, the one named last changes fastest.
Arguments:
- inputs: bfloat16 [2, 4096, 768], P('shard', 'context'), may hold values from -6 to 6
- segments: int32 [2, 4096], P('shard'), may hold values from 0 to 4, as said below
- w_qkv: bfloat16 [768, 3, 768], P('shard', None, 'tensor'), may hold values from -0.21875 to 0.21875
- w_out: bfloat16 [768, 768], P('tensor', 'shard'), may hold values from -3 to 3
- w_fc: bfloat16 [768, 3072], P('shard', 'tensor'), may hold values from -0.21875 to 0.21875
- w_down: bfloat16 [3072, 768], P('tensor', 'shard'), may hold values from -0.109375 to 0.109375
- b_qv: float32 [2, 768], P(None, 'tensor'), may hold values from -3 to 3
- b_out: float32 [768], replicated, may hold values from -2 to 2
- b_fc: float32 [3072], P('tensor'), may hold values from -3 to 3
- b_down: float32 [768], replicated, may hold values from -2 to 2
- first_norm_gain: float32 [768], replicated, may hold values from 0.5 to 1.5
- first_norm_bias: float32 [768], replicated, may hold values from -2 to 2
- second_norm_gain: float32 [768], replicated, may hold values from 0.5 to 1.5
- second_norm_bias: float32 [768], replicated, may hold values from -2 to 2
- cotangent: bfloat16 [2, 4096, 768], P('shard', 'context'), may hold values from -6 to 6
Outputs:
- outputs: float32 [2, 4096, 768], P('shard', 'context')
- block_input_gradient: float32 [2, 4096, 768], P('shard', 'context')
- grad_qkv: float32 [768, 3, 768], P(('shard', 'context'), None, 'tensor')
- grad_out: float32 [768, 768], P('tensor', ('shard', 'context'))
- grad_fc: float32 [768, 3072], P(('shard', 'context'), 'tensor')
- grad_down: float32 [3072, 768], P('tensor', ('shard', 'context'))
- grad_qv_bias: float32 [2, 768], P(None, 'tensor')
- grad_out_bias: float32 [768], replicated
- grad_fc_bias: float32 [3072], P('tensor')
- grad_down_bias: float32 [768], replicated
- first_norm_gain_gradient: float32 [768], replicated
- grad_ln1_bias: float32 [768], replicated
- second_norm_gain_gradient: float32 [768], replicated
- grad_ln2_bias: float32 [768], replicated
Inputs may be any that keep to these rules, and one draw needn't show every extreme that they name: `segments`: in each sequence the document numbers start at 0, never fall, rise by one at each new document and end at 4 or below. Of the 1 sequence of each index of shard, one, chosen by the seed, holds five documents 0 to 4: documents 0 and 1 lie within the first 1024 positions, 3 and 4 within the last 1024, and document 2 begins within the first 1024 positions and ends within the last 1024. In the other sequences every document but the last has between max(1, min(200, 256)) and min(2000, 2048) tokens, and the last takes the rest.
All inputs are finite; a program needn't handle non-finite values.
Results may differ from a plain program's by a relative error of at most 0.02.
Values may be sent and summed in bfloat16 or wider, within the bound.
No kernel may reach another device: no remote copies, remote signals or barrier semaphores. Data moves between devices by JAX's collectives and lax.ppermute only.
A program may use at most 192 MiB of HBM per device.

v0:
```python
import jax
import jax.numpy as jnp
from jax import lax
from jax.sharding import PartitionSpec as P

HD = 64


EPS = 1e-05
NEG = -1e30


def layer_norm_apply(value, gain, shift):
    mean = jnp.mean(value, axis=-1, keepdims=True)
    centred = value - mean
    inverse = lax.rsqrt(jnp.mean(centred * centred, axis=-1, keepdims=True) + EPS)
    normed = centred * inverse
    return (normed * gain + shift, normed, inverse)


def layer_norm_gradient_pass(grad, normed, inverse, gain):
    scaled = grad * gain
    return inverse * (
        scaled
        - jnp.mean(scaled, axis=-1, keepdims=True)
        - normed * jnp.mean(scaled * normed, axis=-1, keepdims=True)
    )


def allowed_pairs(q_seg, q_pos, k_seg, k_pos):
    causal = k_pos[None, :] <= q_pos[:, None]
    return (causal[None] & (k_seg[:, None, :] == q_seg[:, :, None]))[:, None]


def attend_block(carry, k_four, v_four, q_four, q_seg, q_pos, segments, scale):
    run_max, run_sum, acc = carry
    count = k_four.shape[1]
    k_pos = jnp.arange(count, dtype=jnp.int32)
    allowed = allowed_pairs(q_seg, q_pos, segments, k_pos)
    scores = (
        jnp.einsum("sqhd,skhd->shqk", q_four, k_four, preferred_element_type=jnp.float32) * scale
    )
    scores = jnp.where(allowed, scores, NEG)
    new_max = jnp.maximum(run_max, jnp.max(scores, axis=-1))
    weights = jnp.where(allowed, jnp.exp(scores - new_max[..., None]), 0.0)
    run_sum = jnp.sum(weights, axis=-1)
    acc = jnp.einsum(
        "shqk,skhd->shqd", weights.astype(jnp.bfloat16), v_four, preferred_element_type=jnp.float32
    )
    return (new_max, run_sum, acc)


def grad_block(q_four, do_four, lse, delta, q_seg, q_pos, k_four, v_four, k_seg, k_pos, scale):
    allowed = allowed_pairs(q_seg, q_pos, k_seg, k_pos)
    scores = (
        jnp.einsum("sqhd,skhd->shqk", q_four, k_four, preferred_element_type=jnp.float32) * scale
    )
    probs = jnp.where(allowed, jnp.exp(scores - lse[..., None]), 0.0)
    dprob = jnp.einsum("sqhd,skhd->shqk", do_four, v_four, preferred_element_type=jnp.float32)
    dscore = probs * (dprob - delta[..., None])
    return (dscore.astype(jnp.bfloat16), probs.astype(jnp.bfloat16))


def body(
    inputs,
    segments,
    w_qkv,
    w_out,
    w_fc,
    w_down,
    b_qv,
    b_out,
    b_fc,
    b_down,
    first_norm_gain,
    first_norm_bias,
    second_norm_gain,
    second_norm_bias,
    cotangent,
):
    full_qkv, full_out, full_fc, full_down = (
        lax.all_gather(w_qkv, "shard", axis=0, tiled=True),
        lax.all_gather(w_out, "shard", axis=1, tiled=True),
        lax.all_gather(w_fc, "shard", axis=0, tiled=True),
        lax.all_gather(w_down, "shard", axis=1, tiled=True),
    )
    seqs, tok, width = inputs.shape
    length = segments.shape[1]
    cols = full_qkv.shape[2]
    heads = cols // HD
    scale = float(HD) ** (-0.5)
    first = lax.axis_index("context") * tok
    q_pos = first + jnp.arange(tok, dtype=jnp.int32)
    q_seg = lax.dynamic_slice_in_dim(segments, first, tok, 1)
    block = min(1024, length)
    blocks = length // block
    residual_stream = inputs.astype(jnp.float32)
    first_normalized_input, first_standardized_input, first_inverse_deviation = layer_norm_apply(
        residual_stream, first_norm_gain, first_norm_bias
    )
    low_one = first_normalized_input.astype(jnp.bfloat16)
    projected = jnp.einsum("std,dgc->stgc", low_one, full_qkv, preferred_element_type=jnp.float32)
    query = (projected[:, :, 0] + b_qv[0]).astype(jnp.bfloat16)
    keys = projected[:, :, 1].astype(jnp.bfloat16)
    values = (projected[:, :, 2] + b_qv[1]).astype(jnp.bfloat16)
    q_four = query.reshape(seqs, tok, heads, HD)
    start_state = (
        jnp.full((seqs, heads, tok), NEG, jnp.float32),
        jnp.zeros((seqs, heads, tok), jnp.float32),
        jnp.zeros((seqs, heads, tok, HD), jnp.float32),
    )
    piece = (
        lax.all_gather(keys, "context", axis=1, tiled=True),
        lax.all_gather(values, "context", axis=1, tiled=True),
    )
    count = piece[0].shape[1]
    run_max, run_sum, acc = attend_block(
        start_state,
        piece[0].reshape(seqs, count, heads, HD),
        piece[1].reshape(seqs, count, heads, HD),
        q_four,
        q_seg,
        q_pos,
        segments,
        scale,
    )
    lse = run_max + jnp.log(run_sum)
    attended = jnp.transpose(acc / run_sum[..., None], (0, 2, 1, 3)).reshape(seqs, tok, cols)
    attended_low = attended.astype(jnp.bfloat16)
    attn = lax.psum(
        jnp.einsum(
            "stc,cd->std", attended_low, full_out, preferred_element_type=jnp.float32
        ).astype(jnp.bfloat16),
        "tensor",
    ).astype(jnp.float32)
    middle_residual = residual_stream + attn + b_out
    second_normalized_input, second_standardized_input, second_inverse_deviation = layer_norm_apply(
        middle_residual, second_norm_gain, second_norm_bias
    )
    low_two = second_normalized_input.astype(jnp.bfloat16)
    hidden_pre = (
        jnp.einsum("std,df->stf", low_two, full_fc, preferred_element_type=jnp.float32) + b_fc
    )
    act_low = jax.nn.gelu(hidden_pre, approximate=True).astype(jnp.bfloat16)
    mlp = lax.psum(
        jnp.einsum("stf,fd->std", act_low, full_down, preferred_element_type=jnp.float32).astype(
            jnp.bfloat16
        ),
        "tensor",
    ).astype(jnp.float32)
    outputs = middle_residual + mlp + b_down
    upper_output_gradient = cotangent.astype(jnp.float32)
    grad_down = jnp.einsum("stf,std->fd", act_low, cotangent, preferred_element_type=jnp.float32)
    grad_down_bias = jnp.sum(upper_output_gradient, axis=(0, 1))
    d_act = jnp.einsum("std,fd->stf", cotangent, full_down, preferred_element_type=jnp.float32)
    unused, gelu_back = jax.vjp(lambda value: jax.nn.gelu(value, approximate=True), hidden_pre)
    d_hidden = gelu_back(d_act)[0].astype(jnp.bfloat16)
    grad_fc = jnp.einsum("std,stf->df", low_two, d_hidden, preferred_element_type=jnp.float32)
    grad_fc_bias = jnp.sum(d_hidden.astype(jnp.float32), axis=(0, 1))
    second_norm_backward_result = lax.psum(
        jnp.einsum("stf,df->std", d_hidden, full_fc, preferred_element_type=jnp.float32).astype(
            jnp.bfloat16
        ),
        "tensor",
    ).astype(jnp.float32)
    middle_residual_gradient = upper_output_gradient + layer_norm_gradient_pass(
        second_norm_backward_result,
        second_standardized_input,
        second_inverse_deviation,
        second_norm_gain,
    )
    second_norm_gain_gradient = jnp.sum(
        second_norm_backward_result * second_standardized_input, axis=(0, 1)
    )
    grad_ln2_bias = jnp.sum(second_norm_backward_result, axis=(0, 1))
    branch_low = middle_residual_gradient.astype(jnp.bfloat16)
    grad_out = jnp.einsum(
        "stc,std->cd", attended_low, branch_low, preferred_element_type=jnp.float32
    )
    grad_out_bias = jnp.sum(middle_residual_gradient, axis=(0, 1))
    d_att = jnp.einsum(
        "std,cd->stc", branch_low, full_out, preferred_element_type=jnp.float32
    ).astype(jnp.bfloat16)
    do_four = d_att.reshape(seqs, tok, heads, HD)
    delta = jnp.transpose(
        jnp.sum(do_four.astype(jnp.float32) * attended.reshape(seqs, tok, heads, HD), axis=-1),
        (0, 2, 1),
    )
    whole_keys, whole_values = (
        lax.all_gather(keys, "context", axis=1, tiled=True),
        lax.all_gather(values, "context", axis=1, tiled=True),
    )

    def block_grads(start):
        k_four = lax.dynamic_slice_in_dim(whole_keys, start, block, 1).reshape(
            seqs, block, heads, HD
        )
        v_four = lax.dynamic_slice_in_dim(whole_values, start, block, 1).reshape(
            seqs, block, heads, HD
        )
        k_seg = lax.dynamic_slice_in_dim(segments, start, block, 1)
        k_pos = start + jnp.arange(block, dtype=jnp.int32)
        dscore, prob_low = grad_block(
            q_four, do_four, lse, delta, q_seg, q_pos, k_four, v_four, k_seg, k_pos, scale
        )
        return (k_four, dscore, prob_low)

    zero_query = jnp.zeros((seqs, tok, heads, HD), jnp.float32)

    def back_step(index, carry):
        grad_q, grad_k_all, grad_v_all = carry
        start = index * block
        k_four, dscore, prob_low = block_grads(start)
        grad_q = grad_q + jnp.einsum(
            "shqk,skhd->sqhd", dscore, k_four, preferred_element_type=jnp.float32
        )
        grad_k_blk = (
            jnp.einsum("shqk,sqhd->skhd", dscore, q_four, preferred_element_type=jnp.float32)
            * scale
        )
        grad_v_blk = jnp.einsum(
            "shqk,sqhd->skhd", prob_low, do_four, preferred_element_type=jnp.float32
        )
        grad_k_all = lax.dynamic_update_slice_in_dim(grad_k_all, grad_k_blk, start, 1)
        grad_v_all = lax.dynamic_update_slice_in_dim(grad_v_all, grad_v_blk, start, 1)
        return (grad_q, grad_k_all, grad_v_all)

    empty_all = jnp.zeros((seqs, length, heads, HD), jnp.float32)
    grad_q, grad_k_all, grad_v_all = lax.fori_loop(
        0, blocks, back_step, (zero_query, empty_all, empty_all)
    )
    grad_keys, grad_values = (
        lax.psum_scatter(
            grad_k_all.astype(jnp.bfloat16), "context", scatter_dimension=1, tiled=True
        ).astype(jnp.float32),
        lax.psum_scatter(
            grad_v_all.astype(jnp.bfloat16), "context", scatter_dimension=1, tiled=True
        ).astype(jnp.float32),
    )
    grad_query_low = (grad_q * scale).reshape(seqs, tok, cols).astype(jnp.bfloat16)
    grad_key_low = grad_keys.reshape(seqs, tok, cols).astype(jnp.bfloat16)
    grad_value_low = grad_values.reshape(seqs, tok, cols).astype(jnp.bfloat16)
    stacked = jnp.stack((grad_query_low, grad_key_low, grad_value_low), axis=2)
    grad_qkv = jnp.einsum("std,stgc->dgc", low_one, stacked, preferred_element_type=jnp.float32)
    grad_qv_bias = jnp.stack(
        (
            jnp.sum(grad_query_low.astype(jnp.float32), axis=(0, 1)),
            jnp.sum(grad_value_low.astype(jnp.float32), axis=(0, 1)),
        )
    )
    first_norm_backward_result = lax.psum(
        jnp.einsum("stgc,dgc->std", stacked, full_qkv, preferred_element_type=jnp.float32).astype(
            jnp.bfloat16
        ),
        "tensor",
    ).astype(jnp.float32)
    block_input_gradient = middle_residual_gradient + layer_norm_gradient_pass(
        first_norm_backward_result,
        first_standardized_input,
        first_inverse_deviation,
        first_norm_gain,
    )
    first_norm_gain_gradient = jnp.sum(
        first_norm_backward_result * first_standardized_input, axis=(0, 1)
    )
    grad_ln1_bias = jnp.sum(first_norm_backward_result, axis=(0, 1))
    grad_qkv, grad_out, grad_fc, grad_down = (
        lax.psum_scatter(grad_qkv, ("shard", "context"), scatter_dimension=0, tiled=True),
        lax.psum_scatter(grad_out, ("shard", "context"), scatter_dimension=1, tiled=True),
        lax.psum_scatter(grad_fc, ("shard", "context"), scatter_dimension=0, tiled=True),
        lax.psum_scatter(grad_down, ("shard", "context"), scatter_dimension=1, tiled=True),
    )
    small = lax.psum(
        (
            grad_qv_bias,
            grad_out_bias,
            grad_fc_bias,
            grad_down_bias,
            first_norm_gain_gradient,
            grad_ln1_bias,
            second_norm_gain_gradient,
            grad_ln2_bias,
        ),
        ("shard", "context"),
    )
    return (
        outputs,
        block_input_gradient,
        grad_qkv,
        grad_out,
        grad_fc,
        grad_down,
        small[0],
        small[1],
        small[2],
        small[3],
        small[4],
        small[5],
        small[6],
        small[7],
    )


def solution(mesh):
    placed = (
        P("shard", "context", None),
        P("shard", None),
        P("shard", None, "tensor"),
        P("tensor", "shard"),
        P("shard", "tensor"),
        P("tensor", "shard"),
        P(None, "tensor"),
        P(),
        P("tensor"),
        P(),
        P(),
        P(),
        P(),
        P(),
        P("shard", "context", None),
    )
    return jax.shard_map(
        body,
        mesh=mesh,
        in_specs=placed,
        out_specs=(
            P("shard", "context", None),
            P("shard", "context", None),
            P(("shard", "context"), None, "tensor"),
            P("tensor", ("shard", "context")),
            P(("shard", "context"), "tensor"),
            P("tensor", ("shard", "context")),
            P(None, "tensor"),
            P(),
            P("tensor"),
            P(),
            P(),
            P(),
            P(),
            P(),
        ),
        check_vma=False,
    )
```

profile of v0, /device:TPU:0, one launch (start us, length us, event | category | flops | bytes accessed | tf_op | source)
XLA Modules:
  0.0 798.2 jit_solution(13710485058156912055)
XLA Ops:
  8.1 1.8 convert_reduce_fusion.2
  10.0 2.0 fusion.45
  12.0 2.5 all_gather.20
  18.2 2.0 fusion.93
  21.6 2.2 all_gather.23
  23.8 5.4 fusion.29
  29.3 22.6 %all-gather.12.cloned.1.call-done = bf16[1,4096,1,192]{1,3,2,0:T(8,128)(2,1)} async-done(((bf16[1,1024,1,192]{1,3,2,0:T(8,128)(2,1)}), bf16[1,4096,1,192]{1,3,2,0:T(8,128)(2,1)}) %all-gather.12.cloned.1.call-update) | async-done | bytes 1572880 | tf_op jit(solution)/shard_map/all_gather | solution.py:113
  51.9 21.1 %fusion.23 = (f32[3,1024]{1,0:T(4,128)S(1)}, f32[3,1024,4096]{2,1,0:T(8,128)}) fusion(pred[1024,4096]{1,0:T(8,128)(4,1)} %fusion.29, bf16[4096,3,64]{0,2,1:T(8,128)(2,1)} %bitcast.199, f32[1024,3,64]{0,2,1:T(8,128)S(1)} %bitcast.197, f32[3,64]{1,0:T(4,128)S(1)} %add.241), kind=kOutput, calls=%fused_computation.29 | convolution fusion | flops 1648751616 | bytes 56898304 | tf_op jit(solution)/shard_map/sqhd,skhd->shqk/dot_general | solution.py:41
  73.1 24.6 %fusion.24 = f32[3,1024]{1,0:T(4,128)S(1)} fusion(f32[3,1024,4096]{2,1,0:T(8,128)} %get-tuple-element.336, f32[3,1024]{1,0:T(4,128)S(1)} %broadcast_maximum_fusion, pred[1024,4096]{1,0:T(8,128)(4,1)} %fusion.29), kind=kLoop, calls=%fused_computation.30 | loop fusion | flops 62911488 | bytes 54550528 | tf_op jit(solution)/shard_map/reduce_sum | solution.py:46
  97.7 22.1 %fusion.106 = (bf16[1,1024,3,64]{1,3,2,0:T(8,128)(2,1)S(1)}, f32[1,1024,3,64]{1,3,2,0:T(8,128)}) fusion(f32[3,1024]{1,0:T(4,128)S(1)} %fusion.24, bf16[4096,3,64]{0,2,1:T(8,128)(2,1)} %bitcast.201, f32[3,1024,4096]{2,1,0:T(8,128)} %get-tuple-element.336, f32[3,1024]{1,0:T(4,128)S(1)} %broadcast_maximum_fusion, pred[1024,4096]{1,0:T(8,128)(4,1)} %fusion.29), kind=kOutput, calls=%fused_computation.146 | convolution fusion | flops 1673920512 | bytes 57303040 | tf_op jit(solution)/shard_map/shqk,skhd->shqd/dot_general | solution.py:47
  120.5 1.8 fusion.75
  123.8 67.8 %all-reduce.6.cloned.1.call-done = bf16[1,1024,768]{2,1,0:T(8,128)(2,1)} async-done(((bf16[1,1024,768]{2,1,0:T(8,128)(2,1)}), bf16[1,1024,768]{2,1,0:T(8,128)(2,1)}) %all-reduce.6.cloned.1.call-update) | async-done | bytes 1572880 | tf_op jit(solution)/shard_map/psum | solution.py:130
  191.6 2.1 fusion.91
  194.6 2.1 fusion.60
  196.7 4.8 fusion.107
  201.5 6.4 convert_reduce_fusion.4
  209.1 2.6 fusion.77
  214.8 65.2 %all-reduce.8.cloned.1.call-done = bf16[1,1024,768]{2,1,0:T(8,128)(2,1)} async-done(((bf16[1,1024,768]{2,1,0:T(8,128)(2,1)}), bf16[1,1024,768]{2,1,0:T(8,128)(2,1)}) %all-reduce.8.cloned.1.call-update) | async-done | bytes 1572880 | tf_op jit(solution)/shard_map/psum | solution.py:160
  280.0 3.9 fusion.58
  284.0 2.7 fusion.105
  291.8 134.4 %while.18 = (s32[]{:T(128)}, f32[1,1024,3,64]{1,3,2,0:T(8,128)S(1)}, bf16[1,4096,3,64]{1,3,2,0:T(8,128)(2,1)}, bf16[1,4096,3,64]{1,3,2,0:T(8,128)(2,1)}, bf16[1,...) while((s32[]{:T(128)}, ...), condition=%wide.region_13.14_spmd.clone, body=%wide.region_12.13_spmd.clone.sunk | while | flops 2048460800 | bytes 101011872 | solution.py:229
  293.7 1.6 constant_dynamic-slice_fusion.6
  295.3 6.4 fusion.155
  301.6 7.2 fusion.156
  308.9 2.6 copy-done
  311.5 2.8 fusion.158
  314.3 4.2 fusion.157
  318.5 6.9 fusion.159
  328.9 6.4 fusion.155
  335.2 7.2 fusion.156
  342.5 2.6 copy-done
  345.1 2.9 fusion.158
  347.9 4.2 fusion.157
  352.1 6.9 fusion.159
  360.9 1.6 constant_dynamic-slice_fusion.6
  362.5 6.4 fusion.155
  368.9 7.2 fusion.156
  376.1 2.6 copy-done
  378.7 2.8 fusion.158
  381.5 4.2 fusion.157
  385.7 6.9 fusion.159
  396.1 6.4 fusion.155
  402.5 7.2 fusion.156
  409.7 2.6 copy-done
  412.3 2.8 fusion.158
  415.1 4.2 fusion.157
  419.3 6.9 fusion.159
  427.2 3.5 fusion.79
  430.8 5.8 fusion.76
  437.3 19.0 %reduce-scatter.11.cloned.1.call-done = bf16[1,1024,3,64]{1,3,2,0:T(8,128)(2,1)} async-done(((bf16[1,4096,3,64]{1,3,2,0:T(8,128)(2,1)}), bf16[1,1024,3,64]{1,3,2,0:T(8,128)(2,1)}) %reduce-scatter.11.cloned.1.call-update) | async-done | bytes 393232 | tf_op jit(solution)/shard_map/reduce_scatter | solution.py:236
  456.4 33.8 %reduce-scatter.9.cloned.1.call-done = bf16[1,1024,3,64]{1,3,2,0:T(8,128)(2,1)} async-done(((bf16[1,4096,3,64]{1,3,2,0:T(8,128)(2,1)}), bf16[1,1024,3,64]{1,3,2,0:T(8,128)(2,1)}) %reduce-scatter.9.cloned.1.call-update) | async-done | bytes 393232 | tf_op jit(solution)/shard_map/reduce_scatter | solution.py:233
  490.2 4.1 fusion.78
  494.4 4.9 fusion.108
  499.3 5.3 fusion.67
  504.7 4.4 fusion.61
  510.6 17.7 %reduce-scatter.19.cloned.1.call-done = f32[96,192]{1,0:T(8,128)} async-done(((f32[768,192]{1,0:T(8,128)}), f32[96,192]{1,0:T(8,128)}) %reduce-scatter.19.cloned.1.call-update) | async-done | bytes 73744
  528.3 1.6 copy.43
  532.2 120.0 %all-reduce.10.cloned.1.call-done = (bf16[1,1024,768]{2,1,0:T(8,128)(2,1)}, bf16[1,1024,768]{2,1,0:T(8,128)(2,1)}) async-done(((bf16[1,1024,768]{2,1,0:T(8,128)(2,1)}, bf16[1,1024,768]{2,1,0:T(8,128)(2,1)}), (bf16[1,1024,768]{2,1,0:T(8,128)(2,1)}, bf16[1,1024,768]{2,1,0:T(8,128)(2,1)})) %all-reduce.10.cloned.1.call-update) | async-done | bytes 3145744 | tf_op jit(solution)/shard_map/psum | solution.py:145
  652.2 2.9 fusion.59
  655.2 27.3 %all-reduce = (f32[2,192]{1,0:T(2,128)}, f32[768]{0:T(1024)}, f32[768]{0:T(1024)}, f32[768]{0:T(1024)}, f32[768]{0:T(1024)}, /*index=5*/f32[768]{0:T(1024)}, f32[768]{0:T(1024)}, f32[768]{0:T(1024)}) all-reduce(f32[2,192]{1,0:T(2,128)S(1)} %pad_maximum_fusion, ...), channel_id=1, replica_groups=mesh['shard'=2,'context'=4,'tensor'=4] {'shard','context'}, use_global_device_ids=true, to_apply=%region_25.26 | all-reduce | flops 5760 | bytes 46080 | tf_op jit(solution)/shard_map/psum | solution.py:273
  682.5 5.5 fusion.44
  687.9 9.8 %reduce-scatter.15.cloned.1.call-done = f32[96,768]{1,0:T(8,128)} async-done(((f32[768,768]{1,0:T(8,128)}), f32[96,768]{1,0:T(8,128)}) %reduce-scatter.15.cloned.1.call-update) | async-done | bytes 294928 | tf_op jit(solution)/shard_map/reduce_scatter | solution.py:270
  697.7 46.7 %reduce-scatter.17.cloned.1.call-done = f32[768,96]{0,1:T(8,128)} async-done(((f32[768,768]{0,1:T(8,128)}), f32[768,96]{0,1:T(8,128)}) %reduce-scatter.17.cloned.1.call-update) | async-done | bytes 294928 | tf_op jit(solution)/shard_map/reduce_scatter | solution.py:271
  744.4 46.4 %reduce-scatter.13.cloned.1.call-done = f32[96,3,192]{2,0,1:T(8,128)} async-done(((f32[768,3,192]{2,0,1:T(8,128)}), f32[96,3,192]{2,0,1:T(8,128)}) %reduce-scatter.13.cloned.1.call-update) | async-done | bytes 221200 | tf_op jit(solution)/shard_map/reduce_scatter | solution.py:268
  (207 shorter events, 33.8 us)
Async XLA Ops:
  8.0 6.5 copy-start.1
  8.0 6.5 copy-start.34
  8.0 6.5 copy-start.50
  8.1 43.9 %all-gather.12.cloned.1.call-start = ((), (), s32[]{:S(2)}) async-start(), calls=%async_computation.16 | async-start | bytes 1966080 | tf_op jit(solution)/shard_map/all_gather | solution.py:113
  10.0 5.9 copy-start.25
  15.9 5.7 copy-start.22
  16.0 7.9 copy-start.24
  18.2 79.5 %all-gather.6.cloned.1.call-start = ((), (), s32[]{:S(2)}) async-start(), calls=%async_computation.6 | async-start | bytes 1966080 | tf_op jit(solution)/shard_map/all_gather | solution.py:114
  20.3 171.3 %all-reduce.6.cloned.1.call-start = ((), (), s32[]{:S(2)}) async-start(), calls=%async_computation.7 | async-start | bytes 3145728 | tf_op jit(solution)/shard_map/psum | solution.py:130
  21.5 51.5 %copy-start.9 = (f32[1,1024,1,192]{1,3,2,0:T(8,128)}, f32[1,1024,1,192]{1,3,2,0:T(8,128)S(1)}, u32[]{:S(2)}) copy-start(f32[1,1024,1,192]{1,3,2,0:T(8,128)S(1)} %slice.21) | copy-start | bytes 2359300
  21.6 51.4 %copy-start.42 = (f32[3,64]{1,0:T(4,128)}, f32[3,64]{1,0:T(4,128)S(1)}, u32[]{:S(2)}) copy-start(f32[3,64]{1,0:T(4,128)S(1)} %add.241) | copy-start | bytes 2308
  23.8 96.0 %copy-start.10 = (bf16[192,768]{1,0:T(8,128)(2,1)}, bf16[192,768]{1,0:T(8,128)(2,1)S(1)}, u32[]{:S(2)}) copy-start(bf16[192,768]{1,0:T(8,128)(2,1)S(1)} %all_gather.23) | copy-start | bytes 884740
  73.0 24.6 %copy-start.28 = (f32[3,1024]{1,0:T(4,128)}, f32[3,1024]{1,0:T(4,128)S(1)}, u32[]{:S(2)}) copy-start(f32[3,1024]{1,0:T(4,128)S(1)} %get-tuple-element.335) | copy-start | bytes 36868
  97.6 22.2 %copy-start.27 = (f32[3,1024]{1,0:T(4,128)}, f32[3,1024]{1,0:T(4,128)S(1)}, u32[]{:S(2)}) copy-start(f32[3,1024]{1,0:T(4,128)S(1)} %fusion.24) | copy-start | bytes 36868
  119.8 71.8 %copy-start.23 = (f32[768]{0:T(1024)S(1)}, f32[768]{0:T(1024)}, u32[]{:S(2)}) copy-start(f32[768]{0:T(1024)} %param.24) | copy-start | bytes 9220
  122.3 74.3 %all-gather.8.cloned.1.call-start = ((), (), s32[]{:S(2)}) async-start(), calls=%async_computation.8 | async-start | bytes 1769472 | tf_op jit(solution)/shard_map/all_gather | solution.py:84
  122.9 78.6 %all-gather.10.cloned.1.call-start = ((), (), s32[]{:S(2)}) async-start(), calls=%async_computation.9 | async-start | bytes 1769472 | tf_op jit(solution)/shard_map/all_gather | solution.py:85
  123.5 71.1 %copy-start.31 = (f32[768]{0:T(1024)S(1)}, f32[768]{0:T(1024)}, u32[]{:S(2)}) copy-start(f32[768]{0:T(1024)} %param.29) | copy-start | bytes 9220
  123.5 71.1 %copy-start.45 = (f32[768]{0:T(1024)S(1)}, f32[768]{0:T(1024)}, u32[]{:S(2)}) copy-start(f32[768]{0:T(1024)} %param.30) | copy-start | bytes 9220
  123.5 156.5 %all-reduce.8.cloned.1.call-start = ((), (), s32[]{:S(2)}) async-start(), calls=%async_computation.10 | async-start | bytes 3145728 | tf_op jit(solution)/shard_map/psum | solution.py:160
  196.7 4.8 copy-start.48
  201.5 7.6 copy-start.47
  211.7 244.7 %reduce-scatter.11.cloned.1.call-start = ((), (), s32[]{:S(2)}) async-start(), calls=%async_computation.12 | async-start | bytes 1966080 | tf_op jit(solution)/shard_map/reduce_scatter | solution.py:236
  286.6 5.2 copy-start.5
  293.7 8.0 copy-start.6
  295.2 6.4 copy-start.33
  295.3 6.4 copy-start.40
  314.3 4.2 copy-start.7
  314.3 4.2 copy-start.41
  327.3 8.0 copy-start.6
  328.8 6.4 copy-start.33
  328.9 6.4 copy-start.40
  347.9 4.2 copy-start.7
  347.9 4.2 copy-start.41
  360.9 8.0 copy-start.6
  362.5 6.4 copy-start.33
  362.5 6.4 copy-start.40
  381.5 4.2 copy-start.7
  381.5 4.2 copy-start.41
  394.5 8.0 copy-start.6
  396.1 6.4 copy-start.33
  396.1 6.4 copy-start.40
  415.1 4.2 copy-start.7
  415.1 4.2 copy-start.41
  426.2 64.0 %reduce-scatter.9.cloned.1.call-start = ((), (), s32[]{:S(2)}) async-start(), calls=%async_computation.11 | async-start | bytes 1966080 | tf_op jit(solution)/shard_map/reduce_scatter | solution.py:233
  426.3 4.5 copy-start.49
  426.8 101.5 %reduce-scatter.19.cloned.1.call-start = ((), (), s32[]{:S(2)}) async-start(), calls=%async_computation.17 | async-start | bytes 884736
  430.7 221.5 %all-reduce.10.cloned.1.call-start = ((), (), s32[]{:S(2)}) async-start(), calls=%async_computation.18 | async-start | bytes 6291456 | tf_op jit(solution)/shard_map/psum | solution.py:145
  437.3 56.9 %copy-start.21 = (bf16[1,1024,3,64]{1,3,2,0:T(8,128)(2,1)}, bf16[1,1024,3,64]{1,3,2,0:T(8,128)(2,1)S(1)}, u32[]{:S(2)}) copy-start(bf16[1,1024,3,64]{1,3,2,0:T(8,128)(2,1)S(1)} %get-tuple-element.325) | copy-start | bytes 1179652
  494.3 5.0 copy-start.14
  494.3 203.4 %reduce-scatter.15.cloned.1.call-start = ((), (), s32[]{:S(2)}) async-start(), calls=%async_computation.14 | async-start | bytes 2654208 | tf_op jit(solution)/shard_map/reduce_scatter | solution.py:270
  499.2 5.4 copy-start.20
  499.2 5.4 copy-start.26
  499.3 5.4 copy-start.30
  499.3 5.4 copy-start.35
  499.3 245.1 %reduce-scatter.17.cloned.1.call-start = ((), (), s32[]{:S(2)}) async-start(), calls=%async_computation.15 | async-start | bytes 2654208 | tf_op jit(solution)/shard_map/reduce_scatter | solution.py:271
  504.6 286.2 %reduce-scatter.13.cloned.1.call-start = ((), (), s32[]{:S(2)}) async-start(), calls=%async_computation.13 | async-start | bytes 2654208 | tf_op jit(solution)/shard_map/reduce_scatter | solution.py:268
  509.1 173.3 %copy-start.3 = (bf16[1,1024,768]{2,1,0:T(8,128)(2,1)S(1)}, bf16[1,1024,768]{2,1,0:T(8,128)(2,1)}, u32[]{:S(2)}) copy-start(bf16[1,1024,768]{2,1,0:T(8,128)(2,1)} %all-reduce.6.cloned.1.call-done) | copy-start | bytes 4718596
  530.7 124.4 %copy-start.36 = (f32[768]{0:T(1024)S(1)}, f32[768]{0:T(1024)}, u32[]{:S(2)}) copy-start(f32[768]{0:T(1024)} %get-tuple-element.278) | copy-start | bytes 9220
  530.7 124.4 %copy-start.37 = (f32[768]{0:T(1024)S(1)}, f32[768]{0:T(1024)}, u32[]{:S(2)}) copy-start(f32[768]{0:T(1024)} %get-tuple-element.284) | copy-start | bytes 9220
  530.7 124.5 %copy-start.38 = (f32[768]{0:T(1024)S(1)}, f32[768]{0:T(1024)}, u32[]{:S(2)}) copy-start(f32[768]{0:T(1024)} %get-tuple-element.322) | copy-start | bytes 9220
  530.7 124.5 %copy-start.39 = (f32[768]{0:T(1024)S(1)}, f32[768]{0:T(1024)}, u32[]{:S(2)}) copy-start(f32[768]{0:T(1024)} %get-tuple-element.330) | copy-start | bytes 9220
  530.7 124.5 %copy-start.44 = (f32[768]{0:T(1024)S(1)}, f32[768]{0:T(1024)}, u32[]{:S(2)}) copy-start(f32[768]{0:T(1024)} %get-tuple-element.339) | copy-start | bytes 9220
  530.7 151.8 %copy-start.43 = (f32[768]{0:T(1024)S(1)}, f32[768]{0:T(1024)}, u32[]{:S(2)}) copy-start(f32[768]{0:T(1024)} %param.26) | copy-start | bytes 9220
  (19 other events, 49.7 us)
Sparse Core Ops, SparseCore 0:
  18.3 33.5 all-gather.11
  53.8 30.9 all-gather.5
  122.5 69.0 all-reduce.5
  211.8 68.1 all-reduce.7
  426.4 29.9 reduce-scatter.10
  459.2 30.9 reduce-scatter.8
  493.3 34.9 reduce-scatter.18
  530.8 121.4 all-reduce.9
  656.2 41.5 reduce-scatter.14
  701.9 42.4 reduce-scatter.16
  748.3 42.4 reduce-scatter.12
Sparse Core Ops, SparseCore 1:
  124.3 9.1 all-gather.7
  134.9 10.3 all-gather.9
where the time goes:
time: 802 us; the launch traced here: 798 us
  waiting for transfers between devices  451 us (56%)
  matrix products  199 us (25%)
  other arithmetic  66 us (8%)
  local copies, waits for them, and re-layouts  32.8 us (4%)
  blocking collectives  32 us (4%)
  between operations  16.1 us (2%)
    psum x1, waiting for transfers between devices, body(): lax.psum(jnp.einsum('stf,fd->std', act_low, full_down, preferred_element_...  120 us
    psum x1, waiting for transfers between devices, body(): lax.psum(jnp.einsum('stc,cd->std', attended_low, full_out, preferred_elem...  67.8 us
    psum x1, waiting for transfers between devices, body(): lax.psum(jnp.einsum('stf,df->std', d_hidden, full_fc, preferred_element_t...  65.2 us
    reduce_scatter x1, waiting for transfers between devices, body(): lax.psum_scatter(grad_down, ('shard', 'context'), scatter_dimension=1, ti...  46.7 us
    reduce_scatter x1, waiting for transfers between devices, body(): lax.psum_scatter(grad_qkv, ('shard', 'context'), scatter_dimension=0, til...  46.4 us
    reduce_scatter x1, waiting for transfers between devices, body(): lax.psum_scatter(grad_k_all.astype(jnp.bfloat16), 'context', scatter_dime...  33.8 us
    dot_general x4, matrix products, grad_block(): jnp.einsum('sqhd,skhd->shqk', do_four, v_four, preferred_element_type=jnp...  28.8 us
    dot_general x4, matrix products, back_step(): jnp.einsum('shqk,sqhd->skhd', prob_low, do_four, preferred_element_type=j...  27.6 us
  transfers between devices with their start and end apart: 13, of which 10 were waited for; matrix products, arithmetic and copies ran while one was open for 14% of the time, Pallas kernels for 0%

commit v1 on v0

v1 whole, which is shorter than its diff:
```python
import functools

import jax
import jax.numpy as jnp
from jax import lax
from jax.experimental import pallas as pl
from jax.experimental.pallas import tpu as pltpu
from jax.sharding import PartitionSpec as P

HD = 64
EPS = 1e-05
NEG = -1e30
SCALE = float(HD) ** -0.5
VMEM_LIMIT = 56 * 1024 * 1024
GROUPS = (3,)
BK_F, BQ_F = 512, 512
BK_B, BQ_B = 512, 512
f32 = jnp.float32
bf16 = jnp.bfloat16
VM = pl.BlockSpec(memory_space=pltpu.VMEM)
SM = pl.BlockSpec(memory_space=pltpu.SMEM)
HBM = pl.BlockSpec(memory_space=pl.ANY)


def nn(a, b):
    return lax.dot_general(a, b, (((1,), (0,)), ((), ())), preferred_element_type=f32)


def tn(a, b):
    return lax.dot_general(a, b, (((0,), (0,)), ((), ())), preferred_element_type=f32)


def nt(a, b):
    return lax.dot_general(a, b, (((1,), (1,)), ((), ())), preferred_element_type=f32)


def params():
    return pltpu.CompilerParams(vmem_limit_bytes=VMEM_LIMIT)


def shape(dims, kind=bf16):
    return jax.ShapeDtypeStruct(dims, kind)


def halves(core, width):
    half = width // 2
    own = pl.ds(pl.multiple_of(core * half, 128), half)
    other = pl.ds(pl.multiple_of((1 - core) * half, 128), half)
    return own, other


def norm(value):
    centred = value - jnp.mean(value, axis=-1, keepdims=True)
    inverse = lax.rsqrt(jnp.mean(centred * centred, axis=-1, keepdims=True) + EPS)
    return centred * inverse, inverse


def norm_gradient(grad, normed, inverse, gain):
    scaled = grad * gain
    return inverse * (
        scaled
        - jnp.mean(scaled, axis=-1, keepdims=True)
        - normed * jnp.mean(scaled * normed, axis=-1, keepdims=True)
    )


def project_kernel(sc, x, w_own, w_other, b_qv, gain, shift, low, qt, kt, vt):
    own, other = halves(sc[2], x.shape[1])
    cols = qt.shape[0]
    normed, _ = norm(x[...].astype(f32))
    low[...] = (normed * gain[...] + shift[...]).astype(bf16)
    projected = nn(low[:, own], w_own[...]) + nn(low[:, other], w_other[...])
    qt[...] = ((projected[:, :cols] + b_qv[0:1, :]) * SCALE).T.astype(bf16)
    kt[...] = projected[:, cols : 2 * cols].T.astype(bf16)
    vt[...] = (projected[:, 2 * cols :] + b_qv[1:2, :]).T.astype(bf16)


def project(place, x, w_own, w_other, b_qv, gain, shift):
    tok, width = x.shape
    cols = b_qv.shape[1]
    rows = min(256, tok)
    fixed = lambda a: pl.BlockSpec(a.shape, lambda i: (0,) * a.ndim)
    across = pl.BlockSpec((cols, rows), lambda i: (0, i))
    return pl.pallas_call(
        project_kernel,
        grid=(tok // rows,),
        in_specs=[SM, pl.BlockSpec((rows, width), lambda i: (i, 0))]
        + [fixed(a) for a in (w_own, w_other, b_qv, gain, shift)],
        out_specs=[pl.BlockSpec((rows, width), lambda i: (i, 0)), across, across, across],
        out_shape=[shape((tok, width))] + [shape((cols, tok))] * 3,
        compiler_params=params(),
        name="project",
    )(place, x, w_own, w_other, b_qv, gain, shift)


def key_loop(sc, i, step, carry):
    lo, full, diag, end = sc[4 * i + 4], sc[4 * i + 5], sc[4 * i + 6], sc[4 * i + 7]
    carry = lax.fori_loop(lo, full, functools.partial(step, True), carry)
    carry = lax.fori_loop(full, diag, functools.partial(step, False), carry)
    return lax.fori_loop(diag, end, functools.partial(step, True), carry)


def tile_mask(j, bk, bq, start, qpos):
    kpos = j * bk + lax.broadcasted_iota(jnp.int32, (bk, bq), 0)
    return (kpos >= start) & (kpos <= qpos)


def load_keys(sc, kv, held, sems):
    if len(kv) == 1:
        copies = [pltpu.make_async_copy(kv[0], held, sems.at[0])]
    else:
        rows = kv[0].shape[0]
        copies = [
            pltpu.make_async_copy(
                kv[n], held.at[sc[1] ^ (n % 4), pl.ds((n // 4) * rows, rows), :], sems.at[n]
            )
            for n in range(8)
        ]
    for copy in copies:
        copy.start()
    for copy in copies:
        copy.wait()


def attend_kernel(first_head, heads, bk, bq, parts, n_kv, sc, qt, st, *refs):
    kv, refs = refs[:n_kv], refs[n_kv:]
    lse, ot, out, (held, acc, sems) = refs[0], refs[1], refs[2 : 2 + parts], refs[2 + parts :]
    i = pl.program_id(0)
    per = held.shape[2] // bk
    cols = heads * HD
    start = st[...]
    qpos = sc[0] + i * bq + lax.broadcasted_iota(jnp.int32, (1, bq), 1)

    @pl.when(i == 0)
    def _():
        load_keys(sc, kv, held, sems)

    acc[...] = jnp.zeros_like(acc)

    def step(masked, j, carry):
        r = j // per
        off = pl.multiple_of((j % per) * bk, bk)
        new = []
        if masked:
            ok = tile_mask(j, bk, bq, start, qpos)
        for h in range(heads):
            m, l = carry[h]
            hs = slice(h * HD, (h + 1) * HD)
            s = tn(
                held[r, hs, pl.ds(off, bk)],
                qt[(first_head + h) * HD : (first_head + h + 1) * HD, :],
            )
            if masked:
                s = jnp.where(ok, s, NEG)
            m2 = jnp.maximum(m, jnp.max(s, axis=0, keepdims=True))
            p = jnp.exp(s - m2)
            al = jnp.exp(m - m2)
            l = l * al + jnp.sum(p, axis=0, keepdims=True)
            v = held[r, cols + h * HD : cols + (h + 1) * HD, pl.ds(off, bk)]
            acc[hs, :] = acc[hs, :] * al + nn(v, p.astype(bf16))
            new.append((m2, l))
        return tuple(new)

    one = (jnp.full((1, bq), NEG, f32), jnp.zeros((1, bq), f32))
    res = key_loop(sc, i, step, (one,) * heads)
    here = pl.ds(pl.multiple_of(i * bq, bq), bq)
    for h in range(heads):
        m, l = res[h]
        ot[h * HD : (h + 1) * HD, here] = (acc[h * HD : (h + 1) * HD, :] / l).astype(bf16)
        lse[h : h + 1, :] = m + jnp.log(l)

    @pl.when(i == pl.num_programs(0) - 1)
    def _():
        send_parts(sc[3], ot, out)


def send_parts(me, source, out):
    parts, size = len(out), out[0].shape[1]
    for d in range(parts):
        if size % 128 == 0:
            at = pl.multiple_of(lax.rem(me + d, parts) * size, 128)
            out[d][...] = source[:, pl.ds(at, size)].astype(out[d].dtype)
        else:
            for n in range(parts):

                @pl.when(lax.rem(me + d, parts) == n)
                def _():
                    out[d][...] = source[:, n * size : (n + 1) * size].astype(out[d].dtype)


def take_parts(me, rows, parts, target):
    size = parts[0].shape[1]
    for d in range(len(parts)):
        if size % 128 == 0:
            at = pl.multiple_of(lax.rem(me + d, len(parts)) * size, 128)
            target[:, pl.ds(at, size)] = parts[d][rows, :]
        else:
            for n in range(len(parts)):

                @pl.when(lax.rem(me + d, len(parts)) == n)
                def _():
                    target[:, n * size : (n + 1) * size] = parts[d][rows, :]


def attend(scalars, starts, qt, kv, first_head, heads, bk, bq, parts):
    tok = qt.shape[1]
    cols = heads * HD
    runs = kv[0].shape[0] if len(kv) == 1 else 4
    bk, bq = min(bk, tok), min(bq, tok)
    whole = lambda a, b: pl.BlockSpec((a, b), lambda i: (0, 0))
    return pl.pallas_call(
        functools.partial(attend_kernel, first_head, heads, bk, bq, parts, len(kv)),
        grid=(tok // bq,),
        in_specs=[
            SM,
            pl.BlockSpec((qt.shape[0], bq), lambda i: (0, i)),
            pl.BlockSpec((1, bq), lambda i: (0, i)),
        ]
        + [HBM] * len(kv),
        out_specs=[pl.BlockSpec((heads, bq), lambda i: (0, i)), whole(cols, tok)]
        + [whole(cols, tok // parts)] * parts,
        scratch_shapes=[
            pltpu.VMEM((runs, 2 * cols, tok), bf16),
            pltpu.VMEM((cols, bq), f32),
            pltpu.SemaphoreType.DMA((len(kv),)),
        ],
        out_shape=[shape((heads, tok), f32), shape((cols, tok))]
        + [shape((cols, tok // parts))] * parts,
        compiler_params=params(),
        name="attend",
    )(scalars(bk, bq), qt, starts, *kv)


def attend_back_kernel(first_head, heads, bk, bq, parts, n_kv, sc, qt, st, lse, ot, *refs):
    do_parts, refs = refs[:parts], refs[parts:]
    kv, refs = refs[:n_kv], refs[n_kv:]
    n_out = 1 if n_kv == 1 else 4
    dq, dkv, (held, acc, dqa, do_all, sems) = (
        refs[:parts],
        refs[parts : parts + n_out],
        refs[parts + n_out :],
    )
    i = pl.program_id(0)
    per = held.shape[2] // bk
    cols = heads * HD
    start = st[...]
    qpos = sc[0] + i * bq + lax.broadcasted_iota(jnp.int32, (1, bq), 1)
    here = pl.ds(pl.multiple_of(i * bq, bq), bq)

    @pl.when(i == 0)
    def _():
        acc[...] = jnp.zeros_like(acc)
        dqa[...] = jnp.zeros_like(dqa)
        take_parts(sc[3], slice(first_head * HD, (first_head + heads) * HD), do_parts, do_all)
        load_keys(sc, kv, held, sems)

    delta = [
        jnp.sum(
            do_all[h * HD : (h + 1) * HD, here].astype(f32)
            * ot[h * HD : (h + 1) * HD, :].astype(f32),
            axis=0,
            keepdims=True,
        )
        for h in range(heads)
    ]

    def step(masked, j, carry):
        r = j // per
        off = pl.multiple_of((j % per) * bk, bk)
        if masked:
            ok = tile_mask(j, bk, bq, start, qpos)
        for h in range(heads):
            hs = slice(h * HD, (h + 1) * HD)
            vs = slice(cols + h * HD, cols + (h + 1) * HD)
            k = held[r, hs, pl.ds(off, bk)]
            v = held[r, vs, pl.ds(off, bk)]
            q = qt[(first_head + h) * HD : (first_head + h + 1) * HD, :]
            do = do_all[hs, here]
            s = tn(k, q) - lse[h : h + 1, :]
            if masked:
                s = jnp.where(ok, s, NEG)
            p = jnp.exp(s)
            ds = (p * (tn(v, do) - delta[h])).astype(bf16)
            acc[r, vs, pl.ds(off, bk)] += nt(do, p.astype(bf16))
            acc[r, hs, pl.ds(off, bk)] += nt(q, ds)
            dqa[hs, here] += nn(k, ds)
        return carry

    key_loop(sc, i, step, 0)

    @pl.when(i == pl.num_programs(0) - 1)
    def _():
        dqa[...] = dqa[...] * SCALE
        send_parts(sc[3], dqa, dq)
        if n_out == 1:
            dkv[0][...] = acc[...].astype(bf16)
        else:
            for target, pair, rows in (
                (0, (0, 2), slice(0, cols)),
                (1, (1, 3), slice(0, cols)),
                (2, (0, 1), slice(cols, 2 * cols)),
                (3, (2, 3), slice(cols, 2 * cols)),
            ):
                for n in range(2):
                    dkv[target][n] = acc[sc[1] ^ pair[n], rows, :].astype(bf16)


def attend_back(scalars, starts, qt, lse, ot, do_parts, kv, first_head, heads, bk, bq):
    tok = qt.shape[1]
    cols = heads * HD
    parts = len(do_parts)
    runs = kv[0].shape[0] if len(kv) == 1 else 4
    bk, bq = min(bk, tok), min(bq, tok)
    whole = lambda *dims: pl.BlockSpec(dims, lambda i: (0,) * len(dims))
    out_kv = [(runs, 2 * cols, tok)] if len(kv) == 1 else [(2, cols, tok)] * 4
    return pl.pallas_call(
        functools.partial(attend_back_kernel, first_head, heads, bk, bq, parts, len(kv)),
        grid=(tok // bq,),
        in_specs=[
            SM,
            pl.BlockSpec((qt.shape[0], bq), lambda i: (0, i)),
            pl.BlockSpec((1, bq), lambda i: (0, i)),
            pl.BlockSpec((heads, bq), lambda i: (0, i)),
            pl.BlockSpec((cols, bq), lambda i: (0, i)),
        ]
        + [whole(*d.shape) for d in do_parts]
        + [HBM] * len(kv),
        out_specs=[whole(cols, tok // parts)] * parts + [whole(*d) for d in out_kv],
        scratch_shapes=[
            pltpu.VMEM((runs, 2 * cols, tok), bf16),
            pltpu.VMEM((runs, 2 * cols, tok), f32),
            pltpu.VMEM((cols, tok), f32),
            pltpu.VMEM((cols, tok), bf16),
            pltpu.SemaphoreType.DMA((len(kv),)),
        ],
        out_shape=[shape((cols, tok // parts))] * parts + [shape(d) for d in out_kv],
        compiler_params=params(),
        name="attend_back",
    )(scalars(bk, bq), qt, starts, lse, ot, *do_parts, *kv)


ROOT = 0.7978845608028654


def middle_kernel(n_att, parts, sc, *refs):
    att, refs = refs[:n_att], refs[n_att:]
    (x, cot, wo_own, wo_other, fc_own, fc_other, dn_own, dn_other, b_out, b_fc, b_down, gain, shift) = refs[:13]
    refs = refs[13:]
    outputs, grad_mid, sums, fc_sums = refs[:4]
    d_att, (g_own, g_other, go_own, go_other) = refs[4 : 4 + parts], refs[4 + parts : 8 + parts]
    mid, att_t, low, low_t, cot_t, mlp, back = refs[8 + parts :]
    d = pl.program_id(0)
    width = x.shape[1]
    own, other = halves(sc[2], width)
    half = width // 2
    ffw = fc_own.shape[2]

    @pl.when(d == 0)
    def _():
        group = n_att // parts
        row = 0
        for part in range(parts):
            for g in range(group):
                piece = att[part * group + g]
                att_t[row : row + piece.shape[0], :] = piece[...]
                row += piece.shape[0]
        att_low = att_t[...].T
        mid[:, own] = nn(att_low, wo_own[...])
        mid[:, other] = nn(att_low, wo_other[...])
        mid[...] = x[...].astype(f32) + mid[...] + b_out[...]
        normed, _ = norm(mid[...])
        low[...] = (normed * gain[...] + shift[...]).astype(bf16)
        low_t[...] = low[...].T
        cot_t[...] = cot[...].T
        mlp[...] = jnp.zeros_like(mlp)
        back[...] = jnp.zeros_like(back)

    own_rows = pl.ds(pl.multiple_of(sc[2] * half, half), half)
    other_rows = pl.ds(pl.multiple_of((1 - sc[2]) * half, half), half)
    u = nn(low[:, own], fc_own[0]) + nn(low[:, other], fc_other[0]) + b_fc[0]
    t = jnp.tanh(ROOT * (u + 0.044715 * (u * u * u)))
    act = (0.5 * u * (1.0 + t)).astype(bf16)
    slope = 0.5 * (1.0 + t) + (0.5 * ROOT) * u * (1.0 - t * t) * (1.0 + 0.134145 * (u * u))
    d_act = nt(cot[:, own], dn_own[0]) + nt(cot[:, other], dn_other[0])
    dh = (d_act * slope).astype(bf16)
    mlp[:, own] += nn(act, dn_own[0])
    mlp[:, other] += nn(act, dn_other[0])
    back[:, own] += nt(dh, fc_own[0])
    back[:, other] += nt(dh, fc_other[0])
    g_own[0, :, :ffw] = nn(low_t[own_rows, :], dh).astype(bf16)
    g_other[0, :, :ffw] = nn(low_t[other_rows, :], dh).astype(bf16)
    g_own[0, :, ffw:] = nn(cot_t[own_rows, :], act).astype(bf16)
    g_other[0, :, ffw:] = nn(cot_t[other_rows, :], act).astype(bf16)
    fc_sums[0] = jnp.sum(dh.astype(f32), axis=0, keepdims=True)

    @pl.when(d == parts - 1)
    def _():
        normed, inverse = norm(mid[...])
        outputs[...] = (mid[...] + mlp[...] + b_down[...]).astype(bf16)
        upper = cot[...].astype(f32)
        grad = back[...]
        down = upper + norm_gradient(grad, normed, inverse, gain[...])
        grad_mid[...] = down
        sums[0:1, :] = jnp.sum(down, axis=0, keepdims=True)
        sums[1:2, :] = jnp.sum(upper, axis=0, keepdims=True)
        sums[2:3, :] = jnp.sum(grad * normed, axis=0, keepdims=True)
        sums[3:4, :] = jnp.sum(grad, axis=0, keepdims=True)
        low[...] = down.astype(bf16)
        low_t[...] = low[...].T
        cols = att_t.shape[0] // parts
        go_own[...] = nt(low_t[own_rows, :], att_t[...]).astype(bf16)
        go_other[...] = nt(low_t[other_rows, :], att_t[...]).astype(bf16)
        for part in range(parts):
            rows = slice(part * cols, (part + 1) * cols)
            d_att[part][...] = (
                nt(wo_own[rows, :], low[:, own]) + nt(wo_other[rows, :], low[:, other])
            ).astype(bf16)


def middle(place, att, x, cot, wo, fc, dn, b_out, b_fc, b_down, gain, shift):
    parts, half, ffw = fc[0].shape
    sub, width = x.shape
    cols = wo[0].shape[0] // parts
    whole = lambda *dims: pl.BlockSpec(dims, lambda i: (0,) * len(dims))
    each = lambda *dims: pl.BlockSpec((1,) + dims, lambda i: (i, 0, 0))
    once = lambda a: whole(*a.shape)
    return pl.pallas_call(
        functools.partial(middle_kernel, len(att), parts),
        grid=(parts,),
        in_specs=[SM]
        + [once(a) for a in att]
        + [once(x), once(cot), once(wo[0]), once(wo[1])]
        + [each(half, ffw)] * 2
        + [each(ffw, half)] * 2
        + [once(b_out), each(1, ffw), once(b_down), once(gain), once(shift)],
        out_specs=[whole(sub, width), whole(sub, width), whole(4, width), each(1, ffw)]
        + [whole(cols, sub)] * parts
        + [each(half, 2 * ffw)] * 2
        + [whole(half, parts * cols)] * 2,
        out_shape=[
            shape((sub, width)),
            shape((sub, width), f32),
            shape((4, width), f32),
            shape((parts, 1, ffw), f32),
        ]
        + [shape((cols, sub))] * parts
        + [shape((parts, half, 2 * ffw))] * 2
        + [shape((half, parts * cols))] * 2,
        scratch_shapes=[
            pltpu.VMEM((sub, width), f32),
            pltpu.VMEM((parts * cols, sub), bf16),
            pltpu.VMEM((sub, width), bf16),
            pltpu.VMEM((width, sub), bf16),
            pltpu.VMEM((width, sub), bf16),
            pltpu.VMEM((sub, width), f32),
            pltpu.VMEM((sub, width), f32),
        ],
        compiler_params=params(),
        name="middle",
    )(place, *att, x, cot, wo[0], wo[1], fc[0], fc[1], dn[0], dn[1], b_out, b_fc, b_down, gain, shift)


def last_kernel(parts, pieces, sc, *refs):
    grads, refs = refs[: parts * pieces], refs[parts * pieces :]
    w_own, w_other, x, grad_mid, gain, out, sums, back_t, stacked = refs
    half = w_own.shape[1]
    own_rows = pl.ds(pl.multiple_of(sc[2] * half, half), half)
    other_rows = pl.ds(pl.multiple_of((1 - sc[2]) * half, half), half)
    for part in range(parts):
        row = 0
        for n in range(pieces):
            piece = grads[part * pieces + n]
            stacked[row : row + piece.shape[0], :] = piece[...]
            row += piece.shape[0]
        mine, theirs = nn(w_own[part], stacked[...]), nn(w_other[part], stacked[...])
        if part == 0:
            back_t[own_rows, :], back_t[other_rows, :] = mine, theirs
        else:
            back_t[own_rows, :] += mine
            back_t[other_rows, :] += theirs
    back = back_t[...].T
    normed, inverse = norm(x[...].astype(f32))
    out[...] = (grad_mid[...] + norm_gradient(back, normed, inverse, gain[...])).astype(bf16)
    sums[0:1, :] = jnp.sum(back * normed, axis=0, keepdims=True)
    sums[1:2, :] = jnp.sum(back, axis=0, keepdims=True)


def last(place, grads, pieces, w, x, grad_mid, gain):
    parts = w[0].shape[0]
    sub, width = x.shape
    return pl.pallas_call(
        functools.partial(last_kernel, parts, pieces),
        in_specs=[SM] + [VM] * (len(grads) + 5),
        out_specs=[VM, VM],
        out_shape=[shape((sub, width)), shape((2, width), f32)],
        scratch_shapes=[pltpu.VMEM((width, sub), f32), pltpu.VMEM((w[0].shape[2], sub), bf16)],
        compiler_params=params(),
        name="last",
    )(place, *grads, w[0], w[1], x, grad_mid, gain)


def body(
    n_shard,
    n_context,
    n_tensor,
    inputs,
    segments,
    w_qkv,
    w_out,
    w_fc,
    w_down,
    b_qv,
    b_out,
    b_fc,
    b_down,
    first_norm_gain,
    first_norm_bias,
    second_norm_gain,
    second_norm_bias,
    cotangent,
):
    _, tok, width = inputs.shape
    length = segments.shape[1]
    half, _, cols = w_qkv.shape
    heads = cols // HD
    ffw = w_fc.shape[1]
    sub = tok // n_tensor
    context = lax.axis_index("context")
    tensor = lax.axis_index("tensor")
    core = lax.axis_index("shard")
    first = context * tok
    place = jnp.stack([first, context, core, tensor]).astype(jnp.int32)
    grouped = n_context == 4
    x = inputs[0]
    cot = cotangent[0]
    row = lambda v: v[None, :]

    swap = lambda v: lax.ppermute(v, "shard", [(0, 1), (1, 0)])
    along_x = lambda v: lax.ppermute(v, "context", [(0, 1), (1, 0), (2, 3), (3, 2)])
    along_y = lambda v: lax.ppermute(v, "context", [(0, 2), (2, 0), (1, 3), (3, 1)])
    shift_by = lambda v, d: lax.ppermute(
        v, "tensor", [(s, (s + d) % n_tensor) for s in range(n_tensor)]
    )

    def gather_line(v):
        right, left = [v], [v]
        for s in range(1, n_tensor):
            right.append(
                lax.ppermute(
                    right[-1], "tensor", [(d, d + 1) for d in range(s - 1, n_tensor - 1)]
                )
            )
            left.append(
                lax.ppermute(left[-1], "tensor", [(d, d - 1) for d in range(1, n_tensor - s + 1)])
            )
        return [v] + [right[d] + left[n_tensor - d] for d in range(1, n_tensor)]

    def scatter_line(pieces):
        right = left = None
        for s in range(1, n_tensor):
            r, l = pieces[s], pieces[n_tensor - s]
            if s > 1:
                r = (r.astype(f32) + right.astype(f32)).astype(bf16)
                l = (l.astype(f32) + left.astype(f32)).astype(bf16)
            right = lax.ppermute(r, "tensor", [(d, d + 1) for d in range(s)])
            left = lax.ppermute(
                l, "tensor", [(n_tensor - 1 - d, n_tensor - 2 - d) for d in range(s)]
            )
        return pieces[0].astype(f32) + right.astype(f32) + left.astype(f32)

    def scatter_context(v):
        if not grouped:
            return lax.psum_scatter(v, "context", scatter_dimension=1, tiled=True)
        size = v.shape[1] // 4
        block = lambda n: lax.dynamic_slice_in_dim(v, (context ^ n) * size, size, 1)
        own, by_x, by_y, by_both = (block(n) for n in range(4))
        cut = (v.shape[2] // 256) * 128
        lo = lambda a: a[:, :, :cut]
        hi = lambda a: a[:, :, cut:]
        r = along_x(jnp.stack([lo(by_x), lo(by_both)])).astype(f32)
        s = along_y(jnp.stack([hi(by_y), hi(by_both)])).astype(f32)
        r2 = along_y((lo(by_y).astype(f32) + r[1]).astype(bf16)).astype(f32)
        s2 = along_x((hi(by_x).astype(f32) + s[1]).astype(bf16)).astype(f32)
        return jnp.concatenate(
            [lo(own).astype(f32) + r[0] + r2, hi(own).astype(f32) + s[0] + s2], axis=2
        )

    def scatter_weights(mine, theirs):
        both = (mine.astype(f32) + swap(theirs).astype(f32)).astype(bf16)
        return scatter_context(both)

    bounds = [jnp.sum((segments[0] < d).astype(jnp.int32)) for d in range(1, 5)]
    seg = lax.dynamic_slice_in_dim(segments[0], first, tok, 0)
    starts = jnp.zeros_like(seg)
    for d in range(1, 5):
        starts = jnp.where(seg == d, bounds[d - 1], starts)

    def scalars(bk, bq):
        count = tok // bq
        begin = starts.reshape(count, bq)
        base = first + jnp.arange(count, dtype=jnp.int32) * bq
        lo = begin[:, 0] // bk
        diag = base // bk
        end = (base + bq + bk - 1) // bk
        full = jnp.minimum(jnp.maximum((begin[:, -1] + bk - 1) // bk, lo), diag)
        table = jnp.stack([lo, full, diag, end], axis=1).reshape(-1)
        return jnp.concatenate([place, table.astype(jnp.int32)])

    qkv_own = w_qkv.reshape(half, 3 * cols)
    low_one, qt, kt, vt = project(
        place,
        x,
        qkv_own,
        swap(qkv_own),
        b_qv,
        row(first_norm_gain),
        row(first_norm_bias),
    )

    kv = []
    head = 0
    for g in GROUPS:
        rows = slice(head * HD, (head + g) * HD)
        head += g
        k, v = kt[rows], vt[rows]
        if grouped:
            kx, vy, ky, vx = along_x(k), along_y(v), along_y(k), along_x(v)
            kv.append([k, kx, ky, along_y(kx), v, vx, vy, along_x(vy)])
        else:
            kv.append([lax.all_gather(jnp.concatenate([k, v], axis=0), "context", axis=0)])

    def gather_weights(w):
        own = jnp.stack(gather_line(w))
        return own, swap(own)

    wo = tuple(w.reshape(n_tensor * cols, half) for w in gather_weights(w_out))
    fc = gather_weights(w_fc)
    dn = gather_weights(w_down)

    saved = []
    att = [[] for _ in range(n_tensor)]
    head = 0
    for g, held in zip(GROUPS, kv):
        lse, ot, *out = attend(scalars, row(starts), qt, held, head, g, BK_F, BQ_F, n_tensor)
        saved.append((lse, ot))
        att[0].append(out[0])
        for d in range(1, n_tensor):
            att[d].append(shift_by(out[d], d))
        head += g

    x_sub = lax.dynamic_slice_in_dim(x, tensor * sub, sub, 0)
    cot_sub = lax.dynamic_slice_in_dim(cot, tensor * sub, sub, 0)
    qkv = gather_weights(qkv_own)
    fc_bias = [row(b_fc)[None]]
    fc_bias = jnp.concatenate(gather_line(row(b_fc)[None]), axis=0)
    outputs_sub, grad_mid, sums, fc_sums, *rest = middle(
        place,
        [piece for part in att for piece in part],
        x_sub,
        cot_sub,
        wo,
        fc,
        dn,
        row(b_out),
        fc_bias,
        row(b_down),
        row(second_norm_gain),
        row(second_norm_bias),
    )
    d_att, (g_own, g_other, go_own, go_other) = rest[:n_tensor], rest[n_tensor:]
    do_parts = [d_att[0]] + [
        shift_by(d_att[d], -d) for d in range(1, n_tensor)
    ]

    def spread(v):
        pieces = gather_line(v)
        whole = jnp.zeros((tok, width), f32)
        for d in range(n_tensor):
            at = lax.rem(tensor - d + n_tensor, n_tensor) * sub
            whole = lax.dynamic_update_slice_in_dim(whole, pieces[d].astype(f32), at, 0)
        return whole[None]

    ff_grads = scatter_weights(g_own, g_other)
    out_split = lambda v: jnp.stack(jnp.split(v, n_tensor, axis=1))
    out_grads = scatter_weights(out_split(go_own), out_split(go_other))
    ff_grads = scatter_line([ff_grads[d].astype(bf16) for d in range(n_tensor)])
    out_grads = scatter_line([out_grads[d].astype(bf16) for d in range(n_tensor)])
    outputs = spread(outputs_sub)

    dq_pieces, dkv_pieces, dqkv = [], [], []
    head = 0
    queries, keys, values = [], [], []
    sent = [[] for _ in range(n_tensor)]
    for g, held, (lse, ot) in zip(GROUPS, kv, saved):
        out = attend_back(
            scalars, row(starts), qt, lse, ot, do_parts, held, head, g, BK_B, BQ_B
        )
        dq, dkv = out[:n_tensor], out[n_tensor:]
        if grouped:
            dk_keep, dk_send, dv_keep, dv_send = dkv
            r = along_x(dk_send).astype(f32)
            s = along_y(dv_send).astype(f32)
            r2 = along_y((dk_keep[1].astype(f32) + r[1]).astype(bf16)).astype(f32)
            s2 = along_x((dv_keep[1].astype(f32) + s[1]).astype(bf16)).astype(f32)
            dk = (dk_keep[0].astype(f32) + r[0] + r2).astype(bf16)
            dv = (dv_keep[0].astype(f32) + s[0] + s2).astype(bf16)
        else:
            both = lax.psum_scatter(dkv[0], "context", scatter_dimension=0, tiled=True)[0]
            dk, dv = both[: g * HD], both[g * HD :]
        queries.append(dq)
        keys.append(dk)
        values.append(dv)
        head += g

    def part_of(v, d):
        at = lax.rem(tensor + d, n_tensor) * sub
        return lax.dynamic_slice_in_dim(v, at, sub, 1)

    grads = []
    for d in range(n_tensor):
        pieces = [q[d] for q in queries]
        pieces += [part_of(k, d) for k in keys] + [part_of(v, d) for v in values]
        grads += pieces if d == 0 else [shift_by(p, d) for p in pieces]
    pieces = 3 * len(GROUPS)

    dq_whole = []
    for q in queries:
        whole = jnp.zeros((q[0].shape[0], tok), bf16)
        for d in range(n_tensor):
            at = lax.rem(tensor + d, n_tensor) * sub
            whole = lax.dynamic_update_slice_in_dim(whole, q[d], at, 1)
        dq_whole.append(whole)
    stacked = jnp.concatenate(dq_whole + keys + values, axis=0)
    qkv_grad = jnp.einsum("td,ct->dc", low_one, stacked, preferred_element_type=f32).astype(bf16)
    qv_sums = jnp.sum(stacked.astype(f32), axis=1).reshape(3, cols)
    qkv_mine = lax.dynamic_slice_in_dim(qkv_grad, core * half, half, 0)
    qkv_theirs = lax.dynamic_slice_in_dim(qkv_grad, (1 - core) * half, half, 0)

    input_sub, first_sums = last(
        place, grads, pieces, qkv, x_sub, grad_mid, row(first_norm_gain)
    )
    input_gradient = spread(input_sub)
    qkv_grads = scatter_weights(qkv_mine[None], qkv_theirs[None])[0]

    zero_fc = jnp.zeros((n_tensor, ffw), f32)
    for d in range(n_tensor):
        at = lax.rem(tensor - d + n_tensor, n_tensor)
        zero_fc = lax.dynamic_update_slice_in_dim(zero_fc, fc_sums[d], at, 0)
    zero_qv = lax.dynamic_update_slice_in_dim(
        jnp.zeros((n_tensor, 2 * cols), f32),
        jnp.concatenate([qv_sums[0], qv_sums[2]])[None],
        tensor,
        0,
    )
    small = lax.psum(
        jnp.concatenate(
            [sums.reshape(-1), first_sums.reshape(-1), zero_fc.reshape(-1), zero_qv.reshape(-1)]
        ),
        ("shard", "context", "tensor"),
    )
    table = small[: 6 * width].reshape(6, width)
    fc_total = lax.dynamic_slice_in_dim(small, 6 * width + tensor * ffw, ffw, 0)
    qv_total = lax.dynamic_slice_in_dim(
        small, 6 * width + n_tensor * ffw + tensor * 2 * cols, 2 * cols, 0
    ).reshape(2, cols)
    return (
        outputs,
        input_gradient,
        qkv_grads.astype(f32).reshape(-1, 3, cols),
        out_grads.T,
        ff_grads[:, :ffw],
        ff_grads[:, ffw:].T,
        qv_total,
        table[0],
        fc_total,
        table[1],
        table[4],
        table[5],
        table[2],
        table[3],
    )


def solution(mesh):
    sizes = dict(mesh.shape)
    placed = (
        P("shard", "context", None),
        P("shard", None),
        P("shard", None, "tensor"),
        P("tensor", "shard"),
        P("shard", "tensor"),
        P("tensor", "shard"),
        P(None, "tensor"),
        P(),
        P("tensor"),
        P(),
        P(),
        P(),
        P(),
        P(),
        P("shard", "context", None),
    )
    return jax.shard_map(
        functools.partial(body, sizes["shard"], sizes["context"], sizes["tensor"]),
        mesh=mesh,
        in_specs=placed,
        out_specs=(
            P("shard", "context", None),
            P("shard", "context", None),
            P(("shard", "context"), None, "tensor"),
            P("tensor", ("shard", "context")),
            P(("shard", "context"), "tensor"),
            P("tensor", ("shard", "context")),
            P(None, "tensor"),
            P(),
            P("tensor"),
            P(),
            P(),
            P(),
            P(),
            P(),
        ),
        check_vma=False,
    )
```

time: 802 us -> 537 us (0.67)
  waiting for transfers between devices: 451 us -> 143 us
  matrix products: 199 us -> 2.62 us
  starting transfers between devices: 1.33 us -> 173 us
  Pallas kernels: 0 us -> 52.5 us
  blocking collectives: 32 us -> 57.4 us
  between operations: 16.1 us -> 2.85 us
  other arithmetic: 66 us -> 53.5 us
  local copies, waits for them, and re-layouts: 32.8 us -> 44.1 us
    psum x3 -> x0, waiting for transfers between devices: 253 us -> none  [the longest x1 120 us: body(): lax.psum(jnp.einsum('stf,fd->std', act_low, full_down, preferred_element_...]
    dot_general x32 -> x1, matrix products: 194 us -> 2.62 us  [body(): jnp.einsum('td,ct->dc', low_one, stacked, preferred_element_type=f32)]
    ppermute x0 -> x97, starting transfers between devices: none -> 173 us  [the longest x21 44.1 us: gather_line(): lax.ppermute(right[-1], 'tensor', [(d, d + 1) for d in range(s - 1, n_ten...]
    reduce_scatter x5 -> x0, waiting for transfers between devices: 156 us -> none  [the longest x1 46.7 us: body(): lax.psum_scatter(grad_down, ('shard', 'context'), scatter_dimension=1, ti...]
    ppermute x0 -> x97, waiting for transfers between devices: none -> 143 us  [the longest x21 70.8 us: gather_line(): lax.ppermute(left[-1], 'tensor', [(d, d - 1) for d in range(1, n_tensor -...]
    pallas_call x0 -> x5, Pallas kernels: none -> 52.5 us  [the longest x1 18.2 us: middle(): pl.pallas_call(functools.partial(middle_kernel, len(att), parts), grid=(p...]
    reduce_sum x11 -> x2, other arithmetic: 43 us -> 2.7 us  [the longest x1 1.46 us: body(): bounds = [jnp.sum((segments[0] < d).astype(jnp.int32)) for d in range(1, 5)]]
    psum x1, blocking collectives: 27.3 us -> 57.4 us  [body(): lax.psum(jnp.concatenate([sums.reshape(-1), first_sums.reshape(-1), zero_...]
  transfers between devices with their start and end apart: 13 -> 97, of which waited for: 10 -> 25; matrix products, arithmetic and copies ran while one was open for 14% -> 18% of each run, Pallas kernels for 0% -> 10%
where the time goes in v1:
time: 537 us; the launch traced here: 528 us
  starting transfers between devices  173 us (32%)
  waiting for transfers between devices  143 us (27%)
  blocking collectives  57.4 us (11%)
  other arithmetic  53.5 us (10%)
  Pallas kernels  52.5 us (10%)
  local copies, waits for them, and re-layouts  44.1 us (8%)
    ppermute x21, waiting for transfers between devices, gather_line(): lax.ppermute(left[-1], 'tensor', [(d, d - 1) for d in range(1, n_tensor -...  70.8 us
    psum x1, blocking collectives, body(): lax.psum(jnp.concatenate([sums.reshape(-1), first_sums.reshape(-1), zero_...  57.4 us
    ppermute x21, starting transfers between devices, gather_line(): lax.ppermute(right[-1], 'tensor', [(d, d + 1) for d in range(s - 1, n_ten...  44.1 us
    ppermute x10, waiting for transfers between devices, body(): lax.ppermute(v, 'context', [(0, 1), (1, 0), (2, 3), (3, 2)])  35.3 us
    ppermute x10, starting transfers between devices, body(): lax.ppermute(v, 'context', [(0, 2), (2, 0), (1, 3), (3, 1)])  35 us
    ppermute x6, starting transfers between devices, scatter_line(): right = lax.ppermute(r, 'tensor', [(d, d + 1) for d in range(s)])  27.8 us
    ppermute x21, starting transfers between devices, gather_line(): lax.ppermute(left[-1], 'tensor', [(d, d - 1) for d in range(1, n_tensor -...  27.2 us
    ppermute x15, starting transfers between devices, body(): lax.ppermute(v, 'tensor', [(s, (s + d) % n_tensor) for s in range(n_tenso...  20.9 us
  transfers between devices with their start and end apart: 97, of which 25 were waited for; matrix products, arithmetic and copies ran while one was open for 18% of the time, Pallas kernels for 10%

profile of v1, /device:TPU:0, one launch (start us, length us, event | category | flops | bytes accessed | tf_op | source)
XLA Modules:
  0.0 528.4 jit_solution(4335709200618268238)
XLA Ops:
  0.7 5.9 %collective-permute-start.17 = (bf16[384,768]{1,0:T(8,128)(2,1)}, bf16[384,768]{1,0:T(8,128)(2,1)}, u32[]{:S(2)}, u32[]{:S(2)}) collective-permute-start(bf16[384,768]{1,0:T(8,128)(2,1)} %param.19), channel_id=1, source_target_pairs={{0,1},{1,2},{2,3},{4,5},{5,6},{6,7},{8,9},{9,10},{10,11},{12,13},{... | collective-permute-start | bytes 1769480 | tf_op jit(solution)/shard_map/ppermute | solution.py:549
  10.4 5.8 %collective-permute-start.24 = (bf16[768,384]{1,0:T(8,128)(2,1)}, bf16[768,384]{1,0:T(8,128)(2,1)S(1)}, u32[]{:S(2)}, u32[]{:S(2)}) collective-permute-start(bf16[768,384]{1,0:T(8,128)(2,1)} %param.20), channel_id=1, source_target_pairs={{0,1},{1,2},{2,3},{4,5},{5,6},{6,7},{8,9},{9,10},{10,11},{12,13},{... | collective-permute-start | bytes 1769480 | tf_op jit(solution)/shard_map/ppermute | solution.py:549
  16.3 11.8 %collective-permute-done.11 = bf16[192,384]{1,0:T(8,128)(2,1)S(1)} collective-permute-done((bf16[192,384]{1,0:T(8,128)(2,1)}, bf16[192,384]{1,0:T(8,128)(2,1)S(1)}, u32[]{:S(2)}, u32[]{:S(2)}) %collective-permute-start.11) | collective-permute-done | bytes 147488 | tf_op jit(solution)/shard_map/ppermute | solution.py:554
  28.1 2.7 collective-permute-start.10
  32.2 2.2 collective-permute-done.10
  35.7 6.7 %collective-permute-done.12 = bf16[192,384]{1,0:T(8,128)(2,1)S(1)} collective-permute-done((bf16[192,384]{1,0:T(8,128)(2,1)S(1)}, bf16[192,384]{1,0:T(8,128)(2,1)S(1)}, u32[]{:S(2)}, u32[]{:S(2)}) %collective-permute-start.12) | collective-permute-done | bytes 147488 | tf_op jit(solution)/shard_map/ppermute | solution.py:554
  49.6 2.0 copy.44
  53.5 4.5 fusion.44
  64.3 6.4 %project.1 = (bf16[1024,768]{1,0:T(8,128)(2,1)}, bf16[192,1024]{1,0:T(8,128)(2,1)}, bf16[192,1024]{1,0:T(8,128)(2,1)}, bf16[192,1024]{1,0:T(8,128)(2,1)}) custom-call(s32[4]{0:T(128)} %pad_add_fusion.1.sc, bf16[1024,768]{1,0:T(8,128)(2,1)} %bitcast.237, bf16[384,576]{1,0:T(8,128)(2,1)} %copy-done.7, bf16[384,576]{1,0:T(8,128)(2,1)} %collective-permute-done.w_other, ...), custom_call_target="tpu_custom_call" | custom-call | tf_op jit(solution)/shard_map/project/pallas_call | solution.py:84
  73.4 4.0 collective-permute-done.26
  77.3 6.1 %collective-permute-start.59 = (bf16[384,576]{1,0:T(8,128)(2,1)}, bf16[384,576]{1,0:T(8,128)(2,1)S(1)}, u32[]{:S(2)}, u32[]{:S(2)}) collective-permute-start(bf16[384,576]{1,0:T(8,128)(2,1)} %copy-done.7), channel_id=1, source_target_pairs={{0,1},{1,2},{2,3},{4,5},{5,6},{6,7},{8,9},{9,10},{10,11},{12,13},{... | collective-permute-start | bytes 1327112 | tf_op jit(solution)/shard_map/ppermute | solution.py:549
  86.6 13.8 %collective-permute-done.32 = f32[1,1,768]{2,1,0:T(1,128)S(1)} collective-permute-done((f32[1,1,768]{2,1,0:T(1,128)S(1)}, f32[1,1,768]{2,1,0:T(1,128)S(1)}, u32[]{:S(2)}, u32[]{:S(2)}) %collective-permute-start.32) | collective-permute-done | bytes 3104 | tf_op jit(solution)/shard_map/ppermute | solution.py:554
  109.4 19.9 %collective-permute-done.33 = f32[1,1,768]{2,1,0:T(1,128)S(1)} collective-permute-done((f32[1,1,768]{2,1,0:T(1,128)S(1)}, f32[1,1,768]{2,1,0:T(1,128)S(1)}, u32[]{:S(2)}, u32[]{:S(2)}) %collective-permute-start.33) | collective-permute-done | bytes 3104 | tf_op jit(solution)/shard_map/ppermute | solution.py:554
  138.1 11.0 %collective-permute-done.13 = bf16[192,384]{1,0:T(8,128)(2,1)S(1)} collective-permute-done((bf16[192,384]{1,0:T(8,128)(2,1)S(1)}, bf16[192,384]{1,0:T(8,128)(2,1)S(1)}, u32[]{:S(2)}, u32[]{:S(2)}) %collective-permute-start.13) | collective-permute-done | bytes 147488 | tf_op jit(solution)/shard_map/ppermute | solution.py:554
  153.1 2.6 copy.45
  155.7 2.6 collective-permute-done.1.refs_1_.refs_5_
  159.8 8.4 %collective-permute-done.5.refs_6_.refs_10_ = bf16[192,1024]{1,0:T(8,128)(2,1)} collective-permute-done((bf16[192,1024]{1,0:T(8,128)(2,1)}, bf16[192,1024]{1,0:T(8,128)(2,1)}, u32[]{:S(2)}, u32[]{:S(2)}) %collective-permute-start.5) | collective-permute-done | bytes 393248 | tf_op jit(solution)/shard_map/ppermute | solution.py:540
  171.8 1.9 pad_maximum_fusion.7
  178.9 7.4 %collective-permute-done.6.refs_7_.refs_11_ = bf16[192,1024]{1,0:T(8,128)(2,1)S(1)} collective-permute-done((bf16[192,1024]{1,0:T(8,128)(2,1)}, bf16[192,1024]{1,0:T(8,128)(2,1)S(1)}, u32[]{:S(2)}, u32[]{:S(2)}) %collective-permute-start.6) | collective-permute-done | bytes 393248 | tf_op jit(solution)/shard_map/ppermute | solution.py:539
  191.6 9.6 %attend.1 = (f32[3,1024]{1,0:T(4,128)}, bf16[192,1024]{1,0:T(8,128)(2,1)}, bf16[192,256]{1,0:T(8,128)(2,1)}, bf16[192,256]{1,0:T(8,128)(2,1)}, bf16[192,256]{1,0:T(8,128)(2,1)}, /*index=5*/bf16[192,256]{1,0:T(8,128)(2,1)}) custom-call(s32[12]{0:T(128)} %concatenate.24.sc, bf16[192,1024]{1,0:T(8,128)(2,1)} %get-tuple-element.46.qt, ...), custom_call_target="tpu_custom_call" | custom-call | tf_op jit(solution)/shard_map/attend/pallas_call | solution.py:211
  202.2 1.9 collective-permute-start.8
  204.1 4.3 collective-permute-done.7.refs_1_
  209.0 1.9 collective-permute-done.8.refs_2_
  210.9 2.3 collective-permute-done.9.refs_3_
  213.8 18.2 %middle.1 = (bf16[256,768]{1,0:T(8,128)(2,1)}, f32[256,768]{1,0:T(8,128)}, f32[4,768]{1,0:T(4,128)}, f32[4,1,768]{2,1,0:T(1,128)}, bf16[192,256]{1,0:T(8,128)(2,...) custom-call(s32[4]{0:T(128)} %pad_add_fusion.1.sc, ...), custom_call_target="tpu_custom_call" | custom-call | tf_op jit(solution)/shard_map/middle/pallas_call | solution.py:427
  234.7 3.9 copy.46.refs_13_
  241.3 1.9 broadcast_in_dim.91.clone
  244.8 12.4 %collective-permute-start.78 = (bf16[2,4,96,192]{3,2,1,0:T(8,128)(2,1)S(1)}, bf16[2,4,96,192]{3,2,1,0:T(8,128)(2,1)S(1)}, u32[]{:S(2)}, u32[]{:S(2)}) collective-permute-start(bf16[2,4,96,192]{3,2,1,0:T(8,128)(2,1)S(1)} %pad_maximum_fusion.9), channel_id=1, source_target_pairs={{0,8},{8,0},{4,12},{12,4},{1,9},{9,1},{5,13},{13,5},{2,10},{10,2},... | collective-permute-start | bytes 884744 | tf_op jit(solution)/shard_map/ppermute | solution.py:540
  259.4 4.6 collective-permute-start.37
  264.0 12.7 %attend_back.1 = (bf16[192,256]{1,0:T(8,128)(2,1)}, bf16[192,256]{1,0:T(8,128)(2,1)}, bf16[192,256]{1,0:T(8,128)(2,1)}, bf16[192,256]{1,0:T(8,128)(2,1)}, bf16[2...) custom-call(s32[12]{0:T(128)} %concatenate.24.sc, ...), custom_call_target="tpu_custom_call" | custom-call | tf_op jit(solution)/shard_map/attend_back/pallas_call | solution.py:316
  276.7 12.8 %collective-permute-start.48 = (bf16[2,192,1024]{2,1,0:T(8,128)(2,1)}, bf16[2,192,1024]{2,1,0:T(8,128)(2,1)S(1)}, u32[]{:S(2)}, u32[]{:S(2)}) collective-permute-start(bf16[2,192,1024]{2,1,0:T(8,128)(2,1)} %get-tuple-element.64), channel_id=1, source_target_pairs={{0,8},{8,0},{4,12},{12,4},{1,9},{9,1},{5,13},{13,5},{2,10},{10,2},... | collective-permute-start | bytes 2359304 | tf_op jit(solution)/shard_map/ppermute | solution.py:540
  295.3 2.5 collective-permute-done.79
  297.9 3.3 collective-permute-start.80
  301.2 4.9 collective-permute-done.48
  310.0 4.5 collective-permute-start.81
  316.1 3.6 collective-permute-done.39
  322.7 5.8 %collective-permute-start.82 = (bf16[96,192]{1,0:T(8,128)(2,1)S(1)}, bf16[96,192]{1,0:T(8,128)(2,1)S(1)}, u32[]{:S(2)}, u32[]{:S(2)}) collective-permute-start(bf16[96,192]{1,0:T(8,128)(2,1)S(1)} %get-tuple-element.163), channel_id=1, source_target_pairs={{0,1},{1,2},{2,3},{4,5},{5,6},{6,7},{8,9},{9,10},{10,11},{12,13},{... | collective-permute-start | bytes 110600 | tf_op jit(solution)/shard_map/ppermute | solution.py:565
  330.6 2.6 collective-permute-start.50
  337.2 2.1 convert_dynamic-update-slice_fusion.6
  339.3 2.1 convert_dynamic-update-slice_fusion.5
  343.1 5.1 add_convert_fusion
  348.5 2.0 collective-permute-start.87
  350.6 2.0 convert_dynamic-update-slice_fusion.4
  355.7 16.4 %collective-permute-done.87 = bf16[2,4,96,768]{3,2,1,0:T(8,128)(2,1)S(1)} collective-permute-done((bf16[2,4,96,768]{3,2,1,0:T(8,128)(2,1)S(1)}, bf16[2,4,96,768]{3,2,1,0:T(8,128)(2,1)S(1)}, u32[]{:S(2)}, u32[]{:S(2)}) %collective-permute-start.87) | collective-permute-done | bytes 1179680 | tf_op jit(solution)/shard_map/ppermute | solution.py:539
  375.6 2.6 convolution_convert_fusion
  378.2 1.9 collective-permute-start.55
  380.9 2.9 collective-permute-start.58
  383.8 3.5 collective-permute-start.54
  387.4 4.0 collective-permute-start.57
  394.2 5.7 %last.1 = (bf16[256,768]{1,0:T(8,128)(2,1)}, f32[2,768]{1,0:T(2,128)}) custom-call(s32[4]{0:T(128)} %pad_add_fusion.1.sc, bf16[192,256]{1,0:T(8,128)(2,1)} %get-tuple-element.60.refs_0_, bf16[192,256]{1,0:T(8,128)(2,1)} %get-tuple-element.162.refs_1_, bf16[192,256]{1,0:T(8,128)(2,1)} %get-tuple-element.158.refs_2_, ...), custom_call_target="tpu_custom_call" | custom-call | tf_op jit(solution)/shard_map/last/pallas_call | solution.py:491
  401.2 5.3 %collective-permute-start.66 = (bf16[256,768]{1,0:T(8,128)(2,1)}, bf16[256,768]{1,0:T(8,128)(2,1)}, u32[]{:S(2)}, u32[]{:S(2)}) collective-permute-start(bf16[256,768]{1,0:T(8,128)(2,1)} %get-tuple-element.69), channel_id=1, source_target_pairs={{0,1},{1,2},{2,3},{4,5},{5,6},{6,7},{8,9},{9,10},{10,11},{12,13},{... | collective-permute-start | bytes 1179656 | tf_op jit(solution)/shard_map/ppermute | solution.py:549
  407.2 2.0 fusion.7
  411.6 57.4 %psum.7 = f32[9216]{0:T(1024)S(1)} all-reduce(f32[9216]{0:T(1024)S(1)} %pad_maximum_fusion.13), channel_id=1, replica_groups=mesh['shard'=2,'context'=4,'tensor'=4] {'shard','context','tensor'}, use_global_device_ids=true, to_apply=%region_5.6 | all-reduce | flops 9216 | bytes 73728 | tf_op jit(solution)/shard_map/psum | solution.py:755
  470.7 1.9 fusion.8
  472.8 2.3 collective-permute-start.73
  476.8 2.1 collective-permute-start.75
  483.1 2.0 collective-permute-start.76
  485.1 6.4 %collective-permute-done.90 = bf16[4,96,768]{2,1,0:T(8,128)(2,1)S(1)} collective-permute-done((bf16[4,96,768]{2,1,0:T(8,128)(2,1)S(1)}, bf16[4,96,768]{2,1,0:T(8,128)(2,1)S(1)}, u32[]{:S(2)}, u32[]{:S(2)}) %collective-permute-start.90) | collective-permute-done | bytes 589856 | tf_op jit(solution)/shard_map/ppermute | solution.py:539
  497.1 2.0 collective-permute-done.91
  500.0 4.4 collective-permute-start.92
  507.3 2.0 convert_dynamic-update-slice_fusion.2
  510.4 8.0 %collective-permute-start.93 = (bf16[96,1536]{1,0:T(8,128)(2,1)S(1)}, bf16[96,1536]{1,0:T(8,128)(2,1)S(1)}, u32[]{:S(2)}, u32[]{:S(2)}) collective-permute-start(bf16[96,1536]{1,0:T(8,128)(2,1)S(1)} %get-tuple-element.133), channel_id=1, source_target_pairs={{0,1},{1,2},{2,3},{4,5},{5,6},{6,7},{8,9},{9,10},{10,11},{12,13},{... | collective-permute-start | bytes 884744 | tf_op jit(solution)/shard_map/ppermute | solution.py:565
  520.7 2.0 convert_dynamic-update-slice_fusion
  522.6 4.4 collective-permute-done.96
  (387 shorter events, 133.8 us)
Async XLA Ops:
  0.7 30.1 %collective-permute-start.17 = (bf16[384,768]{1,0:T(8,128)(2,1)}, bf16[384,768]{1,0:T(8,128)(2,1)}, u32[]{:S(2)}, u32[]{:S(2)}) collective-permute-start(bf16[384,768]{1,0:T(8,128)(2,1)} %param.19), channel_id=1, source_target_pairs={{0,1},{1,2},{2,3},{4,5},{5,6},{6,7},{8,9},{9,10},{10,11},{12,13},{... | collective-permute-start | bytes 1769480 | tf_op jit(solution)/shard_map/ppermute | solution.py:549
  6.6 37.2 %collective-permute-start.18 = (bf16[384,768]{1,0:T(8,128)(2,1)}, bf16[384,768]{1,0:T(8,128)(2,1)}, u32[]{:S(2)}, u32[]{:S(2)}) collective-permute-start(bf16[384,768]{1,0:T(8,128)(2,1)} %param.19), channel_id=1, source_target_pairs={{1,0},{2,1},{3,2},{5,4},{6,5},{7,6},{9,8},{10,9},{11,10},{13,12},{... | collective-permute-start | bytes 1769480 | tf_op jit(solution)/shard_map/ppermute | solution.py:554
  7.8 20.2 %collective-permute-start.11 = (bf16[192,384]{1,0:T(8,128)(2,1)}, bf16[192,384]{1,0:T(8,128)(2,1)S(1)}, u32[]{:S(2)}, u32[]{:S(2)}) collective-permute-start(bf16[192,384]{1,0:T(8,128)(2,1)} %param.18), channel_id=1, source_target_pairs={{1,0},{2,1},{3,2},{5,4},{6,5},{7,6},{9,8},{10,9},{11,10},{13,12},{... | collective-permute-start | bytes 442376 | tf_op jit(solution)/shard_map/ppermute | solution.py:554
  9.1 48.9 %collective-permute-start.25 = (bf16[768,384]{1,0:T(8,128)(2,1)}, bf16[768,384]{1,0:T(8,128)(2,1)S(1)}, u32[]{:S(2)}, u32[]{:S(2)}) collective-permute-start(bf16[768,384]{1,0:T(8,128)(2,1)} %param.20), channel_id=1, source_target_pairs={{1,0},{2,1},{3,2},{5,4},{6,5},{7,6},{9,8},{10,9},{11,10},{13,12},{... | collective-permute-start | bytes 1769480 | tf_op jit(solution)/shard_map/ppermute | solution.py:554
  10.4 48.9 %collective-permute-start.24 = (bf16[768,384]{1,0:T(8,128)(2,1)}, bf16[768,384]{1,0:T(8,128)(2,1)S(1)}, u32[]{:S(2)}, u32[]{:S(2)}) collective-permute-start(bf16[768,384]{1,0:T(8,128)(2,1)} %param.20), channel_id=1, source_target_pairs={{0,1},{1,2},{2,3},{4,5},{5,6},{6,7},{8,9},{9,10},{10,11},{12,13},{... | collective-permute-start | bytes 1769480 | tf_op jit(solution)/shard_map/ppermute | solution.py:549
  30.8 30.0 %collective-permute-start.21 = (bf16[384,768]{1,0:T(8,128)(2,1)}, bf16[384,768]{1,0:T(8,128)(2,1)}, u32[]{:S(2)}, u32[]{:S(2)}) collective-permute-start(bf16[384,768]{1,0:T(8,128)(2,1)} %collective-permute-done.17), channel_id=1, source_target_pairs={{1,2},{2,3},{5,6},{6,7},{9,10},{10,11},{13,14},{14,15},{17,18},{18... | collective-permute-start | bytes 1769480 | tf_op jit(solution)/shard_map/ppermute | solution.py:549
  43.7 27.0 %collective-permute-start.19 = (bf16[384,768]{1,0:T(8,128)(2,1)}, bf16[384,768]{1,0:T(8,128)(2,1)}, u32[]{:S(2)}, u32[]{:S(2)}) collective-permute-start(bf16[384,768]{1,0:T(8,128)(2,1)} %collective-permute-done.18), channel_id=1, source_target_pairs={{1,0},{2,1},{5,4},{6,5},{9,8},{10,9},{13,12},{14,13},{17,16},{18,1... | collective-permute-start | bytes 1769480 | tf_op jit(solution)/shard_map/ppermute | solution.py:554
  58.1 19.3 %collective-permute-start.26 = (bf16[768,384]{1,0:T(8,128)(2,1)S(1)}, bf16[768,384]{1,0:T(8,128)(2,1)S(1)}, u32[]{:S(2)}, u32[]{:S(2)}) collective-permute-start(bf16[768,384]{1,0:T(8,128)(2,1)S(1)} %collective-permute-done.25), channel_id=1, source_target_pairs={{1,0},{2,1},{5,4},{6,5},{9,8},{10,9},{13,12},{14,13},{17,16},{18,1... | collective-permute-start | bytes 1769480 | tf_op jit(solution)/shard_map/ppermute | solution.py:554
  59.4 24.0 %collective-permute-start.28 = (bf16[768,384]{1,0:T(8,128)(2,1)S(1)}, bf16[768,384]{1,0:T(8,128)(2,1)S(1)}, u32[]{:S(2)}, u32[]{:S(2)}) collective-permute-start(bf16[768,384]{1,0:T(8,128)(2,1)S(1)} %collective-permute-done.24), channel_id=1, source_target_pairs={{1,2},{2,3},{5,6},{6,7},{9,10},{10,11},{13,14},{14,15},{17,18},{18... | collective-permute-start | bytes 1769480 | tf_op jit(solution)/shard_map/ppermute | solution.py:549
  60.8 24.0 %collective-permute-start.22 = (bf16[384,768]{1,0:T(8,128)(2,1)}, bf16[384,768]{1,0:T(8,128)(2,1)S(1)}, u32[]{:S(2)}, u32[]{:S(2)}) collective-permute-start(bf16[384,768]{1,0:T(8,128)(2,1)} %collective-permute-done.21), channel_id=1, source_target_pairs={{2,3},{6,7},{10,11},{14,15},{18,19},{22,23},{26,27},{30,31}} | collective-permute-start | bytes 1769480 | tf_op jit(solution)/shard_map/ppermute | solution.py:549
  63.0 38.9 %collective-permute-start.60 = (bf16[384,576]{1,0:T(8,128)(2,1)S(1)}, bf16[384,576]{1,0:T(8,128)(2,1)S(1)}, u32[]{:S(2)}, u32[]{:S(2)}) collective-permute-start(bf16[384,576]{1,0:T(8,128)(2,1)S(1)} %copy.41.w_own), channel_id=1, source_target_pairs={{1,0},{2,1},{3,2},{5,4},{6,5},{7,6},{9,8},{10,9},{11,10},{13,12},{... | collective-permute-start | bytes 1327112 | tf_op jit(solution)/shard_map/ppermute | solution.py:554
  70.7 33.2 %collective-permute-start.20 = (bf16[384,768]{1,0:T(8,128)(2,1)}, bf16[384,768]{1,0:T(8,128)(2,1)S(1)}, u32[]{:S(2)}, u32[]{:S(2)}) collective-permute-start(bf16[384,768]{1,0:T(8,128)(2,1)} %collective-permute-done.19), channel_id=1, source_target_pairs={{1,0},{5,4},{9,8},{13,12},{17,16},{21,20},{25,24},{29,28}} | collective-permute-start | bytes 1769480 | tf_op jit(solution)/shard_map/ppermute | solution.py:554
  77.3 25.9 %collective-permute-start.59 = (bf16[384,576]{1,0:T(8,128)(2,1)}, bf16[384,576]{1,0:T(8,128)(2,1)S(1)}, u32[]{:S(2)}, u32[]{:S(2)}) collective-permute-start(bf16[384,576]{1,0:T(8,128)(2,1)} %copy-done.7), channel_id=1, source_target_pairs={{0,1},{1,2},{2,3},{4,5},{5,6},{6,7},{8,9},{9,10},{10,11},{12,13},{... | collective-permute-start | bytes 1327112 | tf_op jit(solution)/shard_map/ppermute | solution.py:549
  83.4 17.0 %collective-permute-start.32 = (f32[1,1,768]{2,1,0:T(1,128)S(1)}, f32[1,1,768]{2,1,0:T(1,128)S(1)}, u32[]{:S(2)}, u32[]{:S(2)}) collective-permute-start(f32[1,1,768]{2,1,0:T(1,128)S(1)} %broadcast_in_dim_broadcast_in_dim.3), channel_id=1, source_target_pairs={{1,0},{2,1},{3,2},{5,4},{6,5},{7,6},{9,8},{10,9},{11,10},{13,12},{... | collective-permute-start | bytes 9224 | tf_op jit(solution)/shard_map/ppermute | solution.py:554
  84.8 47.2 %collective-permute-start.29 = (bf16[768,384]{1,0:T(8,128)(2,1)S(1)}, bf16[768,384]{1,0:T(8,128)(2,1)S(1)}, u32[]{:S(2)}, u32[]{:S(2)}) collective-permute-start(bf16[768,384]{1,0:T(8,128)(2,1)S(1)} %collective-permute-done.28), channel_id=1, source_target_pairs={{2,3},{6,7},{10,11},{14,15},{18,19},{22,23},{26,27},{30,31}} | collective-permute-start | bytes 1769480 | tf_op jit(solution)/shard_map/ppermute | solution.py:549
  101.9 28.1 %collective-permute-start.61 = (bf16[384,576]{1,0:T(8,128)(2,1)S(1)}, bf16[384,576]{1,0:T(8,128)(2,1)S(1)}, u32[]{:S(2)}, u32[]{:S(2)}) collective-permute-start(bf16[384,576]{1,0:T(8,128)(2,1)S(1)} %collective-permute-done.60), channel_id=1, source_target_pairs={{1,0},{2,1},{5,4},{6,5},{9,8},{10,9},{13,12},{14,13},{17,16},{18,1... | collective-permute-start | bytes 1327112 | tf_op jit(solution)/shard_map/ppermute | solution.py:554
  103.2 28.1 %collective-permute-start.63 = (bf16[384,576]{1,0:T(8,128)(2,1)S(1)}, bf16[384,576]{1,0:T(8,128)(2,1)S(1)}, u32[]{:S(2)}, u32[]{:S(2)}) collective-permute-start(bf16[384,576]{1,0:T(8,128)(2,1)S(1)} %collective-permute-done.59), channel_id=1, source_target_pairs={{1,2},{2,3},{5,6},{6,7},{9,10},{10,11},{13,14},{14,15},{17,18},{18... | collective-permute-start | bytes 1327112 | tf_op jit(solution)/shard_map/ppermute | solution.py:549
  103.9 29.5 %collective-permute-start.27 = (bf16[768,384]{1,0:T(8,128)(2,1)S(1)}, bf16[768,384]{1,0:T(8,128)(2,1)S(1)}, u32[]{:S(2)}, u32[]{:S(2)}) collective-permute-start(bf16[768,384]{1,0:T(8,128)(2,1)S(1)} %collective-permute-done.26), channel_id=1, source_target_pairs={{1,0},{5,4},{9,8},{13,12},{17,16},{21,20},{25,24},{29,28}} | collective-permute-start | bytes 1769480 | tf_op jit(solution)/shard_map/ppermute | solution.py:554
  106.4 23.0 %collective-permute-start.33 = (f32[1,1,768]{2,1,0:T(1,128)S(1)}, f32[1,1,768]{2,1,0:T(1,128)S(1)}, u32[]{:S(2)}, u32[]{:S(2)}) collective-permute-start(f32[1,1,768]{2,1,0:T(1,128)S(1)} %collective-permute-done.32), channel_id=1, source_target_pairs={{1,0},{2,1},{5,4},{6,5},{9,8},{10,9},{13,12},{14,13},{17,16},{18,1... | collective-permute-start | bytes 9224 | tf_op jit(solution)/shard_map/ppermute | solution.py:554
  132.0 20.0 %collective-permute-start.62 = (bf16[384,576]{1,0:T(8,128)(2,1)S(1)}, bf16[384,576]{1,0:T(8,128)(2,1)S(1)}, u32[]{:S(2)}, u32[]{:S(2)}) collective-permute-start(bf16[384,576]{1,0:T(8,128)(2,1)S(1)} %collective-permute-done.61), channel_id=1, source_target_pairs={{1,0},{5,4},{9,8},{13,12},{17,16},{21,20},{25,24},{29,28}} | collective-permute-start | bytes 1327112 | tf_op jit(solution)/shard_map/ppermute | solution.py:554
  133.4 79.8 %collective-permute-start.23 = (bf16[4,384,768]{2,1,0:T(8,128)(2,1)}, bf16[4,384,768]{2,1,0:T(8,128)(2,1)}, u32[]{:S(2)}, u32[]{:S(2)}) collective-permute-start(bf16[4,384,768]{2,1,0:T(8,128)(2,1)} %pad_maximum_fusion.refs_8_), channel_id=1, source_target_pairs={{0,16},{16,0},{1,17},{17,1},{2,18},{18,2},{3,19},{19,3},{4,20},{20... | collective-permute-start | bytes 7077896 | tf_op jit(solution)/shard_map/ppermute | solution.py:538
  135.4 77.8 %collective-permute-start.30 = (bf16[4,768,384]{2,1,0:T(8,128)(2,1)}, bf16[4,768,384]{2,1,0:T(8,128)(2,1)}, u32[]{:S(2)}, u32[]{:S(2)}) collective-permute-start(bf16[4,768,384]{2,1,0:T(8,128)(2,1)} %pad_maximum_fusion.1.refs_10_), channel_id=1, source_target_pairs={{0,16},{16,0},{1,17},{17,1},{2,18},{18,2},{3,19},{19,3},{4,20},{20... | collective-permute-start | bytes 7077896 | tf_op jit(solution)/shard_map/ppermute | solution.py:538
  136.0 13.0 %collective-permute-start.13 = (bf16[192,384]{1,0:T(8,128)(2,1)S(1)}, bf16[192,384]{1,0:T(8,128)(2,1)S(1)}, u32[]{:S(2)}, u32[]{:S(2)}) collective-permute-start(bf16[192,384]{1,0:T(8,128)(2,1)S(1)} %copy-done.28), channel_id=1, source_target_pairs={{1,0},{5,4},{9,8},{13,12},{17,16},{21,20},{25,24},{29,28}} | collective-permute-start | bytes 442376 | tf_op jit(solution)/shard_map/ppermute | solution.py:554
  137.4 13.2 %collective-permute-start.15 = (bf16[192,384]{1,0:T(8,128)(2,1)S(1)}, bf16[192,384]{1,0:T(8,128)(2,1)S(1)}, u32[]{:S(2)}, u32[]{:S(2)}) collective-permute-start(bf16[192,384]{1,0:T(8,128)(2,1)S(1)} %collective-permute-done.14), channel_id=1, source_target_pairs={{2,3},{6,7},{10,11},{14,15},{18,19},{22,23},{26,27},{30,31}} | collective-permute-start | bytes 442376 | tf_op jit(solution)/shard_map/ppermute | solution.py:549
  150.6 19.2 %collective-permute-start.2 = (bf16[192,1024]{1,0:T(8,128)(2,1)}, bf16[192,1024]{1,0:T(8,128)(2,1)}, u32[]{:S(2)}, u32[]{:S(2)}) collective-permute-start(bf16[192,1024]{1,0:T(8,128)(2,1)} %get-tuple-element.47.refs_0_.refs_4_), channel_id=1, source_target_pairs={{0,8},{8,0},{4,12},{12,4},{1,9},{9,1},{5,13},{13,5},{2,10},{10,2},... | collective-permute-start | bytes 1179656 | tf_op jit(solution)/shard_map/ppermute | solution.py:540
  152.1 16.2 %collective-permute-start.5 = (bf16[192,1024]{1,0:T(8,128)(2,1)}, bf16[192,1024]{1,0:T(8,128)(2,1)}, u32[]{:S(2)}, u32[]{:S(2)}) collective-permute-start(bf16[192,1024]{1,0:T(8,128)(2,1)} %get-tuple-element.48.refs_4_.refs_8_), channel_id=1, source_target_pairs={{0,8},{8,0},{4,12},{12,4},{1,9},{9,1},{5,13},{13,5},{2,10},{10,2},... | collective-permute-start | bytes 1179656 | tf_op jit(solution)/shard_map/ppermute | solution.py:540
  158.3 15.4 %collective-permute-start.4 = (bf16[192,1024]{1,0:T(8,128)(2,1)}, bf16[192,1024]{1,0:T(8,128)(2,1)S(1)}, u32[]{:S(2)}, u32[]{:S(2)}) collective-permute-start(bf16[192,1024]{1,0:T(8,128)(2,1)} %get-tuple-element.48.refs_4_.refs_8_), channel_id=1, source_target_pairs={{0,4},{4,0},{8,12},{12,8},{1,5},{5,1},{9,13},{13,9},{2,6},{6,2},{1... | collective-permute-start | bytes 1179656 | tf_op jit(solution)/shard_map/ppermute | solution.py:539
  169.8 64.9 %collective-permute-start.65 = (bf16[4,384,576]{1,2,0:T(8,128)(2,1)}, bf16[4,384,576]{1,2,0:T(8,128)(2,1)}, u32[]{:S(2)}, u32[]{:S(2)}) collective-permute-start(bf16[4,384,576]{1,2,0:T(8,128)(2,1)} %copy.45), channel_id=1, source_target_pairs={{0,16},{16,0},{1,17},{17,1},{2,18},{18,2},{3,19},{19,3},{4,20},{20... | collective-permute-start | bytes 5308424 | tf_op jit(solution)/shard_map/ppermute | solution.py:538
  174.5 27.7 %collective-permute-start.16 = (bf16[4,192,384]{2,1,0:T(8,128)(2,1)}, bf16[4,192,384]{2,1,0:T(8,128)(2,1)S(1)}, u32[]{:S(2)}, u32[]{:S(2)}) collective-permute-start(bf16[4,192,384]{2,1,0:T(8,128)(2,1)} %pad_maximum_fusion.7), channel_id=1, source_target_pairs={{0,16},{16,0},{1,17},{17,1},{2,18},{18,2},{3,19},{19,3},{4,20},{20... | collective-permute-start | bytes 1769480 | tf_op jit(solution)/shard_map/ppermute | solution.py:538
  186.2 15.0 %collective-permute-start.36 = (f32[1,1,768]{2,1,0:T(1,128)}, f32[1,1,768]{2,1,0:T(1,128)S(1)}, u32[]{:S(2)}, u32[]{:S(2)}) collective-permute-start(f32[1,1,768]{2,1,0:T(1,128)} %copy-done.54), channel_id=1, source_target_pairs={{2,3},{6,7},{10,11},{14,15},{18,19},{22,23},{26,27},{30,31}} | collective-permute-start | bytes 9224 | tf_op jit(solution)/shard_map/ppermute | solution.py:549
  232.0 109.3 %collective-permute-start.86 = (bf16[4,384,1536]{2,1,0:T(8,128)(2,1)}, bf16[4,384,1536]{2,1,0:T(8,128)(2,1)}, u32[]{:S(2)}, u32[]{:S(2)}) collective-permute-start(bf16[4,384,1536]{2,1,0:T(8,128)(2,1)} %get-tuple-element.74), channel_id=1, source_target_pairs={{0,16},{16,0},{1,17},{17,1},{2,18},{18,2},{3,19},{19,3},{4,20},{20... | collective-permute-start | bytes 14155784 | tf_op jit(solution)/shard_map/ppermute | solution.py:538
  238.6 19.5 %collective-permute-start.43 = (bf16[192,256]{1,0:T(8,128)(2,1)}, bf16[192,256]{1,0:T(8,128)(2,1)S(1)}, u32[]{:S(2)}, u32[]{:S(2)}) collective-permute-start(bf16[192,256]{1,0:T(8,128)(2,1)} %get-tuple-element.57), channel_id=1, source_target_pairs={{0,3},{1,0},{2,1},{3,2},{4,7},{5,4},{6,5},{7,6},{8,11},{9,8},{10,9... | collective-permute-start | bytes 294920 | tf_op jit(solution)/shard_map/ppermute | solution.py:541
  240.4 19.0 %collective-permute-start.44 = (bf16[192,256]{1,0:T(8,128)(2,1)}, bf16[192,256]{1,0:T(8,128)(2,1)S(1)}, u32[]{:S(2)}, u32[]{:S(2)}) collective-permute-start(bf16[192,256]{1,0:T(8,128)(2,1)} %get-tuple-element.58), channel_id=1, source_target_pairs={{0,2},{1,3},{2,0},{3,1},{4,6},{5,7},{6,4},{7,5},{8,10},{9,11},{10,... | collective-permute-start | bytes 294920 | tf_op jit(solution)/shard_map/ppermute | solution.py:541
  240.4 23.6 %collective-permute-start.45 = (bf16[192,256]{1,0:T(8,128)(2,1)}, bf16[192,256]{1,0:T(8,128)(2,1)}, u32[]{:S(2)}, u32[]{:S(2)}) collective-permute-start(bf16[192,256]{1,0:T(8,128)(2,1)} %get-tuple-element.59), channel_id=1, source_target_pairs={{0,1},{1,2},{2,3},{3,0},{4,5},{5,6},{6,7},{7,4},{8,9},{9,10},{10,1... | collective-permute-start | bytes 294920 | tf_op jit(solution)/shard_map/ppermute | solution.py:541
  244.8 47.1 %collective-permute-start.78 = (bf16[2,4,96,192]{3,2,1,0:T(8,128)(2,1)S(1)}, bf16[2,4,96,192]{3,2,1,0:T(8,128)(2,1)S(1)}, u32[]{:S(2)}, u32[]{:S(2)}) collective-permute-start(bf16[2,4,96,192]{3,2,1,0:T(8,128)(2,1)S(1)} %pad_maximum_fusion.9), channel_id=1, source_target_pairs={{0,8},{8,0},{4,12},{12,4},{1,9},{9,1},{5,13},{13,5},{2,10},{10,2},... | collective-permute-start | bytes 884744 | tf_op jit(solution)/shard_map/ppermute | solution.py:540
  258.1 39.7 %collective-permute-start.38 = (bf16[256,768]{1,0:T(8,128)(2,1)S(1)}, bf16[256,768]{1,0:T(8,128)(2,1)S(1)}, u32[]{:S(2)}, u32[]{:S(2)}) collective-permute-start(bf16[256,768]{1,0:T(8,128)(2,1)S(1)} %copy-done.19), channel_id=1, source_target_pairs={{1,0},{2,1},{3,2},{5,4},{6,5},{7,6},{9,8},{10,9},{11,10},{13,12},{... | collective-permute-start | bytes 1179656 | tf_op jit(solution)/shard_map/ppermute | solution.py:554
  259.4 55.2 %collective-permute-start.37 = (bf16[256,768]{1,0:T(8,128)(2,1)S(1)}, bf16[256,768]{1,0:T(8,128)(2,1)S(1)}, u32[]{:S(2)}, u32[]{:S(2)}) collective-permute-start(bf16[256,768]{1,0:T(8,128)(2,1)S(1)} %copy-done.19), channel_id=1, source_target_pairs={{0,1},{1,2},{2,3},{4,5},{5,6},{6,7},{8,9},{9,10},{10,11},{12,13},{... | collective-permute-start | bytes 1179656 | tf_op jit(solution)/shard_map/ppermute | solution.py:549
  276.7 29.4 %collective-permute-start.48 = (bf16[2,192,1024]{2,1,0:T(8,128)(2,1)}, bf16[2,192,1024]{2,1,0:T(8,128)(2,1)S(1)}, u32[]{:S(2)}, u32[]{:S(2)}) collective-permute-start(bf16[2,192,1024]{2,1,0:T(8,128)(2,1)} %get-tuple-element.64), channel_id=1, source_target_pairs={{0,8},{8,0},{4,12},{12,4},{1,9},{9,1},{5,13},{13,5},{2,10},{10,2},... | collective-permute-start | bytes 2359304 | tf_op jit(solution)/shard_map/ppermute | solution.py:540
  297.7 23.4 %collective-permute-start.46 = (bf16[2,192,1024]{2,1,0:T(8,128)(2,1)S(1)}, bf16[2,192,1024]{2,1,0:T(8,128)(2,1)S(1)}, u32[]{:S(2)}, u32[]{:S(2)}) collective-permute-start(bf16[2,192,1024]{2,1,0:T(8,128)(2,1)S(1)} %copy-done.58), channel_id=1, source_target_pairs={{0,4},{4,0},{8,12},{12,8},{1,5},{5,1},{9,13},{13,9},{2,6},{6,2},{1... | collective-permute-start | bytes 2359304 | tf_op jit(solution)/shard_map/ppermute | solution.py:539
  297.9 10.7 %collective-permute-start.80 = (bf16[96,192]{1,0:T(8,128)(2,1)S(1)}, bf16[96,192]{1,0:T(8,128)(2,1)S(1)}, u32[]{:S(2)}, u32[]{:S(2)}) collective-permute-start(bf16[96,192]{1,0:T(8,128)(2,1)S(1)} %get-tuple-element.167), channel_id=1, source_target_pairs={{0,1},{4,5},{8,9},{12,13},{16,17},{20,21},{24,25},{28,29}} | collective-permute-start | bytes 110600 | tf_op jit(solution)/shard_map/ppermute | solution.py:565
  308.5 11.2 %collective-permute-start.39 = (bf16[256,768]{1,0:T(8,128)(2,1)S(1)}, bf16[256,768]{1,0:T(8,128)(2,1)}, u32[]{:S(2)}, u32[]{:S(2)}) collective-permute-start(bf16[256,768]{1,0:T(8,128)(2,1)S(1)} %collective-permute-done.38), channel_id=1, source_target_pairs={{1,0},{2,1},{5,4},{6,5},{9,8},{10,9},{13,12},{14,13},{17,16},{18,1... | collective-permute-start | bytes 1179656 | tf_op jit(solution)/shard_map/ppermute | solution.py:554
  310.0 12.6 %collective-permute-start.81 = (bf16[96,192]{1,0:T(8,128)(2,1)S(1)}, bf16[96,192]{1,0:T(8,128)(2,1)S(1)}, u32[]{:S(2)}, u32[]{:S(2)}) collective-permute-start(bf16[96,192]{1,0:T(8,128)(2,1)S(1)} %get-tuple-element.165), channel_id=1, source_target_pairs={{0,1},{1,2},{4,5},{5,6},{8,9},{9,10},{12,13},{13,14},{16,17},{17,1... | collective-permute-start | bytes 110600 | tf_op jit(solution)/shard_map/ppermute | solution.py:565
  319.8 10.9 %collective-permute-start.41 = (bf16[256,768]{1,0:T(8,128)(2,1)S(1)}, bf16[256,768]{1,0:T(8,128)(2,1)}, u32[]{:S(2)}, u32[]{:S(2)}) collective-permute-start(bf16[256,768]{1,0:T(8,128)(2,1)S(1)} %collective-permute-done.37), channel_id=1, source_target_pairs={{1,2},{2,3},{5,6},{6,7},{9,10},{10,11},{13,14},{14,15},{17,18},{18... | collective-permute-start | bytes 1179656 | tf_op jit(solution)/shard_map/ppermute | solution.py:549
  321.2 16.0 %collective-permute-start.40 = (bf16[256,768]{1,0:T(8,128)(2,1)}, bf16[256,768]{1,0:T(8,128)(2,1)}, u32[]{:S(2)}, u32[]{:S(2)}) collective-permute-start(bf16[256,768]{1,0:T(8,128)(2,1)} %collective-permute-done.39), channel_id=1, source_target_pairs={{1,0},{5,4},{9,8},{13,12},{17,16},{21,20},{25,24},{29,28}} | collective-permute-start | bytes 1179656 | tf_op jit(solution)/shard_map/ppermute | solution.py:554
  330.6 47.6 %collective-permute-start.50 = (bf16[192,256]{1,0:T(8,128)(2,1)}, bf16[192,256]{1,0:T(8,128)(2,1)}, u32[]{:S(2)}, u32[]{:S(2)}) collective-permute-start(bf16[192,256]{1,0:T(8,128)(2,1)} %get-tuple-element.65), channel_id=1, source_target_pairs={{0,1},{1,2},{2,3},{3,0},{4,5},{5,6},{6,7},{7,4},{8,9},{9,10},{10,1... | collective-permute-start | bytes 294920 | tf_op jit(solution)/shard_map/ppermute | solution.py:541
  333.3 47.6 %collective-permute-start.53 = (bf16[192,256]{1,0:T(8,128)(2,1)}, bf16[192,256]{1,0:T(8,128)(2,1)}, u32[]{:S(2)}, u32[]{:S(2)}) collective-permute-start(bf16[192,256]{1,0:T(8,128)(2,1)} %get-tuple-element.66), channel_id=1, source_target_pairs={{0,2},{1,3},{2,0},{3,1},{4,6},{5,7},{6,4},{7,5},{8,10},{9,11},{10,... | collective-permute-start | bytes 294920 | tf_op jit(solution)/shard_map/ppermute | solution.py:541
  334.7 13.8 %collective-permute-start.42 = (bf16[256,768]{1,0:T(8,128)(2,1)}, bf16[256,768]{1,0:T(8,128)(2,1)}, u32[]{:S(2)}, u32[]{:S(2)}) collective-permute-start(bf16[256,768]{1,0:T(8,128)(2,1)} %collective-permute-done.41), channel_id=1, source_target_pairs={{2,3},{6,7},{10,11},{14,15},{18,19},{22,23},{26,27},{30,31}} | collective-permute-start | bytes 1179656 | tf_op jit(solution)/shard_map/ppermute | solution.py:549
  337.2 15.4 %collective-permute-start.49 = (bf16[192,1024]{1,0:T(8,128)(2,1)}, bf16[192,1024]{1,0:T(8,128)(2,1)S(1)}, u32[]{:S(2)}, u32[]{:S(2)}) collective-permute-start(bf16[192,1024]{1,0:T(8,128)(2,1)} %fusion.21), channel_id=1, source_target_pairs={{0,4},{4,0},{8,12},{12,8},{1,5},{5,1},{9,13},{13,9},{2,6},{6,2},{1... | collective-permute-start | bytes 1179656 | tf_op jit(solution)/shard_map/ppermute | solution.py:539
  341.4 12.2 %collective-permute-start.47 = (bf16[192,1024]{1,0:T(8,128)(2,1)S(1)}, bf16[192,1024]{1,0:T(8,128)(2,1)S(1)}, u32[]{:S(2)}, u32[]{:S(2)}) collective-permute-start(bf16[192,1024]{1,0:T(8,128)(2,1)S(1)} %copy-done.24), channel_id=1, source_target_pairs={{0,8},{8,0},{4,12},{12,4},{1,9},{9,1},{5,13},{13,5},{2,10},{10,2},... | collective-permute-start | bytes 1179656 | tf_op jit(solution)/shard_map/ppermute | solution.py:540
  348.5 23.6 %collective-permute-start.87 = (bf16[2,4,96,768]{3,2,1,0:T(8,128)(2,1)S(1)}, bf16[2,4,96,768]{3,2,1,0:T(8,128)(2,1)S(1)}, u32[]{:S(2)}, u32[]{:S(2)}) collective-permute-start(bf16[2,4,96,768]{3,2,1,0:T(8,128)(2,1)S(1)} %pad_maximum_fusion.4), channel_id=1, source_target_pairs={{0,4},{4,0},{8,12},{12,8},{1,5},{5,1},{9,13},{13,9},{2,6},{6,2},{1... | collective-permute-start | bytes 3538952 | tf_op jit(solution)/shard_map/ppermute | solution.py:539
  352.5 31.3 %collective-permute-start.56 = (bf16[192,256]{1,0:T(8,128)(2,1)}, bf16[192,256]{1,0:T(8,128)(2,1)}, u32[]{:S(2)}, u32[]{:S(2)}) collective-permute-start(bf16[192,256]{1,0:T(8,128)(2,1)} %get-tuple-element.67), channel_id=1, source_target_pairs={{0,3},{1,0},{2,1},{3,2},{4,7},{5,4},{6,5},{7,6},{8,11},{9,8},{10,9... | collective-permute-start | bytes 294920 | tf_op jit(solution)/shard_map/ppermute | solution.py:541
  373.8 33.4 %collective-permute-start.88 = (bf16[4,96,768]{2,1,0:T(8,128)(2,1)S(1)}, bf16[4,96,768]{2,1,0:T(8,128)(2,1)S(1)}, u32[]{:S(2)}, u32[]{:S(2)}) collective-permute-start(bf16[4,96,768]{2,1,0:T(8,128)(2,1)S(1)} %fusion.5), channel_id=1, source_target_pairs={{0,8},{8,0},{4,12},{12,4},{1,9},{9,1},{5,13},{13,5},{2,10},{10,2},... | collective-permute-start | bytes 1769480 | tf_op jit(solution)/shard_map/ppermute | solution.py:540
  391.4 79.3 %collective-permute-start.72 = (bf16[1,384,576]{1,2,0:T(8,128)(2,1)S(1)}, bf16[1,384,576]{1,2,0:T(8,128)(2,1)}, u32[]{:S(2)}, u32[]{:S(2)}) collective-permute-start(bf16[1,384,576]{1,2,0:T(8,128)(2,1)S(1)} %dynamic-slice_bitcast_fusion.4), channel_id=1, source_target_pairs={{0,16},{16,0},{1,17},{17,1},{2,18},{18,2},{3,19},{19,3},{4,20},{20... | collective-permute-start | bytes 1327112 | tf_op jit(solution)/shard_map/ppermute | solution.py:538
  399.9 79.1 %collective-permute-start.67 = (bf16[256,768]{1,0:T(8,128)(2,1)}, bf16[256,768]{1,0:T(8,128)(2,1)}, u32[]{:S(2)}, u32[]{:S(2)}) collective-permute-start(bf16[256,768]{1,0:T(8,128)(2,1)} %get-tuple-element.69), channel_id=1, source_target_pairs={{1,0},{2,1},{3,2},{5,4},{6,5},{7,6},{9,8},{10,9},{11,10},{13,12},{... | collective-permute-start | bytes 1179656 | tf_op jit(solution)/shard_map/ppermute | solution.py:554
  401.2 79.1 %collective-permute-start.66 = (bf16[256,768]{1,0:T(8,128)(2,1)}, bf16[256,768]{1,0:T(8,128)(2,1)}, u32[]{:S(2)}, u32[]{:S(2)}) collective-permute-start(bf16[256,768]{1,0:T(8,128)(2,1)} %get-tuple-element.69), channel_id=1, source_target_pairs={{0,1},{1,2},{2,3},{4,5},{5,6},{6,7},{8,9},{9,10},{10,11},{12,13},{... | collective-permute-start | bytes 1179656 | tf_op jit(solution)/shard_map/ppermute | solution.py:549
  410.4 64.7 %collective-permute-start.89 = (bf16[2,4,96,768]{3,2,1,0:T(8,128)(2,1)}, bf16[2,4,96,768]{3,2,1,0:T(8,128)(2,1)S(1)}, u32[]{:S(2)}, u32[]{:S(2)}) collective-permute-start(bf16[2,4,96,768]{3,2,1,0:T(8,128)(2,1)} %pad_maximum_fusion.5), channel_id=1, source_target_pairs={{0,8},{8,0},{4,12},{12,4},{1,9},{9,1},{5,13},{13,5},{2,10},{10,2},... | collective-permute-start | bytes 3538952 | tf_op jit(solution)/shard_map/ppermute | solution.py:540
  476.5 15.0 %collective-permute-start.90 = (bf16[4,96,768]{2,1,0:T(8,128)(2,1)S(1)}, bf16[4,96,768]{2,1,0:T(8,128)(2,1)S(1)}, u32[]{:S(2)}, u32[]{:S(2)}) collective-permute-start(bf16[4,96,768]{2,1,0:T(8,128)(2,1)S(1)} %fusion.1), channel_id=1, source_target_pairs={{0,4},{4,0},{8,12},{12,8},{1,5},{5,1},{9,13},{13,9},{2,6},{6,2},{1... | collective-permute-start | bytes 1769480 | tf_op jit(solution)/shard_map/ppermute | solution.py:539
  479.0 16.8 %collective-permute-start.68 = (bf16[256,768]{1,0:T(8,128)(2,1)}, bf16[256,768]{1,0:T(8,128)(2,1)S(1)}, u32[]{:S(2)}, u32[]{:S(2)}) collective-permute-start(bf16[256,768]{1,0:T(8,128)(2,1)} %collective-permute-done.67), channel_id=1, source_target_pairs={{1,0},{2,1},{5,4},{6,5},{9,8},{10,9},{13,12},{14,13},{17,16},{18,1... | collective-permute-start | bytes 1179656 | tf_op jit(solution)/shard_map/ppermute | solution.py:554
  480.3 26.4 %collective-permute-start.70 = (bf16[256,768]{1,0:T(8,128)(2,1)}, bf16[256,768]{1,0:T(8,128)(2,1)S(1)}, u32[]{:S(2)}, u32[]{:S(2)}) collective-permute-start(bf16[256,768]{1,0:T(8,128)(2,1)} %collective-permute-done.66), channel_id=1, source_target_pairs={{1,2},{2,3},{5,6},{6,7},{9,10},{10,11},{13,14},{14,15},{17,18},{18... | collective-permute-start | bytes 1179656 | tf_op jit(solution)/shard_map/ppermute | solution.py:549
  481.1 13.7 %collective-permute-start.74 = (bf16[1,96,256]{1,2,0:T(8,128)(2,1)S(1)}, bf16[1,96,256]{1,2,0:T(8,128)(2,1)S(1)}, u32[]{:S(2)}, u32[]{:S(2)}) collective-permute-start(bf16[1,96,256]{1,2,0:T(8,128)(2,1)S(1)} %fusion.32), channel_id=1, source_target_pairs={{0,8},{8,0},{4,12},{12,4},{1,9},{9,1},{5,13},{13,5},{2,10},{10,2},... | collective-permute-start | bytes 147464 | tf_op jit(solution)/shard_map/ppermute | solution.py:540
  483.1 12.5 %collective-permute-start.76 = (bf16[1,96,320]{1,2,0:T(8,128)(2,1)S(1)}, bf16[1,96,320]{1,2,0:T(8,128)(2,1)S(1)}, u32[]{:S(2)}, u32[]{:S(2)}) collective-permute-start(bf16[1,96,320]{1,2,0:T(8,128)(2,1)S(1)} %fusion.28), channel_id=1, source_target_pairs={{0,4},{4,0},{8,12},{12,8},{1,5},{5,1},{9,13},{13,9},{2,6},{6,2},{1... | collective-permute-start | bytes 184328 | tf_op jit(solution)/shard_map/ppermute | solution.py:539
  495.8 11.6 %collective-permute-start.69 = (bf16[256,768]{1,0:T(8,128)(2,1)S(1)}, bf16[256,768]{1,0:T(8,128)(2,1)S(1)}, u32[]{:S(2)}, u32[]{:S(2)}) collective-permute-start(bf16[256,768]{1,0:T(8,128)(2,1)S(1)} %collective-permute-done.68), channel_id=1, source_target_pairs={{1,0},{5,4},{9,8},{13,12},{17,16},{21,20},{25,24},{29,28}} | collective-permute-start | bytes 1179656 | tf_op jit(solution)/shard_map/ppermute | solution.py:554
  506.7 14.0 %collective-permute-start.71 = (bf16[256,768]{1,0:T(8,128)(2,1)S(1)}, bf16[256,768]{1,0:T(8,128)(2,1)S(1)}, u32[]{:S(2)}, u32[]{:S(2)}) collective-permute-start(bf16[256,768]{1,0:T(8,128)(2,1)S(1)} %collective-permute-done.70), channel_id=1, source_target_pairs={{2,3},{6,7},{10,11},{14,15},{18,19},{22,23},{26,27},{30,31}} | collective-permute-start | bytes 1179656 | tf_op jit(solution)/shard_map/ppermute | solution.py:549
  510.4 12.2 %collective-permute-start.93 = (bf16[96,1536]{1,0:T(8,128)(2,1)S(1)}, bf16[96,1536]{1,0:T(8,128)(2,1)S(1)}, u32[]{:S(2)}, u32[]{:S(2)}) collective-permute-start(bf16[96,1536]{1,0:T(8,128)(2,1)S(1)} %get-tuple-element.133), channel_id=1, source_target_pairs={{0,1},{1,2},{2,3},{4,5},{5,6},{6,7},{8,9},{9,10},{10,11},{12,13},{... | collective-permute-start | bytes 884744 | tf_op jit(solution)/shard_map/ppermute | solution.py:565
  (92 other events, 1211.0 us)

commit v2 on v1

--- a/solution.py
+++ b/solution.py
@@ -38,6 +38,12 @@
     return pltpu.CompilerParams(vmem_limit_bytes=VMEM_LIMIT)
 
 
+def cost(microseconds):
+    return pl.CostEstimate(
+        flops=int(microseconds * 1.15e9), bytes_accessed=1 << 20, transcendentals=0
+    )
+
+
 def shape(dims, kind=bf16):
     return jax.ShapeDtypeStruct(dims, kind)
 
@@ -64,18 +70,18 @@
     )
 
 
-def project_kernel(sc, x, w_own, w_other, b_qv, gain, shift, low, qt, kt, vt):
+def project_kernel(sc, x, w_own, w_other, b_qv, rows, low, qt, kt, vt):
     own, other = halves(sc[2], x.shape[1])
     cols = qt.shape[0]
     normed, _ = norm(x[...].astype(f32))
-    low[...] = (normed * gain[...] + shift[...]).astype(bf16)
+    low[...] = (normed * rows[0:1, :] + rows[1:2, :]).astype(bf16)
     projected = nn(low[:, own], w_own[...]) + nn(low[:, other], w_other[...])
     qt[...] = ((projected[:, :cols] + b_qv[0:1, :]) * SCALE).T.astype(bf16)
     kt[...] = projected[:, cols : 2 * cols].T.astype(bf16)
     vt[...] = (projected[:, 2 * cols :] + b_qv[1:2, :]).T.astype(bf16)
 
 
-def project(place, x, w_own, w_other, b_qv, gain, shift):
+def project(place, x, w_own, w_other, b_qv, table):
     tok, width = x.shape
     cols = b_qv.shape[1]
     rows = min(256, tok)
@@ -85,12 +91,13 @@
         project_kernel,
         grid=(tok // rows,),
         in_specs=[SM, pl.BlockSpec((rows, width), lambda i: (i, 0))]
-        + [fixed(a) for a in (w_own, w_other, b_qv, gain, shift)],
+        + [fixed(a) for a in (w_own, w_other, b_qv, table)],
         out_specs=[pl.BlockSpec((rows, width), lambda i: (i, 0)), across, across, across],
         out_shape=[shape((tok, width))] + [shape((cols, tok))] * 3,
         compiler_params=params(),
+        cost_estimate=cost(7),
         name="project",
-    )(place, x, w_own, w_other, b_qv, gain, shift)
+    )(place, x, w_own, w_other, b_qv, table)
 
 
 def key_loop(sc, i, step, carry):
@@ -109,12 +116,15 @@
     if len(kv) == 1:
         copies = [pltpu.make_async_copy(kv[0], held, sems.at[0])]
     else:
-        rows = kv[0].shape[0]
+        k, k_x, k_yd, v, v_y, v_xd = kv
+        rows = k.shape[0]
+        pieces = [(k, 0, 0), (k_x, 0, 1), (k_yd.at[0], 0, 2), (k_yd.at[1], 0, 3)]
+        pieces += [(v, 1, 0), (v_y, 1, 2), (v_xd.at[0], 1, 1), (v_xd.at[1], 1, 3)]
         copies = [
             pltpu.make_async_copy(
-                kv[n], held.at[sc[1] ^ (n % 4), pl.ds((n // 4) * rows, rows), :], sems.at[n]
+                piece, held.at[sc[1] ^ run, pl.ds(which * rows, rows), :], sems.at[n]
             )
-            for n in range(8)
+            for n, (piece, which, run) in enumerate(pieces)
         ]
     for copy in copies:
         copy.start()
@@ -222,11 +232,12 @@
         scratch_shapes=[
             pltpu.VMEM((runs, 2 * cols, tok), bf16),
             pltpu.VMEM((cols, bq), f32),
-            pltpu.SemaphoreType.DMA((len(kv),)),
+            pltpu.SemaphoreType.DMA((8,)),
         ],
         out_shape=[shape((heads, tok), f32), shape((cols, tok))]
         + [shape((cols, tok // parts))] * parts,
         compiler_params=params(),
+        cost_estimate=cost(20),
         name="attend",
     )(scalars(bk, bq), qt, starts, *kv)
 
@@ -331,10 +342,11 @@
             pltpu.VMEM((runs, 2 * cols, tok), f32),
             pltpu.VMEM((cols, tok), f32),
             pltpu.VMEM((cols, tok), bf16),
-            pltpu.SemaphoreType.DMA((len(kv),)),
+            pltpu.SemaphoreType.DMA((8,)),
         ],
         out_shape=[shape((cols, tok // parts))] * parts + [shape(d) for d in out_kv],
         compiler_params=params(),
+        cost_estimate=cost(26),
         name="attend_back",
     )(scalars(bk, bq), qt, starts, lse, ot, *do_parts, *kv)
 
@@ -344,16 +356,18 @@
 
 def middle_kernel(n_att, parts, sc, *refs):
     att, refs = refs[:n_att], refs[n_att:]
-    (x, cot, wo_own, wo_other, fc_own, fc_other, dn_own, dn_other, b_out, b_fc, b_down, gain, shift) = refs[:13]
-    refs = refs[13:]
+    x, cot, od_own, od_other, fc_own, fc_other, b_fc, rows = refs[:8]
+    refs = refs[8:]
     outputs, grad_mid, sums, fc_sums = refs[:4]
-    d_att, (g_own, g_other, go_own, go_other) = refs[4 : 4 + parts], refs[4 + parts : 8 + parts]
-    mid, att_t, low, low_t, cot_t, mlp, back = refs[8 + parts :]
+    d_att, (g_own, g_other) = refs[4 : 4 + parts], refs[4 + parts : 6 + parts]
+    mid, att_t, low, low_t, cot_t, mlp, back = refs[6 + parts :]
     d = pl.program_id(0)
     width = x.shape[1]
     own, other = halves(sc[2], width)
     half = width // 2
     ffw = fc_own.shape[2]
+    cols = att_t.shape[0] // parts
+    b_out, b_down, gain, shift = (rows[n : n + 1, :] for n in range(2, 6))
 
     @pl.when(d == 0)
     def _():
@@ -365,11 +379,16 @@
                 att_t[row : row + piece.shape[0], :] = piece[...]
                 row += piece.shape[0]
         att_low = att_t[...].T
-        mid[:, own] = nn(att_low, wo_own[...])
-        mid[:, other] = nn(att_low, wo_other[...])
-        mid[...] = x[...].astype(f32) + mid[...] + b_out[...]
+        mine = theirs = 0.0
+        for part in range(parts):
+            piece = att_low[:, part * cols : (part + 1) * cols]
+            mine += nn(piece, od_own[part, :cols, :])
+            theirs += nn(piece, od_other[part, :cols, :])
+        mid[:, own] = mine
+        mid[:, other] = theirs
+        mid[...] = x[...].astype(f32) + mid[...] + b_out
         normed, _ = norm(mid[...])
-        low[...] = (normed * gain[...] + shift[...]).astype(bf16)
+        low[...] = (normed * gain + shift).astype(bf16)
         low_t[...] = low[...].T
         cot_t[...] = cot[...].T
         mlp[...] = jnp.zeros_like(mlp)
@@ -377,29 +396,30 @@
 
     own_rows = pl.ds(pl.multiple_of(sc[2] * half, half), half)
     other_rows = pl.ds(pl.multiple_of((1 - sc[2]) * half, half), half)
+    dn_own, dn_other = od_own[d, cols:, :], od_other[d, cols:, :]
     u = nn(low[:, own], fc_own[0]) + nn(low[:, other], fc_other[0]) + b_fc[0]
     t = jnp.tanh(ROOT * (u + 0.044715 * (u * u * u)))
     act = (0.5 * u * (1.0 + t)).astype(bf16)
     slope = 0.5 * (1.0 + t) + (0.5 * ROOT) * u * (1.0 - t * t) * (1.0 + 0.134145 * (u * u))
-    d_act = nt(cot[:, own], dn_own[0]) + nt(cot[:, other], dn_other[0])
+    d_act = nt(cot[:, own], dn_own) + nt(cot[:, other], dn_other)
     dh = (d_act * slope).astype(bf16)
-    mlp[:, own] += nn(act, dn_own[0])
-    mlp[:, other] += nn(act, dn_other[0])
+    mlp[:, own] += nn(act, dn_own)
+    mlp[:, other] += nn(act, dn_other)
     back[:, own] += nt(dh, fc_own[0])
     back[:, other] += nt(dh, fc_other[0])
-    g_own[0, :, :ffw] = nn(low_t[own_rows, :], dh).astype(bf16)
-    g_other[0, :, :ffw] = nn(low_t[other_rows, :], dh).astype(bf16)
-    g_own[0, :, ffw:] = nn(cot_t[own_rows, :], act).astype(bf16)
-    g_other[0, :, ffw:] = nn(cot_t[other_rows, :], act).astype(bf16)
-    fc_sums[0] = jnp.sum(dh.astype(f32), axis=0, keepdims=True)
+    g_own[d, :, :ffw] = nn(low_t[own_rows, :], dh).astype(bf16)
+    g_other[d, :, :ffw] = nn(low_t[other_rows, :], dh).astype(bf16)
+    g_own[d, :, ffw : 2 * ffw] = nn(cot_t[own_rows, :], act).astype(bf16)
+    g_other[d, :, ffw : 2 * ffw] = nn(cot_t[other_rows, :], act).astype(bf16)
+    fc_sums[lax.rem(sc[3] - d + parts, parts)] = jnp.sum(dh.astype(f32), axis=0, keepdims=True)
 
     @pl.when(d == parts - 1)
     def _():
         normed, inverse = norm(mid[...])
-        outputs[...] = (mid[...] + mlp[...] + b_down[...]).astype(bf16)
+        outputs[...] = (mid[...] + mlp[...] + b_down).astype(bf16)
         upper = cot[...].astype(f32)
         grad = back[...]
-        down = upper + norm_gradient(grad, normed, inverse, gain[...])
+        down = upper + norm_gradient(grad, normed, inverse, gain)
         grad_mid[...] = down
         sums[0:1, :] = jnp.sum(down, axis=0, keepdims=True)
         sums[1:2, :] = jnp.sum(upper, axis=0, keepdims=True)
@@ -407,36 +427,36 @@
         sums[3:4, :] = jnp.sum(grad, axis=0, keepdims=True)
         low[...] = down.astype(bf16)
         low_t[...] = low[...].T
-        cols = att_t.shape[0] // parts
-        go_own[...] = nt(low_t[own_rows, :], att_t[...]).astype(bf16)
-        go_other[...] = nt(low_t[other_rows, :], att_t[...]).astype(bf16)
         for part in range(parts):
-            rows = slice(part * cols, (part + 1) * cols)
+            at = slice(part * cols, (part + 1) * cols)
+            g_own[part, :, 2 * ffw :] = nt(low_t[own_rows, :], att_t[at, :]).astype(bf16)
+            g_other[part, :, 2 * ffw :] = nt(low_t[other_rows, :], att_t[at, :]).astype(bf16)
             d_att[part][...] = (
-                nt(wo_own[rows, :], low[:, own]) + nt(wo_other[rows, :], low[:, other])
+                nt(od_own[part, :cols, :], low[:, own]) + nt(od_other[part, :cols, :], low[:, other])
             ).astype(bf16)
 
 
-def middle(place, att, x, cot, wo, fc, dn, b_out, b_fc, b_down, gain, shift):
+def middle(place, att, x, cot, od, fc, b_fc, table):
     parts, half, ffw = fc[0].shape
     sub, width = x.shape
-    cols = wo[0].shape[0] // parts
-    whole = lambda *dims: pl.BlockSpec(dims, lambda i: (0,) * len(dims))
+    cols = od[0].shape[1] - ffw
+    whole = lambda *dims: pl.BlockSpec(
+        dims, lambda i: (0,) * len(dims), pipeline_mode=pl.Buffered(1)
+    )
     each = lambda *dims: pl.BlockSpec((1,) + dims, lambda i: (i, 0, 0))
     once = lambda a: whole(*a.shape)
+    grads = (parts, half, 2 * ffw + cols)
     return pl.pallas_call(
         functools.partial(middle_kernel, len(att), parts),
         grid=(parts,),
         in_specs=[SM]
         + [once(a) for a in att]
-        + [once(x), once(cot), once(wo[0]), once(wo[1])]
+        + [once(x), once(cot), once(od[0]), once(od[1])]
         + [each(half, ffw)] * 2
-        + [each(ffw, half)] * 2
-        + [once(b_out), each(1, ffw), once(b_down), once(gain), once(shift)],
-        out_specs=[whole(sub, width), whole(sub, width), whole(4, width), each(1, ffw)]
+        + [each(1, ffw), once(table)],
+        out_specs=[whole(sub, width), whole(sub, width), whole(4, width), whole(parts, 1, ffw)]
         + [whole(cols, sub)] * parts
-        + [each(half, 2 * ffw)] * 2
-        + [whole(half, parts * cols)] * 2,
+        + [whole(*grads)] * 2,
         out_shape=[
             shape((sub, width)),
             shape((sub, width), f32),
@@ -444,8 +464,7 @@
             shape((parts, 1, ffw), f32),
         ]
         + [shape((cols, sub))] * parts
-        + [shape((parts, half, 2 * ffw))] * 2
-        + [shape((half, parts * cols))] * 2,
+        + [shape(grads)] * 2,
         scratch_shapes=[
             pltpu.VMEM((sub, width), f32),
             pltpu.VMEM((parts * cols, sub), bf16),
@@ -456,16 +475,20 @@
             pltpu.VMEM((sub, width), f32),
         ],
         compiler_params=params(),
+        cost_estimate=cost(19),
         name="middle",
-    )(place, *att, x, cot, wo[0], wo[1], fc[0], fc[1], dn[0], dn[1], b_out, b_fc, b_down, gain, shift)
+    )(place, *att, x, cot, od[0], od[1], fc[0], fc[1], b_fc, table)
 
 
 def last_kernel(parts, pieces, sc, *refs):
     grads, refs = refs[: parts * pieces], refs[parts * pieces :]
-    w_own, w_other, x, grad_mid, gain, out, sums, back_t, stacked = refs
+    w_own, w_other, x, grad_mid, rows, mid_sums, fc_sums, out, sums, back_t, stacked = refs
     half = w_own.shape[1]
+    wide = w_own.shape[2]
     own_rows = pl.ds(pl.multiple_of(sc[2] * half, half), half)
     other_rows = pl.ds(pl.multiple_of((1 - sc[2]) * half, half), half)
+    ones = jnp.ones((8, x.shape[0]), bf16)
+    sums[...] = jnp.zeros_like(sums)
     for part in range(parts):
         row = 0
         for n in range(pieces):
@@ -478,25 +501,32 @@
         else:
             back_t[own_rows, :] += mine
             back_t[other_rows, :] += theirs
+        at = lax.rem(sc[3] - part + parts, parts)
+        sums[pl.ds(6 + parts + at, 1), :wide] = nt(ones, stacked[...])[0:1, :]
     back = back_t[...].T
     normed, inverse = norm(x[...].astype(f32))
-    out[...] = (grad_mid[...] + norm_gradient(back, normed, inverse, gain[...])).astype(bf16)
-    sums[0:1, :] = jnp.sum(back * normed, axis=0, keepdims=True)
-    sums[1:2, :] = jnp.sum(back, axis=0, keepdims=True)
-
-
-def last(place, grads, pieces, w, x, grad_mid, gain):
+    out[...] = (grad_mid[...] + norm_gradient(back, normed, inverse, rows[0:1, :])).astype(bf16)
+    sums[0:4, :] = mid_sums[...]
+    sums[4:5, :] = jnp.sum(back * normed, axis=0, keepdims=True)
+    sums[5:6, :] = jnp.sum(back, axis=0, keepdims=True)
+    for part in range(parts):
+        sums[6 + part : 7 + part, :] = fc_sums[part]
+
+
+def last(place, grads, pieces, w, x, grad_mid, table, mid_sums, fc_sums):
     parts = w[0].shape[0]
     sub, width = x.shape
+    rows = 8 * ((6 + 2 * parts + 7) // 8)
     return pl.pallas_call(
         functools.partial(last_kernel, parts, pieces),
-        in_specs=[SM] + [VM] * (len(grads) + 5),
+        in_specs=[SM] + [VM] * (len(grads) + 7),
         out_specs=[VM, VM],
-        out_shape=[shape((sub, width)), shape((2, width), f32)],
+        out_shape=[shape((sub, width)), shape((rows, width), f32)],
         scratch_shapes=[pltpu.VMEM((width, sub), f32), pltpu.VMEM((w[0].shape[2], sub), bf16)],
         compiler_params=params(),
+        cost_estimate=cost(6),
         name="last",
-    )(place, *grads, w[0], w[1], x, grad_mid, gain)
+    )(place, *grads, w[0], w[1], x, grad_mid, table, mid_sums, fc_sums)
 
 
 def body(
@@ -534,6 +564,20 @@
     x = inputs[0]
     cot = cotangent[0]
     row = lambda v: v[None, :]
+    zero = jnp.zeros_like(b_out)
+    table = jnp.stack(
+        [
+            first_norm_gain,
+            first_norm_bias,
+            b_out,
+            b_down,
+            second_norm_gain,
+            second_norm_bias,
+            zero,
+            zero,
+        ]
+    )
+    after = lambda v, dep: lax.optimization_barrier((v, dep))[0]
 
     swap = lambda v: lax.ppermute(v, "shard", [(0, 1), (1, 0)])
     along_x = lambda v: lax.ppermute(v, "context", [(0, 1), (1, 0), (2, 3), (3, 2)])
@@ -542,31 +586,29 @@
         v, "tensor", [(s, (s + d) % n_tensor) for s in range(n_tensor)]
     )
 
+    def gather_direct(v):
+        return [v] + [shift_by(v, d) for d in range(1, n_tensor)]
+
     def gather_line(v):
-        right, left = [v], [v]
-        for s in range(1, n_tensor):
-            right.append(
-                lax.ppermute(
-                    right[-1], "tensor", [(d, d + 1) for d in range(s - 1, n_tensor - 1)]
-                )
-            )
-            left.append(
-                lax.ppermute(left[-1], "tensor", [(d, d - 1) for d in range(1, n_tensor - s + 1)])
-            )
-        return [v] + [right[d] + left[n_tensor - d] for d in range(1, n_tensor)]
-
-    def scatter_line(pieces):
-        right = left = None
-        for s in range(1, n_tensor):
-            r, l = pieces[s], pieces[n_tensor - s]
-            if s > 1:
-                r = (r.astype(f32) + right.astype(f32)).astype(bf16)
-                l = (l.astype(f32) + left.astype(f32)).astype(bf16)
-            right = lax.ppermute(r, "tensor", [(d, d + 1) for d in range(s)])
-            left = lax.ppermute(
-                l, "tensor", [(n_tensor - 1 - d, n_tensor - 2 - d) for d in range(s)]
-            )
-        return pieces[0].astype(f32) + right.astype(f32) + left.astype(f32)
+        if n_tensor != 4:
+            return gather_direct(v)
+        move = lambda a, perm: lax.ppermute(a, "tensor", perm)
+        two = move(v, [(0, 2), (1, 3), (2, 0), (3, 1)])
+        right = move(v, [(0, 1), (1, 2), (2, 3)])
+        left = move(v, [(3, 2), (2, 1), (1, 0)])
+        far = move(two, [(2, 3), (1, 0)])
+        return [
+            v,
+            jnp.where(tensor == 0, far, right),
+            two,
+            jnp.where(tensor == 3, far, left),
+        ]
+
+    def scatter_direct(pieces):
+        total = pieces[0].astype(f32)
+        for d in range(1, n_tensor):
+            total += shift_by(pieces[d].astype(bf16), -d).astype(f32)
+        return total
 
     def scatter_context(v):
         if not grouped:
@@ -613,8 +655,7 @@
         qkv_own,
         swap(qkv_own),
         b_qv,
-        row(first_norm_gain),
-        row(first_norm_bias),
+        table,
     )
 
     kv = []
@@ -624,18 +665,17 @@
         head += g
         k, v = kt[rows], vt[rows]
         if grouped:
-            kx, vy, ky, vx = along_x(k), along_y(v), along_y(k), along_x(v)
-            kv.append([k, kx, ky, along_y(kx), v, vx, vy, along_x(vy)])
+            kx, vy = along_x(k), along_y(v)
+            kv.append([k, kx, along_y(jnp.stack([k, kx])), v, vy, along_x(jnp.stack([v, vy]))])
         else:
             kv.append([lax.all_gather(jnp.concatenate([k, v], axis=0), "context", axis=0)])
 
-    def gather_weights(w):
-        own = jnp.stack(gather_line(w))
+    def gather_weights(w, gather):
+        own = jnp.stack(gather(w))
         return own, swap(own)
 
-    wo = tuple(w.reshape(n_tensor * cols, half) for w in gather_weights(w_out))
-    fc = gather_weights(w_fc)
-    dn = gather_weights(w_down)
+    od = gather_weights(jnp.concatenate([w_out, w_down], axis=0), gather_line)
+    fc = gather_weights(w_fc, gather_line)
 
     saved = []
     att = [[] for _ in range(n_tensor)]
@@ -650,41 +690,41 @@
 
     x_sub = lax.dynamic_slice_in_dim(x, tensor * sub, sub, 0)
     cot_sub = lax.dynamic_slice_in_dim(cot, tensor * sub, sub, 0)
-    qkv = gather_weights(qkv_own)
-    fc_bias = [row(b_fc)[None]]
-    fc_bias = jnp.concatenate(gather_line(row(b_fc)[None]), axis=0)
-    outputs_sub, grad_mid, sums, fc_sums, *rest = middle(
+    qkv = gather_weights(after(qkv_own, saved[-1][1]), gather_direct)
+    all_bias = lax.all_gather(row(b_fc), "tensor", axis=0)
+    fc_bias = jnp.stack(
+        [
+            lax.dynamic_index_in_dim(
+                all_bias, lax.rem(tensor - d + n_tensor, n_tensor), 0, keepdims=False
+            )
+            for d in range(n_tensor)
+        ]
+    )
+    outputs_sub, grad_mid, mid_sums, fc_sums, *rest = middle(
         place,
         [piece for part in att for piece in part],
         x_sub,
         cot_sub,
-        wo,
+        od,
         fc,
-        dn,
-        row(b_out),
         fc_bias,
-        row(b_down),
-        row(second_norm_gain),
-        row(second_norm_bias),
-    )
-    d_att, (g_own, g_other, go_own, go_other) = rest[:n_tensor], rest[n_tensor:]
+        table,
+    )
+    d_att, (g_own, g_other) = rest[:n_tensor], rest[n_tensor:]
     do_parts = [d_att[0]] + [
         shift_by(d_att[d], -d) for d in range(1, n_tensor)
     ]
 
     def spread(v):
-        pieces = gather_line(v)
+        pieces = gather_direct(v)
         whole = jnp.zeros((tok, width), f32)
         for d in range(n_tensor):
             at = lax.rem(tensor - d + n_tensor, n_tensor) * sub
             whole = lax.dynamic_update_slice_in_dim(whole, pieces[d].astype(f32), at, 0)
         return whole[None]
 
-    ff_grads = scatter_weights(g_own, g_other)
-    out_split = lambda v: jnp.stack(jnp.split(v, n_tensor, axis=1))
-    out_grads = scatter_weights(out_split(go_own), out_split(go_other))
-    ff_grads = scatter_line([ff_grads[d].astype(bf16) for d in range(n_tensor)])
-    out_grads = scatter_line([out_grads[d].astype(bf16) for d in range(n_tensor)])
+    wide_grads = scatter_weights(g_own, g_other)
+    wide_grads = scatter_direct([wide_grads[d] for d in range(n_tensor)])
     outputs = spread(outputs_sub)
 
     dq_pieces, dkv_pieces, dqkv = [], [], []
@@ -717,11 +757,11 @@
         return lax.dynamic_slice_in_dim(v, at, sub, 1)
 
     grads = []
+    both = jnp.concatenate(keys + values, axis=0)
     for d in range(n_tensor):
-        pieces = [q[d] for q in queries]
-        pieces += [part_of(k, d) for k in keys] + [part_of(v, d) for v in values]
+        pieces = [q[d] for q in queries] + [part_of(both, d)]
         grads += pieces if d == 0 else [shift_by(p, d) for p in pieces]
-    pieces = 3 * len(GROUPS)
+    pieces = len(GROUPS) + 1
 
     dq_whole = []
     for q in queries:
@@ -730,54 +770,43 @@
             at = lax.rem(tensor + d, n_tensor) * sub
             whole = lax.dynamic_update_slice_in_dim(whole, q[d], at, 1)
         dq_whole.append(whole)
-    stacked = jnp.concatenate(dq_whole + keys + values, axis=0)
+    stacked = jnp.concatenate(dq_whole + [both], axis=0)
     qkv_grad = jnp.einsum("td,ct->dc", low_one, stacked, preferred_element_type=f32).astype(bf16)
-    qv_sums = jnp.sum(stacked.astype(f32), axis=1).reshape(3, cols)
     qkv_mine = lax.dynamic_slice_in_dim(qkv_grad, core * half, half, 0)
     qkv_theirs = lax.dynamic_slice_in_dim(qkv_grad, (1 - core) * half, half, 0)
 
-    input_sub, first_sums = last(
-        place, grads, pieces, qkv, x_sub, grad_mid, row(first_norm_gain)
+    input_sub, small = last(
+        place, grads, pieces, qkv, x_sub, grad_mid, table, mid_sums, fc_sums
     )
     input_gradient = spread(input_sub)
     qkv_grads = scatter_weights(qkv_mine[None], qkv_theirs[None])[0]
 
-    zero_fc = jnp.zeros((n_tensor, ffw), f32)
-    for d in range(n_tensor):
-        at = lax.rem(tensor - d + n_tensor, n_tensor)
-        zero_fc = lax.dynamic_update_slice_in_dim(zero_fc, fc_sums[d], at, 0)
-    zero_qv = lax.dynamic_update_slice_in_dim(
-        jnp.zeros((n_tensor, 2 * cols), f32),
-        jnp.concatenate([qv_sums[0], qv_sums[2]])[None],
-        tensor,
-        0,
-    )
-    small = lax.psum(
-        jnp.concatenate(
-            [sums.reshape(-1), first_sums.reshape(-1), zero_fc.reshape(-1), zero_qv.reshape(-1)]
-        ),
-        ("shard", "context", "tensor"),
-    )
-    table = small[: 6 * width].reshape(6, width)
-    fc_total = lax.dynamic_slice_in_dim(small, 6 * width + tensor * ffw, ffw, 0)
-    qv_total = lax.dynamic_slice_in_dim(
-        small, 6 * width + n_tensor * ffw + tensor * 2 * cols, 2 * cols, 0
-    ).reshape(2, cols)
+    if grouped and n_tensor == 4 and n_shard == 2:
+        small += swap(small)
+        small += along_x(small)
+        small += along_y(small)
+        small += lax.ppermute(small, "tensor", [(0, 1), (1, 0), (2, 3), (3, 2)])
+        small += lax.ppermute(small, "tensor", [(0, 2), (2, 0), (1, 3), (3, 1)])
+    else:
+        small = lax.psum(small, ("shard", "context", "tensor"))
+    fc_total = lax.dynamic_index_in_dim(small, 6 + tensor, 0, keepdims=False)
+    qv_total = lax.dynamic_index_in_dim(small, 6 + n_tensor + tensor, 0, keepdims=False)
+    qv_total = jnp.stack([qv_total[:cols], qv_total[2 * cols : 3 * cols]])
     return (
         outputs,
         input_gradient,
         qkv_grads.astype(f32).reshape(-1, 3, cols),
-        out_grads.T,
-        ff_grads[:, :ffw],
-        ff_grads[:, ffw:].T,
+        wide_grads[:, 2 * ffw :].T,
+        wide_grads[:, :ffw],
+        wide_grads[:, ffw : 2 * ffw].T,
         qv_total,
-        table[0],
+        small[0],
         fc_total,
-        table[1],
-        table[4],
-        table[5],
-        table[2],
-        table[3],
+        small[1],
+        small[4],
+        small[5],
+        small[2],
+        small[3],
     )
 
 

time: 537 us -> 481 us (0.90); the launches traced: 528 us -> 479 us
  waiting for transfers between devices: 143 us -> 194 us
  starting transfers between devices: 173 us -> 126 us
  blocking collectives: 57.4 us -> 26.2 us
  other arithmetic: 53.5 us -> 34.4 us
    ppermute x54 -> x10, starting transfers between devices: 105 us -> 28.8 us  [the longest x8 20.5 us: gather_line(): move = lambda a, perm: lax.ppermute(a, 'tensor', perm)]
    psum x1 -> x0, blocking collectives: 57.4 us -> none  [body(): lax.psum(jnp.concatenate([sums.reshape(-1), first_sums.reshape(-1), zero_...]
    ppermute x15 -> x24, waiting for transfers between devices: 10.5 us -> 54.4 us  [body(): lax.ppermute(v, 'tensor', [(s, (s + d) % n_tensor) for s in range(n_tenso...]
    ppermute x15 -> x24, starting transfers between devices: 20.9 us -> 51.9 us  [body(): lax.ppermute(v, 'tensor', [(s, (s + d) % n_tensor) for s in range(n_tenso...]
    ppermute x54 -> x10, waiting for transfers between devices: 80.8 us -> 54.4 us  [the longest x8 30.5 us: gather_line(): move = lambda a, perm: lax.ppermute(a, 'tensor', perm)]
    all_gather x0 -> x1, blocking collectives: none -> 26.2 us  [body(): all_bias = lax.all_gather(row(b_fc), 'tensor', axis=0)]
    ppermute x10 -> x9, waiting for transfers between devices: 16 us -> 34.2 us  [body(): lax.ppermute(v, 'context', [(0, 2), (2, 0), (1, 3), (3, 1)])]
    ppermute x10 -> x9, waiting for transfers between devices: 35.3 us -> 50.9 us  [body(): lax.ppermute(v, 'context', [(0, 1), (1, 0), (2, 3), (3, 2)])]
  transfers between devices with their start and end apart: 97 -> 59, of which waited for: 25 -> 23; matrix products, arithmetic and copies ran while one was open for 18% -> 14% of each run, Pallas kernels for 10% -> 12%
where the time goes in v2:
time: 481 us; the launch traced here: 479 us
  waiting for transfers between devices  194 us (40%)
  starting transfers between devices  126 us (26%)
  Pallas kernels  56.1 us (12%)
  local copies, waits for them, and re-layouts  40.2 us (8%)
  other arithmetic  34.4 us (7%)
  blocking collectives  26.2 us (5%)
    ppermute x24, waiting for transfers between devices, body(): lax.ppermute(v, 'tensor', [(s, (s + d) % n_tensor) for s in range(n_tenso...  54.4 us
    ppermute x24, starting transfers between devices, body(): lax.ppermute(v, 'tensor', [(s, (s + d) % n_tensor) for s in range(n_tenso...  51.9 us
    ppermute x9, waiting for transfers between devices, body(): lax.ppermute(v, 'context', [(0, 1), (1, 0), (2, 3), (3, 2)])  50.9 us
    ppermute x9, starting transfers between devices, body(): lax.ppermute(v, 'context', [(0, 2), (2, 0), (1, 3), (3, 1)])  35.6 us
    ppermute x9, waiting for transfers between devices, body(): lax.ppermute(v, 'context', [(0, 2), (2, 0), (1, 3), (3, 1)])  34.2 us
    ppermute x8, waiting for transfers between devices, gather_line(): move = lambda a, perm: lax.ppermute(a, 'tensor', perm)  30.5 us
    all_gather x1, blocking collectives, body(): all_bias = lax.all_gather(row(b_fc), 'tensor', axis=0)  26.2 us
    ppermute x1, waiting for transfers between devices, body(): small += lax.ppermute(small, 'tensor', [(0, 2), (2, 0), (1, 3), (3, 1)])  23.9 us
  transfers between devices with their start and end apart: 59, of which 23 were waited for; matrix products, arithmetic and copies ran while one was open for 14% of the time, Pallas kernels for 12%

profile of v2, /device:TPU:0, one launch (start us, length us, event | category | flops | bytes accessed | tf_op | source)
XLA Modules:
  0.0 479.3 jit_solution(6471251942415050183)
XLA Ops:
  4.7 3.8 collective-permute-start.8
  8.5 4.4 collective-permute-start.10
  17.6 6.3 %project.1 = (bf16[1024,768]{1,0:T(8,128)(2,1)}, bf16[192,1024]{1,0:T(8,128)(2,1)}, bf16[192,1024]{1,0:T(8,128)(2,1)}, bf16[192,1024]{1,0:T(8,128)(2,1)}) custom-call(s32[4]{0:T(128)} %pad_add_fusion.1.sc, bf16[1024,768]{1,0:T(8,128)(2,1)} %bitcast.171, bf16[384,576]{1,0:T(8,128)(2,1)} %copy-done.9, bf16[384,576]{1,0:T(8,128)(2,1)} %copy-done.27, ...), custom_call_target="tpu_custom_call" | custom-call | flops 8049999872 | bytes 1048576 | tf_op jit(solution)/shard_map/project/pallas_call | solution.py:90
  23.9 1.6 collective-permute-start.3
  26.2 1.8 dynamic-slice_bitcast_fusion.6.refs_4_.refs_10_
  28.0 13.8 %collective-permute-done.8 = bf16[960,384]{1,0:T(8,128)(2,1)} collective-permute-done((bf16[960,384]{1,0:T(8,128)(2,1)S(1)}, bf16[960,384]{1,0:T(8,128)(2,1)}, u32[]{:S(2)}, u32[]{:S(2)}) %collective-permute-start.8) | collective-permute-done | bytes 737312 | tf_op jit(solution)/shard_map/ppermute | solution.py:595
  43.6 3.8 fusion.48
  48.2 1.9 collective-permute-start.1
  51.4 7.6 %collective-permute-done.1.refs_1_.refs_5_ = bf16[192,1024]{1,0:T(8,128)(2,1)S(1)} collective-permute-done((bf16[192,1024]{1,0:T(8,128)(2,1)}, bf16[192,1024]{1,0:T(8,128)(2,1)S(1)}, u32[]{:S(2)}, u32[]{:S(2)}) %collective-permute-start.1) | collective-permute-done | bytes 393248 | tf_op jit(solution)/shard_map/ppermute | solution.py:583
  59.0 6.0 %collective-permute-start.15 = (bf16[384,768]{1,0:T(8,128)(2,1)}, bf16[384,768]{1,0:T(8,128)(2,1)}, u32[]{:S(2)}, u32[]{:S(2)}) collective-permute-start(bf16[384,768]{1,0:T(8,128)(2,1)} %param.19), channel_id=1, source_target_pairs={{0,1},{1,2},{2,3},{4,5},{5,6},{6,7},{8,9},{9,10},{10,11},{12,13},{... | collective-permute-start | bytes 1769480 | tf_op jit(solution)/shard_map/ppermute | solution.py:595
  65.9 16.7 %collective-permute-done.13 = bf16[384,768]{1,0:T(8,128)(2,1)} collective-permute-done((bf16[384,768]{1,0:T(8,128)(2,1)}, bf16[384,768]{1,0:T(8,128)(2,1)}, u32[]{:S(2)}, u32[]{:S(2)}) %collective-permute-start.13) | collective-permute-done | bytes 589856 | tf_op jit(solution)/shard_map/ppermute | solution.py:595
  85.2 1.6 collective-permute-start.4
  86.8 1.5 collective-permute-start.2
  88.3 1.5 select_bitcast_fusion.1
  89.8 2.8 pad_maximum_fusion.1.refs_6_
  93.4 26.2 %all-gather.1 = f32[4,1,768]{2,1,0:T(1,128)S(1)} all-gather(f32[1,1,768]{2,1,0:T(1,128)S(1)} %reshape.230), channel_id=2, replica_groups=mesh['shard'=2,'context'=4,'tensor'=4] {'tensor'}, dimensions={0}, use_global_device_ids=true | all-gather | bytes 15360 | tf_op jit(solution)/shard_map/all_gather | solution.py:694
  121.0 2.9 pad_maximum_fusion.2.refs_8_
  124.0 9.6 %attend.1 = (f32[3,1024]{1,0:T(4,128)}, bf16[192,1024]{1,0:T(8,128)(2,1)}, bf16[192,256]{1,0:T(8,128)(2,1)}, bf16[192,256]{1,0:T(8,128)(2,1)}, bf16[192,256]{1,0:T(8,128)(2,1)}, /*index=5*/bf16[192,256]{1,0:T(8,128)(2,1)}) custom-call(s32[12]{0:T(128)} %concatenate.22.sc, bf16[192,1024]{1,0:T(8,128)(2,1)} %get-tuple-element.45.qt, ...), custom_call_target="tpu_custom_call" | custom-call | flops 23000000512 | bytes 1048576 | tf_op jit(solution)/shard_map/attend/pallas_call | solution.py:221
  134.4 3.1 collective-permute-start.7
  138.3 3.0 collective-permute-done.5.refs_1_
  141.4 3.3 collective-permute-done.6.refs_2_
  144.7 3.1 collective-permute-start.36
  147.8 21.7 %middle.1 = (bf16[256,768]{1,0:T(8,128)(2,1)}, f32[256,768]{1,0:T(8,128)}, f32[4,768]{1,0:T(4,128)}, f32[4,1,768]{2,1,0:T(1,128)}, bf16[192,256]{1,0:T(8,128)(2,...) custom-call(s32[4]{0:T(128)} %pad_add_fusion.1.sc, ...), custom_call_target="tpu_custom_call" | custom-call | flops 21849999360 | bytes 1048576 | tf_op jit(solution)/shard_map/middle/pallas_call | solution.py:449
  169.5 21.2 %collective-permute-start.21 = (bf16[192,256]{1,0:T(8,128)(2,1)}, bf16[192,256]{1,0:T(8,128)(2,1)S(1)}, u32[]{:S(2)}, u32[]{:S(2)}) collective-permute-start(bf16[192,256]{1,0:T(8,128)(2,1)} %get-tuple-element.56), channel_id=1, source_target_pairs={{0,3},{1,0},{2,1},{3,2},{4,7},{5,4},{6,5},{7,6},{8,11},{9,8},{10,9... | collective-permute-start | bytes 294920 | tf_op jit(solution)/shard_map/ppermute | solution.py:585
  190.7 1.5 collective-permute-start.22
  192.2 1.4 collective-permute-start.23
  194.1 2.5 copy.46
  196.6 8.2 %copy.48 = bf16[4,384,1728]{1,2,0:T(8,128)(2,1)} copy(bf16[4,384,1728]{2,1,0:T(8,128)(2,1)} %get-tuple-element.74) | data formatting | bytes 10616832 | tf_op jit(solution)/shard_map/middle/pallas_call | solution.py:449
  206.0 12.6 %attend_back.1 = (bf16[192,256]{1,0:T(8,128)(2,1)}, bf16[192,256]{1,0:T(8,128)(2,1)}, bf16[192,256]{1,0:T(8,128)(2,1)}, bf16[192,256]{1,0:T(8,128)(2,1)}, bf16[2...) custom-call(s32[12]{0:T(128)} %concatenate.22.sc, ...), custom_call_target="tpu_custom_call" | custom-call | flops 29899999232 | bytes 1048576 | tf_op jit(solution)/shard_map/attend_back/pallas_call | solution.py:327
  218.6 24.6 %collective-permute-start.26 = (bf16[2,192,1024]{2,1,0:T(8,128)(2,1)}, bf16[2,192,1024]{2,1,0:T(8,128)(2,1)S(1)}, u32[]{:S(2)}, u32[]{:S(2)}) collective-permute-start(bf16[2,192,1024]{2,1,0:T(8,128)(2,1)} %get-tuple-element.63), channel_id=1, source_target_pairs={{0,8},{8,0},{4,12},{12,4},{1,9},{9,1},{5,13},{13,5},{2,10},{10,2},... | collective-permute-start | bytes 2359304 | tf_op jit(solution)/shard_map/ppermute | solution.py:584
  243.2 3.9 copy.47.refs_9_
  248.6 12.5 %collective-permute-done.26 = bf16[2,192,1024]{2,1,0:T(8,128)(2,1)S(1)} collective-permute-done((bf16[2,192,1024]{2,1,0:T(8,128)(2,1)}, bf16[2,192,1024]{2,1,0:T(8,128)(2,1)S(1)}, u32[]{:S(2)}, u32[]{:S(2)}) %collective-permute-start.26) | collective-permute-done | bytes 786464 | tf_op jit(solution)/shard_map/ppermute | solution.py:584
  262.9 1.5 collective-permute-start.25
  264.4 7.6 %collective-permute-done.27 = bf16[192,1024]{1,0:T(8,128)(2,1)S(1)} collective-permute-done((bf16[192,1024]{1,0:T(8,128)(2,1)S(1)}, bf16[192,1024]{1,0:T(8,128)(2,1)S(1)}, u32[]{:S(2)}, u32[]{:S(2)}) %collective-permute-start.27) | collective-permute-done | bytes 393248 | tf_op jit(solution)/shard_map/ppermute | solution.py:583
  273.1 2.3 collective-permute-start.32
  276.4 9.1 %collective-permute-done.30.refs_4_ = bf16[192,256]{1,0:T(8,128)(2,1)S(1)} collective-permute-done((bf16[192,256]{1,0:T(8,128)(2,1)S(1)}, bf16[192,256]{1,0:T(8,128)(2,1)S(1)}, u32[]{:S(2)}, u32[]{:S(2)}) %collective-permute-start.30) | collective-permute-done | bytes 98336 | tf_op jit(solution)/shard_map/ppermute | solution.py:585
  285.7 3.0 collective-permute-start.19
  288.7 6.2 %collective-permute-start.20 = (bf16[256,768]{1,0:T(8,128)(2,1)S(1)}, bf16[256,768]{1,0:T(8,128)(2,1)S(1)}, u32[]{:S(2)}, u32[]{:S(2)}) collective-permute-start(bf16[256,768]{1,0:T(8,128)(2,1)S(1)} %copy-done.10), channel_id=1, source_target_pairs={{0,3},{1,0},{2,1},{3,2},{4,7},{5,4},{6,5},{7,6},{8,11},{9,8},{10,9... | collective-permute-start | bytes 1179656 | tf_op jit(solution)/shard_map/ppermute | solution.py:585
  294.9 5.4 %collective-permute-done.31.refs_5_ = bf16[384,256]{1,0:T(8,128)(2,1)S(1)} collective-permute-done((bf16[384,256]{1,0:T(8,128)(2,1)S(1)}, bf16[384,256]{1,0:T(8,128)(2,1)S(1)}, u32[]{:S(2)}, u32[]{:S(2)}) %collective-permute-start.31) | collective-permute-done | bytes 196640 | tf_op jit(solution)/shard_map/ppermute | solution.py:585
  301.0 5.9 %last.1 = (bf16[256,768]{1,0:T(8,128)(2,1)}, f32[16,768]{1,0:T(8,128)}) custom-call(s32[4]{0:T(128)} %pad_add_fusion.1.sc, bf16[192,256]{1,0:T(8,128)(2,1)} %get-tuple-element.59.refs_0_, bf16[384,256]{1,0:T(8,128)(2,1)} %get-tuple-element.141.refs_1_, bf16[192,256]{1,0:T(8,128)(2,1)} %copy-done.31, bf16[384,256]{1,0:T(8,128)(2,1)} %copy-done.28, ...), custom_call_target="tpu_custom_call" | custom-call | flops 6899999744 | bytes 1048576 | tf_op jit(solution)/shard_map/last/pallas_call | solution.py:520
  307.0 8.3 %collective-permute-done.19 = bf16[256,768]{1,0:T(8,128)(2,1)S(1)} collective-permute-done((bf16[256,768]{1,0:T(8,128)(2,1)S(1)}, bf16[256,768]{1,0:T(8,128)(2,1)S(1)}, u32[]{:S(2)}, u32[]{:S(2)}) %collective-permute-start.19) | collective-permute-done | bytes 393248 | tf_op jit(solution)/shard_map/ppermute | solution.py:585
  316.5 1.7 collective-permute-done.20
  318.4 1.9 collective-permute-done.55
  322.3 2.1 collective-permute-done.56
  324.4 6.4 %collective-permute-start.57 = (f32[16,768]{1,0:T(8,128)S(1)}, f32[16,768]{1,0:T(8,128)S(1)}, u32[]{:S(2)}, u32[]{:S(2)}) collective-permute-start(f32[16,768]{1,0:T(8,128)S(1)} %add.322), channel_id=1, source_target_pairs={{0,1},{1,0},{2,3},{3,2},{4,5},{5,4},{6,7},{7,6},{8,9},{9,8},{10,11... | collective-permute-start | bytes 147464 | tf_op jit(solution)/shard_map/ppermute | solution.py:788
  331.1 3.4 collective-permute-start.39
  334.5 1.9 collective-permute-start.58
  336.4 1.9 broadcast_in_dim.63.clone.1
  339.2 23.9 %collective-permute-done.58 = f32[16,768]{1,0:T(8,128)S(1)} collective-permute-done((f32[16,768]{1,0:T(8,128)S(1)}, f32[16,768]{1,0:T(8,128)S(1)}, u32[]{:S(2)}, u32[]{:S(2)}) %collective-permute-start.58) | collective-permute-done | bytes 49184 | tf_op jit(solution)/shard_map/ppermute | solution.py:789
  364.7 8.2 %copy.49 = bf16[4,384,1728]{2,1,0:T(8,128)(2,1)} copy(bf16[4,384,1728]{1,2,0:T(8,128)(2,1)} %collective-permute-done.46) | data formatting | bytes 10616832 | tf_op jit(solution)/shard_map/ppermute | solution.py:582
  372.9 5.5 %add_convert_fusion = bf16[4,384,1728]{2,1,0:T(8,128)(2,1)S(1)} fusion(bf16[4,384,1728]{2,1,0:T(8,128)(2,1)} %copy.49, bf16[4,384,1728]{2,1,0:T(8,128)(2,1)} %get-tuple-element.73), kind=kLoop, calls=%fused_computation | loop fusion | flops 10616832 | bytes 15925248 | tf_op jit(solution)/shard_map/convert_element_type | solution.py:631
  381.0 1.6 collective-permute-start.42
  382.9 26.4 %collective-permute-done.42 = bf16[2,1,96,256]{2,3,1,0:T(8,128)(2,1)S(1)} collective-permute-done((bf16[2,1,96,256]{2,3,1,0:T(8,128)(2,1)S(1)}, bf16[2,1,96,256]{2,3,1,0:T(8,128)(2,1)S(1)}, u32[]{:S(2)}, u32[]{:S(2)}) %collective-permute-start.42) | collective-permute-done | bytes 98336 | tf_op jit(solution)/shard_map/ppermute | solution.py:583
  409.2 1.4 collective-permute-start.44
  410.8 8.4 %collective-permute-done.44 = bf16[2,1,96,320]{2,3,1,0:T(8,128)(2,1)S(1)} collective-permute-done((bf16[2,1,96,320]{2,3,1,0:T(8,128)(2,1)S(1)}, bf16[2,1,96,320]{2,3,1,0:T(8,128)(2,1)S(1)}, u32[]{:S(2)}, u32[]{:S(2)}) %collective-permute-start.44) | collective-permute-done | bytes 122912 | tf_op jit(solution)/shard_map/ppermute | solution.py:584
  420.5 2.9 collective-permute-done.43
  423.4 2.4 collective-permute-start.40
  426.0 1.4 collective-permute-start.45
  428.7 1.5 collective-permute-start.48
  433.2 7.5 %collective-permute-done.48 = bf16[4,96,768]{2,1,0:T(8,128)(2,1)S(1)} collective-permute-done((bf16[4,96,768]{2,1,0:T(8,128)(2,1)S(1)}, bf16[4,96,768]{2,1,0:T(8,128)(2,1)S(1)}, u32[]{:S(2)}, u32[]{:S(2)}) %collective-permute-start.48) | collective-permute-done | bytes 589856 | tf_op jit(solution)/shard_map/ppermute | solution.py:584
  440.9 6.4 %collective-permute-done.50 = bf16[4,96,960]{2,1,0:T(8,128)(2,1)S(1)} collective-permute-done((bf16[4,96,960]{2,1,0:T(8,128)(2,1)S(1)}, bf16[4,96,960]{2,1,0:T(8,128)(2,1)S(1)}, u32[]{:S(2)}, u32[]{:S(2)}) %collective-permute-start.50) | collective-permute-done | bytes 737312 | tf_op jit(solution)/shard_map/ppermute | solution.py:583
  452.8 6.3 %collective-permute-done.51 = bf16[96,1728]{1,0:T(8,128)(2,1)} collective-permute-done((bf16[96,1728]{1,0:T(8,128)(2,1)}, bf16[96,1728]{1,0:T(8,128)(2,1)}, u32[]{:S(2)}, u32[]{:S(2)}) %collective-permute-start.51) | collective-permute-done | bytes 331808 | tf_op jit(solution)/shard_map/ppermute | solution.py:585
  459.1 17.2 %collective-permute-done.52 = bf16[96,1728]{1,0:T(8,128)(2,1)} collective-permute-done((bf16[96,1728]{1,0:T(8,128)(2,1)}, bf16[96,1728]{1,0:T(8,128)(2,1)}, u32[]{:S(2)}, u32[]{:S(2)}) %collective-permute-start.52) | collective-permute-done | bytes 331808 | tf_op jit(solution)/shard_map/ppermute | solution.py:585
  476.3 1.4 fusion.27
  (238 shorter events, 50.3 us)
Async XLA Ops:
  0.6 46.8 %copy-start = (bf16[1,1024,768]{2,1,0:T(8,128)(2,1)S(1)}, bf16[1,1024,768]{2,1,0:T(8,128)(2,1)}, u32[]{:S(2)}) copy-start(bf16[1,1024,768]{2,1,0:T(8,128)(2,1)} %param.29) | copy-start | bytes 4718596
  2.1 14.7 %collective-permute-start = (bf16[384,576]{1,0:T(8,128)(2,1)S(1)}, bf16[384,576]{1,0:T(8,128)(2,1)S(1)}, u32[]{:S(2)}, u32[]{:S(2)}) collective-permute-start(bf16[384,576]{1,0:T(8,128)(2,1)S(1)} %copy.41.w_own), channel_id=1, source_target_pairs={{0,16},{16,0},{1,17},{17,1},{2,18},{18,2},{3,19},{19,3},{4,20},{20... | collective-permute-start | bytes 1327112 | tf_op jit(solution)/shard_map/ppermute | solution.py:582
  4.7 37.1 %collective-permute-start.8 = (bf16[960,384]{1,0:T(8,128)(2,1)S(1)}, bf16[960,384]{1,0:T(8,128)(2,1)}, u32[]{:S(2)}, u32[]{:S(2)}) collective-permute-start(bf16[960,384]{1,0:T(8,128)(2,1)S(1)} %constant_dynamic-update-slice_fusion.4), channel_id=1, source_target_pairs={{0,2},{1,3},{2,0},{3,1},{4,6},{5,7},{6,4},{7,5},{8,10},{9,11},{10,... | collective-permute-start | bytes 2211848 | tf_op jit(solution)/shard_map/ppermute | solution.py:595
  8.5 75.3 %collective-permute-start.10 = (bf16[960,384]{1,0:T(8,128)(2,1)S(1)}, bf16[960,384]{1,0:T(8,128)(2,1)}, u32[]{:S(2)}, u32[]{:S(2)}) collective-permute-start(bf16[960,384]{1,0:T(8,128)(2,1)S(1)} %constant_dynamic-update-slice_fusion.4), channel_id=1, source_target_pairs={{0,1},{1,2},{2,3},{4,5},{5,6},{6,7},{8,9},{9,10},{10,11},{12,13},{... | collective-permute-start | bytes 2211848 | tf_op jit(solution)/shard_map/ppermute | solution.py:595
  12.9 72.3 %collective-permute-start.11 = (bf16[960,384]{1,0:T(8,128)(2,1)S(1)}, bf16[960,384]{1,0:T(8,128)(2,1)}, u32[]{:S(2)}, u32[]{:S(2)}) collective-permute-start(bf16[960,384]{1,0:T(8,128)(2,1)S(1)} %constant_dynamic-update-slice_fusion.4), channel_id=1, source_target_pairs={{3,2},{2,1},{1,0},{7,6},{6,5},{5,4},{11,10},{10,9},{9,8},{15,14},{... | collective-permute-start | bytes 2211848 | tf_op jit(solution)/shard_map/ppermute | solution.py:595
  14.2 68.4 %collective-permute-start.13 = (bf16[384,768]{1,0:T(8,128)(2,1)}, bf16[384,768]{1,0:T(8,128)(2,1)}, u32[]{:S(2)}, u32[]{:S(2)}) collective-permute-start(bf16[384,768]{1,0:T(8,128)(2,1)} %param.19), channel_id=1, source_target_pairs={{0,2},{1,3},{2,0},{3,1},{4,6},{5,7},{6,4},{7,5},{8,10},{9,11},{10,... | collective-permute-start | bytes 1769480 | tf_op jit(solution)/shard_map/ppermute | solution.py:595
  23.9 41.0 %copy-start.11 = (bf16[192,1024]{1,0:T(8,128)(2,1)S(1)}, bf16[192,1024]{1,0:T(8,128)(2,1)}, u32[]{:S(2)}) copy-start(bf16[192,1024]{1,0:T(8,128)(2,1)} %get-tuple-element.46.refs_0_.refs_4_) | copy-start | bytes 1179652
  23.9 24.3 %collective-permute-start.3 = (bf16[192,1024]{1,0:T(8,128)(2,1)}, bf16[192,1024]{1,0:T(8,128)(2,1)S(1)}, u32[]{:S(2)}, u32[]{:S(2)}) collective-permute-start(bf16[192,1024]{1,0:T(8,128)(2,1)} %get-tuple-element.47.refs_3_.refs_7_), channel_id=1, source_target_pairs={{0,8},{8,0},{4,12},{12,4},{1,9},{9,1},{5,13},{13,5},{2,10},{10,2},... | collective-permute-start | bytes 1179656 | tf_op jit(solution)/shard_map/ppermute | solution.py:584
  41.8 45.0 %collective-permute-start.9 = (bf16[960,384]{1,0:T(8,128)(2,1)}, bf16[960,384]{1,0:T(8,128)(2,1)}, u32[]{:S(2)}, u32[]{:S(2)}) collective-permute-start(bf16[960,384]{1,0:T(8,128)(2,1)} %collective-permute-done.8), channel_id=1, source_target_pairs={{2,3},{1,0},{6,7},{5,4},{10,11},{9,8},{14,15},{13,12},{18,19},{17,... | collective-permute-start | bytes 2211848 | tf_op jit(solution)/shard_map/ppermute | solution.py:595
  48.2 10.7 %collective-permute-start.1 = (bf16[192,1024]{1,0:T(8,128)(2,1)}, bf16[192,1024]{1,0:T(8,128)(2,1)S(1)}, u32[]{:S(2)}, u32[]{:S(2)}) collective-permute-start(bf16[192,1024]{1,0:T(8,128)(2,1)} %get-tuple-element.46.refs_0_.refs_4_), channel_id=1, source_target_pairs={{0,4},{4,0},{8,12},{12,8},{1,5},{5,1},{9,13},{13,9},{2,6},{6,2},{1... | collective-permute-start | bytes 1179656 | tf_op jit(solution)/shard_map/ppermute | solution.py:583
  59.0 27.8 %copy-start.13 = (bf16[192,1024]{1,0:T(8,128)(2,1)}, bf16[192,1024]{1,0:T(8,128)(2,1)S(1)}, u32[]{:S(2)}) copy-start(bf16[192,1024]{1,0:T(8,128)(2,1)S(1)} %collective-permute-done.1.refs_1_.refs_5_) | copy-start | bytes 1179652
  59.0 33.7 %collective-permute-start.15 = (bf16[384,768]{1,0:T(8,128)(2,1)}, bf16[384,768]{1,0:T(8,128)(2,1)}, u32[]{:S(2)}, u32[]{:S(2)}) collective-permute-start(bf16[384,768]{1,0:T(8,128)(2,1)} %param.19), channel_id=1, source_target_pairs={{0,1},{1,2},{2,3},{4,5},{5,6},{6,7},{8,9},{9,10},{10,11},{12,13},{... | collective-permute-start | bytes 1769480 | tf_op jit(solution)/shard_map/ppermute | solution.py:595
  82.6 37.1 %collective-permute-start.16 = (bf16[384,768]{1,0:T(8,128)(2,1)}, bf16[384,768]{1,0:T(8,128)(2,1)}, u32[]{:S(2)}, u32[]{:S(2)}) collective-permute-start(bf16[384,768]{1,0:T(8,128)(2,1)} %param.19), channel_id=1, source_target_pairs={{3,2},{2,1},{1,0},{7,6},{6,5},{5,4},{11,10},{10,9},{9,8},{15,14},{... | collective-permute-start | bytes 1769480 | tf_op jit(solution)/shard_map/ppermute | solution.py:595
  83.9 35.8 %collective-permute-start.14 = (bf16[384,768]{1,0:T(8,128)(2,1)}, bf16[384,768]{1,0:T(8,128)(2,1)}, u32[]{:S(2)}, u32[]{:S(2)}) collective-permute-start(bf16[384,768]{1,0:T(8,128)(2,1)} %collective-permute-done.13), channel_id=1, source_target_pairs={{2,3},{1,0},{6,7},{5,4},{10,11},{9,8},{14,15},{13,12},{18,19},{17,... | collective-permute-start | bytes 1769480 | tf_op jit(solution)/shard_map/ppermute | solution.py:595
  85.2 38.8 %collective-permute-start.4 = (bf16[2,192,1024]{2,1,0:T(8,128)(2,1)S(1)}, bf16[2,192,1024]{2,1,0:T(8,128)(2,1)}, u32[]{:S(2)}, u32[]{:S(2)}) collective-permute-start(bf16[2,192,1024]{2,1,0:T(8,128)(2,1)S(1)} %pad_maximum_fusion.7), channel_id=1, source_target_pairs={{0,4},{4,0},{8,12},{12,8},{1,5},{5,1},{9,13},{13,9},{2,6},{6,2},{1... | collective-permute-start | bytes 2359304 | tf_op jit(solution)/shard_map/ppermute | solution.py:583
  86.8 37.2 %collective-permute-start.2 = (bf16[2,192,1024]{2,1,0:T(8,128)(2,1)}, bf16[2,192,1024]{2,1,0:T(8,128)(2,1)}, u32[]{:S(2)}, u32[]{:S(2)}) collective-permute-start(bf16[2,192,1024]{2,1,0:T(8,128)(2,1)} %pad_maximum_fusion.6), channel_id=1, source_target_pairs={{0,8},{8,0},{4,12},{12,4},{1,9},{9,1},{5,13},{13,5},{2,10},{10,2},... | collective-permute-start | bytes 2359304 | tf_op jit(solution)/shard_map/ppermute | solution.py:584
  92.6 55.2 %collective-permute-start.12 = (bf16[4,960,384]{2,1,0:T(8,128)(2,1)}, bf16[4,960,384]{2,1,0:T(8,128)(2,1)}, u32[]{:S(2)}, u32[]{:S(2)}) collective-permute-start(bf16[4,960,384]{2,1,0:T(8,128)(2,1)} %pad_maximum_fusion.1.refs_6_), channel_id=1, source_target_pairs={{0,16},{16,0},{1,17},{17,1},{2,18},{18,2},{3,19},{19,3},{4,20},{20... | collective-permute-start | bytes 8847368 | tf_op jit(solution)/shard_map/ppermute | solution.py:582
  123.9 23.9 %collective-permute-start.17 = (bf16[4,384,768]{2,1,0:T(8,128)(2,1)}, bf16[4,384,768]{2,1,0:T(8,128)(2,1)}, u32[]{:S(2)}, u32[]{:S(2)}) collective-permute-start(bf16[4,384,768]{2,1,0:T(8,128)(2,1)} %pad_maximum_fusion.2.refs_8_), channel_id=1, source_target_pairs={{0,16},{16,0},{1,17},{17,1},{2,18},{18,2},{3,19},{19,3},{4,20},{20... | collective-permute-start | bytes 7077896 | tf_op jit(solution)/shard_map/ppermute | solution.py:582
  133.6 7.8 %collective-permute-start.5 = (bf16[192,256]{1,0:T(8,128)(2,1)}, bf16[192,256]{1,0:T(8,128)(2,1)S(1)}, u32[]{:S(2)}, u32[]{:S(2)}) collective-permute-start(bf16[192,256]{1,0:T(8,128)(2,1)} %get-tuple-element.49), channel_id=1, source_target_pairs={{0,1},{1,2},{2,3},{3,0},{4,5},{5,6},{6,7},{7,4},{8,9},{9,10},{10,1... | collective-permute-start | bytes 294920 | tf_op jit(solution)/shard_map/ppermute | solution.py:585
  133.7 11.0 %collective-permute-start.6 = (bf16[192,256]{1,0:T(8,128)(2,1)}, bf16[192,256]{1,0:T(8,128)(2,1)S(1)}, u32[]{:S(2)}, u32[]{:S(2)}) collective-permute-start(bf16[192,256]{1,0:T(8,128)(2,1)} %get-tuple-element.50), channel_id=1, source_target_pairs={{0,2},{1,3},{2,0},{3,1},{4,6},{5,7},{6,4},{7,5},{8,10},{9,11},{10,... | collective-permute-start | bytes 294920 | tf_op jit(solution)/shard_map/ppermute | solution.py:585
  134.4 10.3 %collective-permute-start.7 = (bf16[192,256]{1,0:T(8,128)(2,1)}, bf16[192,256]{1,0:T(8,128)(2,1)S(1)}, u32[]{:S(2)}, u32[]{:S(2)}) collective-permute-start(bf16[192,256]{1,0:T(8,128)(2,1)} %get-tuple-element.51), channel_id=1, source_target_pairs={{0,3},{1,0},{2,1},{3,2},{4,7},{5,4},{6,5},{7,6},{8,11},{9,8},{10,9... | collective-permute-start | bytes 294920 | tf_op jit(solution)/shard_map/ppermute | solution.py:585
  141.4 50.9 %collective-permute-start.34 = (bf16[384,576]{1,0:T(8,128)(2,1)S(1)}, bf16[384,576]{1,0:T(8,128)(2,1)S(1)}, u32[]{:S(2)}, u32[]{:S(2)}) collective-permute-start(bf16[384,576]{1,0:T(8,128)(2,1)S(1)} %copy.42), channel_id=1, source_target_pairs={{0,1},{1,2},{2,3},{3,0},{4,5},{5,6},{6,7},{7,4},{8,9},{9,10},{10,1... | collective-permute-start | bytes 1327112 | tf_op jit(solution)/shard_map/ppermute | solution.py:585
  144.6 49.0 %collective-permute-start.35 = (bf16[384,576]{1,0:T(8,128)(2,1)S(1)}, bf16[384,576]{1,0:T(8,128)(2,1)S(1)}, u32[]{:S(2)}, u32[]{:S(2)}) collective-permute-start(bf16[384,576]{1,0:T(8,128)(2,1)S(1)} %copy.42), channel_id=1, source_target_pairs={{0,2},{1,3},{2,0},{3,1},{4,6},{5,7},{6,4},{7,5},{8,10},{9,11},{10,... | collective-permute-start | bytes 1327112 | tf_op jit(solution)/shard_map/ppermute | solution.py:585
  144.7 49.0 %collective-permute-start.36 = (bf16[384,576]{1,0:T(8,128)(2,1)S(1)}, bf16[384,576]{1,0:T(8,128)(2,1)S(1)}, u32[]{:S(2)}, u32[]{:S(2)}) collective-permute-start(bf16[384,576]{1,0:T(8,128)(2,1)S(1)} %copy.42), channel_id=1, source_target_pairs={{0,3},{1,0},{2,1},{3,2},{4,7},{5,4},{6,5},{7,6},{8,11},{9,8},{10,9... | collective-permute-start | bytes 1327112 | tf_op jit(solution)/shard_map/ppermute | solution.py:585
  169.5 35.8 %collective-permute-start.21 = (bf16[192,256]{1,0:T(8,128)(2,1)}, bf16[192,256]{1,0:T(8,128)(2,1)S(1)}, u32[]{:S(2)}, u32[]{:S(2)}) collective-permute-start(bf16[192,256]{1,0:T(8,128)(2,1)} %get-tuple-element.56), channel_id=1, source_target_pairs={{0,3},{1,0},{2,1},{3,2},{4,7},{5,4},{6,5},{7,6},{8,11},{9,8},{10,9... | collective-permute-start | bytes 294920 | tf_op jit(solution)/shard_map/ppermute | solution.py:585
  190.7 14.6 %collective-permute-start.22 = (bf16[192,256]{1,0:T(8,128)(2,1)}, bf16[192,256]{1,0:T(8,128)(2,1)}, u32[]{:S(2)}, u32[]{:S(2)}) collective-permute-start(bf16[192,256]{1,0:T(8,128)(2,1)} %get-tuple-element.57), channel_id=1, source_target_pairs={{0,2},{1,3},{2,0},{3,1},{4,6},{5,7},{6,4},{7,5},{8,10},{9,11},{10,... | collective-permute-start | bytes 294920 | tf_op jit(solution)/shard_map/ppermute | solution.py:585
  192.2 13.1 %collective-permute-start.23 = (bf16[192,256]{1,0:T(8,128)(2,1)}, bf16[192,256]{1,0:T(8,128)(2,1)}, u32[]{:S(2)}, u32[]{:S(2)}) collective-permute-start(bf16[192,256]{1,0:T(8,128)(2,1)} %get-tuple-element.58), channel_id=1, source_target_pairs={{0,1},{1,2},{2,3},{3,0},{4,5},{5,6},{6,7},{7,4},{8,9},{9,10},{10,1... | collective-permute-start | bytes 294920 | tf_op jit(solution)/shard_map/ppermute | solution.py:585
  196.6 46.6 %collective-permute-start.37 = (bf16[4,384,576]{1,2,0:T(8,128)(2,1)}, bf16[4,384,576]{1,2,0:T(8,128)(2,1)}, u32[]{:S(2)}, u32[]{:S(2)}) collective-permute-start(bf16[4,384,576]{1,2,0:T(8,128)(2,1)} %copy.46), channel_id=1, source_target_pairs={{0,16},{16,0},{1,17},{17,1},{2,18},{18,2},{3,19},{19,3},{4,20},{20... | collective-permute-start | bytes 5308424 | tf_op jit(solution)/shard_map/ppermute | solution.py:582
  204.8 159.9 %collective-permute-start.46 = (bf16[4,384,1728]{1,2,0:T(8,128)(2,1)}, bf16[4,384,1728]{1,2,0:T(8,128)(2,1)}, u32[]{:S(2)}, u32[]{:S(2)}) collective-permute-start(bf16[4,384,1728]{1,2,0:T(8,128)(2,1)} %copy.48), channel_id=1, source_target_pairs={{0,16},{16,0},{1,17},{17,1},{2,18},{18,2},{3,19},{19,3},{4,20},{20... | collective-permute-start | bytes 15925256 | tf_op jit(solution)/shard_map/ppermute | solution.py:582
  218.6 28.5 %copy-start.10 = (bf16[256,768]{1,0:T(8,128)(2,1)S(1)}, bf16[256,768]{1,0:T(8,128)(2,1)}, u32[]{:S(2)}) copy-start(bf16[256,768]{1,0:T(8,128)(2,1)} %get-tuple-element.52) | copy-start | bytes 1179652
  218.6 42.5 %collective-permute-start.26 = (bf16[2,192,1024]{2,1,0:T(8,128)(2,1)}, bf16[2,192,1024]{2,1,0:T(8,128)(2,1)S(1)}, u32[]{:S(2)}, u32[]{:S(2)}) collective-permute-start(bf16[2,192,1024]{2,1,0:T(8,128)(2,1)} %get-tuple-element.63), channel_id=1, source_target_pairs={{0,8},{8,0},{4,12},{12,4},{1,9},{9,1},{5,13},{13,5},{2,10},{10,2},... | collective-permute-start | bytes 2359304 | tf_op jit(solution)/shard_map/ppermute | solution.py:584
  243.2 19.4 %collective-permute-start.24 = (bf16[2,192,1024]{2,1,0:T(8,128)(2,1)}, bf16[2,192,1024]{2,1,0:T(8,128)(2,1)S(1)}, u32[]{:S(2)}, u32[]{:S(2)}) collective-permute-start(bf16[2,192,1024]{2,1,0:T(8,128)(2,1)} %get-tuple-element.61), channel_id=1, source_target_pairs={{0,4},{4,0},{8,12},{12,8},{1,5},{5,1},{9,13},{13,9},{2,6},{6,2},{1... | collective-permute-start | bytes 2359304 | tf_op jit(solution)/shard_map/ppermute | solution.py:583
  247.1 38.4 %collective-permute-start.18 = (bf16[256,768]{1,0:T(8,128)(2,1)S(1)}, bf16[256,768]{1,0:T(8,128)(2,1)S(1)}, u32[]{:S(2)}, u32[]{:S(2)}) collective-permute-start(bf16[256,768]{1,0:T(8,128)(2,1)S(1)} %copy-done.10), channel_id=1, source_target_pairs={{0,1},{1,2},{2,3},{3,0},{4,5},{5,6},{6,7},{7,4},{8,9},{9,10},{10,1... | collective-permute-start | bytes 1179656 | tf_op jit(solution)/shard_map/ppermute | solution.py:585
  248.0 28.4 %collective-permute-start.28 = (bf16[192,256]{1,0:T(8,128)(2,1)S(1)}, bf16[192,256]{1,0:T(8,128)(2,1)S(1)}, u32[]{:S(2)}, u32[]{:S(2)}) collective-permute-start(bf16[192,256]{1,0:T(8,128)(2,1)S(1)} %copy-done.18), channel_id=1, source_target_pairs={{0,1},{1,2},{2,3},{3,0},{4,5},{5,6},{6,7},{7,4},{8,9},{9,10},{10,1... | collective-permute-start | bytes 294920 | tf_op jit(solution)/shard_map/ppermute | solution.py:585
  261.4 10.6 %collective-permute-start.27 = (bf16[192,1024]{1,0:T(8,128)(2,1)S(1)}, bf16[192,1024]{1,0:T(8,128)(2,1)S(1)}, u32[]{:S(2)}, u32[]{:S(2)}) collective-permute-start(bf16[192,1024]{1,0:T(8,128)(2,1)S(1)} %fusion.29), channel_id=1, source_target_pairs={{0,4},{4,0},{8,12},{12,8},{1,5},{5,1},{9,13},{13,9},{2,6},{6,2},{1... | collective-permute-start | bytes 1179656 | tf_op jit(solution)/shard_map/ppermute | solution.py:583
  262.9 10.2 %collective-permute-start.25 = (bf16[192,1024]{1,0:T(8,128)(2,1)S(1)}, bf16[192,1024]{1,0:T(8,128)(2,1)S(1)}, u32[]{:S(2)}, u32[]{:S(2)}) collective-permute-start(bf16[192,1024]{1,0:T(8,128)(2,1)S(1)} %fusion.28), channel_id=1, source_target_pairs={{0,8},{8,0},{4,12},{12,4},{1,9},{9,1},{5,13},{13,5},{2,10},{10,2},... | collective-permute-start | bytes 1179656 | tf_op jit(solution)/shard_map/ppermute | solution.py:584
  272.0 13.5 %collective-permute-start.30 = (bf16[192,256]{1,0:T(8,128)(2,1)S(1)}, bf16[192,256]{1,0:T(8,128)(2,1)S(1)}, u32[]{:S(2)}, u32[]{:S(2)}) collective-permute-start(bf16[192,256]{1,0:T(8,128)(2,1)S(1)} %copy-done.17), channel_id=1, source_target_pairs={{0,2},{1,3},{2,0},{3,1},{4,6},{5,7},{6,4},{7,5},{8,10},{9,11},{10,... | collective-permute-start | bytes 294920 | tf_op jit(solution)/shard_map/ppermute | solution.py:585
  273.1 12.6 %collective-permute-start.32 = (bf16[192,256]{1,0:T(8,128)(2,1)S(1)}, bf16[192,256]{1,0:T(8,128)(2,1)S(1)}, u32[]{:S(2)}, u32[]{:S(2)}) collective-permute-start(bf16[192,256]{1,0:T(8,128)(2,1)S(1)} %copy-done.16), channel_id=1, source_target_pairs={{0,3},{1,0},{2,1},{3,2},{4,7},{5,4},{6,5},{7,6},{8,11},{9,8},{10,9... | collective-permute-start | bytes 294920 | tf_op jit(solution)/shard_map/ppermute | solution.py:585
  276.4 12.3 %collective-permute-start.29 = (bf16[384,256]{1,0:T(8,128)(2,1)S(1)}, bf16[384,256]{1,0:T(8,128)(2,1)S(1)}, u32[]{:S(2)}, u32[]{:S(2)}) collective-permute-start(bf16[384,256]{1,0:T(8,128)(2,1)S(1)} %get-tuple-element.142), channel_id=1, source_target_pairs={{0,1},{1,2},{2,3},{3,0},{4,5},{5,6},{6,7},{7,4},{8,9},{9,10},{10,1... | collective-permute-start | bytes 589832 | tf_op jit(solution)/shard_map/ppermute | solution.py:585
  285.5 14.8 %collective-permute-start.31 = (bf16[384,256]{1,0:T(8,128)(2,1)S(1)}, bf16[384,256]{1,0:T(8,128)(2,1)S(1)}, u32[]{:S(2)}, u32[]{:S(2)}) collective-permute-start(bf16[384,256]{1,0:T(8,128)(2,1)S(1)} %get-tuple-element.143), channel_id=1, source_target_pairs={{0,2},{1,3},{2,0},{3,1},{4,6},{5,7},{6,4},{7,5},{8,10},{9,11},{10,... | collective-permute-start | bytes 589832 | tf_op jit(solution)/shard_map/ppermute | solution.py:585
  285.5 14.8 %collective-permute-start.33 = (bf16[384,256]{1,0:T(8,128)(2,1)S(1)}, bf16[384,256]{1,0:T(8,128)(2,1)S(1)}, u32[]{:S(2)}, u32[]{:S(2)}) collective-permute-start(bf16[384,256]{1,0:T(8,128)(2,1)S(1)} %get-tuple-element.140), channel_id=1, source_target_pairs={{0,3},{1,0},{2,1},{3,2},{4,7},{5,4},{6,5},{7,6},{8,11},{9,8},{10,9... | collective-permute-start | bytes 589832 | tf_op jit(solution)/shard_map/ppermute | solution.py:585
  285.7 29.6 %collective-permute-start.19 = (bf16[256,768]{1,0:T(8,128)(2,1)S(1)}, bf16[256,768]{1,0:T(8,128)(2,1)S(1)}, u32[]{:S(2)}, u32[]{:S(2)}) collective-permute-start(bf16[256,768]{1,0:T(8,128)(2,1)S(1)} %copy-done.10), channel_id=1, source_target_pairs={{0,2},{1,3},{2,0},{3,1},{4,6},{5,7},{6,4},{7,5},{8,10},{9,11},{10,... | collective-permute-start | bytes 1179656 | tf_op jit(solution)/shard_map/ppermute | solution.py:585
  288.7 29.6 %collective-permute-start.20 = (bf16[256,768]{1,0:T(8,128)(2,1)S(1)}, bf16[256,768]{1,0:T(8,128)(2,1)S(1)}, u32[]{:S(2)}, u32[]{:S(2)}) collective-permute-start(bf16[256,768]{1,0:T(8,128)(2,1)S(1)} %copy-done.10), channel_id=1, source_target_pairs={{0,3},{1,0},{2,1},{3,2},{4,7},{5,4},{6,5},{7,6},{8,11},{9,8},{10,9... | collective-permute-start | bytes 1179656 | tf_op jit(solution)/shard_map/ppermute | solution.py:585
  306.9 8.4 %collective-permute-start.54 = (f32[16,768]{1,0:T(8,128)}, f32[16,768]{1,0:T(8,128)S(1)}, u32[]{:S(2)}, u32[]{:S(2)}) collective-permute-start(f32[16,768]{1,0:T(8,128)} %get-tuple-element.75), channel_id=1, source_target_pairs={{0,16},{16,0},{1,17},{17,1},{2,18},{18,2},{3,19},{19,3},{4,20},{20... | collective-permute-start | bytes 147464 | tf_op jit(solution)/shard_map/ppermute | solution.py:582
  316.2 4.1 collective-permute-start.55
  320.2 4.2 collective-permute-start.56
  324.4 10.1 %collective-permute-start.57 = (f32[16,768]{1,0:T(8,128)S(1)}, f32[16,768]{1,0:T(8,128)S(1)}, u32[]{:S(2)}, u32[]{:S(2)}) collective-permute-start(f32[16,768]{1,0:T(8,128)S(1)} %add.322), channel_id=1, source_target_pairs={{0,1},{1,0},{2,3},{3,2},{4,5},{5,4},{6,7},{7,6},{8,9},{9,8},{10,11... | collective-permute-start | bytes 147464 | tf_op jit(solution)/shard_map/ppermute | solution.py:788
  330.9 33.5 %collective-permute-start.41 = (bf16[1,384,576]{1,2,0:T(8,128)(2,1)S(1)}, bf16[1,384,576]{1,2,0:T(8,128)(2,1)S(1)}, u32[]{:S(2)}, u32[]{:S(2)}) collective-permute-start(bf16[1,384,576]{1,2,0:T(8,128)(2,1)S(1)} %dynamic-slice_bitcast_fusion.4), channel_id=1, source_target_pairs={{0,16},{16,0},{1,17},{17,1},{2,18},{18,2},{3,19},{19,3},{4,20},{20... | collective-permute-start | bytes 1327112 | tf_op jit(solution)/shard_map/ppermute | solution.py:582
  331.0 95.0 %collective-permute-start.38 = (bf16[256,768]{1,0:T(8,128)(2,1)S(1)}, bf16[256,768]{1,0:T(8,128)(2,1)S(1)}, u32[]{:S(2)}, u32[]{:S(2)}) collective-permute-start(bf16[256,768]{1,0:T(8,128)(2,1)S(1)} %copy-done.14), channel_id=1, source_target_pairs={{0,1},{1,2},{2,3},{3,0},{4,5},{5,6},{6,7},{7,4},{8,9},{9,10},{10,1... | collective-permute-start | bytes 1179656 | tf_op jit(solution)/shard_map/ppermute | solution.py:585
  331.1 100.3 %collective-permute-start.39 = (bf16[256,768]{1,0:T(8,128)(2,1)S(1)}, bf16[256,768]{1,0:T(8,128)(2,1)S(1)}, u32[]{:S(2)}, u32[]{:S(2)}) collective-permute-start(bf16[256,768]{1,0:T(8,128)(2,1)S(1)} %copy-done.14), channel_id=1, source_target_pairs={{0,2},{1,3},{2,0},{3,1},{4,6},{5,7},{6,4},{7,5},{8,10},{9,11},{10,... | collective-permute-start | bytes 1179656 | tf_op jit(solution)/shard_map/ppermute | solution.py:585
  334.5 28.6 %collective-permute-start.58 = (f32[16,768]{1,0:T(8,128)S(1)}, f32[16,768]{1,0:T(8,128)S(1)}, u32[]{:S(2)}, u32[]{:S(2)}) collective-permute-start(f32[16,768]{1,0:T(8,128)S(1)} %add.323), channel_id=1, source_target_pairs={{0,2},{2,0},{1,3},{3,1},{4,6},{6,4},{5,7},{7,5},{8,10},{10,8},{9,1... | collective-permute-start | bytes 147464 | tf_op jit(solution)/shard_map/ppermute | solution.py:789
  364.5 61.3 %copy-start.5 = (bf16[1,384,576]{1,2,0:T(8,128)(2,1)}, bf16[1,384,576]{1,2,0:T(8,128)(2,1)S(1)}, u32[]{:S(2)}) copy-start(bf16[1,384,576]{1,2,0:T(8,128)(2,1)S(1)} %fusion.14) | copy-start | bytes 1327108
  378.6 49.7 %collective-permute-start.47 = (bf16[2,4,96,768]{3,2,1,0:T(8,128)(2,1)S(1)}, bf16[2,4,96,768]{3,2,1,0:T(8,128)(2,1)S(1)}, u32[]{:S(2)}, u32[]{:S(2)}) collective-permute-start(bf16[2,4,96,768]{3,2,1,0:T(8,128)(2,1)S(1)} %pad_maximum_fusion.5), channel_id=1, source_target_pairs={{0,4},{4,0},{8,12},{12,8},{1,5},{5,1},{9,13},{13,9},{2,6},{6,2},{1... | collective-permute-start | bytes 3538952 | tf_op jit(solution)/shard_map/ppermute | solution.py:583
  379.7 50.5 %collective-permute-start.49 = (bf16[2,4,96,960]{3,2,1,0:T(8,128)(2,1)S(1)}, bf16[2,4,96,960]{3,2,1,0:T(8,128)(2,1)S(1)}, u32[]{:S(2)}, u32[]{:S(2)}) collective-permute-start(bf16[2,4,96,960]{3,2,1,0:T(8,128)(2,1)S(1)} %pad_maximum_fusion.4), channel_id=1, source_target_pairs={{0,8},{8,0},{4,12},{12,4},{1,9},{9,1},{5,13},{13,5},{2,10},{10,2},... | collective-permute-start | bytes 4423688 | tf_op jit(solution)/shard_map/ppermute | solution.py:584
  381.0 28.2 %collective-permute-start.42 = (bf16[2,1,96,256]{2,3,1,0:T(8,128)(2,1)S(1)}, bf16[2,1,96,256]{2,3,1,0:T(8,128)(2,1)S(1)}, u32[]{:S(2)}, u32[]{:S(2)}) collective-permute-start(bf16[2,1,96,256]{2,3,1,0:T(8,128)(2,1)S(1)} %pad_maximum_fusion.10), channel_id=1, source_target_pairs={{0,4},{4,0},{8,12},{12,8},{1,5},{5,1},{9,13},{13,9},{2,6},{6,2},{1... | collective-permute-start | bytes 294920 | tf_op jit(solution)/shard_map/ppermute | solution.py:583
  409.2 10.0 %collective-permute-start.44 = (bf16[2,1,96,320]{2,3,1,0:T(8,128)(2,1)S(1)}, bf16[2,1,96,320]{2,3,1,0:T(8,128)(2,1)S(1)}, u32[]{:S(2)}, u32[]{:S(2)}) collective-permute-start(bf16[2,1,96,320]{2,3,1,0:T(8,128)(2,1)S(1)} %pad_maximum_fusion.9), channel_id=1, source_target_pairs={{0,8},{8,0},{4,12},{12,4},{1,9},{9,1},{5,13},{13,5},{2,10},{10,2},... | collective-permute-start | bytes 368648 | tf_op jit(solution)/shard_map/ppermute | solution.py:584
  419.2 4.3 collective-permute-start.43
  423.4 8.9 %collective-permute-start.40 = (bf16[256,768]{1,0:T(8,128)(2,1)S(1)}, bf16[256,768]{1,0:T(8,128)(2,1)S(1)}, u32[]{:S(2)}, u32[]{:S(2)}) collective-permute-start(bf16[256,768]{1,0:T(8,128)(2,1)S(1)} %copy-done.14), channel_id=1, source_target_pairs={{0,3},{1,0},{2,1},{3,2},{4,7},{5,4},{6,5},{7,6},{8,11},{9,8},{10,9... | collective-permute-start | bytes 1179656 | tf_op jit(solution)/shard_map/ppermute | solution.py:585
  426.0 24.9 %collective-permute-start.45 = (bf16[1,96,320]{1,2,0:T(8,128)(2,1)S(1)}, bf16[1,96,320]{1,2,0:T(8,128)(2,1)S(1)}, u32[]{:S(2)}, u32[]{:S(2)}) collective-permute-start(bf16[1,96,320]{1,2,0:T(8,128)(2,1)S(1)} %fusion.35), channel_id=1, source_target_pairs={{0,4},{4,0},{8,12},{12,8},{1,5},{5,1},{9,13},{13,9},{2,6},{6,2},{1... | collective-permute-start | bytes 184328 | tf_op jit(solution)/shard_map/ppermute | solution.py:583
  428.7 12.0 %collective-permute-start.48 = (bf16[4,96,768]{2,1,0:T(8,128)(2,1)S(1)}, bf16[4,96,768]{2,1,0:T(8,128)(2,1)S(1)}, u32[]{:S(2)}, u32[]{:S(2)}) collective-permute-start(bf16[4,96,768]{2,1,0:T(8,128)(2,1)S(1)} %fusion.6), channel_id=1, source_target_pairs={{0,8},{8,0},{4,12},{12,4},{1,9},{9,1},{5,13},{13,5},{2,10},{10,2},... | collective-permute-start | bytes 1769480 | tf_op jit(solution)/shard_map/ppermute | solution.py:584
  430.8 16.5 %collective-permute-start.50 = (bf16[4,96,960]{2,1,0:T(8,128)(2,1)S(1)}, bf16[4,96,960]{2,1,0:T(8,128)(2,1)S(1)}, u32[]{:S(2)}, u32[]{:S(2)}) collective-permute-start(bf16[4,96,960]{2,1,0:T(8,128)(2,1)S(1)} %fusion.2), channel_id=1, source_target_pairs={{0,4},{4,0},{8,12},{12,8},{1,5},{5,1},{9,13},{13,9},{2,6},{6,2},{1... | collective-permute-start | bytes 2211848 | tf_op jit(solution)/shard_map/ppermute | solution.py:583
  448.8 10.3 %collective-permute-start.51 = (bf16[96,1728]{1,0:T(8,128)(2,1)}, bf16[96,1728]{1,0:T(8,128)(2,1)}, u32[]{:S(2)}, u32[]{:S(2)}) collective-permute-start(bf16[96,1728]{1,0:T(8,128)(2,1)} %get-tuple-element.137), channel_id=1, source_target_pairs={{0,3},{1,0},{2,1},{3,2},{4,7},{5,4},{6,5},{7,6},{8,11},{9,8},{10,9... | collective-permute-start | bytes 995336 | tf_op jit(solution)/shard_map/ppermute | solution.py:585
  448.8 27.5 %collective-permute-start.52 = (bf16[96,1728]{1,0:T(8,128)(2,1)}, bf16[96,1728]{1,0:T(8,128)(2,1)}, u32[]{:S(2)}, u32[]{:S(2)}) collective-permute-start(bf16[96,1728]{1,0:T(8,128)(2,1)} %get-tuple-element.139), channel_id=1, source_target_pairs={{0,2},{1,3},{2,0},{3,1},{4,6},{5,7},{6,4},{7,5},{8,10},{9,11},{10,... | collective-permute-start | bytes 995336 | tf_op jit(solution)/shard_map/ppermute | solution.py:585
  449.9 26.4 %collective-permute-start.53 = (bf16[96,1728]{1,0:T(8,128)(2,1)}, bf16[96,1728]{1,0:T(8,128)(2,1)}, u32[]{:S(2)}, u32[]{:S(2)}) collective-permute-start(bf16[96,1728]{1,0:T(8,128)(2,1)} %get-tuple-element.138), channel_id=1, source_target_pairs={{0,1},{1,2},{2,3},{3,0},{4,5},{5,6},{6,7},{7,4},{8,9},{9,10},{10,1... | collective-permute-start | bytes 995336 | tf_op jit(solution)/shard_map/ppermute | solution.py:585
  (34 other events, 307.9 us)

commit v3 on v2

--- a/solution.py
+++ b/solution.py
@@ -356,8 +356,8 @@
 
 def middle_kernel(n_att, parts, sc, *refs):
     att, refs = refs[:n_att], refs[n_att:]
-    x, cot, od_own, od_other, fc_own, fc_other, b_fc, rows = refs[:8]
-    refs = refs[8:]
+    x, cot, of_own, of_other, dn_own, dn_other, rows = refs[:7]
+    refs = refs[7:]
     outputs, grad_mid, sums, fc_sums = refs[:4]
     d_att, (g_own, g_other) = refs[4 : 4 + parts], refs[4 + parts : 6 + parts]
     mid, att_t, low, low_t, cot_t, mlp, back = refs[6 + parts :]
@@ -365,7 +365,8 @@
     width = x.shape[1]
     own, other = halves(sc[2], width)
     half = width // 2
-    ffw = fc_own.shape[2]
+    ffw = dn_own.shape[1]
+    count = ffw // half
     cols = att_t.shape[0] // parts
     b_out, b_down, gain, shift = (rows[n : n + 1, :] for n in range(2, 6))
 
@@ -382,8 +383,8 @@
         mine = theirs = 0.0
         for part in range(parts):
             piece = att_low[:, part * cols : (part + 1) * cols]
-            mine += nn(piece, od_own[part, :cols, :])
-            theirs += nn(piece, od_other[part, :cols, :])
+            mine += nn(piece, of_own[part, :cols, :])
+            theirs += nn(piece, of_other[part, :cols, :])
         mid[:, own] = mine
         mid[:, other] = theirs
         mid[...] = x[...].astype(f32) + mid[...] + b_out
@@ -396,17 +397,26 @@
 
     own_rows = pl.ds(pl.multiple_of(sc[2] * half, half), half)
     other_rows = pl.ds(pl.multiple_of((1 - sc[2]) * half, half), half)
-    dn_own, dn_other = od_own[d, cols:, :], od_other[d, cols:, :]
-    u = nn(low[:, own], fc_own[0]) + nn(low[:, other], fc_other[0]) + b_fc[0]
+    terms = of_own[d, cols : cols + 16, :].astype(f32)
+    pieces = [slice(cols + 16 + n * half, cols + 16 + (n + 1) * half) for n in range(count)]
+    u = [
+        nn(low[:, own], of_own[d, at, :])
+        + nn(low[:, other], of_other[d, at, :])
+        + sum(terms[t * count + n : t * count + n + 1, :] for t in range(3))
+        for n, at in enumerate(pieces)
+    ]
+    u = jnp.concatenate(u, axis=1)
     t = jnp.tanh(ROOT * (u + 0.044715 * (u * u * u)))
     act = (0.5 * u * (1.0 + t)).astype(bf16)
     slope = 0.5 * (1.0 + t) + (0.5 * ROOT) * u * (1.0 - t * t) * (1.0 + 0.134145 * (u * u))
-    d_act = nt(cot[:, own], dn_own) + nt(cot[:, other], dn_other)
+    d_act = nt(cot[:, own], dn_own[0]) + nt(cot[:, other], dn_other[0])
     dh = (d_act * slope).astype(bf16)
-    mlp[:, own] += nn(act, dn_own)
-    mlp[:, other] += nn(act, dn_other)
-    back[:, own] += nt(dh, fc_own[0])
-    back[:, other] += nt(dh, fc_other[0])
+    mlp[:, own] += nn(act, dn_own[0])
+    mlp[:, other] += nn(act, dn_other[0])
+    for n, at in enumerate(pieces):
+        dh_n = dh[:, n * half : (n + 1) * half]
+        back[:, own] += nt(dh_n, of_own[d, at, :])
+        back[:, other] += nt(dh_n, of_other[d, at, :])
     g_own[d, :, :ffw] = nn(low_t[own_rows, :], dh).astype(bf16)
     g_other[d, :, :ffw] = nn(low_t[other_rows, :], dh).astype(bf16)
     g_own[d, :, ffw : 2 * ffw] = nn(cot_t[own_rows, :], act).astype(bf16)
@@ -427,36 +437,48 @@
         sums[3:4, :] = jnp.sum(grad, axis=0, keepdims=True)
         low[...] = down.astype(bf16)
         low_t[...] = low[...].T
+        g_own[:, :, 2 * ffw + cols :] = jnp.zeros_like(g_own[:, :, 2 * ffw + cols :])
+        g_other[:, :, 2 * ffw + cols :] = jnp.zeros_like(g_other[:, :, 2 * ffw + cols :])
         for part in range(parts):
             at = slice(part * cols, (part + 1) * cols)
-            g_own[part, :, 2 * ffw :] = nt(low_t[own_rows, :], att_t[at, :]).astype(bf16)
-            g_other[part, :, 2 * ffw :] = nt(low_t[other_rows, :], att_t[at, :]).astype(bf16)
+            g_own[part, :, 2 * ffw : 2 * ffw + cols] = nt(low_t[own_rows, :], att_t[at, :]).astype(bf16)
+            g_other[part, :, 2 * ffw : 2 * ffw + cols] = nt(low_t[other_rows, :], att_t[at, :]).astype(bf16)
             d_att[part][...] = (
-                nt(od_own[part, :cols, :], low[:, own]) + nt(od_other[part, :cols, :], low[:, other])
+                nt(of_own[part, :cols, :], low[:, own]) + nt(of_other[part, :cols, :], low[:, other])
             ).astype(bf16)
 
 
-def middle(place, att, x, cot, od, fc, b_fc, table):
-    parts, half, ffw = fc[0].shape
+def middle(place, att, x, cot, of, dn, cols, table):
+    parts, ffw, half = dn[0].shape
     sub, width = x.shape
-    cols = od[0].shape[1] - ffw
     whole = lambda *dims: pl.BlockSpec(
-        dims, lambda i: (0,) * len(dims), pipeline_mode=pl.Buffered(1)
-    )
-    each = lambda *dims: pl.BlockSpec((1,) + dims, lambda i: (i, 0, 0))
+        dims, lambda i, sc: (0,) * len(dims), pipeline_mode=pl.Buffered(1)
+    )
+    placed = pl.BlockSpec(
+        (1, ffw, half), lambda i, sc: (lax.rem(sc[3] - i + parts, parts), 0, 0)
+    )
     once = lambda a: whole(*a.shape)
-    grads = (parts, half, 2 * ffw + cols)
+    grads = (parts, half, 128 * ((2 * ffw + cols + 127) // 128))
     return pl.pallas_call(
         functools.partial(middle_kernel, len(att), parts),
-        grid=(parts,),
-        in_specs=[SM]
-        + [once(a) for a in att]
-        + [once(x), once(cot), once(od[0]), once(od[1])]
-        + [each(half, ffw)] * 2
-        + [each(1, ffw), once(table)],
-        out_specs=[whole(sub, width), whole(sub, width), whole(4, width), whole(parts, 1, ffw)]
-        + [whole(cols, sub)] * parts
-        + [whole(*grads)] * 2,
+        grid_spec=pltpu.PrefetchScalarGridSpec(
+            num_scalar_prefetch=1,
+            grid=(parts,),
+            in_specs=[once(a) for a in att]
+            + [once(x), once(cot), once(of[0]), once(of[1]), placed, placed, once(table)],
+            out_specs=[whole(sub, width), whole(sub, width), whole(4, width), whole(parts, 1, ffw)]
+            + [whole(cols, sub)] * parts
+            + [whole(*grads)] * 2,
+            scratch_shapes=[
+                pltpu.VMEM((sub, width), f32),
+                pltpu.VMEM((parts * cols, sub), bf16),
+                pltpu.VMEM((sub, width), bf16),
+                pltpu.VMEM((width, sub), bf16),
+                pltpu.VMEM((width, sub), bf16),
+                pltpu.VMEM((sub, width), f32),
+                pltpu.VMEM((sub, width), f32),
+            ],
+        ),
         out_shape=[
             shape((sub, width)),
             shape((sub, width), f32),
@@ -465,19 +487,10 @@
         ]
         + [shape((cols, sub))] * parts
         + [shape(grads)] * 2,
-        scratch_shapes=[
-            pltpu.VMEM((sub, width), f32),
-            pltpu.VMEM((parts * cols, sub), bf16),
-            pltpu.VMEM((sub, width), bf16),
-            pltpu.VMEM((width, sub), bf16),
-            pltpu.VMEM((width, sub), bf16),
-            pltpu.VMEM((sub, width), f32),
-            pltpu.VMEM((sub, width), f32),
-        ],
         compiler_params=params(),
         cost_estimate=cost(19),
         name="middle",
-    )(place, *att, x, cot, od[0], od[1], fc[0], fc[1], b_fc, table)
+    )(place, *att, x, cot, of[0], of[1], dn[0], dn[1], table)
 
 
 def last_kernel(parts, pieces, sc, *refs):
@@ -489,19 +502,20 @@
     other_rows = pl.ds(pl.multiple_of((1 - sc[2]) * half, half), half)
     ones = jnp.ones((8, x.shape[0]), bf16)
     sums[...] = jnp.zeros_like(sums)
+    stacked[...] = jnp.zeros_like(stacked)
     for part in range(parts):
         row = 0
         for n in range(pieces):
             piece = grads[part * pieces + n]
             stacked[row : row + piece.shape[0], :] = piece[...]
             row += piece.shape[0]
-        mine, theirs = nn(w_own[part], stacked[...]), nn(w_other[part], stacked[...])
+        at = lax.rem(sc[3] - part + parts, parts)
+        mine, theirs = nn(w_own[at], stacked[...]), nn(w_other[at], stacked[...])
         if part == 0:
             back_t[own_rows, :], back_t[other_rows, :] = mine, theirs
         else:
             back_t[own_rows, :] += mine
             back_t[other_rows, :] += theirs
-        at = lax.rem(sc[3] - part + parts, parts)
         sums[pl.ds(6 + parts + at, 1), :wide] = nt(ones, stacked[...])[0:1, :]
     back = back_t[...].T
     normed, inverse = norm(x[...].astype(f32))
@@ -527,6 +541,69 @@
         cost_estimate=cost(6),
         name="last",
     )(place, *grads, w[0], w[1], x, grad_mid, table, mid_sums, fc_sums)
+
+
+def fold_kernel(cut, sc, mine, theirs, lo_send, lo_keep, hi_send, hi_keep):
+    i = pl.program_id(0)
+    total = (mine[...].astype(f32) + theirs[...].astype(f32)).astype(bf16)
+    lo, hi = total[None, :, :, :cut], total[None, :, :, cut:]
+
+    @pl.when(i < 2)
+    def _():
+        lo_send[...] = lo
+
+    @pl.when(i >= 2)
+    def _():
+        lo_keep[...] = lo
+
+    @pl.when((i == 1) | (i == 2))
+    def _():
+        hi_send[...] = hi
+
+    @pl.when((i == 0) | (i == 3))
+    def _():
+        hi_keep[...] = hi
+
+
+def fold(place, mine, theirs):
+    parts, rows, wide = mine.shape
+    size = rows // 4
+    cut = (wide // 256) * 128 if wide % 256 == 0 else (wide // 256 + 1) * 128
+    block = pl.BlockSpec(
+        (parts, size, wide),
+        lambda i, sc: (
+            0,
+            sc[1] ^ jnp.where(i == 0, 1, jnp.where(i == 1, 3, jnp.where(i == 2, 2, 0))),
+            0,
+        ),
+    )
+    out = lambda width, index: pl.BlockSpec(
+        (1, parts, size, width), lambda i, sc: (index(i), 0, 0, 0)
+    )
+    lo, hi = cut, wide - cut
+    return pl.pallas_call(
+        functools.partial(fold_kernel, cut),
+        grid_spec=pltpu.PrefetchScalarGridSpec(
+            num_scalar_prefetch=1,
+            grid=(4,),
+            in_specs=[block, block],
+            out_specs=[
+                out(lo, lambda i: jnp.minimum(i, 1)),
+                out(lo, lambda i: jnp.where(i == 3, 0, 1)),
+                out(hi, lambda i: jnp.where(i < 2, 1, 0)),
+                out(hi, lambda i: jnp.where(i == 3, 0, 1)),
+            ],
+        ),
+        out_shape=[
+            shape((2, parts, size, lo)),
+            shape((2, parts, size, lo)),
+            shape((2, parts, size, hi)),
+            shape((2, parts, size, hi)),
+        ],
+        compiler_params=params(),
+        cost_estimate=cost(1 + 6 * parts / 4),
+        name="fold",
+    )(place, mine, theirs)
 
 
 def body(
@@ -589,14 +666,14 @@
     def gather_direct(v):
         return [v] + [shift_by(v, d) for d in range(1, n_tensor)]
 
-    def gather_line(v):
+    def gather_line(v, hold=None):
         if n_tensor != 4:
             return gather_direct(v)
         move = lambda a, perm: lax.ppermute(a, "tensor", perm)
         two = move(v, [(0, 2), (1, 3), (2, 0), (3, 1)])
         right = move(v, [(0, 1), (1, 2), (2, 3)])
         left = move(v, [(3, 2), (2, 1), (1, 0)])
-        far = move(two, [(2, 3), (1, 0)])
+        far = move(two if hold is None else after(two, hold), [(2, 3), (1, 0)])
         return [
             v,
             jnp.where(tensor == 0, far, right),
@@ -604,32 +681,49 @@
             jnp.where(tensor == 3, far, left),
         ]
 
-    def scatter_direct(pieces):
-        total = pieces[0].astype(f32)
-        for d in range(1, n_tensor):
-            total += shift_by(pieces[d].astype(bf16), -d).astype(f32)
-        return total
-
-    def scatter_context(v):
+    def scatter_line(pieces):
+        if n_tensor != 4:
+            total = pieces[0].astype(f32)
+            for d in range(1, n_tensor):
+                total += shift_by(pieces[d].astype(bf16), -d).astype(f32)
+            return total
+        move = lambda a, perm: lax.ppermute(a.astype(bf16), "tensor", perm)
+        far = move(jnp.where(tensor == 0, pieces[1], pieces[3]), [(0, 1), (3, 2)])
+        right = move(pieces[3], [(0, 1), (1, 2), (2, 3)])
+        left = move(pieces[1], [(3, 2), (2, 1), (1, 0)])
+        two = move(
+            pieces[2].astype(f32) + far.astype(f32), [(0, 2), (1, 3), (2, 0), (3, 1)]
+        )
+        return (
+            pieces[0].astype(f32) + right.astype(f32) + left.astype(f32) + two.astype(f32)
+        )
+
+    def scatter_begin(mine, theirs):
+        theirs = swap(theirs)
         if not grouped:
-            return lax.psum_scatter(v, "context", scatter_dimension=1, tiled=True)
-        size = v.shape[1] // 4
-        block = lambda n: lax.dynamic_slice_in_dim(v, (context ^ n) * size, size, 1)
-        own, by_x, by_y, by_both = (block(n) for n in range(4))
-        cut = (v.shape[2] // 256) * 128
-        lo = lambda a: a[:, :, :cut]
-        hi = lambda a: a[:, :, cut:]
-        r = along_x(jnp.stack([lo(by_x), lo(by_both)])).astype(f32)
-        s = along_y(jnp.stack([hi(by_y), hi(by_both)])).astype(f32)
-        r2 = along_y((lo(by_y).astype(f32) + r[1]).astype(bf16)).astype(f32)
-        s2 = along_x((hi(by_x).astype(f32) + s[1]).astype(bf16)).astype(f32)
-        return jnp.concatenate(
-            [lo(own).astype(f32) + r[0] + r2, hi(own).astype(f32) + s[0] + s2], axis=2
+            both = (mine.astype(f32) + theirs.astype(f32)).astype(bf16)
+            return lax.psum_scatter(both, "context", scatter_dimension=1, tiled=True)
+        return fold(place, mine, theirs)
+
+    def scatter_first(state):
+        if not grouped:
+            return state
+        lo_send, lo_keep, hi_send, hi_keep = state
+        r, s = along_x(lo_send).astype(f32), along_y(hi_send).astype(f32)
+        return (
+            lo_keep[0].astype(f32) + r[0],
+            hi_keep[0].astype(f32) + s[0],
+            (lo_keep[1].astype(f32) + r[1]).astype(bf16),
+            (hi_keep[1].astype(f32) + s[1]).astype(bf16),
         )
 
-    def scatter_weights(mine, theirs):
-        both = (mine.astype(f32) + swap(theirs).astype(f32)).astype(bf16)
-        return scatter_context(both)
+    def scatter_second(state):
+        if not grouped:
+            return state
+        lo, hi, lo_send, hi_send = state
+        lo += along_y(lo_send).astype(f32)
+        hi += along_x(hi_send).astype(f32)
+        return jnp.concatenate([lo, hi], axis=2)
 
     bounds = [jnp.sum((segments[0] < d).astype(jnp.int32)) for d in range(1, 5)]
     seg = lax.dynamic_slice_in_dim(segments[0], first, tok, 0)
@@ -666,7 +760,8 @@
         k, v = kt[rows], vt[rows]
         if grouped:
             kx, vy = along_x(k), along_y(v)
-            kv.append([k, kx, along_y(jnp.stack([k, kx])), v, vy, along_x(jnp.stack([v, vy]))])
+            k_two, v_two = jnp.stack([k, kx]), jnp.stack([v, vy])
+            kv.append([k, kx, along_y(k_two), v, vy, along_x(v_two)])
         else:
             kv.append([lax.all_gather(jnp.concatenate([k, v], axis=0), "context", axis=0)])
 
@@ -674,9 +769,16 @@
         own = jnp.stack(gather(w))
         return own, swap(own)
 
-    od = gather_weights(jnp.concatenate([w_out, w_down], axis=0), gather_line)
-    fc = gather_weights(w_fc, gather_line)
-
+    terms, rest = [], b_fc
+    for _ in range(3):
+        term = lax.reduce_precision(rest, 8, 7)
+        terms.append(term.astype(bf16).reshape(ffw // half, half))
+        rest = rest - term
+    terms = jnp.concatenate(terms, axis=0)
+    terms = jnp.pad(terms, ((0, 16 - terms.shape[0]), (0, 0)))
+    packed = jnp.concatenate([w_out, terms, w_fc[:, :half], w_fc[:, half:]], axis=0)
+    gathered = lax.all_gather(w_down, "tensor", axis=0)
+    dn = (gathered, swap(gathered))
     saved = []
     att = [[] for _ in range(n_tensor)]
     head = 0
@@ -688,26 +790,17 @@
             att[d].append(shift_by(out[d], d))
         head += g
 
+    of = gather_weights(packed, lambda w: gather_line(w, saved[-1][0]))
     x_sub = lax.dynamic_slice_in_dim(x, tensor * sub, sub, 0)
     cot_sub = lax.dynamic_slice_in_dim(cot, tensor * sub, sub, 0)
-    qkv = gather_weights(after(qkv_own, saved[-1][1]), gather_direct)
-    all_bias = lax.all_gather(row(b_fc), "tensor", axis=0)
-    fc_bias = jnp.stack(
-        [
-            lax.dynamic_index_in_dim(
-                all_bias, lax.rem(tensor - d + n_tensor, n_tensor), 0, keepdims=False
-            )
-            for d in range(n_tensor)
-        ]
-    )
     outputs_sub, grad_mid, mid_sums, fc_sums, *rest = middle(
         place,
         [piece for part in att for piece in part],
         x_sub,
         cot_sub,
-        od,
-        fc,
-        fc_bias,
+        of,
+        dn,
+        cols,
         table,
     )
     d_att, (g_own, g_other) = rest[:n_tensor], rest[n_tensor:]
@@ -716,16 +809,17 @@
     ]
 
     def spread(v):
-        pieces = gather_direct(v)
+        pieces = gather_line(v)
         whole = jnp.zeros((tok, width), f32)
         for d in range(n_tensor):
             at = lax.rem(tensor - d + n_tensor, n_tensor) * sub
             whole = lax.dynamic_update_slice_in_dim(whole, pieces[d].astype(f32), at, 0)
         return whole[None]
 
-    wide_grads = scatter_weights(g_own, g_other)
-    wide_grads = scatter_direct([wide_grads[d] for d in range(n_tensor)])
-    outputs = spread(outputs_sub)
+    folded = scatter_begin(g_own, g_other)
+    hop_one = folded[0] if grouped else folded
+    outputs = lax.all_gather(after(outputs_sub, do_parts[-1]), "tensor", axis=0, tiled=True)
+    wide = scatter_first(folded)
 
     dq_pieces, dkv_pieces, dqkv = [], [], []
     head = 0
@@ -733,11 +827,12 @@
     sent = [[] for _ in range(n_tensor)]
     for g, held, (lse, ot) in zip(GROUPS, kv, saved):
         out = attend_back(
-            scalars, row(starts), qt, lse, ot, do_parts, held, head, g, BK_B, BQ_B
+            scalars, row(starts), after(qt, hop_one), lse, ot, do_parts, held, head, g, BK_B, BQ_B
         )
         dq, dkv = out[:n_tensor], out[n_tensor:]
         if grouped:
             dk_keep, dk_send, dv_keep, dv_send = dkv
+            dk_send, dv_send = after((dk_send, dv_send), (wide[2], wide[3]))
             r = along_x(dk_send).astype(f32)
             s = along_y(dv_send).astype(f32)
             r2 = along_y((dk_keep[1].astype(f32) + r[1]).astype(bf16)).astype(f32)
@@ -752,6 +847,9 @@
         values.append(dv)
         head += g
 
+    wide = scatter_second(wide)
+    wide_grads = scatter_line([wide[d] for d in range(n_tensor)])
+
     def part_of(v, d):
         at = lax.rem(tensor + d, n_tensor) * sub
         return lax.dynamic_slice_in_dim(v, at, sub, 1)
@@ -770,16 +868,23 @@
             at = lax.rem(tensor + d, n_tensor) * sub
             whole = lax.dynamic_update_slice_in_dim(whole, q[d], at, 1)
         dq_whole.append(whole)
-    stacked = jnp.concatenate(dq_whole + [both], axis=0)
-    qkv_grad = jnp.einsum("td,ct->dc", low_one, stacked, preferred_element_type=f32).astype(bf16)
+    qkv_wide = jnp.pad(qkv_own, ((0, 0), (0, -3 * cols % 128)))
+    qkv = lax.all_gather(after(qkv_wide, queries[-1][0]), "tensor", axis=0)
+    qkv = (qkv, swap(qkv))
+    input_sub, small = last(
+        place, grads, pieces, qkv, x_sub, grad_mid, table, mid_sums, fc_sums
+    )
+    input_gradient = spread(input_sub)
+    outputs = after(outputs, input_sub).astype(f32)[None]
+    stacked = jnp.concatenate(
+        dq_whole + [both, jnp.zeros((-3 * cols % 128, tok), bf16)], axis=0
+    )
+    qkv_grad = jnp.einsum(
+        "td,ct->dc", low_one, after(stacked, input_sub), preferred_element_type=f32
+    ).astype(bf16)
     qkv_mine = lax.dynamic_slice_in_dim(qkv_grad, core * half, half, 0)
     qkv_theirs = lax.dynamic_slice_in_dim(qkv_grad, (1 - core) * half, half, 0)
-
-    input_sub, small = last(
-        place, grads, pieces, qkv, x_sub, grad_mid, table, mid_sums, fc_sums
-    )
-    input_gradient = spread(input_sub)
-    qkv_grads = scatter_weights(qkv_mine[None], qkv_theirs[None])[0]
+    qkv_grads = scatter_second(scatter_first(scatter_begin(qkv_mine[None], qkv_theirs[None])))[0]
 
     if grouped and n_tensor == 4 and n_shard == 2:
         small += swap(small)
@@ -795,8 +900,8 @@
     return (
         outputs,
         input_gradient,
-        qkv_grads.astype(f32).reshape(-1, 3, cols),
-        wide_grads[:, 2 * ffw :].T,
+        qkv_grads[:, : 3 * cols].astype(f32).reshape(-1, 3, cols),
+        wide_grads[:, 2 * ffw : 2 * ffw + cols].T,
         wide_grads[:, :ffw],
         wide_grads[:, ffw : 2 * ffw].T,
         qv_total,

time: 481 us -> 420 us (0.87)
  starting transfers between devices: 126 us -> 88.4 us
  blocking collectives: 26.2 us -> 0 us
  Pallas kernels: 56.1 us -> 70.4 us
  between operations: 1.59 us -> 14.6 us
  local copies, waits for them, and re-layouts: 40.2 us -> 28.1 us
  waiting for transfers between devices: 194 us -> 184 us
    ppermute x24 -> x12, waiting for transfers between devices: 54.4 us -> 15.9 us  [body(): lax.ppermute(v, 'tensor', [(s, (s + d) % n_tensor) for s in range(n_tenso...]
    ppermute x8, waiting for transfers between devices: 30.5 us -> 67.3 us  [gather_line(): move = lambda a, perm: lax.ppermute(a, 'tensor', perm)]
    ppermute x24 -> x12, starting transfers between devices: 51.9 us -> 17.2 us  [body(): lax.ppermute(v, 'tensor', [(s, (s + d) % n_tensor) for s in range(n_tenso...]
    ppermute x9, waiting for transfers between devices: 50.9 us -> 18.9 us  [body(): lax.ppermute(v, 'context', [(0, 1), (1, 0), (2, 3), (3, 2)])]
    all_gather x1 -> x0, blocking collectives: 26.2 us -> none  [body(): all_bias = lax.all_gather(row(b_fc), 'tensor', axis=0)]
    ppermute x1, waiting for transfers between devices: 23.9 us -> 4.6 us  [body(): small += lax.ppermute(small, 'tensor', [(0, 2), (2, 0), (1, 3), (3, 1)])]
    ppermute x0 -> x4, waiting for transfers between devices: none -> 17.9 us  [scatter_line(): move = lambda a, perm: lax.ppermute(a.astype(bf16), 'tensor', perm)]
    ppermute x9, waiting for transfers between devices: 34.2 us -> 51.8 us  [body(): lax.ppermute(v, 'context', [(0, 2), (2, 0), (1, 3), (3, 1)])]
  transfers between devices with their start and end apart: 59 -> 54, of which waited for: 23 -> 25; matrix products, arithmetic and copies ran while one was open for 14% -> 12% of each run, Pallas kernels for 12% -> 7%
where the time goes in v3:
time: 420 us; the launch traced here: 417 us
  waiting for transfers between devices  184 us (44%)
  starting transfers between devices  88.4 us (21%)
  Pallas kernels  70.4 us (17%)
  other arithmetic  30.2 us (7%)
  local copies, waits for them, and re-layouts  28.1 us (7%)
  between operations  14.6 us (3%)
    ppermute x8, waiting for transfers between devices, gather_line(): move = lambda a, perm: lax.ppermute(a, 'tensor', perm)  67.3 us
    ppermute x9, waiting for transfers between devices, body(): lax.ppermute(v, 'context', [(0, 2), (2, 0), (1, 3), (3, 1)])  51.8 us
    ppermute x9, starting transfers between devices, body(): lax.ppermute(v, 'context', [(0, 2), (2, 0), (1, 3), (3, 1)])  25.6 us
    pallas_call x1, Pallas kernels, middle(): pl.pallas_call(functools.partial(middle_kernel, len(att), parts), grid_sp...  23 us
    ppermute x9, waiting for transfers between devices, body(): lax.ppermute(v, 'context', [(0, 1), (1, 0), (2, 3), (3, 2)])  18.9 us
    ppermute x8, starting transfers between devices, gather_line(): move = lambda a, perm: lax.ppermute(a, 'tensor', perm)  17.9 us
    ppermute x4, waiting for transfers between devices, scatter_line(): move = lambda a, perm: lax.ppermute(a.astype(bf16), 'tensor', perm)  17.9 us
    ppermute x12, starting transfers between devices, body(): lax.ppermute(v, 'tensor', [(s, (s + d) % n_tensor) for s in range(n_tenso...  17.2 us
  transfers between devices with their start and end apart: 54, of which 25 were waited for; matrix products, arithmetic and copies ran while one was open for 12% of the time, Pallas kernels for 7%

profile of v3, /device:TPU:0, one launch (start us, length us, event | category | flops | bytes accessed | tf_op | source)
XLA Modules:
  0.0 417.4 jit_solution(16248012560694034938)
XLA Ops:
  15.1 6.4 %project.1 = (bf16[1024,768]{1,0:T(8,128)(2,1)}, bf16[192,1024]{1,0:T(8,128)(2,1)}, bf16[192,1024]{1,0:T(8,128)(2,1)}, bf16[192,1024]{1,0:T(8,128)(2,1)}) custom-call(s32[4]{0:T(128)} %pad_add_fusion.1.sc, bf16[1024,768]{1,0:T(8,128)(2,1)} %bitcast.122, bf16[384,576]{1,0:T(8,128)(2,1)} %copy-done.16, bf16[384,576]{1,0:T(8,128)(2,1)} %copy-done.35, ...), custom_call_target="tpu_custom_call" | custom-call | flops 8049999872 | bytes 1048576 | tf_op jit(solution)/shard_map/project/pallas_call | solution.py:90
  21.5 2.6 collective-permute-start.3
  24.2 1.5 collective-permute-start.1
  25.9 8.2 %collective-permute-done.3.refs_4_.refs_8_ = bf16[192,1024]{1,0:T(8,128)(2,1)S(1)} collective-permute-done((bf16[192,1024]{1,0:T(8,128)(2,1)}, bf16[192,1024]{1,0:T(8,128)(2,1)S(1)}, u32[]{:S(2)}, u32[]{:S(2)}) %collective-permute-start.3) | collective-permute-done | bytes 393248 | tf_op jit(solution)/shard_map/ppermute | solution.py:661
  35.3 1.8 collective-permute-start.4
  37.2 1.6 collective-permute-start.2
  40.1 2.6 collective-permute-start.8
  42.7 3.5 collective-permute-start.10
  48.8 3.8 fusion.54
  53.5 1.3 collective-permute-done.4.refs_5_.refs_9_
  54.8 1.4 collective-permute-done.2.refs_2_.refs_6_
  56.2 9.5 %attend.1 = (f32[3,1024]{1,0:T(4,128)}, bf16[192,1024]{1,0:T(8,128)(2,1)}, bf16[192,256]{1,0:T(8,128)(2,1)}, bf16[192,256]{1,0:T(8,128)(2,1)}, bf16[192,256]{1,0:T(8,128)(2,1)}, /*index=5*/bf16[192,256]{1,0:T(8,128)(2,1)}) custom-call(s32[12]{0:T(128)} %concatenate.25.sc, bf16[192,1024]{1,0:T(8,128)(2,1)} %get-tuple-element.75.qt, ...), custom_call_target="tpu_custom_call" | custom-call | flops 23000000512 | bytes 1048576 | tf_op jit(solution)/shard_map/attend/pallas_call | solution.py:221
  65.8 44.0 %collective-permute-done.8 = bf16[976,384]{1,0:T(8,128)(2,1)} collective-permute-done((bf16[976,384]{1,0:T(8,128)(2,1)}, bf16[976,384]{1,0:T(8,128)(2,1)}, u32[]{:S(2)}, u32[]{:S(2)}) %collective-permute-start.8) | collective-permute-done | bytes 749600 | tf_op jit(solution)/shard_map/ppermute | solution.py:672
  111.1 23.3 %collective-permute-done.9 = bf16[976,384]{1,0:T(8,128)(2,1)S(1)} collective-permute-done((bf16[976,384]{1,0:T(8,128)(2,1)}, bf16[976,384]{1,0:T(8,128)(2,1)S(1)}, u32[]{:S(2)}, u32[]{:S(2)}) %collective-permute-start.9) | collective-permute-done | bytes 749600 | tf_op jit(solution)/shard_map/ppermute | solution.py:672
  134.6 1.6 pad_maximum_fusion.refs_6_
  136.9 4.0 collective-permute-start.7
  140.9 2.1 dynamic-slice_bitcast_fusion.2
  142.9 1.4 collective-permute-done.5.refs_1_
  144.3 3.3 collective-permute-done.6.refs_2_
  148.3 23.0 %middle.1 = (bf16[256,768]{1,0:T(8,128)(2,1)}, f32[256,768]{1,0:T(8,128)}, f32[4,768]{1,0:T(4,128)}, f32[4,1,768]{2,1,0:T(1,128)}, bf16[192,256]{1,0:T(8,128)(2,...) custom-call(s32[4]{0:T(128)} %pad_add_fusion.1.sc, ...), custom_call_target="tpu_custom_call" | custom-call | flops 21849999360 | bytes 1048576 | tf_op jit(solution)/shard_map/middle/pallas_call | solution.py:462
  172.1 1.8 collective-permute-start.14
  173.9 2.0 collective-permute-start.16
  176.0 4.7 %collective-permute-done.15.theirs = bf16[4,384,1792]{2,1,0:T(8,128)(2,1)} collective-permute-done((bf16[4,384,1792]{2,1,0:T(8,128)(2,1)}, bf16[4,384,1792]{2,1,0:T(8,128)(2,1)}, u32[]{:S(2)}, u32[]{:S(2)}) %collective-permute-start.15) | collective-permute-done | bytes 5505056 | tf_op jit(solution)/shard_map/ppermute | solution.py:659
  180.7 8.7 %fold.2 = (bf16[2,4,96,896]{3,2,1,0:T(8,128)(2,1)}, bf16[2,4,96,896]{3,2,1,0:T(8,128)(2,1)}, bf16[2,4,96,896]{3,2,1,0:T(8,128)(2,1)}, bf16[2,4,96,896]{3,2,1,0:T(8,128)(2,1)}) custom-call(s32[4]{0:T(128)} %pad_add_fusion.1.sc, bf16[4,384,1792]{2,1,0:T(8,128)(2,1)} %get-tuple-element.72.mine, bf16[4,384,1792]{2,1,0:T(8,128)(2,1)} %collective-permute-done.15.theirs), custom_call_target="tpu_custom_call" | custom-call | flops 8049999872 | bytes 1048576 | tf_op jit(solution)/shard_map/fold/pallas_call | solution.py:584
  190.1 12.7 %attend_back.1 = (bf16[192,256]{1,0:T(8,128)(2,1)}, bf16[192,256]{1,0:T(8,128)(2,1)}, bf16[192,256]{1,0:T(8,128)(2,1)}, bf16[192,256]{1,0:T(8,128)(2,1)}, bf16[2...) custom-call(s32[12]{0:T(128)} %concatenate.25.sc, ...), custom_call_target="tpu_custom_call" | custom-call | flops 29899999232 | bytes 1048576 | tf_op jit(solution)/shard_map/attend_back/pallas_call | solution.py:327
  202.8 13.3 %collective-permute-start.19 = (bf16[2,4,96,896]{3,2,1,0:T(8,128)(2,1)}, bf16[2,4,96,896]{3,2,1,0:T(8,128)(2,1)S(1)}, u32[]{:S(2)}, u32[]{:S(2)}) collective-permute-start(bf16[2,4,96,896]{3,2,1,0:T(8,128)(2,1)} %get-tuple-element.86), channel_id=1, source_target_pairs={{0,8},{8,0},{4,12},{12,4},{1,9},{9,1},{5,13},{13,5},{2,10},{10,2},... | collective-permute-start | bytes 4128776 | tf_op jit(solution)/shard_map/ppermute | solution.py:661
  216.2 1.9 collective-permute-start.24
  218.1 28.7 %collective-permute-done.19 = bf16[2,4,96,896]{3,2,1,0:T(8,128)(2,1)S(1)} collective-permute-done((bf16[2,4,96,896]{3,2,1,0:T(8,128)(2,1)}, bf16[2,4,96,896]{3,2,1,0:T(8,128)(2,1)S(1)}, u32[]{:S(2)}, u32[]{:S(2)}) %collective-permute-start.19) | collective-permute-done | bytes 1376288 | tf_op jit(solution)/shard_map/ppermute | solution.py:661
  248.7 1.8 collective-permute-start.40
  252.6 13.0 %collective-permute-done.41 = bf16[4,96,896]{2,1,0:T(8,128)(2,1)S(1)} collective-permute-done((bf16[4,96,896]{2,1,0:T(8,128)(2,1)S(1)}, bf16[4,96,896]{2,1,0:T(8,128)(2,1)S(1)}, u32[]{:S(2)}, u32[]{:S(2)}) %collective-permute-start.41) | collective-permute-done | bytes 688160 | tf_op jit(solution)/shard_map/ppermute | solution.py:660
  265.8 1.3 collective-permute-done.40
  268.4 4.5 %collective-permute-start.44 = (bf16[96,1792]{1,0:T(8,128)(2,1)}, bf16[96,1792]{1,0:T(8,128)(2,1)}, u32[]{:S(2)}, u32[]{:S(2)}) collective-permute-start(bf16[96,1792]{1,0:T(8,128)(2,1)} %get-tuple-element.150), channel_id=1, source_target_pairs={{0,1},{3,2},{4,5},{7,6},{8,9},{11,10},{12,13},{15,14},{16,17},{19,... | collective-permute-start | bytes 1032200 | tf_op jit(solution)/shard_map/ppermute | solution.py:690
  272.9 2.0 collective-permute-start.42
  275.0 7.7 %collective-permute-done.22 = bf16[2,192,1024]{2,1,0:T(8,128)(2,1)S(1)} collective-permute-done((bf16[2,192,1024]{2,1,0:T(8,128)(2,1)S(1)}, bf16[2,192,1024]{2,1,0:T(8,128)(2,1)S(1)}, u32[]{:S(2)}, u32[]{:S(2)}) %collective-permute-start.22) | collective-permute-done | bytes 786464 | tf_op jit(solution)/shard_map/ppermute | solution.py:661
  286.0 1.5 collective-permute-start.21
  287.5 4.0 copy.34
  292.8 1.4 collective-permute-done.23
  296.6 3.9 collective-permute-start.45
  302.5 1.3 maximum_maximum_fusion
  303.9 1.8 collective-permute-done.43
  305.7 4.3 %collective-permute-start.28 = (bf16[192,256]{1,0:T(8,128)(2,1)S(1)}, bf16[192,256]{1,0:T(8,128)(2,1)S(1)}, u32[]{:S(2)}, u32[]{:S(2)}) collective-permute-start(bf16[192,256]{1,0:T(8,128)(2,1)S(1)} %copy-done.26), channel_id=1, source_target_pairs={{0,3},{1,0},{2,1},{3,2},{4,7},{5,4},{6,5},{7,6},{8,11},{9,8},{10,9... | collective-permute-start | bytes 294920 | tf_op jit(solution)/shard_map/ppermute | solution.py:662
  310.1 16.1 %collective-permute-done.45 = bf16[96,1792]{1,0:T(8,128)(2,1)S(1)} collective-permute-done((bf16[96,1792]{1,0:T(8,128)(2,1)S(1)}, bf16[96,1792]{1,0:T(8,128)(2,1)S(1)}, u32[]{:S(2)}, u32[]{:S(2)}) %collective-permute-start.45) | collective-permute-done | bytes 344096 | tf_op jit(solution)/shard_map/ppermute | solution.py:690
  328.2 3.1 collective-permute-start.29
  332.1 3.7 collective-permute-done.25.refs_3_
  335.8 6.8 %collective-permute-done.27.refs_5_ = bf16[384,256]{1,0:T(8,128)(2,1)S(1)} collective-permute-done((bf16[384,256]{1,0:T(8,128)(2,1)S(1)}, bf16[384,256]{1,0:T(8,128)(2,1)S(1)}, u32[]{:S(2)}, u32[]{:S(2)}) %collective-permute-start.27) | collective-permute-done | bytes 196640 | tf_op jit(solution)/shard_map/ppermute | solution.py:662
  344.0 6.0 %last.1 = (bf16[256,768]{1,0:T(8,128)(2,1)}, f32[16,768]{1,0:T(8,128)}) custom-call(s32[4]{0:T(128)} %pad_add_fusion.1.sc, bf16[192,256]{1,0:T(8,128)(2,1)} %get-tuple-element.80.refs_0_, bf16[384,256]{1,0:T(8,128)(2,1)} %get-tuple-element.155.refs_1_, bf16[192,256]{1,0:T(8,128)(2,1)} %collective-permute-done.24.refs_2_, bf16[384,256]{1,0:T(8,128)(2,1)} %copy-done.36, ...), custom_call_target="tpu_custom_call" | custom-call | flops 6899999744 | bytes 1048576 | tf_op jit(solution)/shard_map/last/pallas_call | solution.py:534
  350.8 3.0 collective-permute-start.31
  353.8 3.7 collective-permute-start.33
  359.6 2.3 collective-permute-start.47
  361.8 1.4 convolution_convert_fusion
  366.3 1.8 collective-permute-done.48
  368.1 2.7 collective-permute-start.49
  370.8 3.3 bitcast_convert_fusion
  374.1 3.0 collective-permute-done.49
  378.2 4.6 %collective-permute-done.50 = f32[16,768]{1,0:T(8,128)S(1)} collective-permute-done((f32[16,768]{1,0:T(8,128)S(1)}, f32[16,768]{1,0:T(8,128)S(1)}, u32[]{:S(2)}, u32[]{:S(2)}) %collective-permute-start.50) | collective-permute-done | bytes 49184 | tf_op jit(solution)/shard_map/ppermute | solution.py:894
  383.5 4.1 fold.3
  387.6 1.6 collective-permute-start.38
  391.0 1.8 collective-permute-start.36
  393.7 2.0 collective-permute-start.39
  395.7 1.5 collective-permute-done.36
  400.0 2.5 collective-permute-done.37
  403.3 1.8 copy.35
  405.1 1.8 copy.36
  409.2 1.7 copy-done.4
  (241 shorter events, 53.1 us)
Async XLA Ops:
  7.2 129.1 %all-gather.8.cloned.1.call-start = ((), (), s32[]{:S(2)}) async-start(), calls=%async_computation.1 | async-start | bytes 2949120 | tf_op jit(solution)/shard_map/all_gather | solution.py:780
  8.5 5.9 %collective-permute-start = (bf16[384,576]{1,0:T(8,128)(2,1)S(1)}, bf16[384,576]{1,0:T(8,128)(2,1)S(1)}, u32[]{:S(2)}, u32[]{:S(2)}) collective-permute-start(bf16[384,576]{1,0:T(8,128)(2,1)S(1)} %copy.33.w_own), channel_id=1, source_target_pairs={{0,16},{16,0},{1,17},{17,1},{2,18},{18,2},{3,19},{19,3},{4,20},{20... | collective-permute-start | bytes 1327112 | tf_op jit(solution)/shard_map/ppermute | solution.py:659
  21.5 15.6 %copy-start.17 = (bf16[192,1024]{1,0:T(8,128)(2,1)S(1)}, bf16[192,1024]{1,0:T(8,128)(2,1)}, u32[]{:S(2)}) copy-start(bf16[192,1024]{1,0:T(8,128)(2,1)} %get-tuple-element.61.refs_0_.refs_4_) | copy-start | bytes 1179652
  21.5 12.6 %collective-permute-start.3 = (bf16[192,1024]{1,0:T(8,128)(2,1)}, bf16[192,1024]{1,0:T(8,128)(2,1)S(1)}, u32[]{:S(2)}, u32[]{:S(2)}) collective-permute-start(bf16[192,1024]{1,0:T(8,128)(2,1)} %get-tuple-element.62.refs_3_.refs_7_), channel_id=1, source_target_pairs={{0,8},{8,0},{4,12},{12,4},{1,9},{9,1},{5,13},{13,5},{2,10},{10,2},... | collective-permute-start | bytes 1179656 | tf_op jit(solution)/shard_map/ppermute | solution.py:661
  24.2 12.9 %collective-permute-start.1 = (bf16[192,1024]{1,0:T(8,128)(2,1)}, bf16[192,1024]{1,0:T(8,128)(2,1)S(1)}, u32[]{:S(2)}, u32[]{:S(2)}) collective-permute-start(bf16[192,1024]{1,0:T(8,128)(2,1)} %get-tuple-element.61.refs_0_.refs_4_), channel_id=1, source_target_pairs={{0,4},{4,0},{8,12},{12,8},{1,5},{5,1},{9,13},{13,9},{2,6},{6,2},{1... | collective-permute-start | bytes 1179656 | tf_op jit(solution)/shard_map/ppermute | solution.py:660
  35.3 19.5 %collective-permute-start.4 = (bf16[2,192,1024]{2,1,0:T(8,128)(2,1)S(1)}, bf16[2,192,1024]{2,1,0:T(8,128)(2,1)}, u32[]{:S(2)}, u32[]{:S(2)}) collective-permute-start(bf16[2,192,1024]{2,1,0:T(8,128)(2,1)S(1)} %pad_maximum_fusion.2), channel_id=1, source_target_pairs={{0,4},{4,0},{8,12},{12,8},{1,5},{5,1},{9,13},{13,9},{2,6},{6,2},{1... | collective-permute-start | bytes 2359304 | tf_op jit(solution)/shard_map/ppermute | solution.py:660
  37.2 19.0 %collective-permute-start.2 = (bf16[2,192,1024]{2,1,0:T(8,128)(2,1)S(1)}, bf16[2,192,1024]{2,1,0:T(8,128)(2,1)}, u32[]{:S(2)}, u32[]{:S(2)}) collective-permute-start(bf16[2,192,1024]{2,1,0:T(8,128)(2,1)S(1)} %pad_maximum_fusion.1), channel_id=1, source_target_pairs={{0,8},{8,0},{4,12},{12,4},{1,9},{9,1},{5,13},{13,5},{2,10},{10,2},... | collective-permute-start | bytes 2359304 | tf_op jit(solution)/shard_map/ppermute | solution.py:661
  40.1 69.7 %collective-permute-start.8 = (bf16[976,384]{1,0:T(8,128)(2,1)}, bf16[976,384]{1,0:T(8,128)(2,1)}, u32[]{:S(2)}, u32[]{:S(2)}) collective-permute-start(bf16[976,384]{1,0:T(8,128)(2,1)} %get-tuple-element.159), channel_id=1, source_target_pairs={{0,2},{1,3},{2,0},{3,1},{4,6},{5,7},{6,4},{7,5},{8,10},{9,11},{10,... | collective-permute-start | bytes 2248712 | tf_op jit(solution)/shard_map/ppermute | solution.py:672
  42.7 68.5 %collective-permute-start.10 = (bf16[976,384]{1,0:T(8,128)(2,1)}, bf16[976,384]{1,0:T(8,128)(2,1)S(1)}, u32[]{:S(2)}, u32[]{:S(2)}) collective-permute-start(bf16[976,384]{1,0:T(8,128)(2,1)} %get-tuple-element.159), channel_id=1, source_target_pairs={{0,1},{1,2},{2,3},{4,5},{5,6},{6,7},{8,9},{9,10},{10,11},{12,13},{... | collective-permute-start | bytes 2248712 | tf_op jit(solution)/shard_map/ppermute | solution.py:672
  46.2 65.0 %collective-permute-start.11 = (bf16[976,384]{1,0:T(8,128)(2,1)}, bf16[976,384]{1,0:T(8,128)(2,1)S(1)}, u32[]{:S(2)}, u32[]{:S(2)}) collective-permute-start(bf16[976,384]{1,0:T(8,128)(2,1)} %get-tuple-element.159), channel_id=1, source_target_pairs={{3,2},{2,1},{1,0},{7,6},{6,5},{5,4},{11,10},{10,9},{9,8},{15,14},{... | collective-permute-start | bytes 2248712 | tf_op jit(solution)/shard_map/ppermute | solution.py:672
  47.5 240.0 %all-gather.10.cloned.1.call-start = ((), (), s32[]{:S(2)}) async-start(), calls=%async_computation.2 | async-start | bytes 2457600 | tf_op jit(solution)/shard_map/all_gather | solution.py:872
  109.8 24.6 %collective-permute-start.9 = (bf16[976,384]{1,0:T(8,128)(2,1)}, bf16[976,384]{1,0:T(8,128)(2,1)S(1)}, u32[]{:S(2)}, u32[]{:S(2)}) collective-permute-start(bf16[976,384]{1,0:T(8,128)(2,1)} %collective-permute-done.8), channel_id=1, source_target_pairs={{2,3},{1,0},{6,7},{5,4},{10,11},{9,8},{14,15},{13,12},{18,19},{17,... | collective-permute-start | bytes 2248712 | tf_op jit(solution)/shard_map/ppermute | solution.py:672
  111.1 23.5 %copy-start.6 = (bf16[1,976,384]{2,1,0:T(8,128)(2,1)S(1)}, bf16[1,976,384]{2,1,0:T(8,128)(2,1)}, u32[]{:S(2)}) copy-start(bf16[1,976,384]{2,1,0:T(8,128)(2,1)} %get-tuple-element.158) | copy-start | bytes 2248708
  136.2 11.4 %copy-start.5 = (bf16[4,976,384]{2,1,0:T(8,128)(2,1)}, bf16[4,976,384]{2,1,0:T(8,128)(2,1)S(1)}, u32[]{:S(2)}) copy-start(bf16[4,976,384]{2,1,0:T(8,128)(2,1)S(1)} %pad_maximum_fusion.refs_6_) | copy-start | bytes 8994820
  136.2 11.4 %collective-permute-start.12 = (bf16[4,976,384]{2,1,0:T(8,128)(2,1)S(1)}, bf16[4,976,384]{2,1,0:T(8,128)(2,1)}, u32[]{:S(2)}, u32[]{:S(2)}) collective-permute-start(bf16[4,976,384]{2,1,0:T(8,128)(2,1)S(1)} %pad_maximum_fusion.refs_6_), channel_id=1, source_target_pairs={{0,16},{16,0},{1,17},{17,1},{2,18},{18,2},{3,19},{19,3},{4,20},{20... | collective-permute-start | bytes 8994824 | tf_op jit(solution)/shard_map/ppermute | solution.py:659
  136.3 11.3 %collective-permute-start.13 = (bf16[4,768,384]{2,1,0:T(8,128)(2,1)}, bf16[4,768,384]{2,1,0:T(8,128)(2,1)}, u32[]{:S(2)}, u32[]{:S(2)}) collective-permute-start(bf16[4,768,384]{2,1,0:T(8,128)(2,1)} %bitcast.123), channel_id=1, source_target_pairs={{0,16},{16,0},{1,17},{17,1},{2,18},{18,2},{3,19},{19,3},{4,20},{20... | collective-permute-start | bytes 7077896 | tf_op jit(solution)/shard_map/ppermute | solution.py:659
  136.8 7.5 %collective-permute-start.5 = (bf16[192,256]{1,0:T(8,128)(2,1)S(1)}, bf16[192,256]{1,0:T(8,128)(2,1)S(1)}, u32[]{:S(2)}, u32[]{:S(2)}) collective-permute-start(bf16[192,256]{1,0:T(8,128)(2,1)S(1)} %copy-done.42), channel_id=1, source_target_pairs={{0,1},{1,2},{2,3},{3,0},{4,5},{5,6},{6,7},{7,4},{8,9},{9,10},{10,1... | collective-permute-start | bytes 294920 | tf_op jit(solution)/shard_map/ppermute | solution.py:662
  136.8 10.8 %collective-permute-start.6 = (bf16[192,256]{1,0:T(8,128)(2,1)S(1)}, bf16[192,256]{1,0:T(8,128)(2,1)S(1)}, u32[]{:S(2)}, u32[]{:S(2)}) collective-permute-start(bf16[192,256]{1,0:T(8,128)(2,1)S(1)} %copy-done.40), channel_id=1, source_target_pairs={{0,2},{1,3},{2,0},{3,1},{4,6},{5,7},{6,4},{7,5},{8,10},{9,11},{10,... | collective-permute-start | bytes 294920 | tf_op jit(solution)/shard_map/ppermute | solution.py:662
  136.9 10.7 %collective-permute-start.7 = (bf16[192,256]{1,0:T(8,128)(2,1)S(1)}, bf16[192,256]{1,0:T(8,128)(2,1)S(1)}, u32[]{:S(2)}, u32[]{:S(2)}) collective-permute-start(bf16[192,256]{1,0:T(8,128)(2,1)S(1)} %copy-done.39), channel_id=1, source_target_pairs={{0,3},{1,0},{2,1},{3,2},{4,7},{5,4},{6,5},{7,6},{8,11},{9,8},{10,9... | collective-permute-start | bytes 294920 | tf_op jit(solution)/shard_map/ppermute | solution.py:662
  148.3 23.0 %copy-start.7 = (bf16[384,3,192]{0,2,1:T(8,128)(2,1)S(1)}, bf16[384,3,192]{0,2,1:T(8,128)(2,1)}, u32[]{:S(2)}) copy-start(bf16[384,3,192]{0,2,1:T(8,128)(2,1)} %param.17) | copy-start | bytes 1327108
  171.3 9.4 %collective-permute-start.15 = (bf16[4,384,1792]{2,1,0:T(8,128)(2,1)}, bf16[4,384,1792]{2,1,0:T(8,128)(2,1)}, u32[]{:S(2)}, u32[]{:S(2)}) collective-permute-start(bf16[4,384,1792]{2,1,0:T(8,128)(2,1)} %get-tuple-element.73), channel_id=1, source_target_pairs={{0,16},{16,0},{1,17},{17,1},{2,18},{18,2},{3,19},{19,3},{4,20},{20... | collective-permute-start | bytes 16515080 | tf_op jit(solution)/shard_map/ppermute | solution.py:659
  172.1 17.2 %collective-permute-start.14 = (bf16[192,256]{1,0:T(8,128)(2,1)}, bf16[192,256]{1,0:T(8,128)(2,1)S(1)}, u32[]{:S(2)}, u32[]{:S(2)}) collective-permute-start(bf16[192,256]{1,0:T(8,128)(2,1)} %get-tuple-element.70), channel_id=1, source_target_pairs={{0,1},{1,2},{2,3},{3,0},{4,5},{5,6},{6,7},{7,4},{8,9},{9,10},{10,1... | collective-permute-start | bytes 294920 | tf_op jit(solution)/shard_map/ppermute | solution.py:662
  173.9 15.4 %collective-permute-start.16 = (bf16[192,256]{1,0:T(8,128)(2,1)}, bf16[192,256]{1,0:T(8,128)(2,1)S(1)}, u32[]{:S(2)}, u32[]{:S(2)}) collective-permute-start(bf16[192,256]{1,0:T(8,128)(2,1)} %get-tuple-element.78), channel_id=1, source_target_pairs={{0,3},{1,0},{2,1},{3,2},{4,7},{5,4},{6,5},{7,6},{8,11},{9,8},{10,9... | collective-permute-start | bytes 294920 | tf_op jit(solution)/shard_map/ppermute | solution.py:662
  175.9 13.4 %collective-permute-start.17 = (bf16[192,256]{1,0:T(8,128)(2,1)}, bf16[192,256]{1,0:T(8,128)(2,1)S(1)}, u32[]{:S(2)}, u32[]{:S(2)}) collective-permute-start(bf16[192,256]{1,0:T(8,128)(2,1)} %get-tuple-element.79), channel_id=1, source_target_pairs={{0,2},{1,3},{2,0},{3,1},{4,6},{5,7},{6,4},{7,5},{8,10},{9,11},{10,... | collective-permute-start | bytes 294920 | tf_op jit(solution)/shard_map/ppermute | solution.py:662
  202.8 163.5 %all-gather.6.cloned.1.call-start = ((), (), s32[]{:S(2)}) async-start(), calls=%async_computation | async-start | bytes 1966080 | tf_op jit(solution)/shard_map/all_gather | solution.py:821
  202.8 44.0 %collective-permute-start.19 = (bf16[2,4,96,896]{3,2,1,0:T(8,128)(2,1)}, bf16[2,4,96,896]{3,2,1,0:T(8,128)(2,1)S(1)}, u32[]{:S(2)}, u32[]{:S(2)}) collective-permute-start(bf16[2,4,96,896]{3,2,1,0:T(8,128)(2,1)} %get-tuple-element.86), channel_id=1, source_target_pairs={{0,8},{8,0},{4,12},{12,4},{1,9},{9,1},{5,13},{13,5},{2,10},{10,2},... | collective-permute-start | bytes 4128776 | tf_op jit(solution)/shard_map/ppermute | solution.py:661
  216.1 32.2 %collective-permute-start.18 = (bf16[2,4,96,896]{3,2,1,0:T(8,128)(2,1)}, bf16[2,4,96,896]{3,2,1,0:T(8,128)(2,1)S(1)}, u32[]{:S(2)}, u32[]{:S(2)}) collective-permute-start(bf16[2,4,96,896]{3,2,1,0:T(8,128)(2,1)} %get-tuple-element.74), channel_id=1, source_target_pairs={{0,4},{4,0},{8,12},{12,8},{1,5},{5,1},{9,13},{13,9},{2,6},{6,2},{1... | collective-permute-start | bytes 4128776 | tf_op jit(solution)/shard_map/ppermute | solution.py:660
  216.2 30.8 %copy-start.9 = (bf16[2,4,96,896]{3,2,1,0:T(8,128)(2,1)S(1)}, bf16[2,4,96,896]{3,2,1,0:T(8,128)(2,1)}, u32[]{:S(2)}) copy-start(bf16[2,4,96,896]{3,2,1,0:T(8,128)(2,1)} %get-tuple-element.85) | copy-start | bytes 4128772
  216.2 111.1 %collective-permute-start.24 = (bf16[192,256]{1,0:T(8,128)(2,1)}, bf16[192,256]{1,0:T(8,128)(2,1)}, u32[]{:S(2)}, u32[]{:S(2)}) collective-permute-start(bf16[192,256]{1,0:T(8,128)(2,1)} %get-tuple-element.90), channel_id=1, source_target_pairs={{0,1},{1,2},{2,3},{3,0},{4,5},{5,6},{6,7},{7,4},{8,9},{9,10},{10,1... | collective-permute-start | bytes 294920 | tf_op jit(solution)/shard_map/ppermute | solution.py:662
  247.2 18.4 %collective-permute-start.41 = (bf16[4,96,896]{2,1,0:T(8,128)(2,1)S(1)}, bf16[4,96,896]{2,1,0:T(8,128)(2,1)S(1)}, u32[]{:S(2)}, u32[]{:S(2)}) collective-permute-start(bf16[4,96,896]{2,1,0:T(8,128)(2,1)S(1)} %fusion.15), channel_id=1, source_target_pairs={{0,4},{4,0},{8,12},{12,8},{1,5},{5,1},{9,13},{13,9},{2,6},{6,2},{1... | collective-permute-start | bytes 2064392 | tf_op jit(solution)/shard_map/ppermute | solution.py:660
  248.7 18.4 %collective-permute-start.40 = (bf16[4,96,896]{2,1,0:T(8,128)(2,1)S(1)}, bf16[4,96,896]{2,1,0:T(8,128)(2,1)S(1)}, u32[]{:S(2)}, u32[]{:S(2)}) collective-permute-start(bf16[4,96,896]{2,1,0:T(8,128)(2,1)S(1)} %fusion.14), channel_id=1, source_target_pairs={{0,8},{8,0},{4,12},{12,4},{1,9},{9,1},{5,13},{13,5},{2,10},{10,2},... | collective-permute-start | bytes 2064392 | tf_op jit(solution)/shard_map/ppermute | solution.py:661
  250.7 32.0 %collective-permute-start.22 = (bf16[2,192,1024]{2,1,0:T(8,128)(2,1)S(1)}, bf16[2,192,1024]{2,1,0:T(8,128)(2,1)S(1)}, u32[]{:S(2)}, u32[]{:S(2)}) collective-permute-start(bf16[2,192,1024]{2,1,0:T(8,128)(2,1)S(1)} %copy-done.34), channel_id=1, source_target_pairs={{0,8},{8,0},{4,12},{12,4},{1,9},{9,1},{5,13},{13,5},{2,10},{10,2},... | collective-permute-start | bytes 2359304 | tf_op jit(solution)/shard_map/ppermute | solution.py:661
  251.6 33.0 %collective-permute-start.20 = (bf16[2,192,1024]{2,1,0:T(8,128)(2,1)S(1)}, bf16[2,192,1024]{2,1,0:T(8,128)(2,1)S(1)}, u32[]{:S(2)}, u32[]{:S(2)}) collective-permute-start(bf16[2,192,1024]{2,1,0:T(8,128)(2,1)S(1)} %copy-done.33), channel_id=1, source_target_pairs={{0,4},{4,0},{8,12},{12,8},{1,5},{5,1},{9,13},{13,9},{2,6},{6,2},{1... | collective-permute-start | bytes 2359304 | tf_op jit(solution)/shard_map/ppermute | solution.py:660
  268.4 14.5 %copy-start.13 = (bf16[2,192,1024]{2,1,0:T(8,128)(2,1)S(1)}, bf16[2,192,1024]{2,1,0:T(8,128)(2,1)}, u32[]{:S(2)}) copy-start(bf16[2,192,1024]{2,1,0:T(8,128)(2,1)} %get-tuple-element.88) | copy-start | bytes 2359300
  268.4 23.1 %collective-permute-start.44 = (bf16[96,1792]{1,0:T(8,128)(2,1)}, bf16[96,1792]{1,0:T(8,128)(2,1)}, u32[]{:S(2)}, u32[]{:S(2)}) collective-permute-start(bf16[96,1792]{1,0:T(8,128)(2,1)} %get-tuple-element.150), channel_id=1, source_target_pairs={{0,1},{3,2},{4,5},{7,6},{8,9},{11,10},{12,13},{15,14},{16,17},{19,... | collective-permute-start | bytes 1032200 | tf_op jit(solution)/shard_map/ppermute | solution.py:690
  272.9 31.0 %collective-permute-start.42 = (bf16[96,1792]{1,0:T(8,128)(2,1)}, bf16[96,1792]{1,0:T(8,128)(2,1)}, u32[]{:S(2)}, u32[]{:S(2)}) collective-permute-start(bf16[96,1792]{1,0:T(8,128)(2,1)} %get-tuple-element.149), channel_id=1, source_target_pairs={{0,1},{1,2},{2,3},{4,5},{5,6},{6,7},{8,9},{9,10},{10,11},{12,13},{... | collective-permute-start | bytes 1032200 | tf_op jit(solution)/shard_map/ppermute | solution.py:690
  283.9 10.3 %collective-permute-start.23 = (bf16[192,1024]{1,0:T(8,128)(2,1)}, bf16[192,1024]{1,0:T(8,128)(2,1)}, u32[]{:S(2)}, u32[]{:S(2)}) collective-permute-start(bf16[192,1024]{1,0:T(8,128)(2,1)} %fusion.27), channel_id=1, source_target_pairs={{0,4},{4,0},{8,12},{12,8},{1,5},{5,1},{9,13},{13,9},{2,6},{6,2},{1... | collective-permute-start | bytes 1179656 | tf_op jit(solution)/shard_map/ppermute | solution.py:660
  286.0 10.6 %collective-permute-start.21 = (bf16[192,1024]{1,0:T(8,128)(2,1)S(1)}, bf16[192,1024]{1,0:T(8,128)(2,1)}, u32[]{:S(2)}, u32[]{:S(2)}) collective-permute-start(bf16[192,1024]{1,0:T(8,128)(2,1)S(1)} %fusion.26), channel_id=1, source_target_pairs={{0,8},{8,0},{4,12},{12,4},{1,9},{9,1},{5,13},{13,5},{2,10},{10,2},... | collective-permute-start | bytes 1179656 | tf_op jit(solution)/shard_map/ppermute | solution.py:661
  291.5 51.1 %collective-permute-start.30 = (bf16[4,384,640]{2,1,0:T(8,128)(2,1)}, bf16[4,384,640]{2,1,0:T(8,128)(2,1)S(1)}, u32[]{:S(2)}, u32[]{:S(2)}) collective-permute-start(bf16[4,384,640]{2,1,0:T(8,128)(2,1)} %bitcast.112), channel_id=1, source_target_pairs={{0,16},{16,0},{1,17},{17,1},{2,18},{18,2},{3,19},{19,3},{4,20},{20... | collective-permute-start | bytes 5898248 | tf_op jit(solution)/shard_map/ppermute | solution.py:659
  294.2 11.6 %collective-permute-start.43 = (bf16[96,1792]{1,0:T(8,128)(2,1)S(1)}, bf16[96,1792]{1,0:T(8,128)(2,1)S(1)}, u32[]{:S(2)}, u32[]{:S(2)}) collective-permute-start(bf16[96,1792]{1,0:T(8,128)(2,1)S(1)} %copy-done.21), channel_id=1, source_target_pairs={{3,2},{2,1},{1,0},{7,6},{6,5},{5,4},{11,10},{10,9},{9,8},{15,14},{... | collective-permute-start | bytes 1032200 | tf_op jit(solution)/shard_map/ppermute | solution.py:690
  296.6 29.5 %collective-permute-start.45 = (bf16[96,1792]{1,0:T(8,128)(2,1)S(1)}, bf16[96,1792]{1,0:T(8,128)(2,1)S(1)}, u32[]{:S(2)}, u32[]{:S(2)}) collective-permute-start(bf16[96,1792]{1,0:T(8,128)(2,1)S(1)} %fusion.25), channel_id=1, source_target_pairs={{0,2},{1,3},{2,0},{3,1},{4,6},{5,7},{6,4},{7,5},{8,10},{9,11},{10,... | collective-permute-start | bytes 1032200 | tf_op jit(solution)/shard_map/ppermute | solution.py:690
  303.9 24.3 %collective-permute-start.26 = (bf16[192,256]{1,0:T(8,128)(2,1)S(1)}, bf16[192,256]{1,0:T(8,128)(2,1)S(1)}, u32[]{:S(2)}, u32[]{:S(2)}) collective-permute-start(bf16[192,256]{1,0:T(8,128)(2,1)S(1)} %copy-done.28), channel_id=1, source_target_pairs={{0,2},{1,3},{2,0},{3,1},{4,6},{5,7},{6,4},{7,5},{8,10},{9,11},{10,... | collective-permute-start | bytes 294920 | tf_op jit(solution)/shard_map/ppermute | solution.py:662
  305.7 26.4 %collective-permute-start.28 = (bf16[192,256]{1,0:T(8,128)(2,1)S(1)}, bf16[192,256]{1,0:T(8,128)(2,1)S(1)}, u32[]{:S(2)}, u32[]{:S(2)}) collective-permute-start(bf16[192,256]{1,0:T(8,128)(2,1)S(1)} %copy-done.26), channel_id=1, source_target_pairs={{0,3},{1,0},{2,1},{3,2},{4,7},{5,4},{6,5},{7,6},{8,11},{9,8},{10,9... | collective-permute-start | bytes 294920 | tf_op jit(solution)/shard_map/ppermute | solution.py:662
  326.2 9.6 %collective-permute-start.25 = (bf16[384,256]{1,0:T(8,128)(2,1)S(1)}, bf16[384,256]{1,0:T(8,128)(2,1)S(1)}, u32[]{:S(2)}, u32[]{:S(2)}) collective-permute-start(bf16[384,256]{1,0:T(8,128)(2,1)S(1)} %get-tuple-element.156), channel_id=1, source_target_pairs={{0,1},{1,2},{2,3},{3,0},{4,5},{5,6},{6,7},{7,4},{8,9},{9,10},{10,1... | collective-permute-start | bytes 589832 | tf_op jit(solution)/shard_map/ppermute | solution.py:662
  327.3 15.3 %collective-permute-start.27 = (bf16[384,256]{1,0:T(8,128)(2,1)S(1)}, bf16[384,256]{1,0:T(8,128)(2,1)S(1)}, u32[]{:S(2)}, u32[]{:S(2)}) collective-permute-start(bf16[384,256]{1,0:T(8,128)(2,1)S(1)} %get-tuple-element.157), channel_id=1, source_target_pairs={{0,2},{1,3},{2,0},{3,1},{4,6},{5,7},{6,4},{7,5},{8,10},{9,11},{10,... | collective-permute-start | bytes 589832 | tf_op jit(solution)/shard_map/ppermute | solution.py:662
  328.2 14.4 %copy-start.41 = (bf16[192,256]{1,0:T(8,128)(2,1)}, bf16[192,256]{1,0:T(8,128)(2,1)S(1)}, u32[]{:S(2)}) copy-start(bf16[192,256]{1,0:T(8,128)(2,1)S(1)} %collective-permute-done.26.refs_4_) | copy-start | bytes 294916
  328.2 14.4 %collective-permute-start.29 = (bf16[384,256]{1,0:T(8,128)(2,1)S(1)}, bf16[384,256]{1,0:T(8,128)(2,1)S(1)}, u32[]{:S(2)}, u32[]{:S(2)}) collective-permute-start(bf16[384,256]{1,0:T(8,128)(2,1)S(1)} %get-tuple-element.154), channel_id=1, source_target_pairs={{0,3},{1,0},{2,1},{3,2},{4,7},{5,4},{6,5},{7,6},{8,11},{9,8},{10,9... | collective-permute-start | bytes 589832 | tf_op jit(solution)/shard_map/ppermute | solution.py:662
  344.0 17.9 %copy-start.10 = (bf16[640,1024]{1,0:T(8,128)(2,1)S(1)}, bf16[640,1024]{1,0:T(8,128)(2,1)}, u32[]{:S(2)}) copy-start(bf16[640,1024]{1,0:T(8,128)(2,1)} %maximum_maximum_fusion) | copy-start | bytes 3932164
  344.0 17.9 %copy-start.50 = (bf16[1024,768]{1,0:T(8,128)(2,1)S(1)}, bf16[1024,768]{1,0:T(8,128)(2,1)}, u32[]{:S(2)}) copy-start(bf16[1024,768]{1,0:T(8,128)(2,1)} %get-tuple-element.99) | copy-start | bytes 4718596
  350.0 8.8 %collective-permute-start.46 = (f32[16,768]{1,0:T(8,128)}, f32[16,768]{1,0:T(8,128)S(1)}, u32[]{:S(2)}, u32[]{:S(2)}) collective-permute-start(f32[16,768]{1,0:T(8,128)} %get-tuple-element.105), channel_id=1, source_target_pairs={{0,16},{16,0},{1,17},{17,1},{2,18},{18,2},{3,19},{19,3},{4,20},{20... | collective-permute-start | bytes 147464 | tf_op jit(solution)/shard_map/ppermute | solution.py:659
  350.8 39.0 %collective-permute-start.31 = (bf16[256,768]{1,0:T(8,128)(2,1)}, bf16[256,768]{1,0:T(8,128)(2,1)}, u32[]{:S(2)}, u32[]{:S(2)}) collective-permute-start(bf16[256,768]{1,0:T(8,128)(2,1)} %get-tuple-element.97), channel_id=1, source_target_pairs={{0,2},{1,3},{2,0},{3,1},{4,6},{5,7},{6,4},{7,5},{8,10},{9,11},{10,... | collective-permute-start | bytes 1179656 | tf_op jit(solution)/shard_map/ppermute | solution.py:672
  353.8 53.2 %collective-permute-start.33 = (bf16[256,768]{1,0:T(8,128)(2,1)}, bf16[256,768]{1,0:T(8,128)(2,1)}, u32[]{:S(2)}, u32[]{:S(2)}) collective-permute-start(bf16[256,768]{1,0:T(8,128)(2,1)} %get-tuple-element.97), channel_id=1, source_target_pairs={{0,1},{1,2},{2,3},{4,5},{5,6},{6,7},{8,9},{9,10},{10,11},{12,13},{... | collective-permute-start | bytes 1179656 | tf_op jit(solution)/shard_map/ppermute | solution.py:672
  357.5 50.6 %collective-permute-start.34 = (bf16[256,768]{1,0:T(8,128)(2,1)}, bf16[256,768]{1,0:T(8,128)(2,1)}, u32[]{:S(2)}, u32[]{:S(2)}) collective-permute-start(bf16[256,768]{1,0:T(8,128)(2,1)} %get-tuple-element.97), channel_id=1, source_target_pairs={{3,2},{2,1},{1,0},{7,6},{6,5},{5,4},{11,10},{10,9},{9,8},{15,14},{... | collective-permute-start | bytes 1179656 | tf_op jit(solution)/shard_map/ppermute | solution.py:672
  359.6 4.4 %collective-permute-start.47 = (f32[16,768]{1,0:T(8,128)S(1)}, f32[16,768]{1,0:T(8,128)S(1)}, u32[]{:S(2)}, u32[]{:S(2)}) collective-permute-start(f32[16,768]{1,0:T(8,128)S(1)} %add.323), channel_id=1, source_target_pairs={{0,4},{4,0},{8,12},{12,8},{1,5},{5,1},{9,13},{13,9},{2,6},{6,2},{1... | collective-permute-start | bytes 147464 | tf_op jit(solution)/shard_map/ppermute | solution.py:660
  364.0 4.2 collective-permute-start.48
  366.3 17.2 %collective-permute-start.35 = (bf16[1,384,640]{2,1,0:T(8,128)(2,1)}, bf16[1,384,640]{2,1,0:T(8,128)(2,1)}, u32[]{:S(2)}, u32[]{:S(2)}) collective-permute-start(bf16[1,384,640]{2,1,0:T(8,128)(2,1)} %get-tuple-element.152), channel_id=1, source_target_pairs={{0,16},{16,0},{1,17},{17,1},{2,18},{18,2},{3,19},{19,3},{4,20},{20... | collective-permute-start | bytes 1474568 | tf_op jit(solution)/shard_map/ppermute | solution.py:659
  368.1 8.9 %collective-permute-start.49 = (f32[16,768]{1,0:T(8,128)S(1)}, f32[16,768]{1,0:T(8,128)S(1)}, u32[]{:S(2)}, u32[]{:S(2)}) collective-permute-start(f32[16,768]{1,0:T(8,128)S(1)} %add.325), channel_id=1, source_target_pairs={{0,1},{1,0},{2,3},{3,2},{4,5},{5,4},{6,7},{7,6},{8,9},{9,8},{10,11... | collective-permute-start | bytes 147464 | tf_op jit(solution)/shard_map/ppermute | solution.py:893
  377.1 5.7 %collective-permute-start.50 = (f32[16,768]{1,0:T(8,128)S(1)}, f32[16,768]{1,0:T(8,128)S(1)}, u32[]{:S(2)}, u32[]{:S(2)}) collective-permute-start(f32[16,768]{1,0:T(8,128)S(1)} %add.326), channel_id=1, source_target_pairs={{0,2},{2,0},{1,3},{3,1},{4,6},{6,4},{5,7},{7,5},{8,10},{10,8},{9,1... | collective-permute-start | bytes 147464 | tf_op jit(solution)/shard_map/ppermute | solution.py:894
  387.6 15.0 %copy-start.23 = (bf16[2,1,96,384]{3,2,1,0:T(8,128)(2,1)S(1)}, bf16[2,1,96,384]{3,2,1,0:T(8,128)(2,1)}, u32[]{:S(2)}) copy-start(bf16[2,1,96,384]{3,2,1,0:T(8,128)(2,1)} %get-tuple-element.101) | copy-start | bytes 442372
  387.6 5.3 %collective-permute-start.38 = (bf16[2,1,96,256]{3,2,1,0:T(8,128)(2,1)}, bf16[2,1,96,256]{3,2,1,0:T(8,128)(2,1)S(1)}, u32[]{:S(2)}, u32[]{:S(2)}) collective-permute-start(bf16[2,1,96,256]{3,2,1,0:T(8,128)(2,1)} %get-tuple-element.104), channel_id=1, source_target_pairs={{0,8},{8,0},{4,12},{12,4},{1,9},{9,1},{5,13},{13,5},{2,10},{10,2},... | collective-permute-start | bytes 294920 | tf_op jit(solution)/shard_map/ppermute | solution.py:661
  389.7 17.2 %collective-permute-start.32 = (bf16[256,768]{1,0:T(8,128)(2,1)}, bf16[256,768]{1,0:T(8,128)(2,1)S(1)}, u32[]{:S(2)}, u32[]{:S(2)}) collective-permute-start(bf16[256,768]{1,0:T(8,128)(2,1)} %collective-permute-done.31), channel_id=1, source_target_pairs={{2,3},{1,0},{6,7},{5,4},{10,11},{9,8},{14,15},{13,12},{18,19},{17,... | collective-permute-start | bytes 1179656 | tf_op jit(solution)/shard_map/ppermute | solution.py:672
  391.0 6.2 %collective-permute-start.36 = (bf16[2,1,96,384]{3,2,1,0:T(8,128)(2,1)}, bf16[2,1,96,384]{3,2,1,0:T(8,128)(2,1)S(1)}, u32[]{:S(2)}, u32[]{:S(2)}) collective-permute-start(bf16[2,1,96,384]{3,2,1,0:T(8,128)(2,1)} %get-tuple-element.102), channel_id=1, source_target_pairs={{0,4},{4,0},{8,12},{12,8},{1,5},{5,1},{9,13},{13,9},{2,6},{6,2},{1... | collective-permute-start | bytes 442376 | tf_op jit(solution)/shard_map/ppermute | solution.py:660
  393.7 5.5 %collective-permute-start.39 = (bf16[1,96,256]{2,1,0:T(8,128)(2,1)S(1)}, bf16[1,96,256]{2,1,0:T(8,128)(2,1)S(1)}, u32[]{:S(2)}, u32[]{:S(2)}) collective-permute-start(bf16[1,96,256]{2,1,0:T(8,128)(2,1)S(1)} %fusion.40), channel_id=1, source_target_pairs={{0,4},{4,0},{8,12},{12,8},{1,5},{5,1},{9,13},{13,9},{2,6},{6,2},{1... | collective-permute-start | bytes 147464 | tf_op jit(solution)/shard_map/ppermute | solution.py:660
  398.1 4.4 %collective-permute-start.37 = (bf16[1,96,384]{2,1,0:T(8,128)(2,1)S(1)}, bf16[1,96,384]{2,1,0:T(8,128)(2,1)S(1)}, u32[]{:S(2)}, u32[]{:S(2)}) collective-permute-start(bf16[1,96,384]{2,1,0:T(8,128)(2,1)S(1)} %fusion.39), channel_id=1, source_target_pairs={{0,8},{8,0},{4,12},{12,4},{1,9},{9,1},{5,13},{13,5},{2,10},{10,2},... | collective-permute-start | bytes 221192 | tf_op jit(solution)/shard_map/ppermute | solution.py:661
  (41 other events, 135.0 us)
Sparse Core Ops, SparseCore 0:
  47.6 75.8 all-gather.7
  202.9 54.5 all-gather.9
  259.0 51.9 all-gather.5

commit v4 on v3

--- a/solution.py
+++ b/solution.py
@@ -455,7 +455,7 @@
         dims, lambda i, sc: (0,) * len(dims), pipeline_mode=pl.Buffered(1)
     )
     placed = pl.BlockSpec(
-        (1, ffw, half), lambda i, sc: (lax.rem(sc[3] - i + parts, parts), 0, 0)
+        (1, ffw, half), lambda i, sc: (i, 0, 0)
     )
     once = lambda a: whole(*a.shape)
     grads = (parts, half, 128 * ((2 * ffw + cols + 127) // 128))
@@ -642,7 +642,7 @@
     cot = cotangent[0]
     row = lambda v: v[None, :]
     zero = jnp.zeros_like(b_out)
-    table = jnp.stack(
+    table = jnp.concatenate(
         [
             first_norm_gain,
             first_norm_bias,
@@ -653,7 +653,7 @@
             zero,
             zero,
         ]
-    )
+    ).reshape(8, width)
     after = lambda v, dep: lax.optimization_barrier((v, dep))[0]
 
     swap = lambda v: lax.ppermute(v, "shard", [(0, 1), (1, 0)])
@@ -666,14 +666,23 @@
     def gather_direct(v):
         return [v] + [shift_by(v, d) for d in range(1, n_tensor)]
 
-    def gather_line(v, hold=None):
+    def gather_begin(v):
         if n_tensor != 4:
-            return gather_direct(v)
-        move = lambda a, perm: lax.ppermute(a, "tensor", perm)
-        two = move(v, [(0, 2), (1, 3), (2, 0), (3, 1)])
-        right = move(v, [(0, 1), (1, 2), (2, 3)])
-        left = move(v, [(3, 2), (2, 1), (1, 0)])
-        far = move(two if hold is None else after(two, hold), [(2, 3), (1, 0)])
+            return tuple(gather_direct(v))
+        move = lambda perm: lax.ppermute(v, "tensor", perm)
+        return (
+            v,
+            move([(0, 2), (1, 3), (2, 0), (3, 1)]),
+            move([(0, 1), (1, 2), (2, 3)]),
+            move([(3, 2), (2, 1), (1, 0)]),
+        )
+
+    def gather_end(state, hold=()):
+        if n_tensor != 4:
+            return list(state)
+        v, two, right, left = state
+        two = after(two, hold)
+        far = lax.ppermute(two, "tensor", [(2, 3), (1, 0)])
         return [
             v,
             jnp.where(tensor == 0, far, right),
@@ -752,7 +761,17 @@
         table,
     )
 
+    terms, rest = [], b_fc
+    for _ in range(3):
+        term = lax.reduce_precision(rest, 8, 7)
+        terms.append(term.astype(bf16).reshape(ffw // half, half))
+        rest = rest - term
+    terms = jnp.concatenate(terms, axis=0)
+    terms = jnp.pad(terms, ((0, 16 - terms.shape[0]), (0, 0)))
+    packed = jnp.concatenate([w_out, terms, w_fc[:, :half], w_fc[:, half:]], axis=0)
+    packed = gather_begin(packed)
     kv = []
+    hold = ()
     head = 0
     for g in GROUPS:
         rows = slice(head * HD, (head + g) * HD)
@@ -761,36 +780,30 @@
         if grouped:
             kx, vy = along_x(k), along_y(v)
             k_two, v_two = jnp.stack([k, kx]), jnp.stack([v, vy])
-            kv.append([k, kx, along_y(k_two), v, vy, along_x(v_two)])
+            k_two, v_two = after((k_two, v_two), packed[1])
+            k_yd, v_xd = along_y(k_two), along_x(v_two)
+            hold = (k_two, v_two)
+            kv.append([k, kx, k_yd, v, vy, v_xd])
         else:
             kv.append([lax.all_gather(jnp.concatenate([k, v], axis=0), "context", axis=0)])
 
-    def gather_weights(w, gather):
-        own = jnp.stack(gather(w))
-        return own, swap(own)
-
-    terms, rest = [], b_fc
-    for _ in range(3):
-        term = lax.reduce_precision(rest, 8, 7)
-        terms.append(term.astype(bf16).reshape(ffw // half, half))
-        rest = rest - term
-    terms = jnp.concatenate(terms, axis=0)
-    terms = jnp.pad(terms, ((0, 16 - terms.shape[0]), (0, 0)))
-    packed = jnp.concatenate([w_out, terms, w_fc[:, :half], w_fc[:, half:]], axis=0)
-    gathered = lax.all_gather(w_down, "tensor", axis=0)
-    dn = (gathered, swap(gathered))
+    dn = gather_begin(after(w_down, packed[1]))
     saved = []
     att = [[] for _ in range(n_tensor)]
     head = 0
     for g, held in zip(GROUPS, kv):
-        lse, ot, *out = attend(scalars, row(starts), qt, held, head, g, BK_F, BQ_F, n_tensor)
+        results = attend(scalars, row(starts), after(qt, packed[1:]), held, head, g, BK_F, BQ_F, n_tensor)
+        lse, ot, *out = after(results, dn[1:])
         saved.append((lse, ot))
         att[0].append(out[0])
         for d in range(1, n_tensor):
             att[d].append(shift_by(out[d], d))
         head += g
 
-    of = gather_weights(packed, lambda w: gather_line(w, saved[-1][0]))
+    of = jnp.stack(after(gather_end(packed, hold), saved[-1][0]))
+    of = (of, swap(of))
+    dn = jnp.stack(gather_end(dn, saved[-1][0]))
+    dn = (dn, swap(dn))
     x_sub = lax.dynamic_slice_in_dim(x, tensor * sub, sub, 0)
     cot_sub = lax.dynamic_slice_in_dim(cot, tensor * sub, sub, 0)
     outputs_sub, grad_mid, mid_sums, fc_sums, *rest = middle(
@@ -808,8 +821,7 @@
         shift_by(d_att[d], -d) for d in range(1, n_tensor)
     ]
 
-    def spread(v):
-        pieces = gather_line(v)
+    def spread(pieces):
         whole = jnp.zeros((tok, width), f32)
         for d in range(n_tensor):
             at = lax.rem(tensor - d + n_tensor, n_tensor) * sub
@@ -818,8 +830,10 @@
 
     folded = scatter_begin(g_own, g_other)
     hop_one = folded[0] if grouped else folded
-    outputs = lax.all_gather(after(outputs_sub, do_parts[-1]), "tensor", axis=0, tiled=True)
+    outputs = gather_begin(after(outputs_sub, do_parts))
     wide = scatter_first(folded)
+    wide_sends = wide[2:]
+    wide = scatter_second(wide)
 
     dq_pieces, dkv_pieces, dqkv = [], [], []
     head = 0
@@ -829,14 +843,16 @@
         out = attend_back(
             scalars, row(starts), after(qt, hop_one), lse, ot, do_parts, held, head, g, BK_B, BQ_B
         )
-        dq, dkv = out[:n_tensor], out[n_tensor:]
+        back_done = out[-1]
+        dq, dkv = after(out[:n_tensor], (outputs[1:3], wide_sends)), out[n_tensor:]
         if grouped:
             dk_keep, dk_send, dv_keep, dv_send = dkv
-            dk_send, dv_send = after((dk_send, dv_send), (wide[2], wide[3]))
+            dk_send, dv_send = after((dk_send, dv_send), (wide_sends, outputs[1:3]))
             r = along_x(dk_send).astype(f32)
             s = along_y(dv_send).astype(f32)
             r2 = along_y((dk_keep[1].astype(f32) + r[1]).astype(bf16)).astype(f32)
             s2 = along_x((dv_keep[1].astype(f32) + s[1]).astype(bf16)).astype(f32)
+            back_done = (r2, s2)
             dk = (dk_keep[0].astype(f32) + r[0] + r2).astype(bf16)
             dv = (dv_keep[0].astype(f32) + s[0] + s2).astype(bf16)
         else:
@@ -847,7 +863,6 @@
         values.append(dv)
         head += g
 
-    wide = scatter_second(wide)
     wide_grads = scatter_line([wide[d] for d in range(n_tensor)])
 
     def part_of(v, d):
@@ -869,13 +884,13 @@
             whole = lax.dynamic_update_slice_in_dim(whole, q[d], at, 1)
         dq_whole.append(whole)
     qkv_wide = jnp.pad(qkv_own, ((0, 0), (0, -3 * cols % 128)))
-    qkv = lax.all_gather(after(qkv_wide, queries[-1][0]), "tensor", axis=0)
+    qkv = lax.all_gather(after(qkv_wide, out[-1]), "tensor", axis=0)
     qkv = (qkv, swap(qkv))
     input_sub, small = last(
         place, grads, pieces, qkv, x_sub, grad_mid, table, mid_sums, fc_sums
     )
-    input_gradient = spread(input_sub)
-    outputs = after(outputs, input_sub).astype(f32)[None]
+    input_gradient = spread(gather_direct(input_sub))
+    outputs = spread(after(gather_end(outputs, back_done), input_sub))
     stacked = jnp.concatenate(
         dq_whole + [both, jnp.zeros((-3 * cols % 128, tok), bf16)], axis=0
     )

time: 420 us -> 427 us (1.017)
  other arithmetic: 30.2 us -> 37.5 us
    ppermute x9, waiting for transfers between devices: 51.8 us -> 28 us  [body(): lax.ppermute(v, 'context', [(0, 2), (2, 0), (1, 3), (3, 1)])]
    ppermute x9, starting transfers between devices: 25.6 us -> 10.8 us  [body(): lax.ppermute(v, 'context', [(0, 2), (2, 0), (1, 3), (3, 1)])]
    all_gather x3 -> x1, waiting for transfers between devices: 0.02 us -> 10.8 us  [body(): qkv = lax.all_gather(after(qkv_wide, out[-1]), 'tensor', axis=0)]
    ppermute x12 -> x15, waiting for transfers between devices: 15.9 us -> 25.5 us  [body(): lax.ppermute(v, 'tensor', [(s, (s + d) % n_tensor) for s in range(n_tenso...]
    ppermute x8 -> x12, starting transfers between devices: 17.9 us -> 25.3 us  [the longest x9 21.3 us: gather_begin(): move = lambda perm: lax.ppermute(v, 'tensor', perm)]
    ppermute x12 -> x15, starting transfers between devices: 17.2 us -> 24.6 us  [body(): lax.ppermute(v, 'tensor', [(s, (s + d) % n_tensor) for s in range(n_tenso...]
    dynamic_update_slice x4 -> x8, other arithmetic: 2.28 us -> 8.45 us  [spread(): whole = lax.dynamic_update_slice_in_dim(whole, pieces[d].astype(f32), at, 0)]
    ppermute x1, waiting for transfers between devices: 2.98 us -> 7.77 us  [body(): small += lax.ppermute(small, 'tensor', [(0, 1), (1, 0), (2, 3), (3, 2)])]
  transfers between devices with their start and end apart: 54 -> 59, of which waited for: 25 -> 29; matrix products, arithmetic and copies ran while one was open for 12% -> 14% of each run, Pallas kernels for 7% -> 10%
where the time goes in v4:
time: 427 us; the launch traced here: 426 us
  waiting for transfers between devices  182 us (43%)
  starting transfers between devices  91.6 us (21%)
  Pallas kernels  70 us (16%)
  other arithmetic  37.5 us (9%)
  local copies, waits for them, and re-layouts  28 us (7%)
  between operations  15 us (4%)
    ppermute x9, waiting for transfers between devices, gather_begin(): move = lambda perm: lax.ppermute(v, 'tensor', perm)  56.8 us
    ppermute x9, waiting for transfers between devices, body(): lax.ppermute(v, 'context', [(0, 2), (2, 0), (1, 3), (3, 1)])  28 us
    ppermute x15, waiting for transfers between devices, body(): lax.ppermute(v, 'tensor', [(s, (s + d) % n_tensor) for s in range(n_tenso...  25.5 us
    ppermute x15, starting transfers between devices, body(): lax.ppermute(v, 'tensor', [(s, (s + d) % n_tensor) for s in range(n_tenso...  24.6 us
    pallas_call x1, Pallas kernels, middle(): pl.pallas_call(functools.partial(middle_kernel, len(att), parts), grid_sp...  22.8 us
    ppermute x9, starting transfers between devices, gather_begin(): move = lambda perm: lax.ppermute(v, 'tensor', perm)  21.3 us
    ppermute x4, waiting for transfers between devices, scatter_line(): move = lambda a, perm: lax.ppermute(a.astype(bf16), 'tensor', perm)  20.3 us
    ppermute x9, waiting for transfers between devices, body(): lax.ppermute(v, 'context', [(0, 1), (1, 0), (2, 3), (3, 2)])  17.8 us
  transfers between devices with their start and end apart: 59, of which 29 were waited for; matrix products, arithmetic and copies ran while one was open for 14% of the time, Pallas kernels for 10%

profile of v4, /device:TPU:0, one launch (start us, length us, event | category | flops | bytes accessed | tf_op | source)
XLA Modules:
  0.0 425.8 jit_solution(14554429989822660576)
XLA Ops:
  11.2 3.8 collective-permute-start.1
  17.2 6.3 %project.1 = (bf16[1024,768]{1,0:T(8,128)(2,1)}, bf16[192,1024]{1,0:T(8,128)(2,1)}, bf16[192,1024]{1,0:T(8,128)(2,1)}, bf16[192,1024]{1,0:T(8,128)(2,1)}) custom-call(s32[4]{0:T(128)} %pad_add_fusion.1.sc, bf16[1024,768]{1,0:T(8,128)(2,1)} %bitcast.138, bf16[384,576]{1,0:T(8,128)(2,1)} %copy-done.18, bf16[384,576]{1,0:T(8,128)(2,1)} %copy-done.43, ...), custom_call_target="tpu_custom_call" | custom-call | flops 8049999872 | bytes 1048576 | tf_op jit(solution)/shard_map/project/pallas_call | solution.py:90
  23.5 1.6 collective-permute-start.4
  25.0 1.5 collective-permute-start.5
  26.5 8.3 %collective-permute-done.4.refs_1_.refs_5_ = bf16[192,1024]{1,0:T(8,128)(2,1)S(1)} collective-permute-done((bf16[192,1024]{1,0:T(8,128)(2,1)}, bf16[192,1024]{1,0:T(8,128)(2,1)S(1)}, u32[]{:S(2)}, u32[]{:S(2)}) %collective-permute-start.4) | collective-permute-done | bytes 393248 | tf_op jit(solution)/shard_map/ppermute | solution.py:660
  34.8 2.1 pad_maximum_fusion.2
  37.1 11.4 %collective-permute-done.1 = bf16[976,384]{1,0:T(8,128)(2,1)} collective-permute-done((bf16[976,384]{1,0:T(8,128)(2,1)S(1)}, bf16[976,384]{1,0:T(8,128)(2,1)}, u32[]{:S(2)}, u32[]{:S(2)}) %collective-permute-start.1) | collective-permute-done | bytes 749600 | tf_op jit(solution)/shard_map/ppermute | solution.py:672
  48.5 1.6 collective-permute-start.6
  51.5 3.4 collective-permute-start.2
  57.4 3.8 fusion.53
  63.4 6.2 %collective-permute-done.2 = bf16[976,384]{1,0:T(8,128)(2,1)} collective-permute-done((bf16[976,384]{1,0:T(8,128)(2,1)S(1)}, bf16[976,384]{1,0:T(8,128)(2,1)}, u32[]{:S(2)}, u32[]{:S(2)}) %collective-permute-start.2) | collective-permute-done | bytes 749600 | tf_op jit(solution)/shard_map/ppermute | solution.py:672
  69.7 3.5 collective-permute-start.8
  73.1 3.4 collective-permute-done.3
  76.6 3.1 collective-permute-start.9
  81.0 9.6 %attend.1 = (f32[3,1024]{1,0:T(4,128)}, bf16[192,1024]{1,0:T(8,128)(2,1)}, bf16[192,256]{1,0:T(8,128)(2,1)}, bf16[192,256]{1,0:T(8,128)(2,1)}, bf16[192,256]{1,0:T(8,128)(2,1)}, /*index=5*/bf16[192,256]{1,0:T(8,128)(2,1)}) custom-call(s32[12]{0:T(128)} %concatenate.31.sc, bf16[192,1024]{1,0:T(8,128)(2,1)} %get-tuple-element.116.qt, ...), custom_call_target="tpu_custom_call" | custom-call | flops 23000000512 | bytes 1048576 | tf_op jit(solution)/shard_map/attend/pallas_call | solution.py:221
  90.6 23.0 %collective-permute-done.8 = bf16[768,384]{1,0:T(8,128)(2,1)S(1)} collective-permute-done((bf16[768,384]{1,0:T(8,128)(2,1)}, bf16[768,384]{1,0:T(8,128)(2,1)S(1)}, u32[]{:S(2)}, u32[]{:S(2)}) %collective-permute-start.8) | collective-permute-done | bytes 589856 | tf_op jit(solution)/shard_map/ppermute | solution.py:672
  117.2 2.8 pad_maximum_fusion.refs_6_
  120.1 9.1 %collective-permute-done.16 = bf16[768,384]{1,0:T(8,128)(2,1)S(1)} collective-permute-done((bf16[768,384]{1,0:T(8,128)(2,1)S(1)}, bf16[768,384]{1,0:T(8,128)(2,1)S(1)}, u32[]{:S(2)}, u32[]{:S(2)}) %collective-permute-start.16) | collective-permute-done | bytes 589856 | tf_op jit(solution)/shard_map/ppermute | solution.py:685
  129.3 1.8 pad_maximum_fusion.1.refs_8_
  131.1 1.8 dynamic-slice_bitcast_fusion.3.refs_4_.refs_10_
  132.9 5.3 %collective-permute-start.12 = (bf16[192,256]{1,0:T(8,128)(2,1)S(1)}, bf16[192,256]{1,0:T(8,128)(2,1)S(1)}, u32[]{:S(2)}, u32[]{:S(2)}) collective-permute-start(bf16[192,256]{1,0:T(8,128)(2,1)S(1)} %copy-done.48), channel_id=1, source_target_pairs={{0,2},{1,3},{2,0},{3,1},{4,6},{5,7},{6,4},{7,5},{8,10},{9,11},{10,... | collective-permute-start | bytes 294920 | tf_op jit(solution)/shard_map/ppermute | solution.py:662
  139.5 2.0 collective-permute-done.11.refs_1_
  141.4 4.0 collective-permute-done.12.refs_2_
  146.1 22.8 %middle.1 = (bf16[256,768]{1,0:T(8,128)(2,1)}, f32[256,768]{1,0:T(8,128)}, f32[4,768]{1,0:T(4,128)}, f32[4,1,768]{2,1,0:T(1,128)}, bf16[192,256]{1,0:T(8,128)(2,...) custom-call(s32[4]{0:T(128)} %pad_add_fusion.1.sc, ...), custom_call_target="tpu_custom_call" | custom-call | flops 21849999360 | bytes 1048576 | tf_op jit(solution)/shard_map/middle/pallas_call | solution.py:462
  169.0 2.7 collective-permute-start.18
  173.1 2.1 collective-permute-done.18.refs_1_
  175.2 7.4 %collective-permute-done.19.refs_2_ = bf16[192,256]{1,0:T(8,128)(2,1)S(1)} collective-permute-done((bf16[192,256]{1,0:T(8,128)(2,1)}, bf16[192,256]{1,0:T(8,128)(2,1)S(1)}, u32[]{:S(2)}, u32[]{:S(2)}) %collective-permute-start.19) | collective-permute-done | bytes 98336 | tf_op jit(solution)/shard_map/ppermute | solution.py:662
  184.3 2.9 collective-permute-start.25
  188.5 12.8 %collective-permute-done.21 = bf16[256,768]{1,0:T(8,128)(2,1)} collective-permute-done((bf16[256,768]{1,0:T(8,128)(2,1)}, bf16[256,768]{1,0:T(8,128)(2,1)}, u32[]{:S(2)}, u32[]{:S(2)}) %collective-permute-start.21) | collective-permute-done | bytes 393248 | tf_op jit(solution)/shard_map/ppermute | solution.py:672
  202.8 8.6 %fold.2 = (bf16[2,4,96,896]{3,2,1,0:T(8,128)(2,1)}, bf16[2,4,96,896]{3,2,1,0:T(8,128)(2,1)}, bf16[2,4,96,896]{3,2,1,0:T(8,128)(2,1)}, bf16[2,4,96,896]{3,2,1,0:T(8,128)(2,1)}) custom-call(s32[4]{0:T(128)} %pad_add_fusion.1.sc, bf16[4,384,1792]{2,1,0:T(8,128)(2,1)} %get-tuple-element.113.mine, bf16[4,384,1792]{2,1,0:T(8,128)(2,1)} %collective-permute-done.22.theirs), custom_call_target="tpu_custom_call" | custom-call | flops 8049999872 | bytes 1048576 | tf_op jit(solution)/shard_map/fold/pallas_call | solution.py:584
  212.5 12.6 %attend_back.1 = (bf16[192,256]{1,0:T(8,128)(2,1)}, bf16[192,256]{1,0:T(8,128)(2,1)}, bf16[192,256]{1,0:T(8,128)(2,1)}, bf16[192,256]{1,0:T(8,128)(2,1)}, bf16[2...) custom-call(s32[12]{0:T(128)} %concatenate.31.sc, ...), custom_call_target="tpu_custom_call" | custom-call | flops 29899999232 | bytes 1048576 | tf_op jit(solution)/shard_map/attend_back/pallas_call | solution.py:327
  226.1 1.9 broadcast_select_fusion.2
  228.0 16.0 %collective-permute-done.24 = bf16[2,4,96,896]{3,2,1,0:T(8,128)(2,1)S(1)} collective-permute-done((bf16[2,4,96,896]{3,2,1,0:T(8,128)(2,1)}, bf16[2,4,96,896]{3,2,1,0:T(8,128)(2,1)S(1)}, u32[]{:S(2)}, u32[]{:S(2)}) %collective-permute-start.24) | collective-permute-done | bytes 1376288 | tf_op jit(solution)/shard_map/ppermute | solution.py:661
  244.3 1.6 collective-permute-start.48
  249.4 2.9 collective-permute-start.32
  255.0 7.7 %collective-permute-done.48 = bf16[4,96,896]{2,1,0:T(8,128)(2,1)S(1)} collective-permute-done((bf16[4,96,896]{2,1,0:T(8,128)(2,1)S(1)}, bf16[4,96,896]{2,1,0:T(8,128)(2,1)S(1)}, u32[]{:S(2)}, u32[]{:S(2)}) %collective-permute-start.48) | collective-permute-done | bytes 688160 | tf_op jit(solution)/shard_map/ppermute | solution.py:660
  263.0 1.8 collective-permute-done.47
  266.1 5.7 %collective-permute-start.51 = (bf16[96,1792]{1,0:T(8,128)(2,1)}, bf16[96,1792]{1,0:T(8,128)(2,1)}, u32[]{:S(2)}, u32[]{:S(2)}) collective-permute-start(bf16[96,1792]{1,0:T(8,128)(2,1)} %get-tuple-element.196), channel_id=1, source_target_pairs={{0,1},{3,2},{4,5},{7,6},{8,9},{11,10},{12,13},{15,14},{16,17},{19,... | collective-permute-start | bytes 1032200 | tf_op jit(solution)/shard_map/ppermute | solution.py:699
  271.7 2.0 collective-permute-start.49
  273.7 5.3 %collective-permute-done.28 = bf16[2,192,1024]{2,1,0:T(8,128)(2,1)S(1)} collective-permute-done((bf16[2,192,1024]{2,1,0:T(8,128)(2,1)S(1)}, bf16[2,192,1024]{2,1,0:T(8,128)(2,1)S(1)}, u32[]{:S(2)}, u32[]{:S(2)}) %collective-permute-start.28) | collective-permute-done | bytes 786464 | tf_op jit(solution)/shard_map/ppermute | solution.py:661
  284.2 10.8 %all-gather.3.cloned.1.call-done = bf16[1536,640]{0,1:T(8,128)(2,1)} async-done(((bf16[384,640]{0,1:T(8,128)(2,1)}), bf16[1536,640]{0,1:T(8,128)(2,1)}) %all-gather.3.cloned.1.call-update) | async-done | bytes 1966096 | tf_op jit(solution)/shard_map/all_gather | solution.py:887
  295.0 4.0 copy.34
  302.9 4.9 %collective-permute-start.52 = (bf16[96,1792]{1,0:T(8,128)(2,1)S(1)}, bf16[96,1792]{1,0:T(8,128)(2,1)S(1)}, u32[]{:S(2)}, u32[]{:S(2)}) collective-permute-start(bf16[96,1792]{1,0:T(8,128)(2,1)S(1)} %fusion.25), channel_id=1, source_target_pairs={{0,2},{1,3},{2,0},{3,1},{4,6},{5,7},{6,4},{7,5},{8,10},{9,11},{10,... | collective-permute-start | bytes 1032200 | tf_op jit(solution)/shard_map/ppermute | solution.py:699
  311.2 2.6 collective-permute-done.50
  314.5 17.7 %collective-permute-done.52 = bf16[96,1792]{1,0:T(8,128)(2,1)S(1)} collective-permute-done((bf16[96,1792]{1,0:T(8,128)(2,1)S(1)}, bf16[96,1792]{1,0:T(8,128)(2,1)S(1)}, u32[]{:S(2)}, u32[]{:S(2)}) %collective-permute-start.52) | collective-permute-done | bytes 344096 | tf_op jit(solution)/shard_map/ppermute | solution.py:699
  334.3 3.8 collective-permute-start.37
  338.9 3.4 collective-permute-done.33.refs_3_
  342.3 6.5 %collective-permute-done.35.refs_5_ = bf16[384,256]{1,0:T(8,128)(2,1)S(1)} collective-permute-done((bf16[384,256]{1,0:T(8,128)(2,1)S(1)}, bf16[384,256]{1,0:T(8,128)(2,1)S(1)}, u32[]{:S(2)}, u32[]{:S(2)}) %collective-permute-start.35) | collective-permute-done | bytes 196640 | tf_op jit(solution)/shard_map/ppermute | solution.py:662
  349.6 6.0 %last.1 = (bf16[256,768]{1,0:T(8,128)(2,1)}, f32[16,768]{1,0:T(8,128)}) custom-call(s32[4]{0:T(128)} %pad_add_fusion.1.sc, bf16[192,256]{1,0:T(8,128)(2,1)} %get-tuple-element.132.refs_0_, bf16[384,256]{1,0:T(8,128)(2,1)} %get-tuple-element.201.refs_1_, bf16[192,256]{1,0:T(8,128)(2,1)} %collective-permute-done.32.refs_2_, ...), custom_call_target="tpu_custom_call" | custom-call | flops 6899999744 | bytes 1048576 | tf_op jit(solution)/shard_map/last/pallas_call | solution.py:534
  355.6 4.6 %collective-permute-start.39 = (bf16[256,768]{1,0:T(8,128)(2,1)}, bf16[256,768]{1,0:T(8,128)(2,1)S(1)}, u32[]{:S(2)}, u32[]{:S(2)}) collective-permute-start(bf16[256,768]{1,0:T(8,128)(2,1)} %get-tuple-element.140), channel_id=1, source_target_pairs={{0,1},{1,2},{2,3},{3,0},{4,5},{5,6},{6,7},{7,4},{8,9},{9,10},{10,1... | collective-permute-start | bytes 1179656 | tf_op jit(solution)/shard_map/ppermute | solution.py:662
  360.3 2.4 collective-permute-start.41
  365.6 1.9 broadcast_in_dim.68.clone.1
  368.4 1.9 collective-permute-start.54
  370.3 1.9 broadcast_in_dim.68.clone
  373.1 2.1 collective-permute-start.55
  377.3 1.9 convert_dynamic-update-slice_fusion.5
  379.3 7.8 %collective-permute-done.56 = f32[16,768]{1,0:T(8,128)S(1)} collective-permute-done((f32[16,768]{1,0:T(8,128)S(1)}, f32[16,768]{1,0:T(8,128)S(1)}, u32[]{:S(2)}, u32[]{:S(2)}) %collective-permute-start.56) | collective-permute-done | bytes 49184 | tf_op jit(solution)/shard_map/ppermute | solution.py:908
  387.0 3.0 collective-permute-start.57
  391.0 5.1 %collective-permute-done.57 = f32[16,768]{1,0:T(8,128)S(1)} collective-permute-done((f32[16,768]{1,0:T(8,128)S(1)}, f32[16,768]{1,0:T(8,128)S(1)}, u32[]{:S(2)}, u32[]{:S(2)}) %collective-permute-start.57) | collective-permute-done | bytes 49184 | tf_op jit(solution)/shard_map/ppermute | solution.py:909
  400.1 4.1 fold.3
  404.1 2.3 collective-permute-start.45
  407.4 1.6 collective-permute-start.43
  410.6 1.6 collective-permute-start.46
  414.8 3.1 collective-permute-done.44
  (270 shorter events, 69.7 us)
Async XLA Ops:
  7.2 131.5 %copy-start = (bf16[1,1024,768]{2,1,0:T(8,128)(2,1)S(1)}, bf16[1,1024,768]{2,1,0:T(8,128)(2,1)}, u32[]{:S(2)}) copy-start(bf16[1,1024,768]{2,1,0:T(8,128)(2,1)} %param.29) | copy-start | bytes 4718596
  7.2 287.7 %all-gather.3.cloned.1.call-start = ((), (), s32[]{:S(2)}) async-start(), calls=%async_computation | async-start | bytes 2457600 | tf_op jit(solution)/shard_map/all_gather | solution.py:887
  8.7 7.6 %collective-permute-start = (bf16[384,576]{1,0:T(8,128)(2,1)S(1)}, bf16[384,576]{1,0:T(8,128)(2,1)S(1)}, u32[]{:S(2)}, u32[]{:S(2)}) collective-permute-start(bf16[384,576]{1,0:T(8,128)(2,1)S(1)} %copy.33.w_own), channel_id=1, source_target_pairs={{0,16},{16,0},{1,17},{17,1},{2,18},{18,2},{3,19},{19,3},{4,20},{20... | collective-permute-start | bytes 1327112 | tf_op jit(solution)/shard_map/ppermute | solution.py:659
  11.2 37.2 %collective-permute-start.1 = (bf16[976,384]{1,0:T(8,128)(2,1)S(1)}, bf16[976,384]{1,0:T(8,128)(2,1)}, u32[]{:S(2)}, u32[]{:S(2)}) collective-permute-start(bf16[976,384]{1,0:T(8,128)(2,1)S(1)} %pad_maximum_fusion.4), channel_id=1, source_target_pairs={{0,2},{1,3},{2,0},{3,1},{4,6},{5,7},{6,4},{7,5},{8,10},{9,11},{10,... | collective-permute-start | bytes 2248712 | tf_op jit(solution)/shard_map/ppermute | solution.py:672
  23.5 11.4 %collective-permute-start.4 = (bf16[192,1024]{1,0:T(8,128)(2,1)}, bf16[192,1024]{1,0:T(8,128)(2,1)S(1)}, u32[]{:S(2)}, u32[]{:S(2)}) collective-permute-start(bf16[192,1024]{1,0:T(8,128)(2,1)} %get-tuple-element.85.refs_0_.refs_4_), channel_id=1, source_target_pairs={{0,4},{4,0},{8,12},{12,8},{1,5},{5,1},{9,13},{13,9},{2,6},{6,2},{1... | collective-permute-start | bytes 1179656 | tf_op jit(solution)/shard_map/ppermute | solution.py:660
  25.0 11.9 %collective-permute-start.5 = (bf16[192,1024]{1,0:T(8,128)(2,1)}, bf16[192,1024]{1,0:T(8,128)(2,1)S(1)}, u32[]{:S(2)}, u32[]{:S(2)}) collective-permute-start(bf16[192,1024]{1,0:T(8,128)(2,1)} %get-tuple-element.86.refs_3_.refs_7_), channel_id=1, source_target_pairs={{0,8},{8,0},{4,12},{12,4},{1,9},{9,1},{5,13},{13,5},{2,10},{10,2},... | collective-permute-start | bytes 1179656 | tf_op jit(solution)/shard_map/ppermute | solution.py:661
  48.5 31.2 %collective-permute-start.6 = (bf16[2,192,1024]{2,1,0:T(8,128)(2,1)}, bf16[2,192,1024]{2,1,0:T(8,128)(2,1)}, u32[]{:S(2)}, u32[]{:S(2)}) collective-permute-start(bf16[2,192,1024]{2,1,0:T(8,128)(2,1)} %pad_maximum_fusion.2), channel_id=1, source_target_pairs={{0,8},{8,0},{4,12},{12,4},{1,9},{9,1},{5,13},{13,5},{2,10},{10,2},... | collective-permute-start | bytes 2359304 | tf_op jit(solution)/shard_map/ppermute | solution.py:661
  50.0 30.9 %collective-permute-start.7 = (bf16[2,192,1024]{2,1,0:T(8,128)(2,1)S(1)}, bf16[2,192,1024]{2,1,0:T(8,128)(2,1)}, u32[]{:S(2)}, u32[]{:S(2)}) collective-permute-start(bf16[2,192,1024]{2,1,0:T(8,128)(2,1)S(1)} %pad_maximum_fusion.3), channel_id=1, source_target_pairs={{0,4},{4,0},{8,12},{12,8},{1,5},{5,1},{9,13},{13,9},{2,6},{6,2},{1... | collective-permute-start | bytes 2359304 | tf_op jit(solution)/shard_map/ppermute | solution.py:660
  51.5 18.1 %collective-permute-start.2 = (bf16[976,384]{1,0:T(8,128)(2,1)S(1)}, bf16[976,384]{1,0:T(8,128)(2,1)}, u32[]{:S(2)}, u32[]{:S(2)}) collective-permute-start(bf16[976,384]{1,0:T(8,128)(2,1)S(1)} %pad_maximum_fusion.4), channel_id=1, source_target_pairs={{0,1},{1,2},{2,3},{4,5},{5,6},{6,7},{8,9},{9,10},{10,11},{12,13},{... | collective-permute-start | bytes 2248712 | tf_op jit(solution)/shard_map/ppermute | solution.py:672
  54.9 21.7 %collective-permute-start.3 = (bf16[976,384]{1,0:T(8,128)(2,1)S(1)}, bf16[976,384]{1,0:T(8,128)(2,1)}, u32[]{:S(2)}, u32[]{:S(2)}) collective-permute-start(bf16[976,384]{1,0:T(8,128)(2,1)S(1)} %pad_maximum_fusion.4), channel_id=1, source_target_pairs={{3,2},{2,1},{1,0},{7,6},{6,5},{5,4},{11,10},{10,9},{9,8},{15,14},{... | collective-permute-start | bytes 2248712 | tf_op jit(solution)/shard_map/ppermute | solution.py:672
  62.2 28.4 %collective-permute-start.10 = (bf16[768,384]{1,0:T(8,128)(2,1)}, bf16[768,384]{1,0:T(8,128)(2,1)S(1)}, u32[]{:S(2)}, u32[]{:S(2)}) collective-permute-start(bf16[768,384]{1,0:T(8,128)(2,1)} %param.20), channel_id=1, source_target_pairs={{3,2},{2,1},{1,0},{7,6},{6,5},{5,4},{11,10},{10,9},{9,8},{15,14},{... | collective-permute-start | bytes 1769480 | tf_op jit(solution)/shard_map/ppermute | solution.py:672
  69.7 43.9 %collective-permute-start.8 = (bf16[768,384]{1,0:T(8,128)(2,1)}, bf16[768,384]{1,0:T(8,128)(2,1)S(1)}, u32[]{:S(2)}, u32[]{:S(2)}) collective-permute-start(bf16[768,384]{1,0:T(8,128)(2,1)} %param.20), channel_id=1, source_target_pairs={{0,2},{1,3},{2,0},{3,1},{4,6},{5,7},{6,4},{7,5},{8,10},{9,11},{10,... | collective-permute-start | bytes 1769480 | tf_op jit(solution)/shard_map/ppermute | solution.py:672
  76.6 37.0 %collective-permute-start.9 = (bf16[768,384]{1,0:T(8,128)(2,1)}, bf16[768,384]{1,0:T(8,128)(2,1)S(1)}, u32[]{:S(2)}, u32[]{:S(2)}) collective-permute-start(bf16[768,384]{1,0:T(8,128)(2,1)} %param.20), channel_id=1, source_target_pairs={{0,1},{1,2},{2,3},{4,5},{5,6},{6,7},{8,9},{9,10},{10,11},{12,13},{... | collective-permute-start | bytes 1769480 | tf_op jit(solution)/shard_map/ppermute | solution.py:672
  79.7 36.3 %collective-permute-start.14 = (bf16[976,384]{1,0:T(8,128)(2,1)}, bf16[976,384]{1,0:T(8,128)(2,1)S(1)}, u32[]{:S(2)}, u32[]{:S(2)}) collective-permute-start(bf16[976,384]{1,0:T(8,128)(2,1)} %collective-permute-done.1), channel_id=1, source_target_pairs={{2,3},{1,0},{6,7},{5,4},{10,11},{9,8},{14,15},{13,12},{18,19},{17,... | collective-permute-start | bytes 2248712 | tf_op jit(solution)/shard_map/ppermute | solution.py:685
  113.6 15.6 %collective-permute-start.16 = (bf16[768,384]{1,0:T(8,128)(2,1)S(1)}, bf16[768,384]{1,0:T(8,128)(2,1)S(1)}, u32[]{:S(2)}, u32[]{:S(2)}) collective-permute-start(bf16[768,384]{1,0:T(8,128)(2,1)S(1)} %collective-permute-done.8), channel_id=1, source_target_pairs={{2,3},{1,0},{6,7},{5,4},{10,11},{9,8},{14,15},{13,12},{18,19},{17,... | collective-permute-start | bytes 1769480 | tf_op jit(solution)/shard_map/ppermute | solution.py:685
  120.1 25.3 %collective-permute-start.15 = (bf16[4,976,384]{2,1,0:T(8,128)(2,1)}, bf16[4,976,384]{2,1,0:T(8,128)(2,1)}, u32[]{:S(2)}, u32[]{:S(2)}) collective-permute-start(bf16[4,976,384]{2,1,0:T(8,128)(2,1)} %pad_maximum_fusion.refs_6_), channel_id=1, source_target_pairs={{0,16},{16,0},{1,17},{17,1},{2,18},{18,2},{3,19},{19,3},{4,20},{20... | collective-permute-start | bytes 8994824 | tf_op jit(solution)/shard_map/ppermute | solution.py:659
  131.1 14.3 %collective-permute-start.17 = (bf16[4,768,384]{2,1,0:T(8,128)(2,1)}, bf16[4,768,384]{2,1,0:T(8,128)(2,1)}, u32[]{:S(2)}, u32[]{:S(2)}) collective-permute-start(bf16[4,768,384]{2,1,0:T(8,128)(2,1)} %pad_maximum_fusion.1.refs_8_), channel_id=1, source_target_pairs={{0,16},{16,0},{1,17},{17,1},{2,18},{18,2},{3,19},{19,3},{4,20},{20... | collective-permute-start | bytes 7077896 | tf_op jit(solution)/shard_map/ppermute | solution.py:659
  132.9 8.5 %collective-permute-start.11 = (bf16[192,256]{1,0:T(8,128)(2,1)S(1)}, bf16[192,256]{1,0:T(8,128)(2,1)S(1)}, u32[]{:S(2)}, u32[]{:S(2)}) collective-permute-start(bf16[192,256]{1,0:T(8,128)(2,1)S(1)} %copy-done.51), channel_id=1, source_target_pairs={{0,1},{1,2},{2,3},{3,0},{4,5},{5,6},{6,7},{7,4},{8,9},{9,10},{10,1... | collective-permute-start | bytes 294920 | tf_op jit(solution)/shard_map/ppermute | solution.py:662
  132.9 12.5 %collective-permute-start.12 = (bf16[192,256]{1,0:T(8,128)(2,1)S(1)}, bf16[192,256]{1,0:T(8,128)(2,1)S(1)}, u32[]{:S(2)}, u32[]{:S(2)}) collective-permute-start(bf16[192,256]{1,0:T(8,128)(2,1)S(1)} %copy-done.48), channel_id=1, source_target_pairs={{0,2},{1,3},{2,0},{3,1},{4,6},{5,7},{6,4},{7,5},{8,10},{9,11},{10,... | collective-permute-start | bytes 294920 | tf_op jit(solution)/shard_map/ppermute | solution.py:662
  138.2 7.2 %collective-permute-start.13 = (bf16[192,256]{1,0:T(8,128)(2,1)S(1)}, bf16[192,256]{1,0:T(8,128)(2,1)S(1)}, u32[]{:S(2)}, u32[]{:S(2)}) collective-permute-start(bf16[192,256]{1,0:T(8,128)(2,1)S(1)} %copy-done.46), channel_id=1, source_target_pairs={{0,3},{1,0},{2,1},{3,2},{4,7},{5,4},{6,5},{7,6},{8,11},{9,8},{10,9... | collective-permute-start | bytes 294920 | tf_op jit(solution)/shard_map/ppermute | solution.py:662
  139.5 44.0 %copy-start.6 = (bf16[384,3,192]{0,2,1:T(8,128)(2,1)S(1)}, bf16[384,3,192]{0,2,1:T(8,128)(2,1)}, u32[]{:S(2)}) copy-start(bf16[384,3,192]{0,2,1:T(8,128)(2,1)} %param.17) | copy-start | bytes 1327108
  168.9 33.9 %collective-permute-start.22 = (bf16[4,384,1792]{2,1,0:T(8,128)(2,1)}, bf16[4,384,1792]{2,1,0:T(8,128)(2,1)}, u32[]{:S(2)}, u32[]{:S(2)}) collective-permute-start(bf16[4,384,1792]{2,1,0:T(8,128)(2,1)} %get-tuple-element.114), channel_id=1, source_target_pairs={{0,16},{16,0},{1,17},{17,1},{2,18},{18,2},{3,19},{19,3},{4,20},{20... | collective-permute-start | bytes 16515080 | tf_op jit(solution)/shard_map/ppermute | solution.py:659
  169.0 6.2 %collective-permute-start.18 = (bf16[192,256]{1,0:T(8,128)(2,1)}, bf16[192,256]{1,0:T(8,128)(2,1)S(1)}, u32[]{:S(2)}, u32[]{:S(2)}) collective-permute-start(bf16[192,256]{1,0:T(8,128)(2,1)} %get-tuple-element.109), channel_id=1, source_target_pairs={{0,3},{1,0},{2,1},{3,2},{4,7},{5,4},{6,5},{7,6},{8,11},{9,8},{10,9... | collective-permute-start | bytes 294920 | tf_op jit(solution)/shard_map/ppermute | solution.py:662
  171.7 10.9 %collective-permute-start.19 = (bf16[192,256]{1,0:T(8,128)(2,1)}, bf16[192,256]{1,0:T(8,128)(2,1)S(1)}, u32[]{:S(2)}, u32[]{:S(2)}) collective-permute-start(bf16[192,256]{1,0:T(8,128)(2,1)} %get-tuple-element.110), channel_id=1, source_target_pairs={{0,2},{1,3},{2,0},{3,1},{4,6},{5,7},{6,4},{7,5},{8,10},{9,11},{10,... | collective-permute-start | bytes 294920 | tf_op jit(solution)/shard_map/ppermute | solution.py:662
  173.1 9.6 %collective-permute-start.20 = (bf16[192,256]{1,0:T(8,128)(2,1)}, bf16[192,256]{1,0:T(8,128)(2,1)S(1)}, u32[]{:S(2)}, u32[]{:S(2)}) collective-permute-start(bf16[192,256]{1,0:T(8,128)(2,1)} %get-tuple-element.111), channel_id=1, source_target_pairs={{0,1},{1,2},{2,3},{3,0},{4,5},{5,6},{6,7},{7,4},{8,9},{9,10},{10,1... | collective-permute-start | bytes 294920 | tf_op jit(solution)/shard_map/ppermute | solution.py:662
  175.2 36.2 %copy-start.47 = (bf16[192,256]{1,0:T(8,128)(2,1)}, bf16[192,256]{1,0:T(8,128)(2,1)S(1)}, u32[]{:S(2)}) copy-start(bf16[192,256]{1,0:T(8,128)(2,1)S(1)} %collective-permute-done.18.refs_1_) | copy-start | bytes 294916
  182.7 28.7 %copy-start.49 = (bf16[192,256]{1,0:T(8,128)(2,1)}, bf16[192,256]{1,0:T(8,128)(2,1)S(1)}, u32[]{:S(2)}) copy-start(bf16[192,256]{1,0:T(8,128)(2,1)S(1)} %collective-permute-done.19.refs_2_) | copy-start | bytes 294916
  182.7 28.8 %copy-start.52 = (bf16[192,256]{1,0:T(8,128)(2,1)}, bf16[192,256]{1,0:T(8,128)(2,1)S(1)}, u32[]{:S(2)}) copy-start(bf16[192,256]{1,0:T(8,128)(2,1)S(1)} %collective-permute-done.20.refs_3_) | copy-start | bytes 294916
  182.7 18.6 %collective-permute-start.21 = (bf16[256,768]{1,0:T(8,128)(2,1)}, bf16[256,768]{1,0:T(8,128)(2,1)}, u32[]{:S(2)}, u32[]{:S(2)}) collective-permute-start(bf16[256,768]{1,0:T(8,128)(2,1)} %get-tuple-element.141), channel_id=1, source_target_pairs={{0,2},{1,3},{2,0},{3,1},{4,6},{5,7},{6,4},{7,5},{8,10},{9,11},{10,... | collective-permute-start | bytes 1179656 | tf_op jit(solution)/shard_map/ppermute | solution.py:672
  184.3 41.0 %collective-permute-start.25 = (bf16[256,768]{1,0:T(8,128)(2,1)}, bf16[256,768]{1,0:T(8,128)(2,1)}, u32[]{:S(2)}, u32[]{:S(2)}) collective-permute-start(bf16[256,768]{1,0:T(8,128)(2,1)} %get-tuple-element.141), channel_id=1, source_target_pairs={{0,1},{1,2},{2,3},{4,5},{5,6},{6,7},{8,9},{9,10},{10,11},{12,13},{... | collective-permute-start | bytes 1179656 | tf_op jit(solution)/shard_map/ppermute | solution.py:672
  187.2 38.1 %collective-permute-start.31 = (bf16[256,768]{1,0:T(8,128)(2,1)}, bf16[256,768]{1,0:T(8,128)(2,1)S(1)}, u32[]{:S(2)}, u32[]{:S(2)}) collective-permute-start(bf16[256,768]{1,0:T(8,128)(2,1)} %get-tuple-element.141), channel_id=1, source_target_pairs={{3,2},{2,1},{1,0},{7,6},{6,5},{5,4},{11,10},{10,9},{9,8},{15,14},{... | collective-permute-start | bytes 1179656 | tf_op jit(solution)/shard_map/ppermute | solution.py:672
  201.3 24.8 %collective-permute-start.30 = (bf16[256,768]{1,0:T(8,128)(2,1)}, bf16[256,768]{1,0:T(8,128)(2,1)}, u32[]{:S(2)}, u32[]{:S(2)}) collective-permute-start(bf16[256,768]{1,0:T(8,128)(2,1)} %collective-permute-done.21), channel_id=1, source_target_pairs={{2,3},{1,0},{6,7},{5,4},{10,11},{9,8},{14,15},{13,12},{18,19},{17,... | collective-permute-start | bytes 1179656 | tf_op jit(solution)/shard_map/ppermute | solution.py:685
  211.4 34.5 %collective-permute-start.23 = (bf16[2,4,96,896]{3,2,1,0:T(8,128)(2,1)}, bf16[2,4,96,896]{3,2,1,0:T(8,128)(2,1)S(1)}, u32[]{:S(2)}, u32[]{:S(2)}) collective-permute-start(bf16[2,4,96,896]{3,2,1,0:T(8,128)(2,1)} %get-tuple-element.115), channel_id=1, source_target_pairs={{0,4},{4,0},{8,12},{12,8},{1,5},{5,1},{9,13},{13,9},{2,6},{6,2},{1... | collective-permute-start | bytes 4128776 | tf_op jit(solution)/shard_map/ppermute | solution.py:660
  212.0 31.9 %collective-permute-start.24 = (bf16[2,4,96,896]{3,2,1,0:T(8,128)(2,1)}, bf16[2,4,96,896]{3,2,1,0:T(8,128)(2,1)S(1)}, u32[]{:S(2)}, u32[]{:S(2)}) collective-permute-start(bf16[2,4,96,896]{3,2,1,0:T(8,128)(2,1)} %get-tuple-element.123), channel_id=1, source_target_pairs={{0,8},{8,0},{4,12},{12,4},{1,9},{9,1},{5,13},{13,5},{2,10},{10,2},... | collective-permute-start | bytes 4128776 | tf_op jit(solution)/shard_map/ppermute | solution.py:661
  244.3 18.4 %collective-permute-start.48 = (bf16[4,96,896]{2,1,0:T(8,128)(2,1)S(1)}, bf16[4,96,896]{2,1,0:T(8,128)(2,1)S(1)}, u32[]{:S(2)}, u32[]{:S(2)}) collective-permute-start(bf16[4,96,896]{2,1,0:T(8,128)(2,1)S(1)} %fusion.15), channel_id=1, source_target_pairs={{0,4},{4,0},{8,12},{12,8},{1,5},{5,1},{9,13},{13,9},{2,6},{6,2},{1... | collective-permute-start | bytes 2064392 | tf_op jit(solution)/shard_map/ppermute | solution.py:660
  246.3 18.4 %collective-permute-start.47 = (bf16[4,96,896]{2,1,0:T(8,128)(2,1)S(1)}, bf16[4,96,896]{2,1,0:T(8,128)(2,1)S(1)}, u32[]{:S(2)}, u32[]{:S(2)}) collective-permute-start(bf16[4,96,896]{2,1,0:T(8,128)(2,1)S(1)} %fusion.14), channel_id=1, source_target_pairs={{0,8},{8,0},{4,12},{12,4},{1,9},{9,1},{5,13},{13,5},{2,10},{10,2},... | collective-permute-start | bytes 2064392 | tf_op jit(solution)/shard_map/ppermute | solution.py:661
  247.3 31.7 %collective-permute-start.28 = (bf16[2,192,1024]{2,1,0:T(8,128)(2,1)S(1)}, bf16[2,192,1024]{2,1,0:T(8,128)(2,1)S(1)}, u32[]{:S(2)}, u32[]{:S(2)}) collective-permute-start(bf16[2,192,1024]{2,1,0:T(8,128)(2,1)S(1)} %copy-done.41), channel_id=1, source_target_pairs={{0,8},{8,0},{4,12},{12,4},{1,9},{9,1},{5,13},{13,5},{2,10},{10,2},... | collective-permute-start | bytes 2359304 | tf_op jit(solution)/shard_map/ppermute | solution.py:661
  248.4 33.1 %collective-permute-start.26 = (bf16[2,192,1024]{2,1,0:T(8,128)(2,1)S(1)}, bf16[2,192,1024]{2,1,0:T(8,128)(2,1)S(1)}, u32[]{:S(2)}, u32[]{:S(2)}) collective-permute-start(bf16[2,192,1024]{2,1,0:T(8,128)(2,1)S(1)} %copy-done.40), channel_id=1, source_target_pairs={{0,4},{4,0},{8,12},{12,8},{1,5},{5,1},{9,13},{13,9},{2,6},{6,2},{1... | collective-permute-start | bytes 2359304 | tf_op jit(solution)/shard_map/ppermute | solution.py:660
  249.4 84.9 %collective-permute-start.32 = (bf16[192,256]{1,0:T(8,128)(2,1)}, bf16[192,256]{1,0:T(8,128)(2,1)}, u32[]{:S(2)}, u32[]{:S(2)}) collective-permute-start(bf16[192,256]{1,0:T(8,128)(2,1)} %get-tuple-element.133), channel_id=1, source_target_pairs={{0,1},{1,2},{2,3},{3,0},{4,5},{5,6},{6,7},{7,4},{8,9},{9,10},{10,1... | collective-permute-start | bytes 294920 | tf_op jit(solution)/shard_map/ppermute | solution.py:662
  266.1 32.9 %collective-permute-start.51 = (bf16[96,1792]{1,0:T(8,128)(2,1)}, bf16[96,1792]{1,0:T(8,128)(2,1)}, u32[]{:S(2)}, u32[]{:S(2)}) collective-permute-start(bf16[96,1792]{1,0:T(8,128)(2,1)} %get-tuple-element.196), channel_id=1, source_target_pairs={{0,1},{3,2},{4,5},{7,6},{8,9},{11,10},{12,13},{15,14},{16,17},{19,... | collective-permute-start | bytes 1032200 | tf_op jit(solution)/shard_map/ppermute | solution.py:699
  271.7 39.4 %collective-permute-start.49 = (bf16[96,1792]{1,0:T(8,128)(2,1)}, bf16[96,1792]{1,0:T(8,128)(2,1)}, u32[]{:S(2)}, u32[]{:S(2)}) collective-permute-start(bf16[96,1792]{1,0:T(8,128)(2,1)} %get-tuple-element.195), channel_id=1, source_target_pairs={{0,1},{1,2},{2,3},{4,5},{5,6},{6,7},{8,9},{9,10},{10,11},{12,13},{... | collective-permute-start | bytes 1032200 | tf_op jit(solution)/shard_map/ppermute | solution.py:699
  280.2 20.0 %collective-permute-start.29 = (bf16[192,1024]{1,0:T(8,128)(2,1)}, bf16[192,1024]{1,0:T(8,128)(2,1)}, u32[]{:S(2)}, u32[]{:S(2)}) collective-permute-start(bf16[192,1024]{1,0:T(8,128)(2,1)} %fusion.27), channel_id=1, source_target_pairs={{0,4},{4,0},{8,12},{12,8},{1,5},{5,1},{9,13},{13,9},{2,6},{6,2},{1... | collective-permute-start | bytes 1179656 | tf_op jit(solution)/shard_map/ppermute | solution.py:660
  283.7 19.2 %collective-permute-start.27 = (bf16[192,1024]{1,0:T(8,128)(2,1)}, bf16[192,1024]{1,0:T(8,128)(2,1)}, u32[]{:S(2)}, u32[]{:S(2)}) collective-permute-start(bf16[192,1024]{1,0:T(8,128)(2,1)} %fusion.26), channel_id=1, source_target_pairs={{0,8},{8,0},{4,12},{12,4},{1,9},{9,1},{5,13},{13,5},{2,10},{10,2},... | collective-permute-start | bytes 1179656 | tf_op jit(solution)/shard_map/ppermute | solution.py:661
  298.9 49.9 %collective-permute-start.38 = (bf16[4,384,640]{2,1,0:T(8,128)(2,1)}, bf16[4,384,640]{2,1,0:T(8,128)(2,1)}, u32[]{:S(2)}, u32[]{:S(2)}) collective-permute-start(bf16[4,384,640]{2,1,0:T(8,128)(2,1)} %bitcast.126), channel_id=1, source_target_pairs={{0,16},{16,0},{1,17},{17,1},{2,18},{18,2},{3,19},{19,3},{4,20},{20... | collective-permute-start | bytes 5898248 | tf_op jit(solution)/shard_map/ppermute | solution.py:659
  300.3 13.5 %collective-permute-start.50 = (bf16[96,1792]{1,0:T(8,128)(2,1)S(1)}, bf16[96,1792]{1,0:T(8,128)(2,1)S(1)}, u32[]{:S(2)}, u32[]{:S(2)}) collective-permute-start(bf16[96,1792]{1,0:T(8,128)(2,1)S(1)} %copy-done.25), channel_id=1, source_target_pairs={{3,2},{2,1},{1,0},{7,6},{6,5},{5,4},{11,10},{10,9},{9,8},{15,14},{... | collective-permute-start | bytes 1032200 | tf_op jit(solution)/shard_map/ppermute | solution.py:699
  302.9 29.4 %collective-permute-start.52 = (bf16[96,1792]{1,0:T(8,128)(2,1)S(1)}, bf16[96,1792]{1,0:T(8,128)(2,1)S(1)}, u32[]{:S(2)}, u32[]{:S(2)}) collective-permute-start(bf16[96,1792]{1,0:T(8,128)(2,1)S(1)} %fusion.25), channel_id=1, source_target_pairs={{0,2},{1,3},{2,0},{3,1},{4,6},{5,7},{6,4},{7,5},{8,10},{9,11},{10,... | collective-permute-start | bytes 1032200 | tf_op jit(solution)/shard_map/ppermute | solution.py:699
  311.1 23.2 %collective-permute-start.34 = (bf16[192,256]{1,0:T(8,128)(2,1)S(1)}, bf16[192,256]{1,0:T(8,128)(2,1)S(1)}, u32[]{:S(2)}, u32[]{:S(2)}) collective-permute-start(bf16[192,256]{1,0:T(8,128)(2,1)S(1)} %copy-done.30), channel_id=1, source_target_pairs={{0,2},{1,3},{2,0},{3,1},{4,6},{5,7},{6,4},{7,5},{8,10},{9,11},{10,... | collective-permute-start | bytes 294920 | tf_op jit(solution)/shard_map/ppermute | solution.py:662
  313.7 25.2 %collective-permute-start.36 = (bf16[192,256]{1,0:T(8,128)(2,1)}, bf16[192,256]{1,0:T(8,128)(2,1)}, u32[]{:S(2)}, u32[]{:S(2)}) collective-permute-start(bf16[192,256]{1,0:T(8,128)(2,1)} %get-tuple-element.135), channel_id=1, source_target_pairs={{0,3},{1,0},{2,1},{3,2},{4,7},{5,4},{6,5},{7,6},{8,11},{9,8},{10,9... | collective-permute-start | bytes 294920 | tf_op jit(solution)/shard_map/ppermute | solution.py:662
  332.3 10.1 %collective-permute-start.33 = (bf16[384,256]{1,0:T(8,128)(2,1)}, bf16[384,256]{1,0:T(8,128)(2,1)}, u32[]{:S(2)}, u32[]{:S(2)}) collective-permute-start(bf16[384,256]{1,0:T(8,128)(2,1)} %get-tuple-element.202), channel_id=1, source_target_pairs={{0,1},{1,2},{2,3},{3,0},{4,5},{5,6},{6,7},{7,4},{8,9},{9,10},{10,1... | collective-permute-start | bytes 589832 | tf_op jit(solution)/shard_map/ppermute | solution.py:662
  334.3 14.6 %collective-permute-start.35 = (bf16[384,256]{1,0:T(8,128)(2,1)S(1)}, bf16[384,256]{1,0:T(8,128)(2,1)S(1)}, u32[]{:S(2)}, u32[]{:S(2)}) collective-permute-start(bf16[384,256]{1,0:T(8,128)(2,1)S(1)} %get-tuple-element.203), channel_id=1, source_target_pairs={{0,2},{1,3},{2,0},{3,1},{4,6},{5,7},{6,4},{7,5},{8,10},{9,11},{10,... | collective-permute-start | bytes 589832 | tf_op jit(solution)/shard_map/ppermute | solution.py:662
  334.3 14.5 %collective-permute-start.37 = (bf16[384,256]{1,0:T(8,128)(2,1)S(1)}, bf16[384,256]{1,0:T(8,128)(2,1)S(1)}, u32[]{:S(2)}, u32[]{:S(2)}) collective-permute-start(bf16[384,256]{1,0:T(8,128)(2,1)S(1)} %get-tuple-element.200), channel_id=1, source_target_pairs={{0,3},{1,0},{2,1},{3,2},{4,7},{5,4},{6,5},{7,6},{8,11},{9,8},{10,9... | collective-permute-start | bytes 589832 | tf_op jit(solution)/shard_map/ppermute | solution.py:662
  355.6 41.8 %collective-permute-start.39 = (bf16[256,768]{1,0:T(8,128)(2,1)}, bf16[256,768]{1,0:T(8,128)(2,1)S(1)}, u32[]{:S(2)}, u32[]{:S(2)}) collective-permute-start(bf16[256,768]{1,0:T(8,128)(2,1)} %get-tuple-element.140), channel_id=1, source_target_pairs={{0,1},{1,2},{2,3},{3,0},{4,5},{5,6},{6,7},{7,4},{8,9},{9,10},{10,1... | collective-permute-start | bytes 1179656 | tf_op jit(solution)/shard_map/ppermute | solution.py:662
  360.3 38.1 %collective-permute-start.40 = (bf16[256,768]{1,0:T(8,128)(2,1)}, bf16[256,768]{1,0:T(8,128)(2,1)S(1)}, u32[]{:S(2)}, u32[]{:S(2)}) collective-permute-start(bf16[256,768]{1,0:T(8,128)(2,1)} %get-tuple-element.140), channel_id=1, source_target_pairs={{0,2},{1,3},{2,0},{3,1},{4,6},{5,7},{6,4},{7,5},{8,10},{9,11},{10,... | collective-permute-start | bytes 1179656 | tf_op jit(solution)/shard_map/ppermute | solution.py:662
  360.3 46.2 %collective-permute-start.41 = (bf16[256,768]{1,0:T(8,128)(2,1)}, bf16[256,768]{1,0:T(8,128)(2,1)S(1)}, u32[]{:S(2)}, u32[]{:S(2)}) collective-permute-start(bf16[256,768]{1,0:T(8,128)(2,1)} %get-tuple-element.140), channel_id=1, source_target_pairs={{0,3},{1,0},{2,1},{3,2},{4,7},{5,4},{6,5},{7,6},{8,11},{9,8},{10,9... | collective-permute-start | bytes 1179656 | tf_op jit(solution)/shard_map/ppermute | solution.py:662
  362.7 5.7 %collective-permute-start.53 = (f32[16,768]{1,0:T(8,128)}, f32[16,768]{1,0:T(8,128)S(1)}, u32[]{:S(2)}, u32[]{:S(2)}) collective-permute-start(f32[16,768]{1,0:T(8,128)} %get-tuple-element.151), channel_id=1, source_target_pairs={{0,16},{16,0},{1,17},{17,1},{2,18},{18,2},{3,19},{19,3},{4,20},{20... | collective-permute-start | bytes 147464 | tf_op jit(solution)/shard_map/ppermute | solution.py:659
  365.0 34.2 %collective-permute-start.42 = (bf16[1,384,640]{2,1,0:T(8,128)(2,1)S(1)}, bf16[1,384,640]{2,1,0:T(8,128)(2,1)S(1)}, u32[]{:S(2)}, u32[]{:S(2)}) collective-permute-start(bf16[1,384,640]{2,1,0:T(8,128)(2,1)S(1)} %get-tuple-element.198), channel_id=1, source_target_pairs={{0,16},{16,0},{1,17},{17,1},{2,18},{18,2},{3,19},{19,3},{4,20},{20... | collective-permute-start | bytes 1474568 | tf_op jit(solution)/shard_map/ppermute | solution.py:659
  368.4 4.7 %collective-permute-start.54 = (f32[16,768]{1,0:T(8,128)S(1)}, f32[16,768]{1,0:T(8,128)S(1)}, u32[]{:S(2)}, u32[]{:S(2)}) collective-permute-start(f32[16,768]{1,0:T(8,128)S(1)} %add.331), channel_id=1, source_target_pairs={{0,4},{4,0},{8,12},{12,8},{1,5},{5,1},{9,13},{13,9},{2,6},{6,2},{1... | collective-permute-start | bytes 147464 | tf_op jit(solution)/shard_map/ppermute | solution.py:660
  373.1 4.2 collective-permute-start.55
  377.2 9.8 %collective-permute-start.56 = (f32[16,768]{1,0:T(8,128)S(1)}, f32[16,768]{1,0:T(8,128)S(1)}, u32[]{:S(2)}, u32[]{:S(2)}) collective-permute-start(f32[16,768]{1,0:T(8,128)S(1)} %add.333), channel_id=1, source_target_pairs={{0,1},{1,0},{2,3},{3,2},{4,5},{5,4},{6,7},{7,6},{8,9},{9,8},{10,11... | collective-permute-start | bytes 147464 | tf_op jit(solution)/shard_map/ppermute | solution.py:908
  387.0 9.0 %collective-permute-start.57 = (f32[16,768]{1,0:T(8,128)S(1)}, f32[16,768]{1,0:T(8,128)S(1)}, u32[]{:S(2)}, u32[]{:S(2)}) collective-permute-start(f32[16,768]{1,0:T(8,128)S(1)} %add.334), channel_id=1, source_target_pairs={{0,2},{2,0},{1,3},{3,1},{4,6},{6,4},{5,7},{7,5},{8,10},{10,8},{9,1... | collective-permute-start | bytes 147464 | tf_op jit(solution)/shard_map/ppermute | solution.py:909
  404.1 5.5 %collective-permute-start.45 = (bf16[2,1,96,256]{3,2,1,0:T(8,128)(2,1)}, bf16[2,1,96,256]{3,2,1,0:T(8,128)(2,1)S(1)}, u32[]{:S(2)}, u32[]{:S(2)}) collective-permute-start(bf16[2,1,96,256]{3,2,1,0:T(8,128)(2,1)} %get-tuple-element.150), channel_id=1, source_target_pairs={{0,8},{8,0},{4,12},{12,4},{1,9},{9,1},{5,13},{13,5},{2,10},{10,2},... | collective-permute-start | bytes 294920 | tf_op jit(solution)/shard_map/ppermute | solution.py:661
  407.4 6.0 %collective-permute-start.43 = (bf16[2,1,96,384]{3,2,1,0:T(8,128)(2,1)}, bf16[2,1,96,384]{3,2,1,0:T(8,128)(2,1)S(1)}, u32[]{:S(2)}, u32[]{:S(2)}) collective-permute-start(bf16[2,1,96,384]{3,2,1,0:T(8,128)(2,1)} %get-tuple-element.148), channel_id=1, source_target_pairs={{0,4},{4,0},{8,12},{12,8},{1,5},{5,1},{9,13},{13,9},{2,6},{6,2},{1... | collective-permute-start | bytes 442376 | tf_op jit(solution)/shard_map/ppermute | solution.py:660
  410.6 4.2 collective-permute-start.46
  413.4 4.4 %collective-permute-start.44 = (bf16[1,96,384]{2,1,0:T(8,128)(2,1)S(1)}, bf16[1,96,384]{2,1,0:T(8,128)(2,1)S(1)}, u32[]{:S(2)}, u32[]{:S(2)}) collective-permute-start(bf16[1,96,384]{2,1,0:T(8,128)(2,1)S(1)} %fusion.39), channel_id=1, source_target_pairs={{0,8},{8,0},{4,12},{12,4},{1,9},{9,1},{5,13},{13,5},{2,10},{10,2},... | collective-permute-start | bytes 221192 | tf_op jit(solution)/shard_map/ppermute | solution.py:661
  (52 other events, 297.6 us)
Sparse Core Ops, SparseCore 0:
  225.3 69.6 all-gather.2

commit v5 on v4

--- a/solution.py
+++ b/solution.py
@@ -244,12 +244,12 @@
 
 def attend_back_kernel(first_head, heads, bk, bq, parts, n_kv, sc, qt, st, lse, ot, *refs):
     do_parts, refs = refs[:parts], refs[parts:]
-    kv, refs = refs[:n_kv], refs[n_kv:]
+    kv, refs = refs[:n_kv], refs[n_kv + 1 :]
     n_out = 1 if n_kv == 1 else 4
     dq, dkv, (held, acc, dqa, do_all, sems) = (
         refs[:parts],
         refs[parts : parts + n_out],
-        refs[parts + n_out :],
+        refs[parts + n_out + 1 :],
     )
     i = pl.program_id(0)
     per = held.shape[2] // bk
@@ -316,7 +316,7 @@
                     dkv[target][n] = acc[sc[1] ^ pair[n], rows, :].astype(bf16)
 
 
-def attend_back(scalars, starts, qt, lse, ot, do_parts, kv, first_head, heads, bk, bq):
+def attend_back(scalars, starts, qt, lse, ot, do_parts, kv, carried, first_head, heads, bk, bq):
     tok = qt.shape[1]
     cols = heads * HD
     parts = len(do_parts)
@@ -335,8 +335,8 @@
             pl.BlockSpec((cols, bq), lambda i: (0, i)),
         ]
         + [whole(*d.shape) for d in do_parts]
-        + [HBM] * len(kv),
-        out_specs=[whole(cols, tok // parts)] * parts + [whole(*d) for d in out_kv],
+        + [HBM] * (len(kv) + 1),
+        out_specs=[whole(cols, tok // parts)] * parts + [whole(*d) for d in out_kv] + [HBM],
         scratch_shapes=[
             pltpu.VMEM((runs, 2 * cols, tok), bf16),
             pltpu.VMEM((runs, 2 * cols, tok), f32),
@@ -344,11 +344,14 @@
             pltpu.VMEM((cols, tok), bf16),
             pltpu.SemaphoreType.DMA((8,)),
         ],
-        out_shape=[shape((cols, tok // parts))] * parts + [shape(d) for d in out_kv],
+        out_shape=[shape((cols, tok // parts))] * parts
+        + [shape(d) for d in out_kv]
+        + [shape(carried.shape)],
+        input_output_aliases={5 + parts + len(kv): parts + len(out_kv)},
         compiler_params=params(),
         cost_estimate=cost(26),
         name="attend_back",
-    )(scalars(bk, bq), qt, starts, lse, ot, *do_parts, *kv)
+    )(scalars(bk, bq), qt, starts, lse, ot, *do_parts, *kv, carried)
 
 
 ROOT = 0.7978845608028654
@@ -780,7 +783,7 @@
         if grouped:
             kx, vy = along_x(k), along_y(v)
             k_two, v_two = jnp.stack([k, kx]), jnp.stack([v, vy])
-            k_two, v_two = after((k_two, v_two), packed[1])
+            k_two, v_two = after((k_two, v_two), packed[1:])
             k_yd, v_xd = along_y(k_two), along_x(v_two)
             hold = (k_two, v_two)
             kv.append([k, kx, k_yd, v, vy, v_xd])
@@ -830,7 +833,14 @@
 
     folded = scatter_begin(g_own, g_other)
     hop_one = folded[0] if grouped else folded
-    outputs = gather_begin(after(outputs_sub, do_parts))
+    carried = jnp.pad(qkv_own, ((0, 0), (0, -3 * cols % 128)))
+    folded = scatter_begin(g_own, g_other)
+    hop_one = folded[0] if grouped else folded
+    qkv_wide = jnp.pad(qkv_own, ((0, 0), (0, width - 3 * cols)))
+    outputs_and_qkv = lax.all_gather(
+        jnp.concatenate([outputs_sub, qkv_wide], axis=0), "tensor", axis=0
+    )
+    outputs = gather_direct(after(outputs_sub, do_parts))
     wide = scatter_first(folded)
     wide_sends = wide[2:]
     wide = scatter_second(wide)
@@ -841,18 +851,18 @@
     sent = [[] for _ in range(n_tensor)]
     for g, held, (lse, ot) in zip(GROUPS, kv, saved):
         out = attend_back(
-            scalars, row(starts), after(qt, hop_one), lse, ot, do_parts, held, head, g, BK_B, BQ_B
+            scalars, row(starts), after(qt, hop_one), lse, ot, do_parts, held, carried, head, g, BK_B, BQ_B
         )
         back_done = out[-1]
-        dq, dkv = after(out[:n_tensor], (outputs[1:3], wide_sends)), out[n_tensor:]
+        *out, carried = out
+        dq, dkv = after(out[:n_tensor], (wide_sends, outputs[1:])), out[n_tensor:]
         if grouped:
             dk_keep, dk_send, dv_keep, dv_send = dkv
-            dk_send, dv_send = after((dk_send, dv_send), (wide_sends, outputs[1:3]))
+            dk_send, dv_send = after((dk_send, dv_send), (wide_sends, outputs[1:]))
             r = along_x(dk_send).astype(f32)
             s = along_y(dv_send).astype(f32)
             r2 = along_y((dk_keep[1].astype(f32) + r[1]).astype(bf16)).astype(f32)
             s2 = along_x((dv_keep[1].astype(f32) + s[1]).astype(bf16)).astype(f32)
-            back_done = (r2, s2)
             dk = (dk_keep[0].astype(f32) + r[0] + r2).astype(bf16)
             dv = (dv_keep[0].astype(f32) + s[0] + s2).astype(bf16)
         else:
@@ -872,9 +882,9 @@
     grads = []
     both = jnp.concatenate(keys + values, axis=0)
     for d in range(n_tensor):
-        pieces = [q[d] for q in queries] + [part_of(both, d)]
-        grads += pieces if d == 0 else [shift_by(p, d) for p in pieces]
-    pieces = len(GROUPS) + 1
+        piece = jnp.concatenate([q[d] for q in queries] + [part_of(both, d)], axis=0)
+        grads.append(shift_by(piece, d) if d else piece)
+    pieces = 1
 
     dq_whole = []
     for q in queries:
@@ -883,23 +893,24 @@
             at = lax.rem(tensor + d, n_tensor) * sub
             whole = lax.dynamic_update_slice_in_dim(whole, q[d], at, 1)
         dq_whole.append(whole)
-    qkv_wide = jnp.pad(qkv_own, ((0, 0), (0, -3 * cols % 128)))
-    qkv = lax.all_gather(after(qkv_wide, out[-1]), "tensor", axis=0)
+    qkv = lax.all_gather(carried, "tensor", axis=0)
     qkv = (qkv, swap(qkv))
-    input_sub, small = last(
-        place, grads, pieces, qkv, x_sub, grad_mid, table, mid_sums, fc_sums
-    )
-    input_gradient = spread(gather_direct(input_sub))
-    outputs = spread(after(gather_end(outputs, back_done), input_sub))
     stacked = jnp.concatenate(
         dq_whole + [both, jnp.zeros((-3 * cols % 128, tok), bf16)], axis=0
     )
     qkv_grad = jnp.einsum(
-        "td,ct->dc", low_one, after(stacked, input_sub), preferred_element_type=f32
+        "td,ct->dc", low_one, stacked, preferred_element_type=f32
     ).astype(bf16)
     qkv_mine = lax.dynamic_slice_in_dim(qkv_grad, core * half, half, 0)
     qkv_theirs = lax.dynamic_slice_in_dim(qkv_grad, (1 - core) * half, half, 0)
-    qkv_grads = scatter_second(scatter_first(scatter_begin(qkv_mine[None], qkv_theirs[None])))[0]
+    qkv_folded = scatter_begin(qkv_mine[None], qkv_theirs[None])
+
+    input_sub, small = last(
+        place, grads, pieces, qkv, x_sub, after(grad_mid, qkv_folded), table, mid_sums, fc_sums
+    )
+    input_gradient = spread(gather_direct(input_sub))
+    outputs = spread(outputs)
+    qkv_grads = scatter_second(scatter_first(qkv_folded))[0]
 
     if grouped and n_tensor == 4 and n_shard == 2:
         small += swap(small)

time: 427 us -> 420 us (0.984)
  starting transfers between devices: 91.6 us -> 104 us
  local copies, waits for them, and re-layouts: 28 us -> 17.8 us
  other arithmetic: 37.5 us -> 28.2 us
    ppermute x1, waiting for transfers between devices: 5.12 us -> 31.8 us  [body(): small += lax.ppermute(small, 'tensor', [(0, 2), (2, 0), (1, 3), (3, 1)])]
    ppermute x9 -> x6, waiting for transfers between devices: 56.8 us -> 34.7 us  [gather_begin(): move = lambda perm: lax.ppermute(v, 'tensor', perm)]
    ppermute x15, starting transfers between devices: 24.6 us -> 40.6 us  [body(): lax.ppermute(v, 'tensor', [(s, (s + d) % n_tensor) for s in range(n_tenso...]
    all_gather x1, waiting for transfers between devices: 10.8 us -> 0.01 us  [body(): qkv = lax.all_gather(carried, 'tensor', axis=0)]
    ppermute x15, waiting for transfers between devices: 25.5 us -> 36.2 us  [body(): lax.ppermute(v, 'tensor', [(s, (s + d) % n_tensor) for s in range(n_tenso...]
    ppermute x9, waiting for transfers between devices: 17.8 us -> 28.1 us  [body(): lax.ppermute(v, 'context', [(0, 1), (1, 0), (2, 3), (3, 2)])]
    ppermute x4, waiting for transfers between devices: 20.3 us -> 11.3 us  [scatter_line(): move = lambda a, perm: lax.ppermute(a.astype(bf16), 'tensor', perm)]
    ppermute x1, waiting for transfers between devices: 7.77 us -> 0.01 us  [body(): small += lax.ppermute(small, 'tensor', [(0, 1), (1, 0), (2, 3), (3, 2)])]
  transfers between devices with their start and end apart: 59 -> 55, of which waited for: 29 -> 23; matrix products, arithmetic and copies ran while one was open for 14% -> 10% of each run, Pallas kernels for 10% -> 9%
where the time goes in v5:
time: 420 us; the launch traced here: 419 us
  waiting for transfers between devices  183 us (44%)
  starting transfers between devices  104 us (25%)
  Pallas kernels  70.1 us (17%)
  other arithmetic  28.2 us (7%)
  local copies, waits for them, and re-layouts  17.8 us (4%)
  between operations  15.1 us (4%)
    ppermute x15, starting transfers between devices, body(): lax.ppermute(v, 'tensor', [(s, (s + d) % n_tensor) for s in range(n_tenso...  40.6 us
    ppermute x15, waiting for transfers between devices, body(): lax.ppermute(v, 'tensor', [(s, (s + d) % n_tensor) for s in range(n_tenso...  36.2 us
    ppermute x6, waiting for transfers between devices, gather_begin(): move = lambda perm: lax.ppermute(v, 'tensor', perm)  34.7 us
    ppermute x1, waiting for transfers between devices, body(): small += lax.ppermute(small, 'tensor', [(0, 2), (2, 0), (1, 3), (3, 1)])  31.8 us
    ppermute x6, starting transfers between devices, gather_begin(): move = lambda perm: lax.ppermute(v, 'tensor', perm)  28.1 us
    ppermute x9, waiting for transfers between devices, body(): lax.ppermute(v, 'context', [(0, 1), (1, 0), (2, 3), (3, 2)])  28.1 us
    ppermute x9, waiting for transfers between devices, body(): lax.ppermute(v, 'context', [(0, 2), (2, 0), (1, 3), (3, 1)])  28 us
    pallas_call x1, Pallas kernels, middle(): pl.pallas_call(functools.partial(middle_kernel, len(att), parts), grid_sp...  22.9 us
  transfers between devices with their start and end apart: 55, of which 23 were waited for; matrix products, arithmetic and copies ran while one was open for 10% of the time, Pallas kernels for 9%

profile of v5, /device:TPU:0, one launch (start us, length us, event | category | flops | bytes accessed | tf_op | source)
XLA Modules:
  0.0 419.4 jit_solution(17931629692296614014)
XLA Ops:
  10.4 4.1 collective-permute-start.1
  14.5 4.3 %collective-permute-start.2 = (bf16[976,384]{1,0:T(8,128)(2,1)S(1)}, bf16[976,384]{1,0:T(8,128)(2,1)}, u32[]{:S(2)}, u32[]{:S(2)}) collective-permute-start(bf16[976,384]{1,0:T(8,128)(2,1)S(1)} %pad_maximum_fusion.4), channel_id=1, source_target_pairs={{0,1},{1,2},{2,3},{4,5},{5,6},{6,7},{8,9},{9,10},{10,11},{12,13},{... | collective-permute-start | bytes 2248712 | tf_op jit(solution)/shard_map/ppermute | solution.py:675
  18.8 1.3 collective-permute-start.3
  22.5 6.4 %project.1 = (bf16[1024,768]{1,0:T(8,128)(2,1)}, bf16[192,1024]{1,0:T(8,128)(2,1)}, bf16[192,1024]{1,0:T(8,128)(2,1)}, bf16[192,1024]{1,0:T(8,128)(2,1)}) custom-call(s32[4]{0:T(128)} %pad_add_fusion.1.sc, bf16[1024,768]{1,0:T(8,128)(2,1)} %bitcast.134, bf16[384,576]{1,0:T(8,128)(2,1)} %copy-done.3, bf16[384,576]{1,0:T(8,128)(2,1)} %collective-permute-done.w_other, ...), custom_call_target="tpu_custom_call" | custom-call | flops 8049999872 | bytes 1048576 | tf_op jit(solution)/shard_map/project/pallas_call | solution.py:90
  28.8 1.6 collective-permute-start.4
  30.4 1.5 collective-permute-start.5
  31.9 8.4 %collective-permute-done.4.refs_1_.refs_5_ = bf16[192,1024]{1,0:T(8,128)(2,1)S(1)} collective-permute-done((bf16[192,1024]{1,0:T(8,128)(2,1)}, bf16[192,1024]{1,0:T(8,128)(2,1)S(1)}, u32[]{:S(2)}, u32[]{:S(2)}) %collective-permute-start.4) | collective-permute-done | bytes 393248 | tf_op jit(solution)/shard_map/ppermute | solution.py:663
  40.2 2.1 pad_maximum_fusion.2
  42.5 5.8 %collective-permute-done.1 = bf16[976,384]{1,0:T(8,128)(2,1)} collective-permute-done((bf16[976,384]{1,0:T(8,128)(2,1)S(1)}, bf16[976,384]{1,0:T(8,128)(2,1)}, u32[]{:S(2)}, u32[]{:S(2)}) %collective-permute-start.1) | collective-permute-done | bytes 749600 | tf_op jit(solution)/shard_map/ppermute | solution.py:675
  48.3 5.4 %collective-permute-done.3 = bf16[976,384]{1,0:T(8,128)(2,1)} collective-permute-done((bf16[976,384]{1,0:T(8,128)(2,1)S(1)}, bf16[976,384]{1,0:T(8,128)(2,1)}, u32[]{:S(2)}, u32[]{:S(2)}) %collective-permute-start.3) | collective-permute-done | bytes 749600 | tf_op jit(solution)/shard_map/ppermute | solution.py:675
  53.6 1.6 collective-permute-start.6
  55.2 1.5 collective-permute-start.7
  57.9 3.8 fusion.61
  63.9 13.2 %collective-permute-start.8 = (bf16[768,384]{1,0:T(8,128)(2,1)}, bf16[768,384]{1,0:T(8,128)(2,1)S(1)}, u32[]{:S(2)}, u32[]{:S(2)}) collective-permute-start(bf16[768,384]{1,0:T(8,128)(2,1)} %param.20), channel_id=1, source_target_pairs={{0,2},{1,3},{2,0},{3,1},{4,6},{5,7},{6,4},{7,5},{8,10},{9,11},{10,... | collective-permute-start | bytes 1769480 | tf_op jit(solution)/shard_map/ppermute | solution.py:675
  77.1 4.0 collective-permute-start.9
  81.1 1.3 collective-permute-start.14
  82.4 9.6 %attend.1 = (f32[3,1024]{1,0:T(4,128)}, bf16[192,1024]{1,0:T(8,128)(2,1)}, bf16[192,256]{1,0:T(8,128)(2,1)}, bf16[192,256]{1,0:T(8,128)(2,1)}, bf16[192,256]{1,0:T(8,128)(2,1)}, /*index=5*/bf16[192,256]{1,0:T(8,128)(2,1)}) custom-call(s32[12]{0:T(128)} %concatenate.43.sc, bf16[192,1024]{1,0:T(8,128)(2,1)} %get-tuple-element.111.qt, ...), custom_call_target="tpu_custom_call" | custom-call | flops 23000000512 | bytes 1048576 | tf_op jit(solution)/shard_map/attend/pallas_call | solution.py:221
  92.0 23.6 %collective-permute-done.8 = bf16[768,384]{1,0:T(8,128)(2,1)S(1)} collective-permute-done((bf16[768,384]{1,0:T(8,128)(2,1)}, bf16[768,384]{1,0:T(8,128)(2,1)S(1)}, u32[]{:S(2)}, u32[]{:S(2)}) %collective-permute-start.8) | collective-permute-done | bytes 589856 | tf_op jit(solution)/shard_map/ppermute | solution.py:675
  115.5 1.3 collective-permute-start.16
  118.1 2.8 pad_maximum_fusion.refs_6_
  121.0 10.5 %collective-permute-done.16 = bf16[768,384]{1,0:T(8,128)(2,1)S(1)} collective-permute-done((bf16[768,384]{1,0:T(8,128)(2,1)S(1)}, bf16[768,384]{1,0:T(8,128)(2,1)S(1)}, u32[]{:S(2)}, u32[]{:S(2)}) %collective-permute-start.16) | collective-permute-done | bytes 589856 | tf_op jit(solution)/shard_map/ppermute | solution.py:688
  131.6 1.8 pad_maximum_fusion.1.refs_8_
  133.4 1.8 dynamic-slice_bitcast_fusion.3.refs_4_.refs_6_
  135.2 5.5 %collective-permute-start.12 = (bf16[192,256]{1,0:T(8,128)(2,1)S(1)}, bf16[192,256]{1,0:T(8,128)(2,1)S(1)}, u32[]{:S(2)}, u32[]{:S(2)}) collective-permute-start(bf16[192,256]{1,0:T(8,128)(2,1)S(1)} %copy-done.41), channel_id=1, source_target_pairs={{0,2},{1,3},{2,0},{3,1},{4,6},{5,7},{6,4},{7,5},{8,10},{9,11},{10,... | collective-permute-start | bytes 294920 | tf_op jit(solution)/shard_map/ppermute | solution.py:665
  141.9 1.9 collective-permute-done.11.refs_1_
  143.8 4.0 collective-permute-done.12.refs_2_
  148.5 22.9 %middle.1 = (bf16[256,768]{1,0:T(8,128)(2,1)}, f32[256,768]{1,0:T(8,128)}, f32[4,768]{1,0:T(4,128)}, f32[4,1,768]{2,1,0:T(1,128)}, bf16[192,256]{1,0:T(8,128)(2,...) custom-call(s32[4]{0:T(128)} %pad_add_fusion.1.sc, ...), custom_call_target="tpu_custom_call" | custom-call | flops 21849999360 | bytes 1048576 | tf_op jit(solution)/shard_map/middle/pallas_call | solution.py:465
  171.4 2.7 collective-permute-start.18
  174.2 1.4 collective-permute-start.19
  175.6 2.1 collective-permute-done.18.refs_1_
  177.7 7.4 %collective-permute-done.19.refs_2_ = bf16[192,256]{1,0:T(8,128)(2,1)S(1)} collective-permute-done((bf16[192,256]{1,0:T(8,128)(2,1)}, bf16[192,256]{1,0:T(8,128)(2,1)S(1)}, u32[]{:S(2)}, u32[]{:S(2)}) %collective-permute-start.19) | collective-permute-done | bytes 98336 | tf_op jit(solution)/shard_map/ppermute | solution.py:665
  187.1 3.1 collective-permute-start.23
  190.2 1.9 broadcast_in_dim.68.clone
  193.0 6.3 %collective-permute-done.21 = bf16[256,768]{1,0:T(8,128)(2,1)S(1)} collective-permute-done((bf16[256,768]{1,0:T(8,128)(2,1)}, bf16[256,768]{1,0:T(8,128)(2,1)S(1)}, u32[]{:S(2)}, u32[]{:S(2)}) %collective-permute-start.21) | collective-permute-done | bytes 393248 | tf_op jit(solution)/shard_map/ppermute | solution.py:665
  200.3 14.4 %collective-permute-done.22 = bf16[256,768]{1,0:T(8,128)(2,1)S(1)} collective-permute-done((bf16[256,768]{1,0:T(8,128)(2,1)}, bf16[256,768]{1,0:T(8,128)(2,1)S(1)}, u32[]{:S(2)}, u32[]{:S(2)}) %collective-permute-start.22) | collective-permute-done | bytes 393248 | tf_op jit(solution)/shard_map/ppermute | solution.py:665
  216.6 8.7 %fold.2 = (bf16[2,4,96,896]{3,2,1,0:T(8,128)(2,1)}, bf16[2,4,96,896]{3,2,1,0:T(8,128)(2,1)}, bf16[2,4,96,896]{3,2,1,0:T(8,128)(2,1)}, bf16[2,4,96,896]{3,2,1,0:T(8,128)(2,1)}) custom-call(s32[4]{0:T(128)} %pad_add_fusion.1.sc, bf16[4,384,1792]{2,1,0:T(8,128)(2,1)} %get-tuple-element.108.mine, bf16[4,384,1792]{2,1,0:T(8,128)(2,1)} %collective-permute-done.24.theirs), custom_call_target="tpu_custom_call" | custom-call | flops 8049999872 | bytes 1048576 | tf_op jit(solution)/shard_map/fold/pallas_call | solution.py:587
  226.3 12.6 %attend_back.1 = (bf16[192,256]{1,0:T(8,128)(2,1)}, bf16[192,256]{1,0:T(8,128)(2,1)}, bf16[192,256]{1,0:T(8,128)(2,1)}, bf16[192,256]{1,0:T(8,128)(2,1)}, bf16[2...) custom-call(s32[12]{0:T(128)} %concatenate.43.sc, ...), custom_call_target="tpu_custom_call", output_to_operand_aliasing={{8}: (15, {})} | custom-call | flops 29899999232 | bytes 1048576 | tf_op jit(solution)/shard_map/attend_back/pallas_call | solution.py:327
  239.0 18.8 %collective-permute-done.26 = bf16[2,4,96,896]{3,2,1,0:T(8,128)(2,1)S(1)} collective-permute-done((bf16[2,4,96,896]{3,2,1,0:T(8,128)(2,1)}, bf16[2,4,96,896]{3,2,1,0:T(8,128)(2,1)S(1)}, u32[]{:S(2)}, u32[]{:S(2)}) %collective-permute-start.26) | collective-permute-done | bytes 1376288 | tf_op jit(solution)/shard_map/ppermute | solution.py:664
  258.1 1.5 collective-permute-start.44
  263.4 13.2 %collective-permute-done.44 = bf16[4,96,896]{2,1,0:T(8,128)(2,1)S(1)} collective-permute-done((bf16[4,96,896]{2,1,0:T(8,128)(2,1)S(1)}, bf16[4,96,896]{2,1,0:T(8,128)(2,1)S(1)}, u32[]{:S(2)}, u32[]{:S(2)}) %collective-permute-start.44) | collective-permute-done | bytes 688160 | tf_op jit(solution)/shard_map/ppermute | solution.py:663
  276.8 1.8 collective-permute-done.43
  279.7 10.1 %collective-permute-start.47 = (bf16[96,1792]{1,0:T(8,128)(2,1)S(1)}, bf16[96,1792]{1,0:T(8,128)(2,1)S(1)}, u32[]{:S(2)}, u32[]{:S(2)}) collective-permute-start(bf16[96,1792]{1,0:T(8,128)(2,1)S(1)} %get-tuple-element.186), channel_id=1, source_target_pairs={{0,1},{3,2},{4,5},{7,6},{8,9},{11,10},{12,13},{15,14},{16,17},{19,... | collective-permute-start | bytes 1032200 | tf_op jit(solution)/shard_map/ppermute | solution.py:702
  289.8 2.0 collective-permute-start.45
  291.8 1.5 collective-permute-start.46
  295.7 9.9 %collective-permute-done.47 = bf16[96,1792]{1,0:T(8,128)(2,1)S(1)} collective-permute-done((bf16[96,1792]{1,0:T(8,128)(2,1)S(1)}, bf16[96,1792]{1,0:T(8,128)(2,1)S(1)}, u32[]{:S(2)}, u32[]{:S(2)}) %collective-permute-start.47) | collective-permute-done | bytes 344096 | tf_op jit(solution)/shard_map/ppermute | solution.py:702
  306.4 1.6 collective-permute-start.48
  308.3 1.6 convolution_convert_fusion
  313.5 3.3 collective-permute-start.33
  316.8 1.9 collective-permute-start.32
  318.7 1.4 collective-permute-done.48
  320.1 14.5 %collective-permute-start.31 = (bf16[576,256]{1,0:T(8,128)(2,1)S(1)}, bf16[576,256]{1,0:T(8,128)(2,1)}, u32[]{:S(2)}, u32[]{:S(2)}) collective-permute-start(bf16[576,256]{1,0:T(8,128)(2,1)S(1)} %pad_maximum_fusion.7), channel_id=1, source_target_pairs={{0,1},{1,2},{2,3},{3,0},{4,5},{5,6},{6,7},{7,4},{8,9},{9,10},{10,1... | collective-permute-start | bytes 884744 | tf_op jit(solution)/shard_map/ppermute | solution.py:665
  334.6 1.3 fusion.27
  337.6 4.1 fold.3
  342.5 4.1 collective-permute-done.41
  347.6 4.3 %collective-permute-done.39 = bf16[2,1,96,384]{3,2,1,0:T(8,128)(2,1)S(1)} collective-permute-done((bf16[2,1,96,384]{3,2,1,0:T(8,128)(2,1)}, bf16[2,1,96,384]{3,2,1,0:T(8,128)(2,1)S(1)}, u32[]{:S(2)}, u32[]{:S(2)}) %collective-permute-start.39) | collective-permute-done | bytes 147488 | tf_op jit(solution)/shard_map/ppermute | solution.py:663
  352.2 5.8 %last.1 = (bf16[256,768]{1,0:T(8,128)(2,1)}, f32[16,768]{1,0:T(8,128)}) custom-call(s32[4]{0:T(128)} %pad_add_fusion.1.sc, bf16[576,256]{1,0:T(8,128)(2,1)} %pad_maximum_fusion.6.refs_0_, bf16[576,256]{1,0:T(8,128)(2,1)} %collective-permute-done.31.refs_1_, bf16[576,256]{1,0:T(8,128)(2,1)} %collective-permute-done.32.refs_2_, ...), custom_call_target="tpu_custom_call" | custom-call | flops 6899999744 | bytes 1048576 | tf_op jit(solution)/shard_map/last/pallas_call | solution.py:537
  358.2 1.3 collective-permute-done.49
  360.3 1.8 collective-permute-start.50
  362.1 2.3 collective-permute-done.50
  365.2 3.4 collective-permute-done.51
  369.7 2.0 collective-permute-start.36
  371.7 3.9 collective-permute-start.37
  377.5 31.8 %collective-permute-done.53 = f32[16,768]{1,0:T(8,128)S(1)} collective-permute-done((f32[16,768]{1,0:T(8,128)S(1)}, f32[16,768]{1,0:T(8,128)S(1)}, u32[]{:S(2)}, u32[]{:S(2)}) %collective-permute-start.53) | collective-permute-done | bytes 49184 | tf_op jit(solution)/shard_map/ppermute | solution.py:920
  410.9 1.7 copy-done.2
  (243 shorter events, 41.1 us)
Async XLA Ops:
  7.2 133.9 %copy-start = (bf16[1,1024,768]{2,1,0:T(8,128)(2,1)S(1)}, bf16[1,1024,768]{2,1,0:T(8,128)(2,1)}, u32[]{:S(2)}) copy-start(bf16[1,1024,768]{2,1,0:T(8,128)(2,1)} %param.29) | copy-start | bytes 4718596
  7.2 12.9 %copy-start.11 = (bf16[384,3,192]{0,2,1:T(8,128)(2,1)S(1)}, bf16[384,3,192]{0,2,1:T(8,128)(2,1)}, u32[]{:S(2)}) copy-start(bf16[384,3,192]{0,2,1:T(8,128)(2,1)} %param.17) | copy-start | bytes 1327108
  7.2 303.7 %all-gather.3.cloned.1.call-start = ((), (), s32[]{:S(2)}) async-start(), calls=%async_computation | async-start | bytes 2457600 | tf_op jit(solution)/shard_map/all_gather | solution.py:896
  8.2 12.4 %copy-start.33 = (f32[768]{0:T(1024)S(1)}, f32[768]{0:T(1024)}, u32[]{:S(2)}) copy-start(f32[768]{0:T(1024)} %param.28) | copy-start | bytes 9220
  10.4 37.9 %collective-permute-start.1 = (bf16[976,384]{1,0:T(8,128)(2,1)S(1)}, bf16[976,384]{1,0:T(8,128)(2,1)}, u32[]{:S(2)}, u32[]{:S(2)}) collective-permute-start(bf16[976,384]{1,0:T(8,128)(2,1)S(1)} %pad_maximum_fusion.4), channel_id=1, source_target_pairs={{0,2},{1,3},{2,0},{3,1},{4,6},{5,7},{6,4},{7,5},{8,10},{9,11},{10,... | collective-permute-start | bytes 2248712 | tf_op jit(solution)/shard_map/ppermute | solution.py:675
  14.5 33.8 %collective-permute-start.2 = (bf16[976,384]{1,0:T(8,128)(2,1)S(1)}, bf16[976,384]{1,0:T(8,128)(2,1)}, u32[]{:S(2)}, u32[]{:S(2)}) collective-permute-start(bf16[976,384]{1,0:T(8,128)(2,1)S(1)} %pad_maximum_fusion.4), channel_id=1, source_target_pairs={{0,1},{1,2},{2,3},{4,5},{5,6},{6,7},{8,9},{9,10},{10,11},{12,13},{... | collective-permute-start | bytes 2248712 | tf_op jit(solution)/shard_map/ppermute | solution.py:675
  18.8 34.8 %collective-permute-start.3 = (bf16[976,384]{1,0:T(8,128)(2,1)S(1)}, bf16[976,384]{1,0:T(8,128)(2,1)}, u32[]{:S(2)}, u32[]{:S(2)}) collective-permute-start(bf16[976,384]{1,0:T(8,128)(2,1)S(1)} %pad_maximum_fusion.4), channel_id=1, source_target_pairs={{3,2},{2,1},{1,0},{7,6},{6,5},{5,4},{11,10},{10,9},{9,8},{15,14},{... | collective-permute-start | bytes 2248712 | tf_op jit(solution)/shard_map/ppermute | solution.py:675
  20.4 2.1 collective-permute-start
  28.8 13.6 %copy-start.20 = (bf16[192,1024]{1,0:T(8,128)(2,1)S(1)}, bf16[192,1024]{1,0:T(8,128)(2,1)}, u32[]{:S(2)}) copy-start(bf16[192,1024]{1,0:T(8,128)(2,1)} %get-tuple-element.81.refs_3_.refs_7_) | copy-start | bytes 1179652
  28.8 11.4 %collective-permute-start.4 = (bf16[192,1024]{1,0:T(8,128)(2,1)}, bf16[192,1024]{1,0:T(8,128)(2,1)S(1)}, u32[]{:S(2)}, u32[]{:S(2)}) collective-permute-start(bf16[192,1024]{1,0:T(8,128)(2,1)} %get-tuple-element.80.refs_0_.refs_4_), channel_id=1, source_target_pairs={{0,4},{4,0},{8,12},{12,8},{1,5},{5,1},{9,13},{13,9},{2,6},{6,2},{1... | collective-permute-start | bytes 1179656 | tf_op jit(solution)/shard_map/ppermute | solution.py:663
  30.4 12.0 %collective-permute-start.5 = (bf16[192,1024]{1,0:T(8,128)(2,1)}, bf16[192,1024]{1,0:T(8,128)(2,1)S(1)}, u32[]{:S(2)}, u32[]{:S(2)}) collective-permute-start(bf16[192,1024]{1,0:T(8,128)(2,1)} %get-tuple-element.81.refs_3_.refs_7_), channel_id=1, source_target_pairs={{0,8},{8,0},{4,12},{12,4},{1,9},{9,1},{5,13},{13,5},{2,10},{10,2},... | collective-permute-start | bytes 1179656 | tf_op jit(solution)/shard_map/ppermute | solution.py:664
  40.2 16.5 %copy-start.27 = (s32[1,4096]{1,0:T(1,128)S(1)}, s32[1,4096]{1,0:T(1,128)}, u32[]{:S(2)}) copy-start(s32[1,4096]{1,0:T(1,128)} %param.16) | copy-start | bytes 49156
  53.6 27.4 %collective-permute-start.6 = (bf16[2,192,1024]{2,1,0:T(8,128)(2,1)}, bf16[2,192,1024]{2,1,0:T(8,128)(2,1)}, u32[]{:S(2)}, u32[]{:S(2)}) collective-permute-start(bf16[2,192,1024]{2,1,0:T(8,128)(2,1)} %pad_maximum_fusion.2), channel_id=1, source_target_pairs={{0,8},{8,0},{4,12},{12,4},{1,9},{9,1},{5,13},{13,5},{2,10},{10,2},... | collective-permute-start | bytes 2359304 | tf_op jit(solution)/shard_map/ppermute | solution.py:664
  55.2 27.2 %collective-permute-start.7 = (bf16[2,192,1024]{2,1,0:T(8,128)(2,1)S(1)}, bf16[2,192,1024]{2,1,0:T(8,128)(2,1)}, u32[]{:S(2)}, u32[]{:S(2)}) collective-permute-start(bf16[2,192,1024]{2,1,0:T(8,128)(2,1)S(1)} %pad_maximum_fusion.3), channel_id=1, source_target_pairs={{0,4},{4,0},{8,12},{12,8},{1,5},{5,1},{9,13},{13,9},{2,6},{6,2},{1... | collective-permute-start | bytes 2359304 | tf_op jit(solution)/shard_map/ppermute | solution.py:663
  62.7 29.3 %collective-permute-start.10 = (bf16[768,384]{1,0:T(8,128)(2,1)}, bf16[768,384]{1,0:T(8,128)(2,1)S(1)}, u32[]{:S(2)}, u32[]{:S(2)}) collective-permute-start(bf16[768,384]{1,0:T(8,128)(2,1)} %param.20), channel_id=1, source_target_pairs={{3,2},{2,1},{1,0},{7,6},{6,5},{5,4},{11,10},{10,9},{9,8},{15,14},{... | collective-permute-start | bytes 1769480 | tf_op jit(solution)/shard_map/ppermute | solution.py:675
  63.9 51.6 %collective-permute-start.8 = (bf16[768,384]{1,0:T(8,128)(2,1)}, bf16[768,384]{1,0:T(8,128)(2,1)S(1)}, u32[]{:S(2)}, u32[]{:S(2)}) collective-permute-start(bf16[768,384]{1,0:T(8,128)(2,1)} %param.20), channel_id=1, source_target_pairs={{0,2},{1,3},{2,0},{3,1},{4,6},{5,7},{6,4},{7,5},{8,10},{9,11},{10,... | collective-permute-start | bytes 1769480 | tf_op jit(solution)/shard_map/ppermute | solution.py:675
  77.1 38.5 %collective-permute-start.9 = (bf16[768,384]{1,0:T(8,128)(2,1)}, bf16[768,384]{1,0:T(8,128)(2,1)S(1)}, u32[]{:S(2)}, u32[]{:S(2)}) collective-permute-start(bf16[768,384]{1,0:T(8,128)(2,1)} %param.20), channel_id=1, source_target_pairs={{0,1},{1,2},{2,3},{4,5},{5,6},{6,7},{8,9},{9,10},{10,11},{12,13},{... | collective-permute-start | bytes 1769480 | tf_op jit(solution)/shard_map/ppermute | solution.py:675
  81.1 35.8 %collective-permute-start.14 = (bf16[976,384]{1,0:T(8,128)(2,1)}, bf16[976,384]{1,0:T(8,128)(2,1)S(1)}, u32[]{:S(2)}, u32[]{:S(2)}) collective-permute-start(bf16[976,384]{1,0:T(8,128)(2,1)} %collective-permute-done.1), channel_id=1, source_target_pairs={{2,3},{1,0},{6,7},{5,4},{10,11},{9,8},{14,15},{13,12},{18,19},{17,... | collective-permute-start | bytes 2248712 | tf_op jit(solution)/shard_map/ppermute | solution.py:688
  115.5 15.9 %collective-permute-start.16 = (bf16[768,384]{1,0:T(8,128)(2,1)S(1)}, bf16[768,384]{1,0:T(8,128)(2,1)S(1)}, u32[]{:S(2)}, u32[]{:S(2)}) collective-permute-start(bf16[768,384]{1,0:T(8,128)(2,1)S(1)} %collective-permute-done.8), channel_id=1, source_target_pairs={{2,3},{1,0},{6,7},{5,4},{10,11},{9,8},{14,15},{13,12},{18,19},{17,... | collective-permute-start | bytes 1769480 | tf_op jit(solution)/shard_map/ppermute | solution.py:688
  121.0 26.8 %collective-permute-start.15 = (bf16[4,976,384]{2,1,0:T(8,128)(2,1)}, bf16[4,976,384]{2,1,0:T(8,128)(2,1)}, u32[]{:S(2)}, u32[]{:S(2)}) collective-permute-start(bf16[4,976,384]{2,1,0:T(8,128)(2,1)} %pad_maximum_fusion.refs_6_), channel_id=1, source_target_pairs={{0,16},{16,0},{1,17},{17,1},{2,18},{18,2},{3,19},{19,3},{4,20},{20... | collective-permute-start | bytes 8994824 | tf_op jit(solution)/shard_map/ppermute | solution.py:662
  133.4 14.4 %collective-permute-start.17 = (bf16[4,768,384]{2,1,0:T(8,128)(2,1)}, bf16[4,768,384]{2,1,0:T(8,128)(2,1)}, u32[]{:S(2)}, u32[]{:S(2)}) collective-permute-start(bf16[4,768,384]{2,1,0:T(8,128)(2,1)} %pad_maximum_fusion.1.refs_8_), channel_id=1, source_target_pairs={{0,16},{16,0},{1,17},{17,1},{2,18},{18,2},{3,19},{19,3},{4,20},{20... | collective-permute-start | bytes 7077896 | tf_op jit(solution)/shard_map/ppermute | solution.py:662
  135.2 8.6 %collective-permute-start.11 = (bf16[192,256]{1,0:T(8,128)(2,1)S(1)}, bf16[192,256]{1,0:T(8,128)(2,1)S(1)}, u32[]{:S(2)}, u32[]{:S(2)}) collective-permute-start(bf16[192,256]{1,0:T(8,128)(2,1)S(1)} %copy-done.42), channel_id=1, source_target_pairs={{0,1},{1,2},{2,3},{3,0},{4,5},{5,6},{6,7},{7,4},{8,9},{9,10},{10,1... | collective-permute-start | bytes 294920 | tf_op jit(solution)/shard_map/ppermute | solution.py:665
  135.2 12.6 %collective-permute-start.12 = (bf16[192,256]{1,0:T(8,128)(2,1)S(1)}, bf16[192,256]{1,0:T(8,128)(2,1)S(1)}, u32[]{:S(2)}, u32[]{:S(2)}) collective-permute-start(bf16[192,256]{1,0:T(8,128)(2,1)S(1)} %copy-done.41), channel_id=1, source_target_pairs={{0,2},{1,3},{2,0},{3,1},{4,6},{5,7},{6,4},{7,5},{8,10},{9,11},{10,... | collective-permute-start | bytes 294920 | tf_op jit(solution)/shard_map/ppermute | solution.py:665
  140.6 7.2 %collective-permute-start.13 = (bf16[192,256]{1,0:T(8,128)(2,1)S(1)}, bf16[192,256]{1,0:T(8,128)(2,1)S(1)}, u32[]{:S(2)}, u32[]{:S(2)}) collective-permute-start(bf16[192,256]{1,0:T(8,128)(2,1)S(1)} %copy-done.40), channel_id=1, source_target_pairs={{0,3},{1,0},{2,1},{3,2},{4,7},{5,4},{6,5},{7,6},{8,11},{9,8},{10,9... | collective-permute-start | bytes 294920 | tf_op jit(solution)/shard_map/ppermute | solution.py:665
  141.9 43.3 %copy-start.4 = (bf16[384,576]{1,0:T(8,128)(2,1)S(1)}, bf16[384,576]{1,0:T(8,128)(2,1)}, u32[]{:S(2)}) copy-start(bf16[384,576]{1,0:T(8,128)(2,1)} %copy-done.3) | copy-start | bytes 1327108
  171.3 45.3 %collective-permute-start.24 = (bf16[4,384,1792]{2,1,0:T(8,128)(2,1)}, bf16[4,384,1792]{2,1,0:T(8,128)(2,1)}, u32[]{:S(2)}, u32[]{:S(2)}) collective-permute-start(bf16[4,384,1792]{2,1,0:T(8,128)(2,1)} %get-tuple-element.109), channel_id=1, source_target_pairs={{0,16},{16,0},{1,17},{17,1},{2,18},{18,2},{3,19},{19,3},{4,20},{20... | collective-permute-start | bytes 16515080 | tf_op jit(solution)/shard_map/ppermute | solution.py:662
  171.4 6.2 %collective-permute-start.18 = (bf16[192,256]{1,0:T(8,128)(2,1)}, bf16[192,256]{1,0:T(8,128)(2,1)S(1)}, u32[]{:S(2)}, u32[]{:S(2)}) collective-permute-start(bf16[192,256]{1,0:T(8,128)(2,1)} %get-tuple-element.104), channel_id=1, source_target_pairs={{0,3},{1,0},{2,1},{3,2},{4,7},{5,4},{6,5},{7,6},{8,11},{9,8},{10,9... | collective-permute-start | bytes 294920 | tf_op jit(solution)/shard_map/ppermute | solution.py:665
  174.2 10.9 %collective-permute-start.19 = (bf16[192,256]{1,0:T(8,128)(2,1)}, bf16[192,256]{1,0:T(8,128)(2,1)S(1)}, u32[]{:S(2)}, u32[]{:S(2)}) collective-permute-start(bf16[192,256]{1,0:T(8,128)(2,1)} %get-tuple-element.105), channel_id=1, source_target_pairs={{0,2},{1,3},{2,0},{3,1},{4,6},{5,7},{6,4},{7,5},{8,10},{9,11},{10,... | collective-permute-start | bytes 294920 | tf_op jit(solution)/shard_map/ppermute | solution.py:665
  175.6 9.6 %collective-permute-start.20 = (bf16[192,256]{1,0:T(8,128)(2,1)}, bf16[192,256]{1,0:T(8,128)(2,1)S(1)}, u32[]{:S(2)}, u32[]{:S(2)}) collective-permute-start(bf16[192,256]{1,0:T(8,128)(2,1)} %get-tuple-element.106), channel_id=1, source_target_pairs={{0,1},{1,2},{2,3},{3,0},{4,5},{5,6},{6,7},{7,4},{8,9},{9,10},{10,1... | collective-permute-start | bytes 294920 | tf_op jit(solution)/shard_map/ppermute | solution.py:665
  177.7 14.4 %copy-start.37 = (bf16[192,256]{1,0:T(8,128)(2,1)}, bf16[192,256]{1,0:T(8,128)(2,1)S(1)}, u32[]{:S(2)}) copy-start(bf16[192,256]{1,0:T(8,128)(2,1)S(1)} %collective-permute-done.18.refs_1_) | copy-start | bytes 294916
  185.1 14.2 %collective-permute-start.21 = (bf16[256,768]{1,0:T(8,128)(2,1)}, bf16[256,768]{1,0:T(8,128)(2,1)S(1)}, u32[]{:S(2)}, u32[]{:S(2)}) collective-permute-start(bf16[256,768]{1,0:T(8,128)(2,1)} %get-tuple-element.107), channel_id=1, source_target_pairs={{0,1},{1,2},{2,3},{3,0},{4,5},{5,6},{6,7},{7,4},{8,9},{9,10},{10,1... | collective-permute-start | bytes 1179656 | tf_op jit(solution)/shard_map/ppermute | solution.py:665
  186.1 28.6 %collective-permute-start.22 = (bf16[256,768]{1,0:T(8,128)(2,1)}, bf16[256,768]{1,0:T(8,128)(2,1)S(1)}, u32[]{:S(2)}, u32[]{:S(2)}) collective-permute-start(bf16[256,768]{1,0:T(8,128)(2,1)} %get-tuple-element.107), channel_id=1, source_target_pairs={{0,2},{1,3},{2,0},{3,1},{4,6},{5,7},{6,4},{7,5},{8,10},{9,11},{10,... | collective-permute-start | bytes 1179656 | tf_op jit(solution)/shard_map/ppermute | solution.py:665
  187.1 28.6 %collective-permute-start.23 = (bf16[256,768]{1,0:T(8,128)(2,1)}, bf16[256,768]{1,0:T(8,128)(2,1)S(1)}, u32[]{:S(2)}, u32[]{:S(2)}) collective-permute-start(bf16[256,768]{1,0:T(8,128)(2,1)} %get-tuple-element.107), channel_id=1, source_target_pairs={{0,3},{1,0},{2,1},{3,2},{4,7},{5,4},{6,5},{7,6},{8,11},{9,8},{10,9... | collective-permute-start | bytes 1179656 | tf_op jit(solution)/shard_map/ppermute | solution.py:665
  225.3 34.4 %collective-permute-start.25 = (bf16[2,4,96,896]{3,2,1,0:T(8,128)(2,1)}, bf16[2,4,96,896]{3,2,1,0:T(8,128)(2,1)S(1)}, u32[]{:S(2)}, u32[]{:S(2)}) collective-permute-start(bf16[2,4,96,896]{3,2,1,0:T(8,128)(2,1)} %get-tuple-element.110), channel_id=1, source_target_pairs={{0,4},{4,0},{8,12},{12,8},{1,5},{5,1},{9,13},{13,9},{2,6},{6,2},{1... | collective-permute-start | bytes 4128776 | tf_op jit(solution)/shard_map/ppermute | solution.py:663
  225.8 31.9 %collective-permute-start.26 = (bf16[2,4,96,896]{3,2,1,0:T(8,128)(2,1)}, bf16[2,4,96,896]{3,2,1,0:T(8,128)(2,1)S(1)}, u32[]{:S(2)}, u32[]{:S(2)}) collective-permute-start(bf16[2,4,96,896]{3,2,1,0:T(8,128)(2,1)} %get-tuple-element.119), channel_id=1, source_target_pairs={{0,8},{8,0},{4,12},{12,4},{1,9},{9,1},{5,13},{13,5},{2,10},{10,2},... | collective-permute-start | bytes 4128776 | tf_op jit(solution)/shard_map/ppermute | solution.py:664
  239.0 19.0 %copy-start.6 = (bf16[2,4,96,896]{3,2,1,0:T(8,128)(2,1)S(1)}, bf16[2,4,96,896]{3,2,1,0:T(8,128)(2,1)}, u32[]{:S(2)}) copy-start(bf16[2,4,96,896]{3,2,1,0:T(8,128)(2,1)} %get-tuple-element.118) | copy-start | bytes 4128772
  258.1 18.4 %collective-permute-start.44 = (bf16[4,96,896]{2,1,0:T(8,128)(2,1)S(1)}, bf16[4,96,896]{2,1,0:T(8,128)(2,1)S(1)}, u32[]{:S(2)}, u32[]{:S(2)}) collective-permute-start(bf16[4,96,896]{2,1,0:T(8,128)(2,1)S(1)} %fusion.21), channel_id=1, source_target_pairs={{0,4},{4,0},{8,12},{12,8},{1,5},{5,1},{9,13},{13,9},{2,6},{6,2},{1... | collective-permute-start | bytes 2064392 | tf_op jit(solution)/shard_map/ppermute | solution.py:663
  260.1 18.4 %collective-permute-start.43 = (bf16[4,96,896]{2,1,0:T(8,128)(2,1)S(1)}, bf16[4,96,896]{2,1,0:T(8,128)(2,1)S(1)}, u32[]{:S(2)}, u32[]{:S(2)}) collective-permute-start(bf16[4,96,896]{2,1,0:T(8,128)(2,1)S(1)} %fusion.20), channel_id=1, source_target_pairs={{0,8},{8,0},{4,12},{12,4},{1,9},{9,1},{5,13},{13,5},{2,10},{10,2},... | collective-permute-start | bytes 2064392 | tf_op jit(solution)/shard_map/ppermute | solution.py:664
  261.0 32.4 %collective-permute-start.29 = (bf16[2,192,1024]{2,1,0:T(8,128)(2,1)S(1)}, bf16[2,192,1024]{2,1,0:T(8,128)(2,1)S(1)}, u32[]{:S(2)}, u32[]{:S(2)}) collective-permute-start(bf16[2,192,1024]{2,1,0:T(8,128)(2,1)S(1)} %copy-done.35), channel_id=1, source_target_pairs={{0,8},{8,0},{4,12},{12,4},{1,9},{9,1},{5,13},{13,5},{2,10},{10,2},... | collective-permute-start | bytes 2359304 | tf_op jit(solution)/shard_map/ppermute | solution.py:664
  262.2 32.7 %collective-permute-start.27 = (bf16[2,192,1024]{2,1,0:T(8,128)(2,1)S(1)}, bf16[2,192,1024]{2,1,0:T(8,128)(2,1)S(1)}, u32[]{:S(2)}, u32[]{:S(2)}) collective-permute-start(bf16[2,192,1024]{2,1,0:T(8,128)(2,1)S(1)} %copy-done.34), channel_id=1, source_target_pairs={{0,4},{4,0},{8,12},{12,8},{1,5},{5,1},{9,13},{13,9},{2,6},{6,2},{1... | collective-permute-start | bytes 2359304 | tf_op jit(solution)/shard_map/ppermute | solution.py:663
  279.7 13.9 %copy-start.8 = (bf16[2,192,1024]{2,1,0:T(8,128)(2,1)S(1)}, bf16[2,192,1024]{2,1,0:T(8,128)(2,1)}, u32[]{:S(2)}) copy-start(bf16[2,192,1024]{2,1,0:T(8,128)(2,1)} %get-tuple-element.125) | copy-start | bytes 2359300
  279.7 25.8 %collective-permute-start.47 = (bf16[96,1792]{1,0:T(8,128)(2,1)S(1)}, bf16[96,1792]{1,0:T(8,128)(2,1)S(1)}, u32[]{:S(2)}, u32[]{:S(2)}) collective-permute-start(bf16[96,1792]{1,0:T(8,128)(2,1)S(1)} %get-tuple-element.186), channel_id=1, source_target_pairs={{0,1},{3,2},{4,5},{7,6},{8,9},{11,10},{12,13},{15,14},{16,17},{19,... | collective-permute-start | bytes 1032200 | tf_op jit(solution)/shard_map/ppermute | solution.py:702
  289.8 23.7 %collective-permute-start.45 = (bf16[96,1792]{1,0:T(8,128)(2,1)}, bf16[96,1792]{1,0:T(8,128)(2,1)}, u32[]{:S(2)}, u32[]{:S(2)}) collective-permute-start(bf16[96,1792]{1,0:T(8,128)(2,1)} %get-tuple-element.185), channel_id=1, source_target_pairs={{0,1},{1,2},{2,3},{4,5},{5,6},{6,7},{8,9},{9,10},{10,11},{12,13},{... | collective-permute-start | bytes 1032200 | tf_op jit(solution)/shard_map/ppermute | solution.py:702
  291.8 24.9 %collective-permute-start.46 = (bf16[96,1792]{1,0:T(8,128)(2,1)}, bf16[96,1792]{1,0:T(8,128)(2,1)}, u32[]{:S(2)}, u32[]{:S(2)}) collective-permute-start(bf16[96,1792]{1,0:T(8,128)(2,1)} %get-tuple-element.187), channel_id=1, source_target_pairs={{3,2},{2,1},{1,0},{7,6},{6,5},{5,4},{11,10},{10,9},{9,8},{15,14},{... | collective-permute-start | bytes 1032200 | tf_op jit(solution)/shard_map/ppermute | solution.py:702
  293.7 14.2 %collective-permute-start.30 = (bf16[192,1024]{1,0:T(8,128)(2,1)S(1)}, bf16[192,1024]{1,0:T(8,128)(2,1)S(1)}, u32[]{:S(2)}, u32[]{:S(2)}) collective-permute-start(bf16[192,1024]{1,0:T(8,128)(2,1)S(1)} %fusion.34), channel_id=1, source_target_pairs={{0,4},{4,0},{8,12},{12,8},{1,5},{5,1},{9,13},{13,9},{2,6},{6,2},{1... | collective-permute-start | bytes 1179656 | tf_op jit(solution)/shard_map/ppermute | solution.py:663
  295.2 12.9 %collective-permute-start.28 = (bf16[192,1024]{1,0:T(8,128)(2,1)S(1)}, bf16[192,1024]{1,0:T(8,128)(2,1)S(1)}, u32[]{:S(2)}, u32[]{:S(2)}) collective-permute-start(bf16[192,1024]{1,0:T(8,128)(2,1)S(1)} %fusion.33), channel_id=1, source_target_pairs={{0,8},{8,0},{4,12},{12,4},{1,9},{9,1},{5,13},{13,5},{2,10},{10,2},... | collective-permute-start | bytes 1179656 | tf_op jit(solution)/shard_map/ppermute | solution.py:664
  306.4 13.7 %collective-permute-start.48 = (bf16[96,1792]{1,0:T(8,128)(2,1)}, bf16[96,1792]{1,0:T(8,128)(2,1)}, u32[]{:S(2)}, u32[]{:S(2)}) collective-permute-start(bf16[96,1792]{1,0:T(8,128)(2,1)} %fusion.31), channel_id=1, source_target_pairs={{0,2},{1,3},{2,0},{3,1},{4,6},{5,7},{6,4},{7,5},{8,10},{9,11},{10,... | collective-permute-start | bytes 1032200 | tf_op jit(solution)/shard_map/ppermute | solution.py:702
  311.0 41.2 %collective-permute-start.34 = (bf16[4,384,640]{2,1,0:T(8,128)(2,1)}, bf16[4,384,640]{2,1,0:T(8,128)(2,1)}, u32[]{:S(2)}, u32[]{:S(2)}) collective-permute-start(bf16[4,384,640]{2,1,0:T(8,128)(2,1)} %bitcast.135), channel_id=1, source_target_pairs={{0,16},{16,0},{1,17},{17,1},{2,18},{18,2},{3,19},{19,3},{4,20},{20... | collective-permute-start | bytes 5898248 | tf_op jit(solution)/shard_map/ppermute | solution.py:662
  312.0 24.8 %collective-permute-start.35 = (bf16[1,384,640]{2,1,0:T(8,128)(2,1)S(1)}, bf16[1,384,640]{2,1,0:T(8,128)(2,1)S(1)}, u32[]{:S(2)}, u32[]{:S(2)}) collective-permute-start(bf16[1,384,640]{2,1,0:T(8,128)(2,1)S(1)} %copy-done.10), channel_id=1, source_target_pairs={{0,16},{16,0},{1,17},{17,1},{2,18},{18,2},{3,19},{19,3},{4,20},{20... | collective-permute-start | bytes 1474568 | tf_op jit(solution)/shard_map/ppermute | solution.py:662
  313.5 38.6 %collective-permute-start.33 = (bf16[576,256]{1,0:T(8,128)(2,1)}, bf16[576,256]{1,0:T(8,128)(2,1)}, u32[]{:S(2)}, u32[]{:S(2)}) collective-permute-start(bf16[576,256]{1,0:T(8,128)(2,1)} %pad_maximum_fusion.9), channel_id=1, source_target_pairs={{0,3},{1,0},{2,1},{3,2},{4,7},{5,4},{6,5},{7,6},{8,11},{9,8},{10,9... | collective-permute-start | bytes 884744 | tf_op jit(solution)/shard_map/ppermute | solution.py:665
  316.8 35.4 %collective-permute-start.32 = (bf16[576,256]{1,0:T(8,128)(2,1)S(1)}, bf16[576,256]{1,0:T(8,128)(2,1)}, u32[]{:S(2)}, u32[]{:S(2)}) collective-permute-start(bf16[576,256]{1,0:T(8,128)(2,1)S(1)} %pad_maximum_fusion.8), channel_id=1, source_target_pairs={{0,2},{1,3},{2,0},{3,1},{4,6},{5,7},{6,4},{7,5},{8,10},{9,11},{10,... | collective-permute-start | bytes 884744 | tf_op jit(solution)/shard_map/ppermute | solution.py:665
  320.1 32.1 %collective-permute-start.31 = (bf16[576,256]{1,0:T(8,128)(2,1)S(1)}, bf16[576,256]{1,0:T(8,128)(2,1)}, u32[]{:S(2)}, u32[]{:S(2)}) collective-permute-start(bf16[576,256]{1,0:T(8,128)(2,1)S(1)} %pad_maximum_fusion.7), channel_id=1, source_target_pairs={{0,1},{1,2},{2,3},{3,0},{4,5},{5,6},{6,7},{7,4},{8,9},{9,10},{10,1... | collective-permute-start | bytes 884744 | tf_op jit(solution)/shard_map/ppermute | solution.py:665
  341.7 4.9 %collective-permute-start.41 = (bf16[2,1,96,256]{3,2,1,0:T(8,128)(2,1)}, bf16[2,1,96,256]{3,2,1,0:T(8,128)(2,1)S(1)}, u32[]{:S(2)}, u32[]{:S(2)}) collective-permute-start(bf16[2,1,96,256]{3,2,1,0:T(8,128)(2,1)} %get-tuple-element.135), channel_id=1, source_target_pairs={{0,8},{8,0},{4,12},{12,4},{1,9},{9,1},{5,13},{13,5},{2,10},{10,2},... | collective-permute-start | bytes 294920 | tf_op jit(solution)/shard_map/ppermute | solution.py:664
  346.6 5.4 %collective-permute-start.39 = (bf16[2,1,96,384]{3,2,1,0:T(8,128)(2,1)}, bf16[2,1,96,384]{3,2,1,0:T(8,128)(2,1)S(1)}, u32[]{:S(2)}, u32[]{:S(2)}) collective-permute-start(bf16[2,1,96,384]{3,2,1,0:T(8,128)(2,1)} %get-tuple-element.133), channel_id=1, source_target_pairs={{0,4},{4,0},{8,12},{12,8},{1,5},{5,1},{9,13},{13,9},{2,6},{6,2},{1... | collective-permute-start | bytes 442376 | tf_op jit(solution)/shard_map/ppermute | solution.py:663
  351.9 10.2 %collective-permute-start.42 = (bf16[1,96,256]{2,1,0:T(8,128)(2,1)S(1)}, bf16[1,96,256]{2,1,0:T(8,128)(2,1)S(1)}, u32[]{:S(2)}, u32[]{:S(2)}) collective-permute-start(bf16[1,96,256]{2,1,0:T(8,128)(2,1)S(1)} %fusion.47), channel_id=1, source_target_pairs={{0,4},{4,0},{8,12},{12,8},{1,5},{5,1},{9,13},{13,9},{2,6},{6,2},{1... | collective-permute-start | bytes 147464 | tf_op jit(solution)/shard_map/ppermute | solution.py:663
  358.1 1.4 collective-permute-start.49
  358.1 7.1 %collective-permute-start.40 = (bf16[1,96,384]{2,1,0:T(8,128)(2,1)S(1)}, bf16[1,96,384]{2,1,0:T(8,128)(2,1)S(1)}, u32[]{:S(2)}, u32[]{:S(2)}) collective-permute-start(bf16[1,96,384]{2,1,0:T(8,128)(2,1)S(1)} %fusion.46), channel_id=1, source_target_pairs={{0,8},{8,0},{4,12},{12,4},{1,9},{9,1},{5,13},{13,5},{2,10},{10,2},... | collective-permute-start | bytes 221192 | tf_op jit(solution)/shard_map/ppermute | solution.py:664
  360.3 4.1 collective-permute-start.50
  364.4 4.2 collective-permute-start.51
  368.6 7.9 %collective-permute-start.52 = (f32[16,768]{1,0:T(8,128)S(1)}, f32[16,768]{1,0:T(8,128)S(1)}, u32[]{:S(2)}, u32[]{:S(2)}) collective-permute-start(f32[16,768]{1,0:T(8,128)S(1)} %add.333), channel_id=1, source_target_pairs={{0,1},{1,0},{2,3},{3,2},{4,5},{5,4},{6,7},{7,6},{8,9},{9,8},{10,11... | collective-permute-start | bytes 147464 | tf_op jit(solution)/shard_map/ppermute | solution.py:919
  369.7 40.9 %collective-permute-start.36 = (bf16[256,768]{1,0:T(8,128)(2,1)S(1)}, bf16[256,768]{1,0:T(8,128)(2,1)S(1)}, u32[]{:S(2)}, u32[]{:S(2)}) collective-permute-start(bf16[256,768]{1,0:T(8,128)(2,1)S(1)} %copy-done.24), channel_id=1, source_target_pairs={{0,1},{1,2},{2,3},{3,0},{4,5},{5,6},{6,7},{7,4},{8,9},{9,10},{10,1... | collective-permute-start | bytes 1179656 | tf_op jit(solution)/shard_map/ppermute | solution.py:665
  371.7 39.0 %collective-permute-start.37 = (bf16[256,768]{1,0:T(8,128)(2,1)S(1)}, bf16[256,768]{1,0:T(8,128)(2,1)S(1)}, u32[]{:S(2)}, u32[]{:S(2)}) collective-permute-start(bf16[256,768]{1,0:T(8,128)(2,1)S(1)} %copy-done.24), channel_id=1, source_target_pairs={{0,2},{1,3},{2,0},{3,1},{4,6},{5,7},{6,4},{7,5},{8,10},{9,11},{10,... | collective-permute-start | bytes 1179656 | tf_op jit(solution)/shard_map/ppermute | solution.py:665
  375.6 35.2 %collective-permute-start.38 = (bf16[256,768]{1,0:T(8,128)(2,1)S(1)}, bf16[256,768]{1,0:T(8,128)(2,1)S(1)}, u32[]{:S(2)}, u32[]{:S(2)}) collective-permute-start(bf16[256,768]{1,0:T(8,128)(2,1)S(1)} %copy-done.24), channel_id=1, source_target_pairs={{0,3},{1,0},{2,1},{3,2},{4,7},{5,4},{6,5},{7,6},{8,11},{9,8},{10,9... | collective-permute-start | bytes 1179656 | tf_op jit(solution)/shard_map/ppermute | solution.py:665
  376.5 32.8 %collective-permute-start.53 = (f32[16,768]{1,0:T(8,128)S(1)}, f32[16,768]{1,0:T(8,128)S(1)}, u32[]{:S(2)}, u32[]{:S(2)}) collective-permute-start(f32[16,768]{1,0:T(8,128)S(1)} %add.334), channel_id=1, source_target_pairs={{0,2},{2,0},{1,3},{3,1},{4,6},{6,4},{5,7},{7,5},{8,10},{10,8},{9,1... | collective-permute-start | bytes 147464 | tf_op jit(solution)/shard_map/ppermute | solution.py:920
  (38 other events, 191.1 us)
Sparse Core Ops, SparseCore 0:
  239.1 67.4 all-gather.2

commit v6 on v5

--- a/solution.py
+++ b/solution.py
@@ -796,16 +796,16 @@
     head = 0
     for g, held in zip(GROUPS, kv):
         results = attend(scalars, row(starts), after(qt, packed[1:]), held, head, g, BK_F, BQ_F, n_tensor)
-        lse, ot, *out = after(results, dn[1:])
+        lse, ot, *out = results
         saved.append((lse, ot))
         att[0].append(out[0])
         for d in range(1, n_tensor):
             att[d].append(shift_by(out[d], d))
         head += g
 
-    of = jnp.stack(after(gather_end(packed, hold), saved[-1][0]))
+    of = jnp.stack(after(gather_end(packed, hold), att[1:]))
     of = (of, swap(of))
-    dn = jnp.stack(gather_end(dn, saved[-1][0]))
+    dn = jnp.stack(gather_end(dn, att[1:]))
     dn = (dn, swap(dn))
     x_sub = lax.dynamic_slice_in_dim(x, tensor * sub, sub, 0)
     cot_sub = lax.dynamic_slice_in_dim(cot, tensor * sub, sub, 0)
@@ -833,14 +833,14 @@
 
     folded = scatter_begin(g_own, g_other)
     hop_one = folded[0] if grouped else folded
-    carried = jnp.pad(qkv_own, ((0, 0), (0, -3 * cols % 128)))
+    qkv_wide = jnp.pad(qkv_own, ((0, 0), (0, width - 3 * cols)))
+    carried = jnp.concatenate([outputs_sub, qkv_wide], axis=0)
     folded = scatter_begin(g_own, g_other)
     hop_one = folded[0] if grouped else folded
     qkv_wide = jnp.pad(qkv_own, ((0, 0), (0, width - 3 * cols)))
     outputs_and_qkv = lax.all_gather(
         jnp.concatenate([outputs_sub, qkv_wide], axis=0), "tensor", axis=0
     )
-    outputs = gather_direct(after(outputs_sub, do_parts))
     wide = scatter_first(folded)
     wide_sends = wide[2:]
     wide = scatter_second(wide)
@@ -855,10 +855,10 @@
         )
         back_done = out[-1]
         *out, carried = out
-        dq, dkv = after(out[:n_tensor], (wide_sends, outputs[1:])), out[n_tensor:]
+        dq, dkv = after(out[:n_tensor], wide_sends), out[n_tensor:]
         if grouped:
             dk_keep, dk_send, dv_keep, dv_send = dkv
-            dk_send, dv_send = after((dk_send, dv_send), (wide_sends, outputs[1:]))
+            dk_send, dv_send = after((dk_send, dv_send), wide_sends)
             r = along_x(dk_send).astype(f32)
             s = along_y(dv_send).astype(f32)
             r2 = along_y((dk_keep[1].astype(f32) + r[1]).astype(bf16)).astype(f32)
@@ -893,7 +893,9 @@
             at = lax.rem(tensor + d, n_tensor) * sub
             whole = lax.dynamic_update_slice_in_dim(whole, q[d], at, 1)
         dq_whole.append(whole)
-    qkv = lax.all_gather(carried, "tensor", axis=0)
+    outputs_and_qkv = lax.all_gather(carried, "tensor", axis=0)
+    outputs = outputs_and_qkv[:, :sub].reshape(tok, width)
+    qkv = outputs_and_qkv[:, sub:]
     qkv = (qkv, swap(qkv))
     stacked = jnp.concatenate(
         dq_whole + [both, jnp.zeros((-3 * cols % 128, tok), bf16)], axis=0
@@ -909,7 +911,7 @@
         place, grads, pieces, qkv, x_sub, after(grad_mid, qkv_folded), table, mid_sums, fc_sums
     )
     input_gradient = spread(gather_direct(input_sub))
-    outputs = spread(outputs)
+    outputs = after(outputs, input_sub).astype(f32)[None]
     qkv_grads = scatter_second(scatter_first(qkv_folded))[0]
 
     if grouped and n_tensor == 4 and n_shard == 2:

time: 420 us -> 412 us (0.981)
  waiting for transfers between devices: 183 us -> 170 us
  local copies, waits for them, and re-layouts: 17.8 us -> 22.4 us
    ppermute x15 -> x12, waiting for transfers between devices: 36.2 us -> 9.31 us  [body(): lax.ppermute(v, 'tensor', [(s, (s + d) % n_tensor) for s in range(n_tenso...]
    ppermute x9, waiting for transfers between devices: 28 us -> 53.1 us  [body(): lax.ppermute(v, 'context', [(0, 2), (2, 0), (1, 3), (3, 1)])]
    ppermute x1, waiting for transfers between devices: 31.8 us -> 7.75 us  [body(): small += lax.ppermute(small, 'tensor', [(0, 2), (2, 0), (1, 3), (3, 1)])]
    ppermute x1, waiting for transfers between devices: 0.01 us -> 22.5 us  [body(): small += lax.ppermute(small, 'tensor', [(0, 1), (1, 0), (2, 3), (3, 2)])]
    ppermute x9, starting transfers between devices: 6.73 us -> 24.3 us  [body(): lax.ppermute(v, 'context', [(0, 2), (2, 0), (1, 3), (3, 1)])]
    ppermute x4, waiting for transfers between devices: 11.3 us -> 0.01 us  [scatter_line(): move = lambda a, perm: lax.ppermute(a.astype(bf16), 'tensor', perm)]
    ppermute x15 -> x12, starting transfers between devices: 40.6 us -> 29.4 us  [body(): lax.ppermute(v, 'tensor', [(s, (s + d) % n_tensor) for s in range(n_tenso...]
    ppermute x4, starting transfers between devices: 15.2 us -> 5.45 us  [scatter_line(): move = lambda a, perm: lax.ppermute(a.astype(bf16), 'tensor', perm)]
  transfers between devices with their start and end apart: 55 -> 52, of which waited for: 23 -> 26; matrix products, arithmetic and copies ran while one was open for 10% -> 10% of each run, Pallas kernels for 9% -> 8%
where the time goes in v6:
time: 412 us; the launch traced here: 411 us
  waiting for transfers between devices  170 us (41%)
  starting transfers between devices  101 us (25%)
  Pallas kernels  70.3 us (17%)
  other arithmetic  28.5 us (7%)
  local copies, waits for them, and re-layouts  22.4 us (5%)
  between operations  15 us (4%)
    ppermute x9, waiting for transfers between devices, body(): lax.ppermute(v, 'context', [(0, 2), (2, 0), (1, 3), (3, 1)])  53.1 us
    ppermute x6, waiting for transfers between devices, gather_begin(): move = lambda perm: lax.ppermute(v, 'tensor', perm)  30.9 us
    ppermute x12, starting transfers between devices, body(): lax.ppermute(v, 'tensor', [(s, (s + d) % n_tensor) for s in range(n_tenso...  29.4 us
    ppermute x9, waiting for transfers between devices, body(): lax.ppermute(v, 'context', [(0, 1), (1, 0), (2, 3), (3, 2)])  25 us
    ppermute x6, starting transfers between devices, gather_begin(): move = lambda perm: lax.ppermute(v, 'tensor', perm)  24.8 us
    ppermute x9, starting transfers between devices, body(): lax.ppermute(v, 'context', [(0, 2), (2, 0), (1, 3), (3, 1)])  24.3 us
    pallas_call x1, Pallas kernels, middle(): pl.pallas_call(functools.partial(middle_kernel, len(att), parts), grid_sp...  23 us
    ppermute x1, waiting for transfers between devices, body(): small += lax.ppermute(small, 'tensor', [(0, 1), (1, 0), (2, 3), (3, 2)])  22.5 us
  transfers between devices with their start and end apart: 52, of which 26 were waited for; matrix products, arithmetic and copies ran while one was open for 10% of the time, Pallas kernels for 8%

profile of v6, /device:TPU:0, one launch (start us, length us, event | category | flops | bytes accessed | tf_op | source)
XLA Modules:
  0.0 410.6 jit_solution(1827918985153156589)
XLA Ops:
  10.3 4.1 collective-permute-start.1
  14.4 4.4 %collective-permute-start.2 = (bf16[976,384]{1,0:T(8,128)(2,1)S(1)}, bf16[976,384]{1,0:T(8,128)(2,1)}, u32[]{:S(2)}, u32[]{:S(2)}) collective-permute-start(bf16[976,384]{1,0:T(8,128)(2,1)S(1)} %pad_maximum_fusion.4), channel_id=1, source_target_pairs={{0,1},{1,2},{2,3},{4,5},{5,6},{6,7},{8,9},{9,10},{10,11},{12,13},{... | collective-permute-start | bytes 2248712 | tf_op jit(solution)/shard_map/ppermute | solution.py:675
  23.0 6.3 %project.1 = (bf16[1024,768]{1,0:T(8,128)(2,1)}, bf16[192,1024]{1,0:T(8,128)(2,1)}, bf16[192,1024]{1,0:T(8,128)(2,1)}, bf16[192,1024]{1,0:T(8,128)(2,1)}) custom-call(s32[4]{0:T(128)} %pad_add_fusion.1.sc, bf16[1024,768]{1,0:T(8,128)(2,1)} %bitcast.127, bf16[384,576]{1,0:T(8,128)(2,1)} %copy-done.4, bf16[384,576]{1,0:T(8,128)(2,1)} %copy-done.38, ...), custom_call_target="tpu_custom_call" | custom-call | flops 8049999872 | bytes 1048576 | tf_op jit(solution)/shard_map/project/pallas_call | solution.py:90
  29.4 1.6 collective-permute-start.5
  30.9 1.5 collective-permute-start.4
  32.4 8.4 %collective-permute-done.5.refs_4_.refs_8_ = bf16[192,1024]{1,0:T(8,128)(2,1)S(1)} collective-permute-done((bf16[192,1024]{1,0:T(8,128)(2,1)}, bf16[192,1024]{1,0:T(8,128)(2,1)S(1)}, u32[]{:S(2)}, u32[]{:S(2)}) %collective-permute-start.5) | collective-permute-done | bytes 393248 | tf_op jit(solution)/shard_map/ppermute | solution.py:664
  42.2 6.0 %collective-permute-done.1 = bf16[976,384]{1,0:T(8,128)(2,1)} collective-permute-done((bf16[976,384]{1,0:T(8,128)(2,1)S(1)}, bf16[976,384]{1,0:T(8,128)(2,1)}, u32[]{:S(2)}, u32[]{:S(2)}) %collective-permute-start.1) | collective-permute-done | bytes 749600 | tf_op jit(solution)/shard_map/ppermute | solution.py:675
  48.2 5.4 %collective-permute-done.3 = bf16[976,384]{1,0:T(8,128)(2,1)} collective-permute-done((bf16[976,384]{1,0:T(8,128)(2,1)S(1)}, bf16[976,384]{1,0:T(8,128)(2,1)}, u32[]{:S(2)}, u32[]{:S(2)}) %collective-permute-start.3) | collective-permute-done | bytes 749600 | tf_op jit(solution)/shard_map/ppermute | solution.py:675
  53.6 1.6 collective-permute-start.6
  55.1 1.5 collective-permute-start.7
  57.9 3.8 fusion.63
  62.6 12.4 %collective-permute-start.13 = (bf16[768,384]{1,0:T(8,128)(2,1)}, bf16[768,384]{1,0:T(8,128)(2,1)}, u32[]{:S(2)}, u32[]{:S(2)}) collective-permute-start(bf16[768,384]{1,0:T(8,128)(2,1)} %param.20), channel_id=1, source_target_pairs={{0,2},{1,3},{2,0},{3,1},{4,6},{5,7},{6,4},{7,5},{8,10},{9,11},{10,... | collective-permute-start | bytes 1769480 | tf_op jit(solution)/shard_map/ppermute | solution.py:675
  77.2 9.5 %attend.1 = (f32[3,1024]{1,0:T(4,128)}, bf16[192,1024]{1,0:T(8,128)(2,1)}, bf16[192,256]{1,0:T(8,128)(2,1)}, bf16[192,256]{1,0:T(8,128)(2,1)}, bf16[192,256]{1,0:T(8,128)(2,1)}, /*index=5*/bf16[192,256]{1,0:T(8,128)(2,1)}) custom-call(s32[12]{0:T(128)} %concatenate.46.sc, bf16[192,1024]{1,0:T(8,128)(2,1)} %get-tuple-element.92.qt, ...), custom_call_target="tpu_custom_call" | custom-call | flops 23000000512 | bytes 1048576 | tf_op jit(solution)/shard_map/attend/pallas_call | solution.py:221
  87.1 7.4 %collective-permute-start.8 = (bf16[192,256]{1,0:T(8,128)(2,1)}, bf16[192,256]{1,0:T(8,128)(2,1)S(1)}, u32[]{:S(2)}, u32[]{:S(2)}) collective-permute-start(bf16[192,256]{1,0:T(8,128)(2,1)} %get-tuple-element.79), channel_id=1, source_target_pairs={{0,1},{1,2},{2,3},{3,0},{4,5},{5,6},{6,7},{7,4},{8,9},{9,10},{10,1... | collective-permute-start | bytes 294920 | tf_op jit(solution)/shard_map/ppermute | solution.py:665
  94.5 4.0 collective-permute-start.9
  98.5 6.9 %collective-permute-done.13 = bf16[768,384]{1,0:T(8,128)(2,1)} collective-permute-done((bf16[768,384]{1,0:T(8,128)(2,1)}, bf16[768,384]{1,0:T(8,128)(2,1)}, u32[]{:S(2)}, u32[]{:S(2)}) %collective-permute-start.13) | collective-permute-done | bytes 589856 | tf_op jit(solution)/shard_map/ppermute | solution.py:675
  106.7 7.0 %collective-permute-done.10.refs_3_ = bf16[192,256]{1,0:T(8,128)(2,1)S(1)} collective-permute-done((bf16[192,256]{1,0:T(8,128)(2,1)}, bf16[192,256]{1,0:T(8,128)(2,1)S(1)}, u32[]{:S(2)}, u32[]{:S(2)}) %collective-permute-start.10) | collective-permute-done | bytes 98336 | tf_op jit(solution)/shard_map/ppermute | solution.py:665
  117.9 1.5 pad_maximum_fusion.refs_6_
  119.8 12.3 %collective-permute-done.16 = bf16[768,384]{1,0:T(8,128)(2,1)S(1)} collective-permute-done((bf16[768,384]{1,0:T(8,128)(2,1)}, bf16[768,384]{1,0:T(8,128)(2,1)S(1)}, u32[]{:S(2)}, u32[]{:S(2)}) %collective-permute-start.16) | collective-permute-done | bytes 589856 | tf_op jit(solution)/shard_map/ppermute | solution.py:675
  132.1 9.9 %collective-permute-done.14 = bf16[768,384]{1,0:T(8,128)(2,1)S(1)} collective-permute-done((bf16[768,384]{1,0:T(8,128)(2,1)}, bf16[768,384]{1,0:T(8,128)(2,1)S(1)}, u32[]{:S(2)}, u32[]{:S(2)}) %collective-permute-start.14) | collective-permute-done | bytes 589856 | tf_op jit(solution)/shard_map/ppermute | solution.py:688
  142.1 3.0 pad_maximum_fusion.1.refs_8_
  145.1 2.1 dynamic-slice_bitcast_fusion.2
  147.2 2.8 collective-permute-done.17.refs_9_
  150.0 23.0 %middle.1 = (bf16[256,768]{1,0:T(8,128)(2,1)}, f32[256,768]{1,0:T(8,128)}, f32[4,768]{1,0:T(4,128)}, f32[4,1,768]{2,1,0:T(1,128)}, bf16[192,256]{1,0:T(8,128)(2,...) custom-call(s32[4]{0:T(128)} %pad_add_fusion.1.sc, ...), custom_call_target="tpu_custom_call" | custom-call | flops 21849999360 | bytes 1048576 | tf_op jit(solution)/shard_map/middle/pallas_call | solution.py:465
  175.2 2.1 fusion.13.refs_10_
  177.3 4.9 %collective-permute-done.18.theirs = bf16[4,384,1792]{2,1,0:T(8,128)(2,1)S(1)} collective-permute-done((bf16[4,384,1792]{2,1,0:T(8,128)(2,1)}, bf16[4,384,1792]{2,1,0:T(8,128)(2,1)S(1)}, u32[]{:S(2)}, u32[]{:S(2)}) %collective-permute-start.18) | collective-permute-done | bytes 5505056 | tf_op jit(solution)/shard_map/ppermute | solution.py:662
  182.2 2.4 copy-done.33
  184.6 8.7 %fold.2 = (bf16[2,4,96,896]{3,2,1,0:T(8,128)(2,1)}, bf16[2,4,96,896]{3,2,1,0:T(8,128)(2,1)}, bf16[2,4,96,896]{3,2,1,0:T(8,128)(2,1)}, bf16[2,4,96,896]{3,2,1,0:T(8,128)(2,1)}) custom-call(s32[4]{0:T(128)} %pad_add_fusion.1.sc, bf16[4,384,1792]{2,1,0:T(8,128)(2,1)} %get-tuple-element.89.mine, bf16[4,384,1792]{2,1,0:T(8,128)(2,1)} %copy-done.33), custom_call_target="tpu_custom_call" | custom-call | flops 8049999872 | bytes 1048576 | tf_op jit(solution)/shard_map/fold/pallas_call | solution.py:587
  194.0 12.6 %attend_back.1 = (bf16[192,256]{1,0:T(8,128)(2,1)}, bf16[192,256]{1,0:T(8,128)(2,1)}, bf16[192,256]{1,0:T(8,128)(2,1)}, bf16[192,256]{1,0:T(8,128)(2,1)}, bf16[2...) custom-call(s32[12]{0:T(128)} %concatenate.46.sc, ...), custom_call_target="tpu_custom_call", output_to_operand_aliasing={{8}: (15, {})} | custom-call | flops 29899999232 | bytes 1048576 | tf_op jit(solution)/shard_map/attend_back/pallas_call | solution.py:327
  206.7 12.6 %collective-permute-start.23 = (bf16[2,4,96,896]{3,2,1,0:T(8,128)(2,1)}, bf16[2,4,96,896]{3,2,1,0:T(8,128)(2,1)S(1)}, u32[]{:S(2)}, u32[]{:S(2)}) collective-permute-start(bf16[2,4,96,896]{3,2,1,0:T(8,128)(2,1)} %get-tuple-element.107), channel_id=1, source_target_pairs={{0,8},{8,0},{4,12},{12,4},{1,9},{9,1},{5,13},{13,5},{2,10},{10,2},... | collective-permute-start | bytes 4128776 | tf_op jit(solution)/shard_map/ppermute | solution.py:664
  219.3 30.7 %collective-permute-done.23 = bf16[2,4,96,896]{3,2,1,0:T(8,128)(2,1)S(1)} collective-permute-done((bf16[2,4,96,896]{3,2,1,0:T(8,128)(2,1)}, bf16[2,4,96,896]{3,2,1,0:T(8,128)(2,1)S(1)}, u32[]{:S(2)}, u32[]{:S(2)}) %collective-permute-start.23) | collective-permute-done | bytes 1376288 | tf_op jit(solution)/shard_map/ppermute | solution.py:664
  251.9 1.8 collective-permute-start.40
  254.0 1.6 collective-permute-start.24
  255.8 13.0 %collective-permute-done.41 = bf16[4,96,896]{2,1,0:T(8,128)(2,1)S(1)} collective-permute-done((bf16[4,96,896]{2,1,0:T(8,128)(2,1)S(1)}, bf16[4,96,896]{2,1,0:T(8,128)(2,1)S(1)}, u32[]{:S(2)}, u32[]{:S(2)}) %collective-permute-start.41) | collective-permute-done | bytes 688160 | tf_op jit(solution)/shard_map/ppermute | solution.py:663
  271.5 1.7 collective-permute-start.44
  273.2 2.0 collective-permute-start.42
  275.2 1.5 collective-permute-start.43
  276.7 9.3 %collective-permute-done.26 = bf16[2,192,1024]{2,1,0:T(8,128)(2,1)S(1)} collective-permute-done((bf16[2,192,1024]{2,1,0:T(8,128)(2,1)S(1)}, bf16[2,192,1024]{2,1,0:T(8,128)(2,1)S(1)}, u32[]{:S(2)}, u32[]{:S(2)}) %collective-permute-start.26) | collective-permute-done | bytes 786464 | tf_op jit(solution)/shard_map/ppermute | solution.py:664
  287.5 1.5 collective-permute-start.25
  290.0 6.4 %collective-permute-done.27 = bf16[192,1024]{1,0:T(8,128)(2,1)S(1)} collective-permute-done((bf16[192,1024]{1,0:T(8,128)(2,1)S(1)}, bf16[192,1024]{1,0:T(8,128)(2,1)S(1)}, u32[]{:S(2)}, u32[]{:S(2)}) %collective-permute-start.27) | collective-permute-done | bytes 393248 | tf_op jit(solution)/shard_map/ppermute | solution.py:663
  297.9 2.6 convolution_convert_fusion
  300.4 2.4 all-gather.3.cloned.1.call-done
  302.9 3.3 slice.197.refs_4_
  309.3 8.0 %collective-permute-start.30 = (bf16[576,256]{1,0:T(8,128)(2,1)}, bf16[576,256]{1,0:T(8,128)(2,1)}, u32[]{:S(2)}, u32[]{:S(2)}) collective-permute-start(bf16[576,256]{1,0:T(8,128)(2,1)} %pad_maximum_fusion.9), channel_id=1, source_target_pairs={{0,3},{1,0},{2,1},{3,2},{4,7},{5,4},{6,5},{7,6},{8,11},{9,8},{10,9... | collective-permute-start | bytes 884744 | tf_op jit(solution)/shard_map/ppermute | solution.py:665
  318.6 2.0 collective-permute-start.28
  323.5 4.1 fold.3
  327.6 1.7 collective-permute-start.38
  330.1 2.4 collective-permute-done.38
  332.5 2.3 collective-permute-start.36
  335.6 2.5 collective-permute-done.36
  338.1 2.0 collective-permute-start.39
  341.1 1.7 collective-permute-start.37
  342.7 2.2 collective-permute-done.29.refs_2_
  345.0 6.1 %last.1 = (bf16[256,768]{1,0:T(8,128)(2,1)}, f32[16,768]{1,0:T(8,128)}) custom-call(s32[4]{0:T(128)} %pad_add_fusion.1.sc, bf16[576,256]{1,0:T(8,128)(2,1)} %pad_maximum_fusion.6.refs_0_, bf16[576,256]{1,0:T(8,128)(2,1)} %collective-permute-done.28.refs_1_, bf16[576,256]{1,0:T(8,128)(2,1)} %collective-permute-done.29.refs_2_, ...), custom_call_target="tpu_custom_call" | custom-call | flops 6899999744 | bytes 1048576 | tf_op jit(solution)/shard_map/last/pallas_call | solution.py:537
  353.3 2.3 collective-permute-start.47
  355.7 2.0 collective-permute-done.47
  357.7 1.7 collective-permute-start.48
  360.4 1.6 slice.190
  363.5 2.8 collective-permute-start.35
  366.5 1.9 bitcast_convert_fusion
  368.4 22.5 %collective-permute-done.49 = f32[16,768]{1,0:T(8,128)S(1)} collective-permute-done((f32[16,768]{1,0:T(8,128)S(1)}, f32[16,768]{1,0:T(8,128)S(1)}, u32[]{:S(2)}, u32[]{:S(2)}) %collective-permute-start.49) | collective-permute-done | bytes 49184 | tf_op jit(solution)/shard_map/ppermute | solution.py:921
  391.0 1.6 collective-permute-start.50
  392.8 7.8 %collective-permute-done.50 = f32[16,768]{1,0:T(8,128)S(1)} collective-permute-done((f32[16,768]{1,0:T(8,128)S(1)}, f32[16,768]{1,0:T(8,128)S(1)}, u32[]{:S(2)}, u32[]{:S(2)}) %collective-permute-start.50) | collective-permute-done | bytes 49184 | tf_op jit(solution)/shard_map/ppermute | solution.py:922
  402.1 1.7 copy-done
  (232 shorter events, 47.4 us)
Async XLA Ops:
  7.2 12.8 %copy-start.11 = (bf16[384,3,192]{0,2,1:T(8,128)(2,1)S(1)}, bf16[384,3,192]{0,2,1:T(8,128)(2,1)}, u32[]{:S(2)}) copy-start(bf16[384,3,192]{0,2,1:T(8,128)(2,1)} %param.17) | copy-start | bytes 1327108
  7.2 295.7 %all-gather.3.cloned.1.call-start = ((), (), s32[]{:S(2)}) async-start(), calls=%async_computation | async-start | bytes 4915200 | tf_op jit(solution)/shard_map/all_gather | solution.py:896
  8.1 12.4 %copy-start.31 = (f32[768]{0:T(1024)S(1)}, f32[768]{0:T(1024)}, u32[]{:S(2)}) copy-start(f32[768]{0:T(1024)} %param.27) | copy-start | bytes 9220
  8.1 12.4 %copy-start.32 = (f32[768]{0:T(1024)S(1)}, f32[768]{0:T(1024)}, u32[]{:S(2)}) copy-start(f32[768]{0:T(1024)} %param.28) | copy-start | bytes 9220
  10.2 19.1 %copy-start.2 = (bf16[976,384]{1,0:T(8,128)(2,1)}, bf16[976,384]{1,0:T(8,128)(2,1)S(1)}, u32[]{:S(2)}) copy-start(bf16[976,384]{1,0:T(8,128)(2,1)S(1)} %pad_maximum_fusion.4) | copy-start | bytes 2248708
  10.3 37.9 %collective-permute-start.1 = (bf16[976,384]{1,0:T(8,128)(2,1)S(1)}, bf16[976,384]{1,0:T(8,128)(2,1)}, u32[]{:S(2)}, u32[]{:S(2)}) collective-permute-start(bf16[976,384]{1,0:T(8,128)(2,1)S(1)} %pad_maximum_fusion.4), channel_id=1, source_target_pairs={{0,2},{1,3},{2,0},{3,1},{4,6},{5,7},{6,4},{7,5},{8,10},{9,11},{10,... | collective-permute-start | bytes 2248712 | tf_op jit(solution)/shard_map/ppermute | solution.py:675
  14.4 33.8 %collective-permute-start.2 = (bf16[976,384]{1,0:T(8,128)(2,1)S(1)}, bf16[976,384]{1,0:T(8,128)(2,1)}, u32[]{:S(2)}, u32[]{:S(2)}) collective-permute-start(bf16[976,384]{1,0:T(8,128)(2,1)S(1)} %pad_maximum_fusion.4), channel_id=1, source_target_pairs={{0,1},{1,2},{2,3},{4,5},{5,6},{6,7},{8,9},{9,10},{10,11},{12,13},{... | collective-permute-start | bytes 2248712 | tf_op jit(solution)/shard_map/ppermute | solution.py:675
  18.7 34.8 %collective-permute-start.3 = (bf16[976,384]{1,0:T(8,128)(2,1)S(1)}, bf16[976,384]{1,0:T(8,128)(2,1)}, u32[]{:S(2)}, u32[]{:S(2)}) collective-permute-start(bf16[976,384]{1,0:T(8,128)(2,1)S(1)} %pad_maximum_fusion.4), channel_id=1, source_target_pairs={{3,2},{2,1},{1,0},{7,6},{6,5},{5,4},{11,10},{10,9},{9,8},{15,14},{... | collective-permute-start | bytes 2248712 | tf_op jit(solution)/shard_map/ppermute | solution.py:675
  20.3 1.9 collective-permute-start
  29.4 12.7 %copy-start.20 = (bf16[192,1024]{1,0:T(8,128)(2,1)S(1)}, bf16[192,1024]{1,0:T(8,128)(2,1)}, u32[]{:S(2)}) copy-start(bf16[192,1024]{1,0:T(8,128)(2,1)} %get-tuple-element.74.refs_0_.refs_4_) | copy-start | bytes 1179652
  29.4 11.4 %collective-permute-start.5 = (bf16[192,1024]{1,0:T(8,128)(2,1)}, bf16[192,1024]{1,0:T(8,128)(2,1)S(1)}, u32[]{:S(2)}, u32[]{:S(2)}) collective-permute-start(bf16[192,1024]{1,0:T(8,128)(2,1)} %get-tuple-element.75.refs_3_.refs_7_), channel_id=1, source_target_pairs={{0,8},{8,0},{4,12},{12,4},{1,9},{9,1},{5,13},{13,5},{2,10},{10,2},... | collective-permute-start | bytes 1179656 | tf_op jit(solution)/shard_map/ppermute | solution.py:664
  30.9 11.1 %collective-permute-start.4 = (bf16[192,1024]{1,0:T(8,128)(2,1)}, bf16[192,1024]{1,0:T(8,128)(2,1)S(1)}, u32[]{:S(2)}, u32[]{:S(2)}) collective-permute-start(bf16[192,1024]{1,0:T(8,128)(2,1)} %get-tuple-element.74.refs_0_.refs_4_), channel_id=1, source_target_pairs={{0,4},{4,0},{8,12},{12,8},{1,5},{5,1},{9,13},{13,9},{2,6},{6,2},{1... | collective-permute-start | bytes 1179656 | tf_op jit(solution)/shard_map/ppermute | solution.py:663
  40.8 15.8 %copy-start.26 = (s32[1,4096]{1,0:T(1,128)S(1)}, s32[1,4096]{1,0:T(1,128)}, u32[]{:S(2)}) copy-start(s32[1,4096]{1,0:T(1,128)} %param.16) | copy-start | bytes 49156
  42.0 13.1 %copy-start.22 = (bf16[192,1024]{1,0:T(8,128)(2,1)}, bf16[192,1024]{1,0:T(8,128)(2,1)S(1)}, u32[]{:S(2)}) copy-start(bf16[192,1024]{1,0:T(8,128)(2,1)S(1)} %collective-permute-done.4.refs_1_.refs_5_) | copy-start | bytes 1179652
  53.6 22.7 %collective-permute-start.6 = (bf16[2,192,1024]{2,1,0:T(8,128)(2,1)S(1)}, bf16[2,192,1024]{2,1,0:T(8,128)(2,1)S(1)}, u32[]{:S(2)}, u32[]{:S(2)}) collective-permute-start(bf16[2,192,1024]{2,1,0:T(8,128)(2,1)S(1)} %pad_maximum_fusion.2), channel_id=1, source_target_pairs={{0,8},{8,0},{4,12},{12,4},{1,9},{9,1},{5,13},{13,5},{2,10},{10,2},... | collective-permute-start | bytes 2359304 | tf_op jit(solution)/shard_map/ppermute | solution.py:664
  55.1 21.2 %collective-permute-start.7 = (bf16[2,192,1024]{2,1,0:T(8,128)(2,1)S(1)}, bf16[2,192,1024]{2,1,0:T(8,128)(2,1)}, u32[]{:S(2)}, u32[]{:S(2)}) collective-permute-start(bf16[2,192,1024]{2,1,0:T(8,128)(2,1)S(1)} %pad_maximum_fusion.3), channel_id=1, source_target_pairs={{0,4},{4,0},{8,12},{12,8},{1,5},{5,1},{9,13},{13,9},{2,6},{6,2},{1... | collective-permute-start | bytes 2359304 | tf_op jit(solution)/shard_map/ppermute | solution.py:663
  62.6 42.8 %collective-permute-start.13 = (bf16[768,384]{1,0:T(8,128)(2,1)}, bf16[768,384]{1,0:T(8,128)(2,1)}, u32[]{:S(2)}, u32[]{:S(2)}) collective-permute-start(bf16[768,384]{1,0:T(8,128)(2,1)} %param.20), channel_id=1, source_target_pairs={{0,2},{1,3},{2,0},{3,1},{4,6},{5,7},{6,4},{7,5},{8,10},{9,11},{10,... | collective-permute-start | bytes 1769480 | tf_op jit(solution)/shard_map/ppermute | solution.py:675
  75.0 41.5 %collective-permute-start.11 = (bf16[976,384]{1,0:T(8,128)(2,1)}, bf16[976,384]{1,0:T(8,128)(2,1)S(1)}, u32[]{:S(2)}, u32[]{:S(2)}) collective-permute-start(bf16[976,384]{1,0:T(8,128)(2,1)} %collective-permute-done.1), channel_id=1, source_target_pairs={{2,3},{1,0},{6,7},{5,4},{10,11},{9,8},{14,15},{13,12},{18,19},{17,... | collective-permute-start | bytes 2248712 | tf_op jit(solution)/shard_map/ppermute | solution.py:688
  86.7 27.0 %collective-permute-start.10 = (bf16[192,256]{1,0:T(8,128)(2,1)}, bf16[192,256]{1,0:T(8,128)(2,1)S(1)}, u32[]{:S(2)}, u32[]{:S(2)}) collective-permute-start(bf16[192,256]{1,0:T(8,128)(2,1)} %get-tuple-element.81), channel_id=1, source_target_pairs={{0,3},{1,0},{2,1},{3,2},{4,7},{5,4},{6,5},{7,6},{8,11},{9,8},{10,9... | collective-permute-start | bytes 294920 | tf_op jit(solution)/shard_map/ppermute | solution.py:665
  87.1 27.9 %collective-permute-start.8 = (bf16[192,256]{1,0:T(8,128)(2,1)}, bf16[192,256]{1,0:T(8,128)(2,1)S(1)}, u32[]{:S(2)}, u32[]{:S(2)}) collective-permute-start(bf16[192,256]{1,0:T(8,128)(2,1)} %get-tuple-element.79), channel_id=1, source_target_pairs={{0,1},{1,2},{2,3},{3,0},{4,5},{5,6},{6,7},{7,4},{8,9},{9,10},{10,1... | collective-permute-start | bytes 294920 | tf_op jit(solution)/shard_map/ppermute | solution.py:665
  94.5 20.5 %collective-permute-start.9 = (bf16[192,256]{1,0:T(8,128)(2,1)}, bf16[192,256]{1,0:T(8,128)(2,1)S(1)}, u32[]{:S(2)}, u32[]{:S(2)}) collective-permute-start(bf16[192,256]{1,0:T(8,128)(2,1)} %get-tuple-element.80), channel_id=1, source_target_pairs={{0,2},{1,3},{2,0},{3,1},{4,6},{5,7},{6,4},{7,5},{8,10},{9,11},{10,... | collective-permute-start | bytes 294920 | tf_op jit(solution)/shard_map/ppermute | solution.py:665
  98.5 19.4 %copy-start.3 = (bf16[976,384]{1,0:T(8,128)(2,1)S(1)}, bf16[976,384]{1,0:T(8,128)(2,1)}, u32[]{:S(2)}) copy-start(bf16[976,384]{1,0:T(8,128)(2,1)} %copy-done.2) | copy-start | bytes 2248708
  105.4 14.4 %collective-permute-start.15 = (bf16[768,384]{1,0:T(8,128)(2,1)}, bf16[768,384]{1,0:T(8,128)(2,1)S(1)}, u32[]{:S(2)}, u32[]{:S(2)}) collective-permute-start(bf16[768,384]{1,0:T(8,128)(2,1)} %param.20), channel_id=1, source_target_pairs={{0,1},{1,2},{2,3},{4,5},{5,6},{6,7},{8,9},{9,10},{10,11},{12,13},{... | collective-permute-start | bytes 1769480 | tf_op jit(solution)/shard_map/ppermute | solution.py:675
  113.7 18.4 %collective-permute-start.16 = (bf16[768,384]{1,0:T(8,128)(2,1)}, bf16[768,384]{1,0:T(8,128)(2,1)S(1)}, u32[]{:S(2)}, u32[]{:S(2)}) collective-permute-start(bf16[768,384]{1,0:T(8,128)(2,1)} %param.20), channel_id=1, source_target_pairs={{3,2},{2,1},{1,0},{7,6},{6,5},{5,4},{11,10},{10,9},{9,8},{15,14},{... | collective-permute-start | bytes 1769480 | tf_op jit(solution)/shard_map/ppermute | solution.py:675
  115.1 26.9 %collective-permute-start.14 = (bf16[768,384]{1,0:T(8,128)(2,1)}, bf16[768,384]{1,0:T(8,128)(2,1)S(1)}, u32[]{:S(2)}, u32[]{:S(2)}) collective-permute-start(bf16[768,384]{1,0:T(8,128)(2,1)} %collective-permute-done.13), channel_id=1, source_target_pairs={{2,3},{1,0},{6,7},{5,4},{10,11},{9,8},{14,15},{13,12},{18,19},{17,... | collective-permute-start | bytes 1769480 | tf_op jit(solution)/shard_map/ppermute | solution.py:688
  119.4 25.7 %copy-start.1 = (bf16[4,976,384]{2,1,0:T(8,128)(2,1)}, bf16[4,976,384]{2,1,0:T(8,128)(2,1)S(1)}, u32[]{:S(2)}) copy-start(bf16[4,976,384]{2,1,0:T(8,128)(2,1)S(1)} %pad_maximum_fusion.refs_6_) | copy-start | bytes 8994820
  119.4 30.6 %collective-permute-start.12 = (bf16[4,976,384]{2,1,0:T(8,128)(2,1)S(1)}, bf16[4,976,384]{2,1,0:T(8,128)(2,1)}, u32[]{:S(2)}, u32[]{:S(2)}) collective-permute-start(bf16[4,976,384]{2,1,0:T(8,128)(2,1)S(1)} %pad_maximum_fusion.refs_6_), channel_id=1, source_target_pairs={{0,16},{16,0},{1,17},{17,1},{2,18},{18,2},{3,19},{19,3},{4,20},{20... | collective-permute-start | bytes 8994824 | tf_op jit(solution)/shard_map/ppermute | solution.py:662
  145.1 4.9 %collective-permute-start.17 = (bf16[4,768,384]{2,1,0:T(8,128)(2,1)}, bf16[4,768,384]{2,1,0:T(8,128)(2,1)}, u32[]{:S(2)}, u32[]{:S(2)}) collective-permute-start(bf16[4,768,384]{2,1,0:T(8,128)(2,1)} %pad_maximum_fusion.1.refs_8_), channel_id=1, source_target_pairs={{0,16},{16,0},{1,17},{17,1},{2,18},{18,2},{3,19},{19,3},{4,20},{20... | collective-permute-start | bytes 7077896 | tf_op jit(solution)/shard_map/ppermute | solution.py:662
  150.0 25.2 %copy-start.5 = (bf16[384,576]{1,0:T(8,128)(2,1)S(1)}, bf16[384,576]{1,0:T(8,128)(2,1)}, u32[]{:S(2)}) copy-start(bf16[384,576]{1,0:T(8,128)(2,1)} %copy-done.4) | copy-start | bytes 1327108
  173.0 9.2 %collective-permute-start.18 = (bf16[4,384,1792]{2,1,0:T(8,128)(2,1)}, bf16[4,384,1792]{2,1,0:T(8,128)(2,1)S(1)}, u32[]{:S(2)}, u32[]{:S(2)}) collective-permute-start(bf16[4,384,1792]{2,1,0:T(8,128)(2,1)} %get-tuple-element.90), channel_id=1, source_target_pairs={{0,16},{16,0},{1,17},{17,1},{2,18},{18,2},{3,19},{19,3},{4,20},{20... | collective-permute-start | bytes 16515080 | tf_op jit(solution)/shard_map/ppermute | solution.py:662
  173.2 20.1 %collective-permute-start.19 = (bf16[192,256]{1,0:T(8,128)(2,1)}, bf16[192,256]{1,0:T(8,128)(2,1)S(1)}, u32[]{:S(2)}, u32[]{:S(2)}) collective-permute-start(bf16[192,256]{1,0:T(8,128)(2,1)} %get-tuple-element.96), channel_id=1, source_target_pairs={{0,3},{1,0},{2,1},{3,2},{4,7},{5,4},{6,5},{7,6},{8,11},{9,8},{10,9... | collective-permute-start | bytes 294920 | tf_op jit(solution)/shard_map/ppermute | solution.py:665
  173.2 20.1 %collective-permute-start.20 = (bf16[192,256]{1,0:T(8,128)(2,1)}, bf16[192,256]{1,0:T(8,128)(2,1)S(1)}, u32[]{:S(2)}, u32[]{:S(2)}) collective-permute-start(bf16[192,256]{1,0:T(8,128)(2,1)} %get-tuple-element.97), channel_id=1, source_target_pairs={{0,2},{1,3},{2,0},{3,1},{4,6},{5,7},{6,4},{7,5},{8,10},{9,11},{10,... | collective-permute-start | bytes 294920 | tf_op jit(solution)/shard_map/ppermute | solution.py:665
  174.3 19.0 %collective-permute-start.21 = (bf16[192,256]{1,0:T(8,128)(2,1)}, bf16[192,256]{1,0:T(8,128)(2,1)S(1)}, u32[]{:S(2)}, u32[]{:S(2)}) collective-permute-start(bf16[192,256]{1,0:T(8,128)(2,1)} %get-tuple-element.98), channel_id=1, source_target_pairs={{0,1},{1,2},{2,3},{3,0},{4,5},{5,6},{6,7},{7,4},{8,9},{9,10},{10,1... | collective-permute-start | bytes 294920 | tf_op jit(solution)/shard_map/ppermute | solution.py:665
  206.7 43.4 %collective-permute-start.23 = (bf16[2,4,96,896]{3,2,1,0:T(8,128)(2,1)}, bf16[2,4,96,896]{3,2,1,0:T(8,128)(2,1)S(1)}, u32[]{:S(2)}, u32[]{:S(2)}) collective-permute-start(bf16[2,4,96,896]{3,2,1,0:T(8,128)(2,1)} %get-tuple-element.107), channel_id=1, source_target_pairs={{0,8},{8,0},{4,12},{12,4},{1,9},{9,1},{5,13},{13,5},{2,10},{10,2},... | collective-permute-start | bytes 4128776 | tf_op jit(solution)/shard_map/ppermute | solution.py:664
  219.2 32.2 %collective-permute-start.22 = (bf16[2,4,96,896]{3,2,1,0:T(8,128)(2,1)}, bf16[2,4,96,896]{3,2,1,0:T(8,128)(2,1)S(1)}, u32[]{:S(2)}, u32[]{:S(2)}) collective-permute-start(bf16[2,4,96,896]{3,2,1,0:T(8,128)(2,1)} %get-tuple-element.91), channel_id=1, source_target_pairs={{0,4},{4,0},{8,12},{12,8},{1,5},{5,1},{9,13},{13,9},{2,6},{6,2},{1... | collective-permute-start | bytes 4128776 | tf_op jit(solution)/shard_map/ppermute | solution.py:663
  219.3 30.9 %copy-start.7 = (bf16[2,4,96,896]{3,2,1,0:T(8,128)(2,1)S(1)}, bf16[2,4,96,896]{3,2,1,0:T(8,128)(2,1)}, u32[]{:S(2)}) copy-start(bf16[2,4,96,896]{3,2,1,0:T(8,128)(2,1)} %get-tuple-element.106) | copy-start | bytes 4128772
  250.4 18.4 %collective-permute-start.41 = (bf16[4,96,896]{2,1,0:T(8,128)(2,1)S(1)}, bf16[4,96,896]{2,1,0:T(8,128)(2,1)S(1)}, u32[]{:S(2)}, u32[]{:S(2)}) collective-permute-start(bf16[4,96,896]{2,1,0:T(8,128)(2,1)S(1)} %fusion.23), channel_id=1, source_target_pairs={{0,4},{4,0},{8,12},{12,8},{1,5},{5,1},{9,13},{13,9},{2,6},{6,2},{1... | collective-permute-start | bytes 2064392 | tf_op jit(solution)/shard_map/ppermute | solution.py:663
  251.9 18.4 %collective-permute-start.40 = (bf16[4,96,896]{2,1,0:T(8,128)(2,1)S(1)}, bf16[4,96,896]{2,1,0:T(8,128)(2,1)S(1)}, u32[]{:S(2)}, u32[]{:S(2)}) collective-permute-start(bf16[4,96,896]{2,1,0:T(8,128)(2,1)S(1)} %fusion.22), channel_id=1, source_target_pairs={{0,8},{8,0},{4,12},{12,4},{1,9},{9,1},{5,13},{13,5},{2,10},{10,2},... | collective-permute-start | bytes 2064392 | tf_op jit(solution)/shard_map/ppermute | solution.py:664
  253.8 32.3 %collective-permute-start.26 = (bf16[2,192,1024]{2,1,0:T(8,128)(2,1)S(1)}, bf16[2,192,1024]{2,1,0:T(8,128)(2,1)S(1)}, u32[]{:S(2)}, u32[]{:S(2)}) collective-permute-start(bf16[2,192,1024]{2,1,0:T(8,128)(2,1)S(1)} %copy-done.35), channel_id=1, source_target_pairs={{0,8},{8,0},{4,12},{12,4},{1,9},{9,1},{5,13},{13,5},{2,10},{10,2},... | collective-permute-start | bytes 2359304 | tf_op jit(solution)/shard_map/ppermute | solution.py:664
  254.0 33.1 %collective-permute-start.24 = (bf16[2,192,1024]{2,1,0:T(8,128)(2,1)S(1)}, bf16[2,192,1024]{2,1,0:T(8,128)(2,1)S(1)}, u32[]{:S(2)}, u32[]{:S(2)}) collective-permute-start(bf16[2,192,1024]{2,1,0:T(8,128)(2,1)S(1)} %copy-done.34), channel_id=1, source_target_pairs={{0,4},{4,0},{8,12},{12,8},{1,5},{5,1},{9,13},{13,9},{2,6},{6,2},{1... | collective-permute-start | bytes 2359304 | tf_op jit(solution)/shard_map/ppermute | solution.py:663
  271.5 14.7 %copy-start.10 = (bf16[2,192,1024]{2,1,0:T(8,128)(2,1)S(1)}, bf16[2,192,1024]{2,1,0:T(8,128)(2,1)}, u32[]{:S(2)}) copy-start(bf16[2,192,1024]{2,1,0:T(8,128)(2,1)} %get-tuple-element.113) | copy-start | bytes 2359300
  271.5 17.6 %collective-permute-start.44 = (bf16[96,1792]{1,0:T(8,128)(2,1)S(1)}, bf16[96,1792]{1,0:T(8,128)(2,1)S(1)}, u32[]{:S(2)}, u32[]{:S(2)}) collective-permute-start(bf16[96,1792]{1,0:T(8,128)(2,1)S(1)} %get-tuple-element.174), channel_id=1, source_target_pairs={{0,1},{3,2},{4,5},{7,6},{8,9},{11,10},{12,13},{15,14},{16,17},{19,... | collective-permute-start | bytes 1032200 | tf_op jit(solution)/shard_map/ppermute | solution.py:702
  273.2 36.1 %collective-permute-start.42 = (bf16[96,1792]{1,0:T(8,128)(2,1)}, bf16[96,1792]{1,0:T(8,128)(2,1)}, u32[]{:S(2)}, u32[]{:S(2)}) collective-permute-start(bf16[96,1792]{1,0:T(8,128)(2,1)} %get-tuple-element.173), channel_id=1, source_target_pairs={{0,1},{1,2},{2,3},{4,5},{5,6},{6,7},{8,9},{9,10},{10,11},{12,13},{... | collective-permute-start | bytes 1032200 | tf_op jit(solution)/shard_map/ppermute | solution.py:702
  275.2 42.1 %collective-permute-start.43 = (bf16[96,1792]{1,0:T(8,128)(2,1)}, bf16[96,1792]{1,0:T(8,128)(2,1)}, u32[]{:S(2)}, u32[]{:S(2)}) collective-permute-start(bf16[96,1792]{1,0:T(8,128)(2,1)} %get-tuple-element.175), channel_id=1, source_target_pairs={{3,2},{2,1},{1,0},{7,6},{6,5},{5,4},{11,10},{10,9},{9,8},{15,14},{... | collective-permute-start | bytes 1032200 | tf_op jit(solution)/shard_map/ppermute | solution.py:702
  286.3 10.1 %collective-permute-start.27 = (bf16[192,1024]{1,0:T(8,128)(2,1)S(1)}, bf16[192,1024]{1,0:T(8,128)(2,1)S(1)}, u32[]{:S(2)}, u32[]{:S(2)}) collective-permute-start(bf16[192,1024]{1,0:T(8,128)(2,1)S(1)} %fusion.36), channel_id=1, source_target_pairs={{0,4},{4,0},{8,12},{12,8},{1,5},{5,1},{9,13},{13,9},{2,6},{6,2},{1... | collective-permute-start | bytes 1179656 | tf_op jit(solution)/shard_map/ppermute | solution.py:663
  287.5 10.1 %collective-permute-start.25 = (bf16[192,1024]{1,0:T(8,128)(2,1)S(1)}, bf16[192,1024]{1,0:T(8,128)(2,1)S(1)}, u32[]{:S(2)}, u32[]{:S(2)}) collective-permute-start(bf16[192,1024]{1,0:T(8,128)(2,1)S(1)} %fusion.35), channel_id=1, source_target_pairs={{0,8},{8,0},{4,12},{12,4},{1,9},{9,1},{5,13},{13,5},{2,10},{10,2},... | collective-permute-start | bytes 1179656 | tf_op jit(solution)/shard_map/ppermute | solution.py:664
  289.8 28.8 %collective-permute-start.45 = (bf16[96,1792]{1,0:T(8,128)(2,1)}, bf16[96,1792]{1,0:T(8,128)(2,1)}, u32[]{:S(2)}, u32[]{:S(2)}) collective-permute-start(bf16[96,1792]{1,0:T(8,128)(2,1)} %fusion.33), channel_id=1, source_target_pairs={{0,2},{1,3},{2,0},{3,1},{4,6},{5,7},{6,4},{7,5},{8,10},{9,11},{10,... | collective-permute-start | bytes 1032200 | tf_op jit(solution)/shard_map/ppermute | solution.py:702
  306.2 38.8 %collective-permute-start.31 = (bf16[4,384,768]{2,1,0:T(8,128)(2,1)}, bf16[4,384,768]{2,1,0:T(8,128)(2,1)}, u32[]{:S(2)}, u32[]{:S(2)}) collective-permute-start(bf16[4,384,768]{2,1,0:T(8,128)(2,1)} %slice.197.refs_4_), channel_id=1, source_target_pairs={{0,16},{16,0},{1,17},{17,1},{2,18},{18,2},{3,19},{19,3},{4,20},{20... | collective-permute-start | bytes 7077896 | tf_op jit(solution)/shard_map/ppermute | solution.py:662
  307.1 15.7 %collective-permute-start.32 = (bf16[1,384,640]{2,1,0:T(8,128)(2,1)S(1)}, bf16[1,384,640]{2,1,0:T(8,128)(2,1)S(1)}, u32[]{:S(2)}, u32[]{:S(2)}) collective-permute-start(bf16[1,384,640]{2,1,0:T(8,128)(2,1)S(1)} %get-tuple-element.176), channel_id=1, source_target_pairs={{0,16},{16,0},{1,17},{17,1},{2,18},{18,2},{3,19},{19,3},{4,20},{20... | collective-permute-start | bytes 1474568 | tf_op jit(solution)/shard_map/ppermute | solution.py:662
  309.3 31.8 %collective-permute-start.30 = (bf16[576,256]{1,0:T(8,128)(2,1)}, bf16[576,256]{1,0:T(8,128)(2,1)}, u32[]{:S(2)}, u32[]{:S(2)}) collective-permute-start(bf16[576,256]{1,0:T(8,128)(2,1)} %pad_maximum_fusion.9), channel_id=1, source_target_pairs={{0,3},{1,0},{2,1},{3,2},{4,7},{5,4},{6,5},{7,6},{8,11},{9,8},{10,9... | collective-permute-start | bytes 884744 | tf_op jit(solution)/shard_map/ppermute | solution.py:665
  317.2 27.7 %collective-permute-start.29 = (bf16[576,256]{1,0:T(8,128)(2,1)S(1)}, bf16[576,256]{1,0:T(8,128)(2,1)}, u32[]{:S(2)}, u32[]{:S(2)}) collective-permute-start(bf16[576,256]{1,0:T(8,128)(2,1)S(1)} %pad_maximum_fusion.8), channel_id=1, source_target_pairs={{0,2},{1,3},{2,0},{3,1},{4,6},{5,7},{6,4},{7,5},{8,10},{9,11},{10,... | collective-permute-start | bytes 884744 | tf_op jit(solution)/shard_map/ppermute | solution.py:665
  318.6 26.4 %collective-permute-start.28 = (bf16[576,256]{1,0:T(8,128)(2,1)S(1)}, bf16[576,256]{1,0:T(8,128)(2,1)}, u32[]{:S(2)}, u32[]{:S(2)}) collective-permute-start(bf16[576,256]{1,0:T(8,128)(2,1)S(1)} %pad_maximum_fusion.7), channel_id=1, source_target_pairs={{0,1},{1,2},{2,3},{3,0},{4,5},{5,6},{6,7},{7,4},{8,9},{9,10},{10,1... | collective-permute-start | bytes 884744 | tf_op jit(solution)/shard_map/ppermute | solution.py:665
  327.6 4.9 %collective-permute-start.38 = (bf16[2,1,96,256]{3,2,1,0:T(8,128)(2,1)}, bf16[2,1,96,256]{3,2,1,0:T(8,128)(2,1)S(1)}, u32[]{:S(2)}, u32[]{:S(2)}) collective-permute-start(bf16[2,1,96,256]{3,2,1,0:T(8,128)(2,1)} %get-tuple-element.122), channel_id=1, source_target_pairs={{0,8},{8,0},{4,12},{12,4},{1,9},{9,1},{5,13},{13,5},{2,10},{10,2},... | collective-permute-start | bytes 294920 | tf_op jit(solution)/shard_map/ppermute | solution.py:664
  332.5 5.6 %collective-permute-start.36 = (bf16[2,1,96,384]{3,2,1,0:T(8,128)(2,1)}, bf16[2,1,96,384]{3,2,1,0:T(8,128)(2,1)S(1)}, u32[]{:S(2)}, u32[]{:S(2)}) collective-permute-start(bf16[2,1,96,384]{3,2,1,0:T(8,128)(2,1)} %get-tuple-element.120), channel_id=1, source_target_pairs={{0,4},{4,0},{8,12},{12,8},{1,5},{5,1},{9,13},{13,9},{2,6},{6,2},{1... | collective-permute-start | bytes 442376 | tf_op jit(solution)/shard_map/ppermute | solution.py:663
  338.1 13.0 %collective-permute-start.39 = (bf16[1,96,256]{2,1,0:T(8,128)(2,1)S(1)}, bf16[1,96,256]{2,1,0:T(8,128)(2,1)S(1)}, u32[]{:S(2)}, u32[]{:S(2)}) collective-permute-start(bf16[1,96,256]{2,1,0:T(8,128)(2,1)S(1)} %fusion.49), channel_id=1, source_target_pairs={{0,4},{4,0},{8,12},{12,8},{1,5},{5,1},{9,13},{13,9},{2,6},{6,2},{1... | collective-permute-start | bytes 147464 | tf_op jit(solution)/shard_map/ppermute | solution.py:663
  341.1 14.6 %collective-permute-start.37 = (bf16[1,96,384]{2,1,0:T(8,128)(2,1)S(1)}, bf16[1,96,384]{2,1,0:T(8,128)(2,1)S(1)}, u32[]{:S(2)}, u32[]{:S(2)}) collective-permute-start(bf16[1,96,384]{2,1,0:T(8,128)(2,1)S(1)} %fusion.48), channel_id=1, source_target_pairs={{0,8},{8,0},{4,12},{12,4},{1,9},{9,1},{5,13},{13,5},{2,10},{10,2},... | collective-permute-start | bytes 221192 | tf_op jit(solution)/shard_map/ppermute | solution.py:664
  351.1 1.4 collective-permute-start.46
  353.3 4.4 %collective-permute-start.47 = (f32[16,768]{1,0:T(8,128)S(1)}, f32[16,768]{1,0:T(8,128)S(1)}, u32[]{:S(2)}, u32[]{:S(2)}) collective-permute-start(f32[16,768]{1,0:T(8,128)S(1)} %add.323), channel_id=1, source_target_pairs={{0,4},{4,0},{8,12},{12,8},{1,5},{5,1},{9,13},{13,9},{2,6},{6,2},{1... | collective-permute-start | bytes 147464 | tf_op jit(solution)/shard_map/ppermute | solution.py:663
  357.7 8.7 %collective-permute-start.48 = (f32[16,768]{1,0:T(8,128)S(1)}, f32[16,768]{1,0:T(8,128)S(1)}, u32[]{:S(2)}, u32[]{:S(2)}) collective-permute-start(f32[16,768]{1,0:T(8,128)S(1)} %add.324), channel_id=1, source_target_pairs={{0,8},{8,0},{4,12},{12,4},{1,9},{9,1},{5,13},{13,5},{2,10},{10,2},... | collective-permute-start | bytes 147464 | tf_op jit(solution)/shard_map/ppermute | solution.py:664
  362.0 39.9 %collective-permute-start.33 = (bf16[256,768]{1,0:T(8,128)(2,1)S(1)}, bf16[256,768]{1,0:T(8,128)(2,1)S(1)}, u32[]{:S(2)}, u32[]{:S(2)}) collective-permute-start(bf16[256,768]{1,0:T(8,128)(2,1)S(1)} %copy-done.23), channel_id=1, source_target_pairs={{0,1},{1,2},{2,3},{3,0},{4,5},{5,6},{6,7},{7,4},{8,9},{9,10},{10,1... | collective-permute-start | bytes 1179656 | tf_op jit(solution)/shard_map/ppermute | solution.py:665
  362.1 39.9 %collective-permute-start.34 = (bf16[256,768]{1,0:T(8,128)(2,1)S(1)}, bf16[256,768]{1,0:T(8,128)(2,1)S(1)}, u32[]{:S(2)}, u32[]{:S(2)}) collective-permute-start(bf16[256,768]{1,0:T(8,128)(2,1)S(1)} %copy-done.23), channel_id=1, source_target_pairs={{0,2},{1,3},{2,0},{3,1},{4,6},{5,7},{6,4},{7,5},{8,10},{9,11},{10,... | collective-permute-start | bytes 1179656 | tf_op jit(solution)/shard_map/ppermute | solution.py:665
  363.5 38.5 %collective-permute-start.35 = (bf16[256,768]{1,0:T(8,128)(2,1)S(1)}, bf16[256,768]{1,0:T(8,128)(2,1)S(1)}, u32[]{:S(2)}, u32[]{:S(2)}) collective-permute-start(bf16[256,768]{1,0:T(8,128)(2,1)S(1)} %copy-done.23), channel_id=1, source_target_pairs={{0,3},{1,0},{2,1},{3,2},{4,7},{5,4},{6,5},{7,6},{8,11},{9,8},{10,9... | collective-permute-start | bytes 1179656 | tf_op jit(solution)/shard_map/ppermute | solution.py:665
  366.4 24.6 %collective-permute-start.49 = (f32[16,768]{1,0:T(8,128)S(1)}, f32[16,768]{1,0:T(8,128)S(1)}, u32[]{:S(2)}, u32[]{:S(2)}) collective-permute-start(f32[16,768]{1,0:T(8,128)S(1)} %add.325), channel_id=1, source_target_pairs={{0,1},{1,0},{2,3},{3,2},{4,5},{5,4},{6,7},{7,6},{8,9},{9,8},{10,11... | collective-permute-start | bytes 147464 | tf_op jit(solution)/shard_map/ppermute | solution.py:921
  391.0 9.6 %collective-permute-start.50 = (f32[16,768]{1,0:T(8,128)S(1)}, f32[16,768]{1,0:T(8,128)S(1)}, u32[]{:S(2)}, u32[]{:S(2)}) collective-permute-start(f32[16,768]{1,0:T(8,128)S(1)} %add.326), channel_id=1, source_target_pairs={{0,2},{2,0},{1,3},{3,1},{4,6},{6,4},{5,7},{7,5},{8,10},{10,8},{9,1... | collective-permute-start | bytes 147464 | tf_op jit(solution)/shard_map/ppermute | solution.py:922
  (34 other events, 129.2 us)
Sparse Core Ops, SparseCore 0:
  206.8 96.0 all-gather.2

commit v7 on v6

--- a/solution.py
+++ b/solution.py
@@ -546,7 +546,8 @@
     )(place, *grads, w[0], w[1], x, grad_mid, table, mid_sums, fc_sums)
 
 
-def fold_kernel(cut, sc, mine, theirs, lo_send, lo_keep, hi_send, hi_keep):
+def fold_kernel(cut, sc, mine, theirs, *refs):
+    lo_send, lo_keep, hi_send, hi_keep = refs[-4:]
     i = pl.program_id(0)
     total = (mine[...].astype(f32) + theirs[...].astype(f32)).astype(bf16)
     lo, hi = total[None, :, :, :cut], total[None, :, :, cut:]
@@ -568,7 +569,7 @@
         hi_keep[...] = hi
 
 
-def fold(place, mine, theirs):
+def fold(place, mine, theirs, hold):
     parts, rows, wide = mine.shape
     size = rows // 4
     cut = (wide // 256) * 128 if wide % 256 == 0 else (wide // 256 + 1) * 128
@@ -589,7 +590,7 @@
         grid_spec=pltpu.PrefetchScalarGridSpec(
             num_scalar_prefetch=1,
             grid=(4,),
-            in_specs=[block, block],
+            in_specs=[block, block] + [HBM] * len(hold),
             out_specs=[
                 out(lo, lambda i: jnp.minimum(i, 1)),
                 out(lo, lambda i: jnp.where(i == 3, 0, 1)),
@@ -606,7 +607,7 @@
         compiler_params=params(),
         cost_estimate=cost(1 + 6 * parts / 4),
         name="fold",
-    )(place, mine, theirs)
+    )(place, mine, theirs, *hold)
 
 
 def body(
@@ -710,12 +711,12 @@
             pieces[0].astype(f32) + right.astype(f32) + left.astype(f32) + two.astype(f32)
         )
 
-    def scatter_begin(mine, theirs):
+    def scatter_begin(mine, theirs, hold=()):
         theirs = swap(theirs)
         if not grouped:
             both = (mine.astype(f32) + theirs.astype(f32)).astype(bf16)
             return lax.psum_scatter(both, "context", scatter_dimension=1, tiled=True)
-        return fold(place, mine, theirs)
+        return fold(place, mine, theirs, hold)
 
     def scatter_first(state):
         if not grouped:
@@ -831,36 +832,24 @@
             whole = lax.dynamic_update_slice_in_dim(whole, pieces[d].astype(f32), at, 0)
         return whole[None]
 
-    folded = scatter_begin(g_own, g_other)
-    hop_one = folded[0] if grouped else folded
+
     qkv_wide = jnp.pad(qkv_own, ((0, 0), (0, width - 3 * cols)))
     carried = jnp.concatenate([outputs_sub, qkv_wide], axis=0)
-    folded = scatter_begin(g_own, g_other)
-    hop_one = folded[0] if grouped else folded
-    qkv_wide = jnp.pad(qkv_own, ((0, 0), (0, width - 3 * cols)))
-    outputs_and_qkv = lax.all_gather(
-        jnp.concatenate([outputs_sub, qkv_wide], axis=0), "tensor", axis=0
-    )
-    wide = scatter_first(folded)
-    wide_sends = wide[2:]
-    wide = scatter_second(wide)
-
-    dq_pieces, dkv_pieces, dqkv = [], [], []
+
     head = 0
     queries, keys, values = [], [], []
     sent = [[] for _ in range(n_tensor)]
     for g, held, (lse, ot) in zip(GROUPS, kv, saved):
         out = attend_back(
-            scalars, row(starts), after(qt, hop_one), lse, ot, do_parts, held, carried, head, g, BK_B, BQ_B
+            scalars, row(starts), qt, lse, ot, do_parts, held, carried, head, g, BK_B, BQ_B
         )
-        back_done = out[-1]
         *out, carried = out
-        dq, dkv = after(out[:n_tensor], wide_sends), out[n_tensor:]
+        dq, dkv = out[:n_tensor], out[n_tensor:]
         if grouped:
             dk_keep, dk_send, dv_keep, dv_send = dkv
-            dk_send, dv_send = after((dk_send, dv_send), wide_sends)
-            r = along_x(dk_send).astype(f32)
-            s = along_y(dv_send).astype(f32)
+            r, s = along_x(dk_send), along_y(dv_send)
+            hold = (r, s)
+            r, s = r.astype(f32), s.astype(f32)
             r2 = along_y((dk_keep[1].astype(f32) + r[1]).astype(bf16)).astype(f32)
             s2 = along_x((dv_keep[1].astype(f32) + s[1]).astype(bf16)).astype(f32)
             dk = (dk_keep[0].astype(f32) + r[0] + r2).astype(bf16)
@@ -873,6 +862,10 @@
         values.append(dv)
         head += g
 
+    folded = scatter_begin(g_own, g_other, hold)
+    wide = scatter_first(folded)
+    both_sends = after(jnp.concatenate(keys + values, axis=0), wide[2:] if grouped else wide)
+    wide = scatter_second(wide)
     wide_grads = scatter_line([wide[d] for d in range(n_tensor)])
 
     def part_of(v, d):
@@ -882,7 +875,7 @@
     grads = []
     both = jnp.concatenate(keys + values, axis=0)
     for d in range(n_tensor):
-        piece = jnp.concatenate([q[d] for q in queries] + [part_of(both, d)], axis=0)
+        piece = jnp.concatenate([q[d] for q in queries] + [part_of(both_sends, d)], axis=0)
         grads.append(shift_by(piece, d) if d else piece)
     pieces = 1
 

time: 412 us -> 424 us (1.029)
  waiting for transfers between devices: 170 us -> 181 us
  local copies, waits for them, and re-layouts: 22.4 us -> 28.1 us
  starting transfers between devices: 101 us -> 95.6 us
    ppermute x4, waiting for transfers between devices: 0.01 us -> 21 us  [scatter_line(): move = lambda a, perm: lax.ppermute(a.astype(bf16), 'tensor', perm)]
    ppermute x12, waiting for transfers between devices: 9.31 us -> 18.5 us  [body(): lax.ppermute(v, 'tensor', [(s, (s + d) % n_tensor) for s in range(n_tenso...]
    ppermute x9, waiting for transfers between devices: 53.1 us -> 44.6 us  [body(): lax.ppermute(v, 'context', [(0, 2), (2, 0), (1, 3), (3, 1)])]
    ppermute x12, starting transfers between devices: 29.4 us -> 21.4 us  [body(): lax.ppermute(v, 'tensor', [(s, (s + d) % n_tensor) for s in range(n_tenso...]
    ppermute x7, waiting for transfers between devices: 9.57 us -> 3.21 us  [body(): swap = lambda v: lax.ppermute(v, 'shard', [(0, 1), (1, 0)])]
    ppermute x6, waiting for transfers between devices: 30.9 us -> 25.7 us  [gather_begin(): move = lambda perm: lax.ppermute(v, 'tensor', perm)]
    unnamed x100 -> x118, local copies, waits for them, and re-layouts: 9.17 us -> 11 us
  transfers between devices with their start and end apart: 52 -> 52, of which waited for: 26 -> 26; matrix products, arithmetic and copies ran while one was open for 10% -> 12% of each run, Pallas kernels for 8% -> 11%
where the time goes in v7:
time: 424 us; the launch traced here: 422 us
  waiting for transfers between devices  181 us (43%)
  starting transfers between devices  95.6 us (23%)
  Pallas kernels  70.1 us (17%)
  other arithmetic  31.3 us (7%)
  local copies, waits for them, and re-layouts  28.1 us (7%)
  between operations  15.1 us (4%)
    ppermute x9, waiting for transfers between devices, body(): lax.ppermute(v, 'context', [(0, 2), (2, 0), (1, 3), (3, 1)])  44.6 us
    ppermute x9, waiting for transfers between devices, body(): lax.ppermute(v, 'context', [(0, 1), (1, 0), (2, 3), (3, 2)])  27 us
    ppermute x9, starting transfers between devices, body(): lax.ppermute(v, 'context', [(0, 2), (2, 0), (1, 3), (3, 1)])  26.9 us
    ppermute x6, waiting for transfers between devices, gather_begin(): move = lambda perm: lax.ppermute(v, 'tensor', perm)  25.7 us
    ppermute x6, starting transfers between devices, gather_begin(): move = lambda perm: lax.ppermute(v, 'tensor', perm)  24.8 us
    pallas_call x1, Pallas kernels, middle(): pl.pallas_call(functools.partial(middle_kernel, len(att), parts), grid_sp...  22.8 us
    ppermute x12, starting transfers between devices, body(): lax.ppermute(v, 'tensor', [(s, (s + d) % n_tensor) for s in range(n_tenso...  21.4 us
    ppermute x1, waiting for transfers between devices, body(): small += lax.ppermute(small, 'tensor', [(0, 1), (1, 0), (2, 3), (3, 2)])  21.2 us
  transfers between devices with their start and end apart: 52, of which 26 were waited for; matrix products, arithmetic and copies ran while one was open for 12% of the time, Pallas kernels for 11%

profile of v7, /device:TPU:0, one launch (start us, length us, event | category | flops | bytes accessed | tf_op | source)
XLA Modules:
  0.0 422.5 jit_solution(15673052047577605350)
XLA Ops:
  10.3 4.1 collective-permute-start.1
  14.4 4.4 %collective-permute-start.2 = (bf16[976,384]{1,0:T(8,128)(2,1)S(1)}, bf16[976,384]{1,0:T(8,128)(2,1)}, u32[]{:S(2)}, u32[]{:S(2)}) collective-permute-start(bf16[976,384]{1,0:T(8,128)(2,1)S(1)} %pad_maximum_fusion.5), channel_id=1, source_target_pairs={{0,1},{1,2},{2,3},{4,5},{5,6},{6,7},{8,9},{9,10},{10,11},{12,13},{... | collective-permute-start | bytes 2248712 | tf_op jit(solution)/shard_map/ppermute | solution.py:676
  23.0 6.3 %project.1 = (bf16[1024,768]{1,0:T(8,128)(2,1)}, bf16[192,1024]{1,0:T(8,128)(2,1)}, bf16[192,1024]{1,0:T(8,128)(2,1)}, bf16[192,1024]{1,0:T(8,128)(2,1)}) custom-call(s32[4]{0:T(128)} %pad_add_fusion.1.sc, bf16[1024,768]{1,0:T(8,128)(2,1)} %bitcast.127, bf16[384,576]{1,0:T(8,128)(2,1)} %copy-done.7, bf16[384,576]{1,0:T(8,128)(2,1)} %copy-done.43, ...), custom_call_target="tpu_custom_call" | custom-call | flops 8049999872 | bytes 1048576 | tf_op jit(solution)/shard_map/project/pallas_call | solution.py:90
  29.4 1.6 collective-permute-start.4
  30.9 1.5 collective-permute-start.5
  32.4 8.4 %collective-permute-done.4.refs_1_.refs_5_ = bf16[192,1024]{1,0:T(8,128)(2,1)S(1)} collective-permute-done((bf16[192,1024]{1,0:T(8,128)(2,1)}, bf16[192,1024]{1,0:T(8,128)(2,1)S(1)}, u32[]{:S(2)}, u32[]{:S(2)}) %collective-permute-start.4) | collective-permute-done | bytes 393248 | tf_op jit(solution)/shard_map/ppermute | solution.py:664
  42.1 6.1 %collective-permute-done.1 = bf16[976,384]{1,0:T(8,128)(2,1)} collective-permute-done((bf16[976,384]{1,0:T(8,128)(2,1)S(1)}, bf16[976,384]{1,0:T(8,128)(2,1)}, u32[]{:S(2)}, u32[]{:S(2)}) %collective-permute-start.1) | collective-permute-done | bytes 749600 | tf_op jit(solution)/shard_map/ppermute | solution.py:676
  48.2 5.4 %collective-permute-done.3 = bf16[976,384]{1,0:T(8,128)(2,1)} collective-permute-done((bf16[976,384]{1,0:T(8,128)(2,1)S(1)}, bf16[976,384]{1,0:T(8,128)(2,1)}, u32[]{:S(2)}, u32[]{:S(2)}) %collective-permute-start.3) | collective-permute-done | bytes 749600 | tf_op jit(solution)/shard_map/ppermute | solution.py:676
  53.6 1.6 collective-permute-start.6
  55.1 1.5 collective-permute-start.7
  57.9 3.8 fusion.59
  62.6 12.4 %collective-permute-start.13 = (bf16[768,384]{1,0:T(8,128)(2,1)}, bf16[768,384]{1,0:T(8,128)(2,1)}, u32[]{:S(2)}, u32[]{:S(2)}) collective-permute-start(bf16[768,384]{1,0:T(8,128)(2,1)} %param.20), channel_id=1, source_target_pairs={{0,2},{1,3},{2,0},{3,1},{4,6},{5,7},{6,4},{7,5},{8,10},{9,11},{10,... | collective-permute-start | bytes 1769480 | tf_op jit(solution)/shard_map/ppermute | solution.py:676
  77.2 9.5 %attend.1 = (f32[3,1024]{1,0:T(4,128)}, bf16[192,1024]{1,0:T(8,128)(2,1)}, bf16[192,256]{1,0:T(8,128)(2,1)}, bf16[192,256]{1,0:T(8,128)(2,1)}, bf16[192,256]{1,0:T(8,128)(2,1)}, /*index=5*/bf16[192,256]{1,0:T(8,128)(2,1)}) custom-call(s32[12]{0:T(128)} %concatenate.45.sc, bf16[192,1024]{1,0:T(8,128)(2,1)} %get-tuple-element.67.qt, ...), custom_call_target="tpu_custom_call" | custom-call | flops 23000000512 | bytes 1048576 | tf_op jit(solution)/shard_map/attend/pallas_call | solution.py:221
  86.8 7.7 %collective-permute-start.8 = (bf16[192,256]{1,0:T(8,128)(2,1)}, bf16[192,256]{1,0:T(8,128)(2,1)S(1)}, u32[]{:S(2)}, u32[]{:S(2)}) collective-permute-start(bf16[192,256]{1,0:T(8,128)(2,1)} %get-tuple-element.75), channel_id=1, source_target_pairs={{0,1},{1,2},{2,3},{3,0},{4,5},{5,6},{6,7},{7,4},{8,9},{9,10},{10,1... | collective-permute-start | bytes 294920 | tf_op jit(solution)/shard_map/ppermute | solution.py:666
  94.5 2.1 collective-permute-start.9
  96.6 2.8 collective-permute-start.10
  99.4 6.1 %collective-permute-done.13 = bf16[768,384]{1,0:T(8,128)(2,1)} collective-permute-done((bf16[768,384]{1,0:T(8,128)(2,1)}, bf16[768,384]{1,0:T(8,128)(2,1)}, u32[]{:S(2)}, u32[]{:S(2)}) %collective-permute-start.13) | collective-permute-done | bytes 589856 | tf_op jit(solution)/shard_map/ppermute | solution.py:676
  108.2 7.5 %collective-permute-done.10.refs_3_ = bf16[192,256]{1,0:T(8,128)(2,1)S(1)} collective-permute-done((bf16[192,256]{1,0:T(8,128)(2,1)}, bf16[192,256]{1,0:T(8,128)(2,1)S(1)}, u32[]{:S(2)}, u32[]{:S(2)}) %collective-permute-start.10) | collective-permute-done | bytes 98336 | tf_op jit(solution)/shard_map/ppermute | solution.py:666
  115.6 1.5 collective-permute-start.14
  118.4 1.5 pad_maximum_fusion.refs_6_
  120.0 8.2 %collective-permute-done.16 = bf16[768,384]{1,0:T(8,128)(2,1)S(1)} collective-permute-done((bf16[768,384]{1,0:T(8,128)(2,1)}, bf16[768,384]{1,0:T(8,128)(2,1)S(1)}, u32[]{:S(2)}, u32[]{:S(2)}) %collective-permute-start.16) | collective-permute-done | bytes 589856 | tf_op jit(solution)/shard_map/ppermute | solution.py:676
  128.3 10.8 %collective-permute-done.14 = bf16[768,384]{1,0:T(8,128)(2,1)S(1)} collective-permute-done((bf16[768,384]{1,0:T(8,128)(2,1)}, bf16[768,384]{1,0:T(8,128)(2,1)S(1)}, u32[]{:S(2)}, u32[]{:S(2)}) %collective-permute-start.14) | collective-permute-done | bytes 589856 | tf_op jit(solution)/shard_map/ppermute | solution.py:689
  139.2 3.0 pad_maximum_fusion.1.refs_8_
  142.2 2.1 dynamic-slice_bitcast_fusion.2
  144.3 2.8 collective-permute-done.17.refs_9_
  147.1 22.8 %middle.1 = (bf16[256,768]{1,0:T(8,128)(2,1)}, f32[256,768]{1,0:T(8,128)}, f32[4,768]{1,0:T(4,128)}, f32[4,1,768]{2,1,0:T(1,128)}, bf16[192,256]{1,0:T(8,128)(2,...) custom-call(s32[4]{0:T(128)} %pad_add_fusion.1.sc, ...), custom_call_target="tpu_custom_call" | custom-call | flops 21849999360 | bytes 1048576 | tf_op jit(solution)/shard_map/middle/pallas_call | solution.py:465
  171.9 2.0 fusion.13.refs_10_
  173.9 2.1 collective-permute-done.18.refs_1_
  176.0 4.4 %collective-permute-done.19.refs_2_ = bf16[192,256]{1,0:T(8,128)(2,1)S(1)} collective-permute-done((bf16[192,256]{1,0:T(8,128)(2,1)}, bf16[192,256]{1,0:T(8,128)(2,1)S(1)}, u32[]{:S(2)}, u32[]{:S(2)}) %collective-permute-start.19) | collective-permute-done | bytes 98336 | tf_op jit(solution)/shard_map/ppermute | solution.py:666
  181.1 12.6 %attend_back.1 = (bf16[192,256]{1,0:T(8,128)(2,1)}, bf16[192,256]{1,0:T(8,128)(2,1)}, bf16[192,256]{1,0:T(8,128)(2,1)}, bf16[192,256]{1,0:T(8,128)(2,1)}, bf16[2...) custom-call(s32[12]{0:T(128)} %concatenate.45.sc, ...), custom_call_target="tpu_custom_call", output_to_operand_aliasing={{8}: (15, {})} | custom-call | flops 29899999232 | bytes 1048576 | tf_op jit(solution)/shard_map/attend_back/pallas_call | solution.py:327
  193.8 16.3 %collective-permute-start.23 = (bf16[2,192,1024]{2,1,0:T(8,128)(2,1)}, bf16[2,192,1024]{2,1,0:T(8,128)(2,1)S(1)}, u32[]{:S(2)}, u32[]{:S(2)}) collective-permute-start(bf16[2,192,1024]{2,1,0:T(8,128)(2,1)} %get-tuple-element.95), channel_id=1, source_target_pairs={{0,8},{8,0},{4,12},{12,4},{1,9},{9,1},{5,13},{13,5},{2,10},{10,2},... | collective-permute-start | bytes 2359304 | tf_op jit(solution)/shard_map/ppermute | solution.py:665
  211.2 16.7 %collective-permute-done.23.refs_1_ = bf16[2,192,1024]{2,1,0:T(8,128)(2,1)S(1)} collective-permute-done((bf16[2,192,1024]{2,1,0:T(8,128)(2,1)}, bf16[2,192,1024]{2,1,0:T(8,128)(2,1)S(1)}, u32[]{:S(2)}, u32[]{:S(2)}) %collective-permute-start.23) | collective-permute-done | bytes 786464 | tf_op jit(solution)/shard_map/ppermute | solution.py:665
  230.3 1.9 collective-permute-start.22
  232.2 7.2 %collective-permute-done.24 = bf16[192,1024]{1,0:T(8,128)(2,1)S(1)} collective-permute-done((bf16[192,1024]{1,0:T(8,128)(2,1)S(1)}, bf16[192,1024]{1,0:T(8,128)(2,1)S(1)}, u32[]{:S(2)}, u32[]{:S(2)}) %collective-permute-start.24) | collective-permute-done | bytes 393248 | tf_op jit(solution)/shard_map/ppermute | solution.py:664
  241.1 1.6 convolution_convert_fusion
  243.7 8.7 %fold.2 = (bf16[2,4,96,896]{3,2,1,0:T(8,128)(2,1)}, bf16[2,4,96,896]{3,2,1,0:T(8,128)(2,1)}, bf16[2,4,96,896]{3,2,1,0:T(8,128)(2,1)}, bf16[2,4,96,896]{3,2,1,0:T(8,128)(2,1)}) custom-call(s32[4]{0:T(128)} %pad_add_fusion.1.sc, bf16[4,384,1792]{2,1,0:T(8,128)(2,1)} %get-tuple-element.96.mine, bf16[4,384,1792]{2,1,0:T(8,128)(2,1)} %collective-permute-done.25.theirs, ...), custom_call_target="tpu_custom_call" | custom-call | flops 8049999872 | bytes 1048576 | tf_op jit(solution)/shard_map/fold/pallas_call | solution.py:588
  255.6 4.1 fold.3
  261.6 26.5 %collective-permute-done.38 = bf16[2,1,96,256]{3,2,1,0:T(8,128)(2,1)S(1)} collective-permute-done((bf16[2,1,96,256]{3,2,1,0:T(8,128)(2,1)}, bf16[2,1,96,256]{3,2,1,0:T(8,128)(2,1)S(1)}, u32[]{:S(2)}, u32[]{:S(2)}) %collective-permute-start.38) | collective-permute-done | bytes 98336 | tf_op jit(solution)/shard_map/ppermute | solution.py:665
  289.2 1.5 collective-permute-start.37
  290.7 1.6 collective-permute-done.39
  292.9 1.6 convert_element_type.266
  295.7 1.4 collective-permute-start.40
  297.8 3.2 slice.197.refs_4_
  301.0 1.6 convert_element_type.270
  305.4 1.8 copy.36
  307.2 1.8 copy.37
  309.1 2.7 slice.190
  313.1 1.5 fusion.4
  314.7 7.1 %collective-permute-done.41 = bf16[4,96,896]{2,1,0:T(8,128)(2,1)} collective-permute-done((bf16[4,96,896]{2,1,0:T(8,128)(2,1)}, bf16[4,96,896]{2,1,0:T(8,128)(2,1)}, u32[]{:S(2)}, u32[]{:S(2)}) %collective-permute-start.41) | collective-permute-done | bytes 688160 | tf_op jit(solution)/shard_map/ppermute | solution.py:664
  323.3 1.4 collective-permute-start.44
  325.5 2.2 collective-permute-start.30
  328.4 4.7 %collective-permute-done.44 = bf16[96,1792]{1,0:T(8,128)(2,1)S(1)} collective-permute-done((bf16[96,1792]{1,0:T(8,128)(2,1)S(1)}, bf16[96,1792]{1,0:T(8,128)(2,1)S(1)}, u32[]{:S(2)}, u32[]{:S(2)}) %collective-permute-start.44) | collective-permute-done | bytes 344096 | tf_op jit(solution)/shard_map/ppermute | solution.py:703
  334.5 5.0 %collective-permute-start.42 = (bf16[96,1792]{1,0:T(8,128)(2,1)S(1)}, bf16[96,1792]{1,0:T(8,128)(2,1)S(1)}, u32[]{:S(2)}, u32[]{:S(2)}) collective-permute-start(bf16[96,1792]{1,0:T(8,128)(2,1)S(1)} %get-tuple-element.161), channel_id=1, source_target_pairs={{0,1},{1,2},{2,3},{4,5},{5,6},{6,7},{8,9},{9,10},{10,11},{12,13},{... | collective-permute-start | bytes 1032200 | tf_op jit(solution)/shard_map/ppermute | solution.py:703
  339.6 1.7 collective-permute-done.29.refs_2_
  341.3 1.7 collective-permute-start.45
  343.0 2.9 collective-permute-done.30.refs_3_
  346.6 6.1 %last.1 = (bf16[256,768]{1,0:T(8,128)(2,1)}, f32[16,768]{1,0:T(8,128)}) custom-call(s32[4]{0:T(128)} %pad_add_fusion.1.sc, bf16[576,256]{1,0:T(8,128)(2,1)} %pad_maximum_fusion.7.refs_0_, bf16[576,256]{1,0:T(8,128)(2,1)} %copy-done.44, bf16[576,256]{1,0:T(8,128)(2,1)} %copy-done.45, bf16[576,256]{1,0:T(8,128)(2,1)} %copy-done.46, ...), custom_call_target="tpu_custom_call" | custom-call | flops 6899999744 | bytes 1048576 | tf_op jit(solution)/shard_map/last/pallas_call | solution.py:537
  353.2 15.7 %collective-permute-done.45 = bf16[96,1792]{1,0:T(8,128)(2,1)S(1)} collective-permute-done((bf16[96,1792]{1,0:T(8,128)(2,1)S(1)}, bf16[96,1792]{1,0:T(8,128)(2,1)S(1)}, u32[]{:S(2)}, u32[]{:S(2)}) %collective-permute-start.45) | collective-permute-done | bytes 344096 | tf_op jit(solution)/shard_map/ppermute | solution.py:703
  371.0 2.3 collective-permute-done.47
  374.7 2.9 collective-permute-start.34
  379.8 1.9 bitcast_convert_fusion
  381.7 21.2 %collective-permute-done.49 = f32[16,768]{1,0:T(8,128)S(1)} collective-permute-done((f32[16,768]{1,0:T(8,128)S(1)}, f32[16,768]{1,0:T(8,128)S(1)}, u32[]{:S(2)}, u32[]{:S(2)}) %collective-permute-start.49) | collective-permute-done | bytes 49184 | tf_op jit(solution)/shard_map/ppermute | solution.py:914
  403.9 8.6 %collective-permute-done.50 = f32[16,768]{1,0:T(8,128)S(1)} collective-permute-done((f32[16,768]{1,0:T(8,128)S(1)}, f32[16,768]{1,0:T(8,128)S(1)}, u32[]{:S(2)}, u32[]{:S(2)}) %collective-permute-start.50) | collective-permute-done | bytes 49184 | tf_op jit(solution)/shard_map/ppermute | solution.py:915
  414.0 1.7 copy-done.3
  (251 shorter events, 52.2 us)
Async XLA Ops:
  7.2 13.3 %copy-start.39 = (f32[768]{0:T(1024)S(1)}, f32[768]{0:T(1024)}, u32[]{:S(2)}) copy-start(f32[768]{0:T(1024)} %param.27) | copy-start | bytes 9220
  7.2 13.3 %copy-start.40 = (f32[768]{0:T(1024)S(1)}, f32[768]{0:T(1024)}, u32[]{:S(2)}) copy-start(f32[768]{0:T(1024)} %param.28) | copy-start | bytes 9220
  7.3 290.5 %all-gather.3.cloned.1.call-start = ((), (), s32[]{:S(2)}) async-start(), calls=%async_computation | async-start | bytes 4915200 | tf_op jit(solution)/shard_map/all_gather | solution.py:889
  10.3 19.1 %copy-start.5 = (bf16[976,384]{1,0:T(8,128)(2,1)}, bf16[976,384]{1,0:T(8,128)(2,1)S(1)}, u32[]{:S(2)}) copy-start(bf16[976,384]{1,0:T(8,128)(2,1)S(1)} %pad_maximum_fusion.5) | copy-start | bytes 2248708
  10.3 37.9 %collective-permute-start.1 = (bf16[976,384]{1,0:T(8,128)(2,1)S(1)}, bf16[976,384]{1,0:T(8,128)(2,1)}, u32[]{:S(2)}, u32[]{:S(2)}) collective-permute-start(bf16[976,384]{1,0:T(8,128)(2,1)S(1)} %pad_maximum_fusion.5), channel_id=1, source_target_pairs={{0,2},{1,3},{2,0},{3,1},{4,6},{5,7},{6,4},{7,5},{8,10},{9,11},{10,... | collective-permute-start | bytes 2248712 | tf_op jit(solution)/shard_map/ppermute | solution.py:676
  14.4 33.8 %collective-permute-start.2 = (bf16[976,384]{1,0:T(8,128)(2,1)S(1)}, bf16[976,384]{1,0:T(8,128)(2,1)}, u32[]{:S(2)}, u32[]{:S(2)}) collective-permute-start(bf16[976,384]{1,0:T(8,128)(2,1)S(1)} %pad_maximum_fusion.5), channel_id=1, source_target_pairs={{0,1},{1,2},{2,3},{4,5},{5,6},{6,7},{8,9},{9,10},{10,11},{12,13},{... | collective-permute-start | bytes 2248712 | tf_op jit(solution)/shard_map/ppermute | solution.py:676
  18.8 34.8 %collective-permute-start.3 = (bf16[976,384]{1,0:T(8,128)(2,1)S(1)}, bf16[976,384]{1,0:T(8,128)(2,1)}, u32[]{:S(2)}, u32[]{:S(2)}) collective-permute-start(bf16[976,384]{1,0:T(8,128)(2,1)S(1)} %pad_maximum_fusion.5), channel_id=1, source_target_pairs={{3,2},{2,1},{1,0},{7,6},{6,5},{5,4},{11,10},{10,9},{9,8},{15,14},{... | collective-permute-start | bytes 2248712 | tf_op jit(solution)/shard_map/ppermute | solution.py:676
  20.3 1.9 collective-permute-start
  29.4 11.4 %collective-permute-start.4 = (bf16[192,1024]{1,0:T(8,128)(2,1)}, bf16[192,1024]{1,0:T(8,128)(2,1)S(1)}, u32[]{:S(2)}, u32[]{:S(2)}) collective-permute-start(bf16[192,1024]{1,0:T(8,128)(2,1)} %get-tuple-element.68.refs_0_.refs_4_), channel_id=1, source_target_pairs={{0,4},{4,0},{8,12},{12,8},{1,5},{5,1},{9,13},{13,9},{2,6},{6,2},{1... | collective-permute-start | bytes 1179656 | tf_op jit(solution)/shard_map/ppermute | solution.py:664
  30.9 11.1 %collective-permute-start.5 = (bf16[192,1024]{1,0:T(8,128)(2,1)}, bf16[192,1024]{1,0:T(8,128)(2,1)S(1)}, u32[]{:S(2)}, u32[]{:S(2)}) collective-permute-start(bf16[192,1024]{1,0:T(8,128)(2,1)} %get-tuple-element.69.refs_3_.refs_7_), channel_id=1, source_target_pairs={{0,8},{8,0},{4,12},{12,4},{1,9},{9,1},{5,13},{13,5},{2,10},{10,2},... | collective-permute-start | bytes 1179656 | tf_op jit(solution)/shard_map/ppermute | solution.py:665
  40.8 15.9 %copy-start.34 = (s32[1,4096]{1,0:T(1,128)S(1)}, s32[1,4096]{1,0:T(1,128)}, u32[]{:S(2)}) copy-start(s32[1,4096]{1,0:T(1,128)} %param.16) | copy-start | bytes 49156
  53.6 22.8 %collective-permute-start.6 = (bf16[2,192,1024]{2,1,0:T(8,128)(2,1)S(1)}, bf16[2,192,1024]{2,1,0:T(8,128)(2,1)S(1)}, u32[]{:S(2)}, u32[]{:S(2)}) collective-permute-start(bf16[2,192,1024]{2,1,0:T(8,128)(2,1)S(1)} %pad_maximum_fusion.2), channel_id=1, source_target_pairs={{0,8},{8,0},{4,12},{12,4},{1,9},{9,1},{5,13},{13,5},{2,10},{10,2},... | collective-permute-start | bytes 2359304 | tf_op jit(solution)/shard_map/ppermute | solution.py:665
  55.1 21.2 %collective-permute-start.7 = (bf16[2,192,1024]{2,1,0:T(8,128)(2,1)S(1)}, bf16[2,192,1024]{2,1,0:T(8,128)(2,1)}, u32[]{:S(2)}, u32[]{:S(2)}) collective-permute-start(bf16[2,192,1024]{2,1,0:T(8,128)(2,1)S(1)} %pad_maximum_fusion.3), channel_id=1, source_target_pairs={{0,4},{4,0},{8,12},{12,8},{1,5},{5,1},{9,13},{13,9},{2,6},{6,2},{1... | collective-permute-start | bytes 2359304 | tf_op jit(solution)/shard_map/ppermute | solution.py:664
  62.6 42.9 %collective-permute-start.13 = (bf16[768,384]{1,0:T(8,128)(2,1)}, bf16[768,384]{1,0:T(8,128)(2,1)}, u32[]{:S(2)}, u32[]{:S(2)}) collective-permute-start(bf16[768,384]{1,0:T(8,128)(2,1)} %param.20), channel_id=1, source_target_pairs={{0,2},{1,3},{2,0},{3,1},{4,6},{5,7},{6,4},{7,5},{8,10},{9,11},{10,... | collective-permute-start | bytes 1769480 | tf_op jit(solution)/shard_map/ppermute | solution.py:676
  75.0 42.1 %collective-permute-start.11 = (bf16[976,384]{1,0:T(8,128)(2,1)}, bf16[976,384]{1,0:T(8,128)(2,1)S(1)}, u32[]{:S(2)}, u32[]{:S(2)}) collective-permute-start(bf16[976,384]{1,0:T(8,128)(2,1)} %collective-permute-done.1), channel_id=1, source_target_pairs={{2,3},{1,0},{6,7},{5,4},{10,11},{9,8},{14,15},{13,12},{18,19},{17,... | collective-permute-start | bytes 2248712 | tf_op jit(solution)/shard_map/ppermute | solution.py:689
  86.8 20.0 %collective-permute-start.8 = (bf16[192,256]{1,0:T(8,128)(2,1)}, bf16[192,256]{1,0:T(8,128)(2,1)S(1)}, u32[]{:S(2)}, u32[]{:S(2)}) collective-permute-start(bf16[192,256]{1,0:T(8,128)(2,1)} %get-tuple-element.75), channel_id=1, source_target_pairs={{0,1},{1,2},{2,3},{3,0},{4,5},{5,6},{6,7},{7,4},{8,9},{9,10},{10,1... | collective-permute-start | bytes 294920 | tf_op jit(solution)/shard_map/ppermute | solution.py:666
  94.5 13.7 %collective-permute-start.9 = (bf16[192,256]{1,0:T(8,128)(2,1)}, bf16[192,256]{1,0:T(8,128)(2,1)S(1)}, u32[]{:S(2)}, u32[]{:S(2)}) collective-permute-start(bf16[192,256]{1,0:T(8,128)(2,1)} %get-tuple-element.76), channel_id=1, source_target_pairs={{0,2},{1,3},{2,0},{3,1},{4,6},{5,7},{6,4},{7,5},{8,10},{9,11},{10,... | collective-permute-start | bytes 294920 | tf_op jit(solution)/shard_map/ppermute | solution.py:666
  96.6 19.0 %collective-permute-start.10 = (bf16[192,256]{1,0:T(8,128)(2,1)}, bf16[192,256]{1,0:T(8,128)(2,1)S(1)}, u32[]{:S(2)}, u32[]{:S(2)}) collective-permute-start(bf16[192,256]{1,0:T(8,128)(2,1)} %get-tuple-element.77), channel_id=1, source_target_pairs={{0,3},{1,0},{2,1},{3,2},{4,7},{5,4},{6,5},{7,6},{8,11},{9,8},{10,9... | collective-permute-start | bytes 294920 | tf_op jit(solution)/shard_map/ppermute | solution.py:666
  99.4 19.0 %copy-start.6 = (bf16[976,384]{1,0:T(8,128)(2,1)S(1)}, bf16[976,384]{1,0:T(8,128)(2,1)}, u32[]{:S(2)}) copy-start(bf16[976,384]{1,0:T(8,128)(2,1)} %copy-done.5) | copy-start | bytes 2248708
  105.5 14.5 %collective-permute-start.15 = (bf16[768,384]{1,0:T(8,128)(2,1)}, bf16[768,384]{1,0:T(8,128)(2,1)S(1)}, u32[]{:S(2)}, u32[]{:S(2)}) collective-permute-start(bf16[768,384]{1,0:T(8,128)(2,1)} %param.20), channel_id=1, source_target_pairs={{0,1},{1,2},{2,3},{4,5},{5,6},{6,7},{8,9},{9,10},{10,11},{12,13},{... | collective-permute-start | bytes 1769480 | tf_op jit(solution)/shard_map/ppermute | solution.py:676
  106.8 21.4 %collective-permute-start.16 = (bf16[768,384]{1,0:T(8,128)(2,1)}, bf16[768,384]{1,0:T(8,128)(2,1)S(1)}, u32[]{:S(2)}, u32[]{:S(2)}) collective-permute-start(bf16[768,384]{1,0:T(8,128)(2,1)} %param.20), channel_id=1, source_target_pairs={{3,2},{2,1},{1,0},{7,6},{6,5},{5,4},{11,10},{10,9},{9,8},{15,14},{... | collective-permute-start | bytes 1769480 | tf_op jit(solution)/shard_map/ppermute | solution.py:676
  115.6 23.4 %collective-permute-start.14 = (bf16[768,384]{1,0:T(8,128)(2,1)}, bf16[768,384]{1,0:T(8,128)(2,1)S(1)}, u32[]{:S(2)}, u32[]{:S(2)}) collective-permute-start(bf16[768,384]{1,0:T(8,128)(2,1)} %collective-permute-done.13), channel_id=1, source_target_pairs={{2,3},{1,0},{6,7},{5,4},{10,11},{9,8},{14,15},{13,12},{18,19},{17,... | collective-permute-start | bytes 1769480 | tf_op jit(solution)/shard_map/ppermute | solution.py:689
  119.9 22.3 %copy-start.4 = (bf16[4,976,384]{2,1,0:T(8,128)(2,1)}, bf16[4,976,384]{2,1,0:T(8,128)(2,1)S(1)}, u32[]{:S(2)}) copy-start(bf16[4,976,384]{2,1,0:T(8,128)(2,1)S(1)} %pad_maximum_fusion.refs_6_) | copy-start | bytes 8994820
  119.9 27.1 %collective-permute-start.12 = (bf16[4,976,384]{2,1,0:T(8,128)(2,1)S(1)}, bf16[4,976,384]{2,1,0:T(8,128)(2,1)}, u32[]{:S(2)}, u32[]{:S(2)}) collective-permute-start(bf16[4,976,384]{2,1,0:T(8,128)(2,1)S(1)} %pad_maximum_fusion.refs_6_), channel_id=1, source_target_pairs={{0,16},{16,0},{1,17},{17,1},{2,18},{18,2},{3,19},{19,3},{4,20},{20... | collective-permute-start | bytes 8994824 | tf_op jit(solution)/shard_map/ppermute | solution.py:663
  142.2 4.9 %collective-permute-start.17 = (bf16[4,768,384]{2,1,0:T(8,128)(2,1)}, bf16[4,768,384]{2,1,0:T(8,128)(2,1)}, u32[]{:S(2)}, u32[]{:S(2)}) collective-permute-start(bf16[4,768,384]{2,1,0:T(8,128)(2,1)} %pad_maximum_fusion.1.refs_8_), channel_id=1, source_target_pairs={{0,16},{16,0},{1,17},{17,1},{2,18},{18,2},{3,19},{19,3},{4,20},{20... | collective-permute-start | bytes 7077896 | tf_op jit(solution)/shard_map/ppermute | solution.py:663
  147.1 24.9 %copy-start.8 = (bf16[384,576]{1,0:T(8,128)(2,1)S(1)}, bf16[384,576]{1,0:T(8,128)(2,1)}, u32[]{:S(2)}) copy-start(bf16[384,576]{1,0:T(8,128)(2,1)} %copy-done.7) | copy-start | bytes 1327108
  169.9 6.1 %collective-permute-start.18 = (bf16[192,256]{1,0:T(8,128)(2,1)}, bf16[192,256]{1,0:T(8,128)(2,1)S(1)}, u32[]{:S(2)}, u32[]{:S(2)}) collective-permute-start(bf16[192,256]{1,0:T(8,128)(2,1)} %get-tuple-element.86), channel_id=1, source_target_pairs={{0,3},{1,0},{2,1},{3,2},{4,7},{5,4},{6,5},{7,6},{8,11},{9,8},{10,9... | collective-permute-start | bytes 294920 | tf_op jit(solution)/shard_map/ppermute | solution.py:666
  169.9 10.5 %collective-permute-start.19 = (bf16[192,256]{1,0:T(8,128)(2,1)}, bf16[192,256]{1,0:T(8,128)(2,1)S(1)}, u32[]{:S(2)}, u32[]{:S(2)}) collective-permute-start(bf16[192,256]{1,0:T(8,128)(2,1)} %get-tuple-element.87), channel_id=1, source_target_pairs={{0,2},{1,3},{2,0},{3,1},{4,6},{5,7},{6,4},{7,5},{8,10},{9,11},{10,... | collective-permute-start | bytes 294920 | tf_op jit(solution)/shard_map/ppermute | solution.py:666
  171.0 9.4 %collective-permute-start.20 = (bf16[192,256]{1,0:T(8,128)(2,1)}, bf16[192,256]{1,0:T(8,128)(2,1)S(1)}, u32[]{:S(2)}, u32[]{:S(2)}) collective-permute-start(bf16[192,256]{1,0:T(8,128)(2,1)} %get-tuple-element.88), channel_id=1, source_target_pairs={{0,1},{1,2},{2,3},{3,0},{4,5},{5,6},{6,7},{7,4},{8,9},{9,10},{10,1... | collective-permute-start | bytes 294920 | tf_op jit(solution)/shard_map/ppermute | solution.py:666
  171.9 71.8 %collective-permute-start.25 = (bf16[4,384,1792]{2,1,0:T(8,128)(2,1)}, bf16[4,384,1792]{2,1,0:T(8,128)(2,1)}, u32[]{:S(2)}, u32[]{:S(2)}) collective-permute-start(bf16[4,384,1792]{2,1,0:T(8,128)(2,1)} %get-tuple-element.97), channel_id=1, source_target_pairs={{0,16},{16,0},{1,17},{17,1},{2,18},{18,2},{3,19},{19,3},{4,20},{20... | collective-permute-start | bytes 16515080 | tf_op jit(solution)/shard_map/ppermute | solution.py:663
  193.7 17.4 %copy-start.24 = (bf16[192,256]{1,0:T(8,128)(2,1)S(1)}, bf16[192,256]{1,0:T(8,128)(2,1)}, u32[]{:S(2)}) copy-start(bf16[192,256]{1,0:T(8,128)(2,1)} %get-tuple-element.103) | copy-start | bytes 294916
  193.8 34.2 %collective-permute-start.23 = (bf16[2,192,1024]{2,1,0:T(8,128)(2,1)}, bf16[2,192,1024]{2,1,0:T(8,128)(2,1)S(1)}, u32[]{:S(2)}, u32[]{:S(2)}) collective-permute-start(bf16[2,192,1024]{2,1,0:T(8,128)(2,1)} %get-tuple-element.95), channel_id=1, source_target_pairs={{0,8},{8,0},{4,12},{12,4},{1,9},{9,1},{5,13},{13,5},{2,10},{10,2},... | collective-permute-start | bytes 2359304 | tf_op jit(solution)/shard_map/ppermute | solution.py:665
  210.1 19.3 %collective-permute-start.21 = (bf16[2,192,1024]{2,1,0:T(8,128)(2,1)}, bf16[2,192,1024]{2,1,0:T(8,128)(2,1)S(1)}, u32[]{:S(2)}, u32[]{:S(2)}) collective-permute-start(bf16[2,192,1024]{2,1,0:T(8,128)(2,1)} %get-tuple-element.93), channel_id=1, source_target_pairs={{0,4},{4,0},{8,12},{12,8},{1,5},{5,1},{9,13},{13,9},{2,6},{6,2},{1... | collective-permute-start | bytes 2359304 | tf_op jit(solution)/shard_map/ppermute | solution.py:664
  210.1 18.0 %copy-start.16 = (bf16[2,192,1024]{2,1,0:T(8,128)(2,1)S(1)}, bf16[2,192,1024]{2,1,0:T(8,128)(2,1)}, u32[]{:S(2)}) copy-start(bf16[2,192,1024]{2,1,0:T(8,128)(2,1)} %get-tuple-element.94) | copy-start | bytes 2359300
  228.8 10.5 %collective-permute-start.24 = (bf16[192,1024]{1,0:T(8,128)(2,1)S(1)}, bf16[192,1024]{1,0:T(8,128)(2,1)S(1)}, u32[]{:S(2)}, u32[]{:S(2)}) collective-permute-start(bf16[192,1024]{1,0:T(8,128)(2,1)S(1)} %fusion.36), channel_id=1, source_target_pairs={{0,4},{4,0},{8,12},{12,8},{1,5},{5,1},{9,13},{13,9},{2,6},{6,2},{1... | collective-permute-start | bytes 1179656 | tf_op jit(solution)/shard_map/ppermute | solution.py:664
  230.3 10.7 %collective-permute-start.22 = (bf16[192,1024]{1,0:T(8,128)(2,1)S(1)}, bf16[192,1024]{1,0:T(8,128)(2,1)S(1)}, u32[]{:S(2)}, u32[]{:S(2)}) collective-permute-start(bf16[192,1024]{1,0:T(8,128)(2,1)S(1)} %fusion.35), channel_id=1, source_target_pairs={{0,8},{8,0},{4,12},{12,4},{1,9},{9,1},{5,13},{13,5},{2,10},{10,2},... | collective-permute-start | bytes 1179656 | tf_op jit(solution)/shard_map/ppermute | solution.py:665
  243.7 11.2 %collective-permute-start.32 = (bf16[1,384,640]{2,1,0:T(8,128)(2,1)S(1)}, bf16[1,384,640]{2,1,0:T(8,128)(2,1)S(1)}, u32[]{:S(2)}, u32[]{:S(2)}) collective-permute-start(bf16[1,384,640]{2,1,0:T(8,128)(2,1)S(1)} %get-tuple-element.164), channel_id=1, source_target_pairs={{0,16},{16,0},{1,17},{17,1},{2,18},{18,2},{3,19},{19,3},{4,20},{20... | collective-permute-start | bytes 1474568 | tf_op jit(solution)/shard_map/ppermute | solution.py:663
  252.3 40.6 %collective-permute-start.26 = (bf16[2,4,96,896]{3,2,1,0:T(8,128)(2,1)}, bf16[2,4,96,896]{3,2,1,0:T(8,128)(2,1)}, u32[]{:S(2)}, u32[]{:S(2)}) collective-permute-start(bf16[2,4,96,896]{3,2,1,0:T(8,128)(2,1)} %get-tuple-element.99), channel_id=1, source_target_pairs={{0,4},{4,0},{8,12},{12,8},{1,5},{5,1},{9,13},{13,9},{2,6},{6,2},{1... | collective-permute-start | bytes 4128776 | tf_op jit(solution)/shard_map/ppermute | solution.py:664
  253.4 47.6 %collective-permute-start.27 = (bf16[2,4,96,896]{3,2,1,0:T(8,128)(2,1)}, bf16[2,4,96,896]{3,2,1,0:T(8,128)(2,1)}, u32[]{:S(2)}, u32[]{:S(2)}) collective-permute-start(bf16[2,4,96,896]{3,2,1,0:T(8,128)(2,1)} %get-tuple-element.101), channel_id=1, source_target_pairs={{0,8},{8,0},{4,12},{12,4},{1,9},{9,1},{5,13},{13,5},{2,10},{10,2},... | collective-permute-start | bytes 4128776 | tf_op jit(solution)/shard_map/ppermute | solution.py:665
  259.7 28.4 %copy-start.32 = (bf16[2,1,96,256]{3,2,1,0:T(8,128)(2,1)S(1)}, bf16[2,1,96,256]{3,2,1,0:T(8,128)(2,1)}, u32[]{:S(2)}) copy-start(bf16[2,1,96,256]{3,2,1,0:T(8,128)(2,1)} %get-tuple-element.111) | copy-start | bytes 294916
  259.7 29.4 %copy-start.31 = (bf16[2,1,96,384]{3,2,1,0:T(8,128)(2,1)S(1)}, bf16[2,1,96,384]{3,2,1,0:T(8,128)(2,1)}, u32[]{:S(2)}) copy-start(bf16[2,1,96,384]{3,2,1,0:T(8,128)(2,1)} %get-tuple-element.109) | copy-start | bytes 442372
  259.7 28.3 %collective-permute-start.38 = (bf16[2,1,96,256]{3,2,1,0:T(8,128)(2,1)}, bf16[2,1,96,256]{3,2,1,0:T(8,128)(2,1)S(1)}, u32[]{:S(2)}, u32[]{:S(2)}) collective-permute-start(bf16[2,1,96,256]{3,2,1,0:T(8,128)(2,1)} %get-tuple-element.110), channel_id=1, source_target_pairs={{0,8},{8,0},{4,12},{12,4},{1,9},{9,1},{5,13},{13,5},{2,10},{10,2},... | collective-permute-start | bytes 294920 | tf_op jit(solution)/shard_map/ppermute | solution.py:665
  260.6 28.5 %collective-permute-start.36 = (bf16[2,1,96,384]{3,2,1,0:T(8,128)(2,1)S(1)}, bf16[2,1,96,384]{3,2,1,0:T(8,128)(2,1)S(1)}, u32[]{:S(2)}, u32[]{:S(2)}) collective-permute-start(bf16[2,1,96,384]{3,2,1,0:T(8,128)(2,1)S(1)} %copy-done.47), channel_id=1, source_target_pairs={{0,4},{4,0},{8,12},{12,8},{1,5},{5,1},{9,13},{13,9},{2,6},{6,2},{1... | collective-permute-start | bytes 442376 | tf_op jit(solution)/shard_map/ppermute | solution.py:664
  288.1 4.2 collective-permute-start.39
  289.2 7.9 %collective-permute-start.37 = (bf16[1,96,384]{2,1,0:T(8,128)(2,1)S(1)}, bf16[1,96,384]{2,1,0:T(8,128)(2,1)S(1)}, u32[]{:S(2)}, u32[]{:S(2)}) collective-permute-start(bf16[1,96,384]{2,1,0:T(8,128)(2,1)S(1)} %fusion.44), channel_id=1, source_target_pairs={{0,8},{8,0},{4,12},{12,4},{1,9},{9,1},{5,13},{13,5},{2,10},{10,2},... | collective-permute-start | bytes 221192 | tf_op jit(solution)/shard_map/ppermute | solution.py:665
  295.7 17.1 %collective-permute-start.40 = (bf16[4,96,896]{2,1,0:T(8,128)(2,1)}, bf16[4,96,896]{2,1,0:T(8,128)(2,1)}, u32[]{:S(2)}, u32[]{:S(2)}) collective-permute-start(bf16[4,96,896]{2,1,0:T(8,128)(2,1)} %fusion.22), channel_id=1, source_target_pairs={{0,8},{8,0},{4,12},{12,4},{1,9},{9,1},{5,13},{13,5},{2,10},{10,2},... | collective-permute-start | bytes 2064392 | tf_op jit(solution)/shard_map/ppermute | solution.py:665
  301.0 44.9 %collective-permute-start.31 = (bf16[4,384,768]{2,1,0:T(8,128)(2,1)}, bf16[4,384,768]{2,1,0:T(8,128)(2,1)}, u32[]{:S(2)}, u32[]{:S(2)}) collective-permute-start(bf16[4,384,768]{2,1,0:T(8,128)(2,1)} %slice.197.refs_4_), channel_id=1, source_target_pairs={{0,16},{16,0},{1,17},{17,1},{2,18},{18,2},{3,19},{19,3},{4,20},{20... | collective-permute-start | bytes 7077896 | tf_op jit(solution)/shard_map/ppermute | solution.py:663
  303.8 18.0 %collective-permute-start.41 = (bf16[4,96,896]{2,1,0:T(8,128)(2,1)}, bf16[4,96,896]{2,1,0:T(8,128)(2,1)}, u32[]{:S(2)}, u32[]{:S(2)}) collective-permute-start(bf16[4,96,896]{2,1,0:T(8,128)(2,1)} %fusion.23), channel_id=1, source_target_pairs={{0,4},{4,0},{8,12},{12,8},{1,5},{5,1},{9,13},{13,9},{2,6},{6,2},{1... | collective-permute-start | bytes 2064392 | tf_op jit(solution)/shard_map/ppermute | solution.py:664
  312.7 21.8 %collective-permute-start.28 = (bf16[576,256]{1,0:T(8,128)(2,1)S(1)}, bf16[576,256]{1,0:T(8,128)(2,1)S(1)}, u32[]{:S(2)}, u32[]{:S(2)}) collective-permute-start(bf16[576,256]{1,0:T(8,128)(2,1)S(1)} %pad_maximum_fusion.8), channel_id=1, source_target_pairs={{0,1},{1,2},{2,3},{3,0},{4,5},{5,6},{6,7},{7,4},{8,9},{9,10},{10,1... | collective-permute-start | bytes 884744 | tf_op jit(solution)/shard_map/ppermute | solution.py:666
  323.3 9.9 %collective-permute-start.44 = (bf16[96,1792]{1,0:T(8,128)(2,1)S(1)}, bf16[96,1792]{1,0:T(8,128)(2,1)S(1)}, u32[]{:S(2)}, u32[]{:S(2)}) collective-permute-start(bf16[96,1792]{1,0:T(8,128)(2,1)S(1)} %get-tuple-element.162), channel_id=1, source_target_pairs={{0,1},{3,2},{4,5},{7,6},{8,9},{11,10},{12,13},{15,14},{16,17},{19,... | collective-permute-start | bytes 1032200 | tf_op jit(solution)/shard_map/ppermute | solution.py:703
  324.7 16.5 %collective-permute-start.29 = (bf16[576,256]{1,0:T(8,128)(2,1)S(1)}, bf16[576,256]{1,0:T(8,128)(2,1)S(1)}, u32[]{:S(2)}, u32[]{:S(2)}) collective-permute-start(bf16[576,256]{1,0:T(8,128)(2,1)S(1)} %pad_maximum_fusion.9), channel_id=1, source_target_pairs={{0,2},{1,3},{2,0},{3,1},{4,6},{5,7},{6,4},{7,5},{8,10},{9,11},{10,... | collective-permute-start | bytes 884744 | tf_op jit(solution)/shard_map/ppermute | solution.py:666
  325.5 20.4 %collective-permute-start.30 = (bf16[576,256]{1,0:T(8,128)(2,1)S(1)}, bf16[576,256]{1,0:T(8,128)(2,1)S(1)}, u32[]{:S(2)}, u32[]{:S(2)}) collective-permute-start(bf16[576,256]{1,0:T(8,128)(2,1)S(1)} %pad_maximum_fusion.10), channel_id=1, source_target_pairs={{0,3},{1,0},{2,1},{3,2},{4,7},{5,4},{6,5},{7,6},{8,11},{9,8},{10,9... | collective-permute-start | bytes 884744 | tf_op jit(solution)/shard_map/ppermute | solution.py:666
  333.1 19.5 %collective-permute-start.43 = (bf16[96,1792]{1,0:T(8,128)(2,1)S(1)}, bf16[96,1792]{1,0:T(8,128)(2,1)S(1)}, u32[]{:S(2)}, u32[]{:S(2)}) collective-permute-start(bf16[96,1792]{1,0:T(8,128)(2,1)S(1)} %get-tuple-element.163), channel_id=1, source_target_pairs={{3,2},{2,1},{1,0},{7,6},{6,5},{5,4},{11,10},{10,9},{9,8},{15,14},{... | collective-permute-start | bytes 1032200 | tf_op jit(solution)/shard_map/ppermute | solution.py:703
  334.5 18.7 %collective-permute-start.42 = (bf16[96,1792]{1,0:T(8,128)(2,1)S(1)}, bf16[96,1792]{1,0:T(8,128)(2,1)S(1)}, u32[]{:S(2)}, u32[]{:S(2)}) collective-permute-start(bf16[96,1792]{1,0:T(8,128)(2,1)S(1)} %get-tuple-element.161), channel_id=1, source_target_pairs={{0,1},{1,2},{2,3},{4,5},{5,6},{6,7},{8,9},{9,10},{10,11},{12,13},{... | collective-permute-start | bytes 1032200 | tf_op jit(solution)/shard_map/ppermute | solution.py:703
  341.3 27.7 %collective-permute-start.45 = (bf16[96,1792]{1,0:T(8,128)(2,1)S(1)}, bf16[96,1792]{1,0:T(8,128)(2,1)S(1)}, u32[]{:S(2)}, u32[]{:S(2)}) collective-permute-start(bf16[96,1792]{1,0:T(8,128)(2,1)S(1)} %fusion.33), channel_id=1, source_target_pairs={{0,2},{1,3},{2,0},{3,1},{4,6},{5,7},{6,4},{7,5},{8,10},{9,11},{10,... | collective-permute-start | bytes 1032200 | tf_op jit(solution)/shard_map/ppermute | solution.py:703
  352.6 16.5 %copy-start.33 = (f32[16,768]{1,0:T(8,128)S(1)}, f32[16,768]{1,0:T(8,128)}, u32[]{:S(2)}) copy-start(f32[16,768]{1,0:T(8,128)} %get-tuple-element.117) | copy-start | bytes 147460
  352.6 16.5 %collective-permute-start.46 = (f32[16,768]{1,0:T(8,128)}, f32[16,768]{1,0:T(8,128)S(1)}, u32[]{:S(2)}, u32[]{:S(2)}) collective-permute-start(f32[16,768]{1,0:T(8,128)} %get-tuple-element.117), channel_id=1, source_target_pairs={{0,16},{16,0},{1,17},{17,1},{2,18},{18,2},{3,19},{19,3},{4,20},{20... | collective-permute-start | bytes 147464 | tf_op jit(solution)/shard_map/ppermute | solution.py:663
  369.2 4.2 collective-permute-start.47
  373.3 5.2 %collective-permute-start.48 = (f32[16,768]{1,0:T(8,128)S(1)}, f32[16,768]{1,0:T(8,128)S(1)}, u32[]{:S(2)}, u32[]{:S(2)}) collective-permute-start(f32[16,768]{1,0:T(8,128)S(1)} %add.324), channel_id=1, source_target_pairs={{0,8},{8,0},{4,12},{12,4},{1,9},{9,1},{5,13},{13,5},{2,10},{10,2},... | collective-permute-start | bytes 147464 | tf_op jit(solution)/shard_map/ppermute | solution.py:665
  374.7 39.0 %collective-permute-start.33 = (bf16[256,768]{1,0:T(8,128)(2,1)S(1)}, bf16[256,768]{1,0:T(8,128)(2,1)S(1)}, u32[]{:S(2)}, u32[]{:S(2)}) collective-permute-start(bf16[256,768]{1,0:T(8,128)(2,1)S(1)} %copy-done.29), channel_id=1, source_target_pairs={{0,1},{1,2},{2,3},{3,0},{4,5},{5,6},{6,7},{7,4},{8,9},{9,10},{10,1... | collective-permute-start | bytes 1179656 | tf_op jit(solution)/shard_map/ppermute | solution.py:666
  374.7 39.1 %collective-permute-start.34 = (bf16[256,768]{1,0:T(8,128)(2,1)S(1)}, bf16[256,768]{1,0:T(8,128)(2,1)S(1)}, u32[]{:S(2)}, u32[]{:S(2)}) collective-permute-start(bf16[256,768]{1,0:T(8,128)(2,1)S(1)} %copy-done.29), channel_id=1, source_target_pairs={{0,2},{1,3},{2,0},{3,1},{4,6},{5,7},{6,4},{7,5},{8,10},{9,11},{10,... | collective-permute-start | bytes 1179656 | tf_op jit(solution)/shard_map/ppermute | solution.py:666
  377.7 36.2 %collective-permute-start.35 = (bf16[256,768]{1,0:T(8,128)(2,1)S(1)}, bf16[256,768]{1,0:T(8,128)(2,1)S(1)}, u32[]{:S(2)}, u32[]{:S(2)}) collective-permute-start(bf16[256,768]{1,0:T(8,128)(2,1)S(1)} %copy-done.29), channel_id=1, source_target_pairs={{0,3},{1,0},{2,1},{3,2},{4,7},{5,4},{6,5},{7,6},{8,11},{9,8},{10,9... | collective-permute-start | bytes 1179656 | tf_op jit(solution)/shard_map/ppermute | solution.py:666
  378.6 24.3 %collective-permute-start.49 = (f32[16,768]{1,0:T(8,128)S(1)}, f32[16,768]{1,0:T(8,128)S(1)}, u32[]{:S(2)}, u32[]{:S(2)}) collective-permute-start(f32[16,768]{1,0:T(8,128)S(1)} %add.325), channel_id=1, source_target_pairs={{0,1},{1,0},{2,3},{3,2},{4,5},{5,4},{6,7},{7,6},{8,9},{9,8},{10,11... | collective-permute-start | bytes 147464 | tf_op jit(solution)/shard_map/ppermute | solution.py:914
  402.9 9.6 %collective-permute-start.50 = (f32[16,768]{1,0:T(8,128)S(1)}, f32[16,768]{1,0:T(8,128)S(1)}, u32[]{:S(2)}, u32[]{:S(2)}) collective-permute-start(f32[16,768]{1,0:T(8,128)S(1)} %add.326), channel_id=1, source_target_pairs={{0,2},{2,0},{1,3},{3,1},{4,6},{6,4},{5,7},{7,5},{8,10},{10,8},{9,1... | collective-permute-start | bytes 147464 | tf_op jit(solution)/shard_map/ppermute | solution.py:915
  (43 other events, 221.3 us)
Sparse Core Ops, SparseCore 0:
  193.9 89.7 all-gather.2

commit v8 on v6

--- a/solution.py
+++ b/solution.py
@@ -915,11 +915,11 @@
     qkv_grads = scatter_second(scatter_first(qkv_folded))[0]
 
     if grouped and n_tensor == 4 and n_shard == 2:
+        small += lax.ppermute(small, "tensor", [(0, 2), (2, 0), (1, 3), (3, 1)])
+        small += lax.ppermute(small, "tensor", [(0, 1), (1, 0), (2, 3), (3, 2)])
         small += swap(small)
         small += along_x(small)
         small += along_y(small)
-        small += lax.ppermute(small, "tensor", [(0, 1), (1, 0), (2, 3), (3, 2)])
-        small += lax.ppermute(small, "tensor", [(0, 2), (2, 0), (1, 3), (3, 1)])
     else:
         small = lax.psum(small, ("shard", "context", "tensor"))
     fc_total = lax.dynamic_index_in_dim(small, 6 + tensor, 0, keepdims=False)

time: 412 us -> 410 us (level); the launches traced: 411 us -> 402 us
  waiting for transfers between devices: 170 us -> 162 us
    ppermute x1, waiting for transfers between devices: 22.5 us -> 4.03 us  [body(): small += lax.ppermute(small, 'tensor', [(0, 1), (1, 0), (2, 3), (3, 2)])]
    ppermute x12, waiting for transfers between devices: 9.31 us -> 24.8 us  [body(): lax.ppermute(v, 'tensor', [(s, (s + d) % n_tensor) for s in range(n_tenso...]
  transfers between devices with their start and end apart: 52 -> 52, of which waited for: 26 -> 27; matrix products, arithmetic and copies ran while one was open for 10% -> 11% of each run, Pallas kernels for 8% -> 9%
where the time goes in v8:
time: 410 us; the launch traced here: 402 us
  waiting for transfers between devices  162 us (40%)
  starting transfers between devices  101 us (25%)
  Pallas kernels  70.3 us (17%)
  other arithmetic  28.5 us (7%)
  local copies, waits for them, and re-layouts  22.4 us (5%)
  between operations  15 us (4%)
    ppermute x9, waiting for transfers between devices, body(): lax.ppermute(v, 'context', [(0, 2), (2, 0), (1, 3), (3, 1)])  55.3 us
    ppermute x6, waiting for transfers between devices, gather_begin(): move = lambda perm: lax.ppermute(v, 'tensor', perm)  30.9 us
    ppermute x12, starting transfers between devices, body(): lax.ppermute(v, 'tensor', [(s, (s + d) % n_tensor) for s in range(n_tenso...  29.4 us
    ppermute x6, starting transfers between devices, gather_begin(): move = lambda perm: lax.ppermute(v, 'tensor', perm)  24.8 us
    ppermute x12, waiting for transfers between devices, body(): lax.ppermute(v, 'tensor', [(s, (s + d) % n_tensor) for s in range(n_tenso...  24.8 us
    ppermute x9, starting transfers between devices, body(): lax.ppermute(v, 'context', [(0, 2), (2, 0), (1, 3), (3, 1)])  24.3 us
    ppermute x9, waiting for transfers between devices, body(): lax.ppermute(v, 'context', [(0, 1), (1, 0), (2, 3), (3, 2)])  23.1 us
    pallas_call x1, Pallas kernels, middle(): pl.pallas_call(functools.partial(middle_kernel, len(att), parts), grid_sp...  23 us
  transfers between devices with their start and end apart: 52, of which 27 were waited for; matrix products, arithmetic and copies ran while one was open for 11% of the time, Pallas kernels for 9%

profile of v8, /device:TPU:0, one launch (start us, length us, event | category | flops | bytes accessed | tf_op | source)
XLA Modules:
  0.0 402.4 jit_solution(1615476033575922196)
XLA Ops:
  10.3 4.1 %collective-permute-start.1 = (bf16[976,384]{1,0:T(8,128)(2,1)S(1)}, bf16[976,384]{1,0:T(8,128)(2,1)}, u32[]{:S(2)}, u32[]{:S(2)}) collective-permute-start(bf16[976,384]{1,0:T(8,128)(2,1)S(1)} %pad_maximum_fusion.4), channel_id=1, source_target_pairs={{0,2},{1,3},{2,0},{3,1},{4,6},{5,7},{6,4},{7,5},{8,10},{9,11},{10,... | collective-permute-start | bytes 2248712 | tf_op jit(solution)/shard_map/ppermute | solution.py:675
  14.4 4.4 %collective-permute-start.2 = (bf16[976,384]{1,0:T(8,128)(2,1)S(1)}, bf16[976,384]{1,0:T(8,128)(2,1)}, u32[]{:S(2)}, u32[]{:S(2)}) collective-permute-start(bf16[976,384]{1,0:T(8,128)(2,1)S(1)} %pad_maximum_fusion.4), channel_id=1, source_target_pairs={{0,1},{1,2},{2,3},{4,5},{5,6},{6,7},{8,9},{9,10},{10,11},{12,13},{... | collective-permute-start | bytes 2248712 | tf_op jit(solution)/shard_map/ppermute | solution.py:675
  23.0 6.3 %project.1 = (bf16[1024,768]{1,0:T(8,128)(2,1)}, bf16[192,1024]{1,0:T(8,128)(2,1)}, bf16[192,1024]{1,0:T(8,128)(2,1)}, bf16[192,1024]{1,0:T(8,128)(2,1)}) custom-call(s32[4]{0:T(128)} %pad_add_fusion.1.sc, bf16[1024,768]{1,0:T(8,128)(2,1)} %bitcast.127, bf16[384,576]{1,0:T(8,128)(2,1)} %copy-done.4, bf16[384,576]{1,0:T(8,128)(2,1)} %copy-done.38, ...), custom_call_target="tpu_custom_call" | custom-call | flops 8049999872 | bytes 1048576 | tf_op jit(solution)/shard_map/project/pallas_call | solution.py:90
  29.4 1.6 collective-permute-start.5
  30.9 1.5 collective-permute-start.4
  32.4 8.4 %collective-permute-done.5.refs_4_.refs_8_ = bf16[192,1024]{1,0:T(8,128)(2,1)S(1)} collective-permute-done((bf16[192,1024]{1,0:T(8,128)(2,1)}, bf16[192,1024]{1,0:T(8,128)(2,1)S(1)}, u32[]{:S(2)}, u32[]{:S(2)}) %collective-permute-start.5) | collective-permute-done | bytes 393248 | tf_op jit(solution)/shard_map/ppermute | solution.py:664
  42.2 6.0 %collective-permute-done.1 = bf16[976,384]{1,0:T(8,128)(2,1)} collective-permute-done((bf16[976,384]{1,0:T(8,128)(2,1)S(1)}, bf16[976,384]{1,0:T(8,128)(2,1)}, u32[]{:S(2)}, u32[]{:S(2)}) %collective-permute-start.1) | collective-permute-done | bytes 749600 | tf_op jit(solution)/shard_map/ppermute | solution.py:675
  48.2 5.4 %collective-permute-done.3 = bf16[976,384]{1,0:T(8,128)(2,1)} collective-permute-done((bf16[976,384]{1,0:T(8,128)(2,1)S(1)}, bf16[976,384]{1,0:T(8,128)(2,1)}, u32[]{:S(2)}, u32[]{:S(2)}) %collective-permute-start.3) | collective-permute-done | bytes 749600 | tf_op jit(solution)/shard_map/ppermute | solution.py:675
  53.6 1.6 collective-permute-start.6
  55.1 1.5 collective-permute-start.7
  57.9 3.8 fusion.63
  62.6 12.4 %collective-permute-start.13 = (bf16[768,384]{1,0:T(8,128)(2,1)}, bf16[768,384]{1,0:T(8,128)(2,1)}, u32[]{:S(2)}, u32[]{:S(2)}) collective-permute-start(bf16[768,384]{1,0:T(8,128)(2,1)} %param.20), channel_id=1, source_target_pairs={{0,2},{1,3},{2,0},{3,1},{4,6},{5,7},{6,4},{7,5},{8,10},{9,11},{10,... | collective-permute-start | bytes 1769480 | tf_op jit(solution)/shard_map/ppermute | solution.py:675
  77.2 9.5 %attend.1 = (f32[3,1024]{1,0:T(4,128)}, bf16[192,1024]{1,0:T(8,128)(2,1)}, bf16[192,256]{1,0:T(8,128)(2,1)}, bf16[192,256]{1,0:T(8,128)(2,1)}, bf16[192,256]{1,0:T(8,128)(2,1)}, /*index=5*/bf16[192,256]{1,0:T(8,128)(2,1)}) custom-call(s32[12]{0:T(128)} %concatenate.46.sc, bf16[192,1024]{1,0:T(8,128)(2,1)} %get-tuple-element.92.qt, ...), custom_call_target="tpu_custom_call" | custom-call | flops 23000000512 | bytes 1048576 | tf_op jit(solution)/shard_map/attend/pallas_call | solution.py:221
  87.1 7.4 %collective-permute-start.8 = (bf16[192,256]{1,0:T(8,128)(2,1)}, bf16[192,256]{1,0:T(8,128)(2,1)S(1)}, u32[]{:S(2)}, u32[]{:S(2)}) collective-permute-start(bf16[192,256]{1,0:T(8,128)(2,1)} %get-tuple-element.79), channel_id=1, source_target_pairs={{0,1},{1,2},{2,3},{3,0},{4,5},{5,6},{6,7},{7,4},{8,9},{9,10},{10,1... | collective-permute-start | bytes 294920 | tf_op jit(solution)/shard_map/ppermute | solution.py:665
  94.5 4.0 collective-permute-start.9
  98.5 6.9 %collective-permute-done.13 = bf16[768,384]{1,0:T(8,128)(2,1)} collective-permute-done((bf16[768,384]{1,0:T(8,128)(2,1)}, bf16[768,384]{1,0:T(8,128)(2,1)}, u32[]{:S(2)}, u32[]{:S(2)}) %collective-permute-start.13) | collective-permute-done | bytes 589856 | tf_op jit(solution)/shard_map/ppermute | solution.py:675
  106.7 7.0 %collective-permute-done.10.refs_3_ = bf16[192,256]{1,0:T(8,128)(2,1)S(1)} collective-permute-done((bf16[192,256]{1,0:T(8,128)(2,1)}, bf16[192,256]{1,0:T(8,128)(2,1)S(1)}, u32[]{:S(2)}, u32[]{:S(2)}) %collective-permute-start.10) | collective-permute-done | bytes 98336 | tf_op jit(solution)/shard_map/ppermute | solution.py:665
  117.9 1.5 pad_maximum_fusion.refs_6_
  119.8 12.3 %collective-permute-done.16 = bf16[768,384]{1,0:T(8,128)(2,1)S(1)} collective-permute-done((bf16[768,384]{1,0:T(8,128)(2,1)}, bf16[768,384]{1,0:T(8,128)(2,1)S(1)}, u32[]{:S(2)}, u32[]{:S(2)}) %collective-permute-start.16) | collective-permute-done | bytes 589856 | tf_op jit(solution)/shard_map/ppermute | solution.py:675
  132.1 9.9 %collective-permute-done.14 = bf16[768,384]{1,0:T(8,128)(2,1)S(1)} collective-permute-done((bf16[768,384]{1,0:T(8,128)(2,1)}, bf16[768,384]{1,0:T(8,128)(2,1)S(1)}, u32[]{:S(2)}, u32[]{:S(2)}) %collective-permute-start.14) | collective-permute-done | bytes 589856 | tf_op jit(solution)/shard_map/ppermute | solution.py:688
  142.1 3.0 pad_maximum_fusion.1.refs_8_
  145.1 2.1 dynamic-slice_bitcast_fusion.2
  147.2 2.8 collective-permute-done.17.refs_9_
  150.0 23.0 %middle.1 = (bf16[256,768]{1,0:T(8,128)(2,1)}, f32[256,768]{1,0:T(8,128)}, f32[4,768]{1,0:T(4,128)}, f32[4,1,768]{2,1,0:T(1,128)}, bf16[192,256]{1,0:T(8,128)(2,...) custom-call(s32[4]{0:T(128)} %pad_add_fusion.1.sc, ...), custom_call_target="tpu_custom_call" | custom-call | flops 21849999360 | bytes 1048576 | tf_op jit(solution)/shard_map/middle/pallas_call | solution.py:465
  175.2 2.1 fusion.13.refs_10_
  177.3 4.9 %collective-permute-done.18.theirs = bf16[4,384,1792]{2,1,0:T(8,128)(2,1)S(1)} collective-permute-done((bf16[4,384,1792]{2,1,0:T(8,128)(2,1)}, bf16[4,384,1792]{2,1,0:T(8,128)(2,1)S(1)}, u32[]{:S(2)}, u32[]{:S(2)}) %collective-permute-start.18) | collective-permute-done | bytes 5505056 | tf_op jit(solution)/shard_map/ppermute | solution.py:662
  182.2 2.4 copy-done.33
  184.6 8.7 %fold.2 = (bf16[2,4,96,896]{3,2,1,0:T(8,128)(2,1)}, bf16[2,4,96,896]{3,2,1,0:T(8,128)(2,1)}, bf16[2,4,96,896]{3,2,1,0:T(8,128)(2,1)}, bf16[2,4,96,896]{3,2,1,0:T(8,128)(2,1)}) custom-call(s32[4]{0:T(128)} %pad_add_fusion.1.sc, bf16[4,384,1792]{2,1,0:T(8,128)(2,1)} %get-tuple-element.89.mine, bf16[4,384,1792]{2,1,0:T(8,128)(2,1)} %copy-done.33), custom_call_target="tpu_custom_call" | custom-call | flops 8049999872 | bytes 1048576 | tf_op jit(solution)/shard_map/fold/pallas_call | solution.py:587
  194.0 12.6 %attend_back.1 = (bf16[192,256]{1,0:T(8,128)(2,1)}, bf16[192,256]{1,0:T(8,128)(2,1)}, bf16[192,256]{1,0:T(8,128)(2,1)}, bf16[192,256]{1,0:T(8,128)(2,1)}, bf16[2...) custom-call(s32[12]{0:T(128)} %concatenate.46.sc, ...), custom_call_target="tpu_custom_call", output_to_operand_aliasing={{8}: (15, {})} | custom-call | flops 29899999232 | bytes 1048576 | tf_op jit(solution)/shard_map/attend_back/pallas_call | solution.py:327
  206.7 12.6 %collective-permute-start.23 = (bf16[2,4,96,896]{3,2,1,0:T(8,128)(2,1)}, bf16[2,4,96,896]{3,2,1,0:T(8,128)(2,1)S(1)}, u32[]{:S(2)}, u32[]{:S(2)}) collective-permute-start(bf16[2,4,96,896]{3,2,1,0:T(8,128)(2,1)} %get-tuple-element.107), channel_id=1, source_target_pairs={{0,8},{8,0},{4,12},{12,4},{1,9},{9,1},{5,13},{13,5},{2,10},{10,2},... | collective-permute-start | bytes 4128776 | tf_op jit(solution)/shard_map/ppermute | solution.py:664
  219.3 30.7 %collective-permute-done.23 = bf16[2,4,96,896]{3,2,1,0:T(8,128)(2,1)S(1)} collective-permute-done((bf16[2,4,96,896]{3,2,1,0:T(8,128)(2,1)}, bf16[2,4,96,896]{3,2,1,0:T(8,128)(2,1)S(1)}, u32[]{:S(2)}, u32[]{:S(2)}) %collective-permute-start.23) | collective-permute-done | bytes 1376288 | tf_op jit(solution)/shard_map/ppermute | solution.py:664
  251.9 1.8 collective-permute-start.40
  254.0 1.6 collective-permute-start.24
  255.8 13.0 %collective-permute-done.41 = bf16[4,96,896]{2,1,0:T(8,128)(2,1)S(1)} collective-permute-done((bf16[4,96,896]{2,1,0:T(8,128)(2,1)S(1)}, bf16[4,96,896]{2,1,0:T(8,128)(2,1)S(1)}, u32[]{:S(2)}, u32[]{:S(2)}) %collective-permute-start.41) | collective-permute-done | bytes 688160 | tf_op jit(solution)/shard_map/ppermute | solution.py:663
  271.5 1.7 collective-permute-start.44
  273.2 2.0 collective-permute-start.42
  275.2 1.5 collective-permute-start.43
  276.7 9.3 %collective-permute-done.26 = bf16[2,192,1024]{2,1,0:T(8,128)(2,1)S(1)} collective-permute-done((bf16[2,192,1024]{2,1,0:T(8,128)(2,1)S(1)}, bf16[2,192,1024]{2,1,0:T(8,128)(2,1)S(1)}, u32[]{:S(2)}, u32[]{:S(2)}) %collective-permute-start.26) | collective-permute-done | bytes 786464 | tf_op jit(solution)/shard_map/ppermute | solution.py:664
  287.5 1.5 collective-permute-start.25
  290.0 6.4 %collective-permute-done.27 = bf16[192,1024]{1,0:T(8,128)(2,1)S(1)} collective-permute-done((bf16[192,1024]{1,0:T(8,128)(2,1)S(1)}, bf16[192,1024]{1,0:T(8,128)(2,1)S(1)}, u32[]{:S(2)}, u32[]{:S(2)}) %collective-permute-start.27) | collective-permute-done | bytes 393248 | tf_op jit(solution)/shard_map/ppermute | solution.py:663
  297.9 2.6 convolution_convert_fusion
  300.4 2.4 all-gather.3.cloned.1.call-done
  302.9 3.3 slice.197.refs_4_
  309.3 8.0 %collective-permute-start.30 = (bf16[576,256]{1,0:T(8,128)(2,1)}, bf16[576,256]{1,0:T(8,128)(2,1)}, u32[]{:S(2)}, u32[]{:S(2)}) collective-permute-start(bf16[576,256]{1,0:T(8,128)(2,1)} %pad_maximum_fusion.9), channel_id=1, source_target_pairs={{0,3},{1,0},{2,1},{3,2},{4,7},{5,4},{6,5},{7,6},{8,11},{9,8},{10,9... | collective-permute-start | bytes 884744 | tf_op jit(solution)/shard_map/ppermute | solution.py:665
  318.6 2.0 collective-permute-start.28
  323.5 4.1 %fold.3 = (bf16[2,1,96,384]{3,2,1,0:T(8,128)(2,1)}, bf16[2,1,96,384]{3,2,1,0:T(8,128)(2,1)}, bf16[2,1,96,256]{3,2,1,0:T(8,128)(2,1)}, bf16[2,1,96,256]{3,2,1,0:T(8,128)(2,1)}) custom-call(s32[4]{0:T(128)} %pad_add_fusion.1.sc, bf16[1,384,640]{2,1,0:T(8,128)(2,1)} %get-tuple-element.177.mine, bf16[1,384,640]{2,1,0:T(8,128)(2,1)} %copy-done.37), custom_call_target="tpu_custom_call" | custom-call | flops 2875000064 | bytes 1048576 | tf_op jit(solution)/shard_map/fold/pallas_call | solution.py:587
  327.6 1.7 collective-permute-start.38
  330.1 2.4 collective-permute-done.38
  332.5 2.3 collective-permute-start.36
  335.6 2.5 collective-permute-done.36
  338.1 2.0 collective-permute-start.39
  341.1 1.7 collective-permute-start.37
  342.7 2.2 collective-permute-done.29.refs_2_
  345.0 6.1 %last.1 = (bf16[256,768]{1,0:T(8,128)(2,1)}, f32[16,768]{1,0:T(8,128)}) custom-call(s32[4]{0:T(128)} %pad_add_fusion.1.sc, bf16[576,256]{1,0:T(8,128)(2,1)} %pad_maximum_fusion.6.refs_0_, bf16[576,256]{1,0:T(8,128)(2,1)} %collective-permute-done.28.refs_1_, bf16[576,256]{1,0:T(8,128)(2,1)} %collective-permute-done.29.refs_2_, ...), custom_call_target="tpu_custom_call" | custom-call | flops 6899999744 | bytes 1048576 | tf_op jit(solution)/shard_map/last/pallas_call | solution.py:537
  352.5 3.8 collective-permute-done.46
  357.2 4.0 %collective-permute-done.47 = f32[16,768]{1,0:T(8,128)S(1)} collective-permute-done((f32[16,768]{1,0:T(8,128)S(1)}, f32[16,768]{1,0:T(8,128)S(1)}, u32[]{:S(2)}, u32[]{:S(2)}) %collective-permute-start.47) | collective-permute-done | bytes 49184 | tf_op jit(solution)/shard_map/ppermute | solution.py:919
  362.3 1.6 slice.190
  365.4 2.8 collective-permute-start.35
  368.3 2.4 collective-permute-start.49
  370.7 1.9 bitcast_convert_fusion
  372.8 1.6 collective-permute-start.50
  374.7 2.2 collective-permute-done.50
  378.3 15.4 %collective-permute-done.34 = bf16[256,768]{1,0:T(8,128)(2,1)S(1)} collective-permute-done((bf16[256,768]{1,0:T(8,128)(2,1)S(1)}, bf16[256,768]{1,0:T(8,128)(2,1)S(1)}, u32[]{:S(2)}, u32[]{:S(2)}) %collective-permute-start.34) | collective-permute-done | bytes 393248 | tf_op jit(solution)/shard_map/ppermute | solution.py:665
  393.9 1.7 copy-done
  (232 shorter events, 47.5 us)
Async XLA Ops:
  7.2 12.8 %copy-start.11 = (bf16[384,3,192]{0,2,1:T(8,128)(2,1)S(1)}, bf16[384,3,192]{0,2,1:T(8,128)(2,1)}, u32[]{:S(2)}) copy-start(bf16[384,3,192]{0,2,1:T(8,128)(2,1)} %param.17) | copy-start | bytes 1327108
  7.2 295.7 %all-gather.3.cloned.1.call-start = ((), (), s32[]{:S(2)}) async-start(), calls=%async_computation | async-start | bytes 4915200 | tf_op jit(solution)/shard_map/all_gather | solution.py:896
  8.1 12.4 %copy-start.31 = (f32[768]{0:T(1024)S(1)}, f32[768]{0:T(1024)}, u32[]{:S(2)}) copy-start(f32[768]{0:T(1024)} %param.27) | copy-start | bytes 9220
  8.1 12.4 %copy-start.32 = (f32[768]{0:T(1024)S(1)}, f32[768]{0:T(1024)}, u32[]{:S(2)}) copy-start(f32[768]{0:T(1024)} %param.28) | copy-start | bytes 9220
  10.2 19.1 %copy-start.2 = (bf16[976,384]{1,0:T(8,128)(2,1)}, bf16[976,384]{1,0:T(8,128)(2,1)S(1)}, u32[]{:S(2)}) copy-start(bf16[976,384]{1,0:T(8,128)(2,1)S(1)} %pad_maximum_fusion.4) | copy-start | bytes 2248708
  10.3 37.9 %collective-permute-start.1 = (bf16[976,384]{1,0:T(8,128)(2,1)S(1)}, bf16[976,384]{1,0:T(8,128)(2,1)}, u32[]{:S(2)}, u32[]{:S(2)}) collective-permute-start(bf16[976,384]{1,0:T(8,128)(2,1)S(1)} %pad_maximum_fusion.4), channel_id=1, source_target_pairs={{0,2},{1,3},{2,0},{3,1},{4,6},{5,7},{6,4},{7,5},{8,10},{9,11},{10,... | collective-permute-start | bytes 2248712 | tf_op jit(solution)/shard_map/ppermute | solution.py:675
  14.4 33.8 %collective-permute-start.2 = (bf16[976,384]{1,0:T(8,128)(2,1)S(1)}, bf16[976,384]{1,0:T(8,128)(2,1)}, u32[]{:S(2)}, u32[]{:S(2)}) collective-permute-start(bf16[976,384]{1,0:T(8,128)(2,1)S(1)} %pad_maximum_fusion.4), channel_id=1, source_target_pairs={{0,1},{1,2},{2,3},{4,5},{5,6},{6,7},{8,9},{9,10},{10,11},{12,13},{... | collective-permute-start | bytes 2248712 | tf_op jit(solution)/shard_map/ppermute | solution.py:675
  18.7 34.8 %collective-permute-start.3 = (bf16[976,384]{1,0:T(8,128)(2,1)S(1)}, bf16[976,384]{1,0:T(8,128)(2,1)}, u32[]{:S(2)}, u32[]{:S(2)}) collective-permute-start(bf16[976,384]{1,0:T(8,128)(2,1)S(1)} %pad_maximum_fusion.4), channel_id=1, source_target_pairs={{3,2},{2,1},{1,0},{7,6},{6,5},{5,4},{11,10},{10,9},{9,8},{15,14},{... | collective-permute-start | bytes 2248712 | tf_op jit(solution)/shard_map/ppermute | solution.py:675
  20.3 1.9 collective-permute-start
  29.4 12.7 %copy-start.20 = (bf16[192,1024]{1,0:T(8,128)(2,1)S(1)}, bf16[192,1024]{1,0:T(8,128)(2,1)}, u32[]{:S(2)}) copy-start(bf16[192,1024]{1,0:T(8,128)(2,1)} %get-tuple-element.74.refs_0_.refs_4_) | copy-start | bytes 1179652
  29.4 11.4 %collective-permute-start.5 = (bf16[192,1024]{1,0:T(8,128)(2,1)}, bf16[192,1024]{1,0:T(8,128)(2,1)S(1)}, u32[]{:S(2)}, u32[]{:S(2)}) collective-permute-start(bf16[192,1024]{1,0:T(8,128)(2,1)} %get-tuple-element.75.refs_3_.refs_7_), channel_id=1, source_target_pairs={{0,8},{8,0},{4,12},{12,4},{1,9},{9,1},{5,13},{13,5},{2,10},{10,2},... | collective-permute-start | bytes 1179656 | tf_op jit(solution)/shard_map/ppermute | solution.py:664
  30.9 11.1 %collective-permute-start.4 = (bf16[192,1024]{1,0:T(8,128)(2,1)}, bf16[192,1024]{1,0:T(8,128)(2,1)S(1)}, u32[]{:S(2)}, u32[]{:S(2)}) collective-permute-start(bf16[192,1024]{1,0:T(8,128)(2,1)} %get-tuple-element.74.refs_0_.refs_4_), channel_id=1, source_target_pairs={{0,4},{4,0},{8,12},{12,8},{1,5},{5,1},{9,13},{13,9},{2,6},{6,2},{1... | collective-permute-start | bytes 1179656 | tf_op jit(solution)/shard_map/ppermute | solution.py:663
  40.8 15.8 %copy-start.26 = (s32[1,4096]{1,0:T(1,128)S(1)}, s32[1,4096]{1,0:T(1,128)}, u32[]{:S(2)}) copy-start(s32[1,4096]{1,0:T(1,128)} %param.16) | copy-start | bytes 49156
  42.0 13.1 %copy-start.22 = (bf16[192,1024]{1,0:T(8,128)(2,1)}, bf16[192,1024]{1,0:T(8,128)(2,1)S(1)}, u32[]{:S(2)}) copy-start(bf16[192,1024]{1,0:T(8,128)(2,1)S(1)} %collective-permute-done.4.refs_1_.refs_5_) | copy-start | bytes 1179652
  53.6 22.7 %collective-permute-start.6 = (bf16[2,192,1024]{2,1,0:T(8,128)(2,1)S(1)}, bf16[2,192,1024]{2,1,0:T(8,128)(2,1)S(1)}, u32[]{:S(2)}, u32[]{:S(2)}) collective-permute-start(bf16[2,192,1024]{2,1,0:T(8,128)(2,1)S(1)} %pad_maximum_fusion.2), channel_id=1, source_target_pairs={{0,8},{8,0},{4,12},{12,4},{1,9},{9,1},{5,13},{13,5},{2,10},{10,2},... | collective-permute-start | bytes 2359304 | tf_op jit(solution)/shard_map/ppermute | solution.py:664
  55.1 21.2 %collective-permute-start.7 = (bf16[2,192,1024]{2,1,0:T(8,128)(2,1)S(1)}, bf16[2,192,1024]{2,1,0:T(8,128)(2,1)}, u32[]{:S(2)}, u32[]{:S(2)}) collective-permute-start(bf16[2,192,1024]{2,1,0:T(8,128)(2,1)S(1)} %pad_maximum_fusion.3), channel_id=1, source_target_pairs={{0,4},{4,0},{8,12},{12,8},{1,5},{5,1},{9,13},{13,9},{2,6},{6,2},{1... | collective-permute-start | bytes 2359304 | tf_op jit(solution)/shard_map/ppermute | solution.py:663
  62.6 42.8 %collective-permute-start.13 = (bf16[768,384]{1,0:T(8,128)(2,1)}, bf16[768,384]{1,0:T(8,128)(2,1)}, u32[]{:S(2)}, u32[]{:S(2)}) collective-permute-start(bf16[768,384]{1,0:T(8,128)(2,1)} %param.20), channel_id=1, source_target_pairs={{0,2},{1,3},{2,0},{3,1},{4,6},{5,7},{6,4},{7,5},{8,10},{9,11},{10,... | collective-permute-start | bytes 1769480 | tf_op jit(solution)/shard_map/ppermute | solution.py:675
  75.0 41.5 %collective-permute-start.11 = (bf16[976,384]{1,0:T(8,128)(2,1)}, bf16[976,384]{1,0:T(8,128)(2,1)S(1)}, u32[]{:S(2)}, u32[]{:S(2)}) collective-permute-start(bf16[976,384]{1,0:T(8,128)(2,1)} %collective-permute-done.1), channel_id=1, source_target_pairs={{2,3},{1,0},{6,7},{5,4},{10,11},{9,8},{14,15},{13,12},{18,19},{17,... | collective-permute-start | bytes 2248712 | tf_op jit(solution)/shard_map/ppermute | solution.py:688
  86.7 27.0 %collective-permute-start.10 = (bf16[192,256]{1,0:T(8,128)(2,1)}, bf16[192,256]{1,0:T(8,128)(2,1)S(1)}, u32[]{:S(2)}, u32[]{:S(2)}) collective-permute-start(bf16[192,256]{1,0:T(8,128)(2,1)} %get-tuple-element.81), channel_id=1, source_target_pairs={{0,3},{1,0},{2,1},{3,2},{4,7},{5,4},{6,5},{7,6},{8,11},{9,8},{10,9... | collective-permute-start | bytes 294920 | tf_op jit(solution)/shard_map/ppermute | solution.py:665
  87.1 27.9 %collective-permute-start.8 = (bf16[192,256]{1,0:T(8,128)(2,1)}, bf16[192,256]{1,0:T(8,128)(2,1)S(1)}, u32[]{:S(2)}, u32[]{:S(2)}) collective-permute-start(bf16[192,256]{1,0:T(8,128)(2,1)} %get-tuple-element.79), channel_id=1, source_target_pairs={{0,1},{1,2},{2,3},{3,0},{4,5},{5,6},{6,7},{7,4},{8,9},{9,10},{10,1... | collective-permute-start | bytes 294920 | tf_op jit(solution)/shard_map/ppermute | solution.py:665
  94.5 20.5 %collective-permute-start.9 = (bf16[192,256]{1,0:T(8,128)(2,1)}, bf16[192,256]{1,0:T(8,128)(2,1)S(1)}, u32[]{:S(2)}, u32[]{:S(2)}) collective-permute-start(bf16[192,256]{1,0:T(8,128)(2,1)} %get-tuple-element.80), channel_id=1, source_target_pairs={{0,2},{1,3},{2,0},{3,1},{4,6},{5,7},{6,4},{7,5},{8,10},{9,11},{10,... | collective-permute-start | bytes 294920 | tf_op jit(solution)/shard_map/ppermute | solution.py:665
  98.5 19.4 %copy-start.3 = (bf16[976,384]{1,0:T(8,128)(2,1)S(1)}, bf16[976,384]{1,0:T(8,128)(2,1)}, u32[]{:S(2)}) copy-start(bf16[976,384]{1,0:T(8,128)(2,1)} %copy-done.2) | copy-start | bytes 2248708
  105.4 14.4 %collective-permute-start.15 = (bf16[768,384]{1,0:T(8,128)(2,1)}, bf16[768,384]{1,0:T(8,128)(2,1)S(1)}, u32[]{:S(2)}, u32[]{:S(2)}) collective-permute-start(bf16[768,384]{1,0:T(8,128)(2,1)} %param.20), channel_id=1, source_target_pairs={{0,1},{1,2},{2,3},{4,5},{5,6},{6,7},{8,9},{9,10},{10,11},{12,13},{... | collective-permute-start | bytes 1769480 | tf_op jit(solution)/shard_map/ppermute | solution.py:675
  113.7 18.4 %collective-permute-start.16 = (bf16[768,384]{1,0:T(8,128)(2,1)}, bf16[768,384]{1,0:T(8,128)(2,1)S(1)}, u32[]{:S(2)}, u32[]{:S(2)}) collective-permute-start(bf16[768,384]{1,0:T(8,128)(2,1)} %param.20), channel_id=1, source_target_pairs={{3,2},{2,1},{1,0},{7,6},{6,5},{5,4},{11,10},{10,9},{9,8},{15,14},{... | collective-permute-start | bytes 1769480 | tf_op jit(solution)/shard_map/ppermute | solution.py:675
  115.1 26.9 %collective-permute-start.14 = (bf16[768,384]{1,0:T(8,128)(2,1)}, bf16[768,384]{1,0:T(8,128)(2,1)S(1)}, u32[]{:S(2)}, u32[]{:S(2)}) collective-permute-start(bf16[768,384]{1,0:T(8,128)(2,1)} %collective-permute-done.13), channel_id=1, source_target_pairs={{2,3},{1,0},{6,7},{5,4},{10,11},{9,8},{14,15},{13,12},{18,19},{17,... | collective-permute-start | bytes 1769480 | tf_op jit(solution)/shard_map/ppermute | solution.py:688
  119.4 25.7 %copy-start.1 = (bf16[4,976,384]{2,1,0:T(8,128)(2,1)}, bf16[4,976,384]{2,1,0:T(8,128)(2,1)S(1)}, u32[]{:S(2)}) copy-start(bf16[4,976,384]{2,1,0:T(8,128)(2,1)S(1)} %pad_maximum_fusion.refs_6_) | copy-start | bytes 8994820
  119.4 30.6 %collective-permute-start.12 = (bf16[4,976,384]{2,1,0:T(8,128)(2,1)S(1)}, bf16[4,976,384]{2,1,0:T(8,128)(2,1)}, u32[]{:S(2)}, u32[]{:S(2)}) collective-permute-start(bf16[4,976,384]{2,1,0:T(8,128)(2,1)S(1)} %pad_maximum_fusion.refs_6_), channel_id=1, source_target_pairs={{0,16},{16,0},{1,17},{17,1},{2,18},{18,2},{3,19},{19,3},{4,20},{20... | collective-permute-start | bytes 8994824 | tf_op jit(solution)/shard_map/ppermute | solution.py:662
  145.1 4.9 %collective-permute-start.17 = (bf16[4,768,384]{2,1,0:T(8,128)(2,1)}, bf16[4,768,384]{2,1,0:T(8,128)(2,1)}, u32[]{:S(2)}, u32[]{:S(2)}) collective-permute-start(bf16[4,768,384]{2,1,0:T(8,128)(2,1)} %pad_maximum_fusion.1.refs_8_), channel_id=1, source_target_pairs={{0,16},{16,0},{1,17},{17,1},{2,18},{18,2},{3,19},{19,3},{4,20},{20... | collective-permute-start | bytes 7077896 | tf_op jit(solution)/shard_map/ppermute | solution.py:662
  150.0 25.2 %copy-start.5 = (bf16[384,576]{1,0:T(8,128)(2,1)S(1)}, bf16[384,576]{1,0:T(8,128)(2,1)}, u32[]{:S(2)}) copy-start(bf16[384,576]{1,0:T(8,128)(2,1)} %copy-done.4) | copy-start | bytes 1327108
  173.0 9.2 %collective-permute-start.18 = (bf16[4,384,1792]{2,1,0:T(8,128)(2,1)}, bf16[4,384,1792]{2,1,0:T(8,128)(2,1)S(1)}, u32[]{:S(2)}, u32[]{:S(2)}) collective-permute-start(bf16[4,384,1792]{2,1,0:T(8,128)(2,1)} %get-tuple-element.90), channel_id=1, source_target_pairs={{0,16},{16,0},{1,17},{17,1},{2,18},{18,2},{3,19},{19,3},{4,20},{20... | collective-permute-start | bytes 16515080 | tf_op jit(solution)/shard_map/ppermute | solution.py:662
  173.2 20.1 %collective-permute-start.19 = (bf16[192,256]{1,0:T(8,128)(2,1)}, bf16[192,256]{1,0:T(8,128)(2,1)S(1)}, u32[]{:S(2)}, u32[]{:S(2)}) collective-permute-start(bf16[192,256]{1,0:T(8,128)(2,1)} %get-tuple-element.96), channel_id=1, source_target_pairs={{0,3},{1,0},{2,1},{3,2},{4,7},{5,4},{6,5},{7,6},{8,11},{9,8},{10,9... | collective-permute-start | bytes 294920 | tf_op jit(solution)/shard_map/ppermute | solution.py:665
  173.2 20.1 %collective-permute-start.20 = (bf16[192,256]{1,0:T(8,128)(2,1)}, bf16[192,256]{1,0:T(8,128)(2,1)S(1)}, u32[]{:S(2)}, u32[]{:S(2)}) collective-permute-start(bf16[192,256]{1,0:T(8,128)(2,1)} %get-tuple-element.97), channel_id=1, source_target_pairs={{0,2},{1,3},{2,0},{3,1},{4,6},{5,7},{6,4},{7,5},{8,10},{9,11},{10,... | collective-permute-start | bytes 294920 | tf_op jit(solution)/shard_map/ppermute | solution.py:665
  174.3 19.0 %collective-permute-start.21 = (bf16[192,256]{1,0:T(8,128)(2,1)}, bf16[192,256]{1,0:T(8,128)(2,1)S(1)}, u32[]{:S(2)}, u32[]{:S(2)}) collective-permute-start(bf16[192,256]{1,0:T(8,128)(2,1)} %get-tuple-element.98), channel_id=1, source_target_pairs={{0,1},{1,2},{2,3},{3,0},{4,5},{5,6},{6,7},{7,4},{8,9},{9,10},{10,1... | collective-permute-start | bytes 294920 | tf_op jit(solution)/shard_map/ppermute | solution.py:665
  206.7 43.4 %collective-permute-start.23 = (bf16[2,4,96,896]{3,2,1,0:T(8,128)(2,1)}, bf16[2,4,96,896]{3,2,1,0:T(8,128)(2,1)S(1)}, u32[]{:S(2)}, u32[]{:S(2)}) collective-permute-start(bf16[2,4,96,896]{3,2,1,0:T(8,128)(2,1)} %get-tuple-element.107), channel_id=1, source_target_pairs={{0,8},{8,0},{4,12},{12,4},{1,9},{9,1},{5,13},{13,5},{2,10},{10,2},... | collective-permute-start | bytes 4128776 | tf_op jit(solution)/shard_map/ppermute | solution.py:664
  219.2 32.2 %collective-permute-start.22 = (bf16[2,4,96,896]{3,2,1,0:T(8,128)(2,1)}, bf16[2,4,96,896]{3,2,1,0:T(8,128)(2,1)S(1)}, u32[]{:S(2)}, u32[]{:S(2)}) collective-permute-start(bf16[2,4,96,896]{3,2,1,0:T(8,128)(2,1)} %get-tuple-element.91), channel_id=1, source_target_pairs={{0,4},{4,0},{8,12},{12,8},{1,5},{5,1},{9,13},{13,9},{2,6},{6,2},{1... | collective-permute-start | bytes 4128776 | tf_op jit(solution)/shard_map/ppermute | solution.py:663
  219.3 30.9 %copy-start.7 = (bf16[2,4,96,896]{3,2,1,0:T(8,128)(2,1)S(1)}, bf16[2,4,96,896]{3,2,1,0:T(8,128)(2,1)}, u32[]{:S(2)}) copy-start(bf16[2,4,96,896]{3,2,1,0:T(8,128)(2,1)} %get-tuple-element.106) | copy-start | bytes 4128772
  250.4 18.4 %collective-permute-start.41 = (bf16[4,96,896]{2,1,0:T(8,128)(2,1)S(1)}, bf16[4,96,896]{2,1,0:T(8,128)(2,1)S(1)}, u32[]{:S(2)}, u32[]{:S(2)}) collective-permute-start(bf16[4,96,896]{2,1,0:T(8,128)(2,1)S(1)} %fusion.23), channel_id=1, source_target_pairs={{0,4},{4,0},{8,12},{12,8},{1,5},{5,1},{9,13},{13,9},{2,6},{6,2},{1... | collective-permute-start | bytes 2064392 | tf_op jit(solution)/shard_map/ppermute | solution.py:663
  251.9 18.4 %collective-permute-start.40 = (bf16[4,96,896]{2,1,0:T(8,128)(2,1)S(1)}, bf16[4,96,896]{2,1,0:T(8,128)(2,1)S(1)}, u32[]{:S(2)}, u32[]{:S(2)}) collective-permute-start(bf16[4,96,896]{2,1,0:T(8,128)(2,1)S(1)} %fusion.22), channel_id=1, source_target_pairs={{0,8},{8,0},{4,12},{12,4},{1,9},{9,1},{5,13},{13,5},{2,10},{10,2},... | collective-permute-start | bytes 2064392 | tf_op jit(solution)/shard_map/ppermute | solution.py:664
  253.8 32.3 %collective-permute-start.26 = (bf16[2,192,1024]{2,1,0:T(8,128)(2,1)S(1)}, bf16[2,192,1024]{2,1,0:T(8,128)(2,1)S(1)}, u32[]{:S(2)}, u32[]{:S(2)}) collective-permute-start(bf16[2,192,1024]{2,1,0:T(8,128)(2,1)S(1)} %copy-done.35), channel_id=1, source_target_pairs={{0,8},{8,0},{4,12},{12,4},{1,9},{9,1},{5,13},{13,5},{2,10},{10,2},... | collective-permute-start | bytes 2359304 | tf_op jit(solution)/shard_map/ppermute | solution.py:664
  254.0 33.1 %collective-permute-start.24 = (bf16[2,192,1024]{2,1,0:T(8,128)(2,1)S(1)}, bf16[2,192,1024]{2,1,0:T(8,128)(2,1)S(1)}, u32[]{:S(2)}, u32[]{:S(2)}) collective-permute-start(bf16[2,192,1024]{2,1,0:T(8,128)(2,1)S(1)} %copy-done.34), channel_id=1, source_target_pairs={{0,4},{4,0},{8,12},{12,8},{1,5},{5,1},{9,13},{13,9},{2,6},{6,2},{1... | collective-permute-start | bytes 2359304 | tf_op jit(solution)/shard_map/ppermute | solution.py:663
  271.5 14.7 %copy-start.10 = (bf16[2,192,1024]{2,1,0:T(8,128)(2,1)S(1)}, bf16[2,192,1024]{2,1,0:T(8,128)(2,1)}, u32[]{:S(2)}) copy-start(bf16[2,192,1024]{2,1,0:T(8,128)(2,1)} %get-tuple-element.113) | copy-start | bytes 2359300
  271.5 17.6 %collective-permute-start.44 = (bf16[96,1792]{1,0:T(8,128)(2,1)S(1)}, bf16[96,1792]{1,0:T(8,128)(2,1)S(1)}, u32[]{:S(2)}, u32[]{:S(2)}) collective-permute-start(bf16[96,1792]{1,0:T(8,128)(2,1)S(1)} %get-tuple-element.174), channel_id=1, source_target_pairs={{0,1},{3,2},{4,5},{7,6},{8,9},{11,10},{12,13},{15,14},{16,17},{19,... | collective-permute-start | bytes 1032200 | tf_op jit(solution)/shard_map/ppermute | solution.py:702
  273.2 36.1 %collective-permute-start.42 = (bf16[96,1792]{1,0:T(8,128)(2,1)}, bf16[96,1792]{1,0:T(8,128)(2,1)}, u32[]{:S(2)}, u32[]{:S(2)}) collective-permute-start(bf16[96,1792]{1,0:T(8,128)(2,1)} %get-tuple-element.173), channel_id=1, source_target_pairs={{0,1},{1,2},{2,3},{4,5},{5,6},{6,7},{8,9},{9,10},{10,11},{12,13},{... | collective-permute-start | bytes 1032200 | tf_op jit(solution)/shard_map/ppermute | solution.py:702
  275.2 42.1 %collective-permute-start.43 = (bf16[96,1792]{1,0:T(8,128)(2,1)}, bf16[96,1792]{1,0:T(8,128)(2,1)}, u32[]{:S(2)}, u32[]{:S(2)}) collective-permute-start(bf16[96,1792]{1,0:T(8,128)(2,1)} %get-tuple-element.175), channel_id=1, source_target_pairs={{3,2},{2,1},{1,0},{7,6},{6,5},{5,4},{11,10},{10,9},{9,8},{15,14},{... | collective-permute-start | bytes 1032200 | tf_op jit(solution)/shard_map/ppermute | solution.py:702
  286.3 10.1 %collective-permute-start.27 = (bf16[192,1024]{1,0:T(8,128)(2,1)S(1)}, bf16[192,1024]{1,0:T(8,128)(2,1)S(1)}, u32[]{:S(2)}, u32[]{:S(2)}) collective-permute-start(bf16[192,1024]{1,0:T(8,128)(2,1)S(1)} %fusion.36), channel_id=1, source_target_pairs={{0,4},{4,0},{8,12},{12,8},{1,5},{5,1},{9,13},{13,9},{2,6},{6,2},{1... | collective-permute-start | bytes 1179656 | tf_op jit(solution)/shard_map/ppermute | solution.py:663
  287.5 10.1 %collective-permute-start.25 = (bf16[192,1024]{1,0:T(8,128)(2,1)S(1)}, bf16[192,1024]{1,0:T(8,128)(2,1)S(1)}, u32[]{:S(2)}, u32[]{:S(2)}) collective-permute-start(bf16[192,1024]{1,0:T(8,128)(2,1)S(1)} %fusion.35), channel_id=1, source_target_pairs={{0,8},{8,0},{4,12},{12,4},{1,9},{9,1},{5,13},{13,5},{2,10},{10,2},... | collective-permute-start | bytes 1179656 | tf_op jit(solution)/shard_map/ppermute | solution.py:664
  289.8 28.8 %collective-permute-start.45 = (bf16[96,1792]{1,0:T(8,128)(2,1)}, bf16[96,1792]{1,0:T(8,128)(2,1)}, u32[]{:S(2)}, u32[]{:S(2)}) collective-permute-start(bf16[96,1792]{1,0:T(8,128)(2,1)} %fusion.33), channel_id=1, source_target_pairs={{0,2},{1,3},{2,0},{3,1},{4,6},{5,7},{6,4},{7,5},{8,10},{9,11},{10,... | collective-permute-start | bytes 1032200 | tf_op jit(solution)/shard_map/ppermute | solution.py:702
  306.2 38.8 %collective-permute-start.31 = (bf16[4,384,768]{2,1,0:T(8,128)(2,1)}, bf16[4,384,768]{2,1,0:T(8,128)(2,1)}, u32[]{:S(2)}, u32[]{:S(2)}) collective-permute-start(bf16[4,384,768]{2,1,0:T(8,128)(2,1)} %slice.197.refs_4_), channel_id=1, source_target_pairs={{0,16},{16,0},{1,17},{17,1},{2,18},{18,2},{3,19},{19,3},{4,20},{20... | collective-permute-start | bytes 7077896 | tf_op jit(solution)/shard_map/ppermute | solution.py:662
  307.1 15.7 %collective-permute-start.32 = (bf16[1,384,640]{2,1,0:T(8,128)(2,1)S(1)}, bf16[1,384,640]{2,1,0:T(8,128)(2,1)S(1)}, u32[]{:S(2)}, u32[]{:S(2)}) collective-permute-start(bf16[1,384,640]{2,1,0:T(8,128)(2,1)S(1)} %get-tuple-element.176), channel_id=1, source_target_pairs={{0,16},{16,0},{1,17},{17,1},{2,18},{18,2},{3,19},{19,3},{4,20},{20... | collective-permute-start | bytes 1474568 | tf_op jit(solution)/shard_map/ppermute | solution.py:662
  309.3 31.8 %collective-permute-start.30 = (bf16[576,256]{1,0:T(8,128)(2,1)}, bf16[576,256]{1,0:T(8,128)(2,1)}, u32[]{:S(2)}, u32[]{:S(2)}) collective-permute-start(bf16[576,256]{1,0:T(8,128)(2,1)} %pad_maximum_fusion.9), channel_id=1, source_target_pairs={{0,3},{1,0},{2,1},{3,2},{4,7},{5,4},{6,5},{7,6},{8,11},{9,8},{10,9... | collective-permute-start | bytes 884744 | tf_op jit(solution)/shard_map/ppermute | solution.py:665
  317.2 27.7 %collective-permute-start.29 = (bf16[576,256]{1,0:T(8,128)(2,1)S(1)}, bf16[576,256]{1,0:T(8,128)(2,1)}, u32[]{:S(2)}, u32[]{:S(2)}) collective-permute-start(bf16[576,256]{1,0:T(8,128)(2,1)S(1)} %pad_maximum_fusion.8), channel_id=1, source_target_pairs={{0,2},{1,3},{2,0},{3,1},{4,6},{5,7},{6,4},{7,5},{8,10},{9,11},{10,... | collective-permute-start | bytes 884744 | tf_op jit(solution)/shard_map/ppermute | solution.py:665
  318.6 26.4 %collective-permute-start.28 = (bf16[576,256]{1,0:T(8,128)(2,1)S(1)}, bf16[576,256]{1,0:T(8,128)(2,1)}, u32[]{:S(2)}, u32[]{:S(2)}) collective-permute-start(bf16[576,256]{1,0:T(8,128)(2,1)S(1)} %pad_maximum_fusion.7), channel_id=1, source_target_pairs={{0,1},{1,2},{2,3},{3,0},{4,5},{5,6},{6,7},{7,4},{8,9},{9,10},{10,1... | collective-permute-start | bytes 884744 | tf_op jit(solution)/shard_map/ppermute | solution.py:665
  327.6 4.9 %collective-permute-start.38 = (bf16[2,1,96,256]{3,2,1,0:T(8,128)(2,1)}, bf16[2,1,96,256]{3,2,1,0:T(8,128)(2,1)S(1)}, u32[]{:S(2)}, u32[]{:S(2)}) collective-permute-start(bf16[2,1,96,256]{3,2,1,0:T(8,128)(2,1)} %get-tuple-element.122), channel_id=1, source_target_pairs={{0,8},{8,0},{4,12},{12,4},{1,9},{9,1},{5,13},{13,5},{2,10},{10,2},... | collective-permute-start | bytes 294920 | tf_op jit(solution)/shard_map/ppermute | solution.py:664
  332.5 5.6 %collective-permute-start.36 = (bf16[2,1,96,384]{3,2,1,0:T(8,128)(2,1)}, bf16[2,1,96,384]{3,2,1,0:T(8,128)(2,1)S(1)}, u32[]{:S(2)}, u32[]{:S(2)}) collective-permute-start(bf16[2,1,96,384]{3,2,1,0:T(8,128)(2,1)} %get-tuple-element.120), channel_id=1, source_target_pairs={{0,4},{4,0},{8,12},{12,8},{1,5},{5,1},{9,13},{13,9},{2,6},{6,2},{1... | collective-permute-start | bytes 442376 | tf_op jit(solution)/shard_map/ppermute | solution.py:663
  338.1 14.4 %collective-permute-start.39 = (bf16[1,96,256]{2,1,0:T(8,128)(2,1)S(1)}, bf16[1,96,256]{2,1,0:T(8,128)(2,1)S(1)}, u32[]{:S(2)}, u32[]{:S(2)}) collective-permute-start(bf16[1,96,256]{2,1,0:T(8,128)(2,1)S(1)} %fusion.49), channel_id=1, source_target_pairs={{0,4},{4,0},{8,12},{12,8},{1,5},{5,1},{9,13},{13,9},{2,6},{6,2},{1... | collective-permute-start | bytes 147464 | tf_op jit(solution)/shard_map/ppermute | solution.py:663
  341.1 16.0 %collective-permute-start.37 = (bf16[1,96,384]{2,1,0:T(8,128)(2,1)S(1)}, bf16[1,96,384]{2,1,0:T(8,128)(2,1)S(1)}, u32[]{:S(2)}, u32[]{:S(2)}) collective-permute-start(bf16[1,96,384]{2,1,0:T(8,128)(2,1)S(1)} %fusion.48), channel_id=1, source_target_pairs={{0,8},{8,0},{4,12},{12,4},{1,9},{9,1},{5,13},{13,5},{2,10},{10,2},... | collective-permute-start | bytes 221192 | tf_op jit(solution)/shard_map/ppermute | solution.py:664
  351.1 5.2 %collective-permute-start.46 = (f32[16,768]{1,0:T(8,128)}, f32[16,768]{1,0:T(8,128)S(1)}, u32[]{:S(2)}, u32[]{:S(2)}) collective-permute-start(f32[16,768]{1,0:T(8,128)} %get-tuple-element.129), channel_id=1, source_target_pairs={{0,2},{2,0},{1,3},{3,1},{4,6},{6,4},{5,7},{7,5},{8,10},{10,8},{9,1... | collective-permute-start | bytes 147464 | tf_op jit(solution)/shard_map/ppermute | solution.py:918
  357.1 4.1 %collective-permute-start.47 = (f32[16,768]{1,0:T(8,128)S(1)}, f32[16,768]{1,0:T(8,128)S(1)}, u32[]{:S(2)}, u32[]{:S(2)}) collective-permute-start(f32[16,768]{1,0:T(8,128)S(1)} %add.323), channel_id=1, source_target_pairs={{0,1},{1,0},{2,3},{3,2},{4,5},{5,4},{6,7},{7,6},{8,9},{9,8},{10,11... | collective-permute-start | bytes 147464 | tf_op jit(solution)/shard_map/ppermute | solution.py:919
  361.2 7.1 %collective-permute-start.48 = (f32[16,768]{1,0:T(8,128)S(1)}, f32[16,768]{1,0:T(8,128)S(1)}, u32[]{:S(2)}, u32[]{:S(2)}) collective-permute-start(f32[16,768]{1,0:T(8,128)S(1)} %add.324), channel_id=1, source_target_pairs={{0,16},{16,0},{1,17},{17,1},{2,18},{18,2},{3,19},{19,3},{4,20},{20... | collective-permute-start | bytes 147464 | tf_op jit(solution)/shard_map/ppermute | solution.py:662
  363.9 14.3 %collective-permute-start.33 = (bf16[256,768]{1,0:T(8,128)(2,1)S(1)}, bf16[256,768]{1,0:T(8,128)(2,1)S(1)}, u32[]{:S(2)}, u32[]{:S(2)}) collective-permute-start(bf16[256,768]{1,0:T(8,128)(2,1)S(1)} %copy-done.23), channel_id=1, source_target_pairs={{0,1},{1,2},{2,3},{3,0},{4,5},{5,6},{6,7},{7,4},{8,9},{9,10},{10,1... | collective-permute-start | bytes 1179656 | tf_op jit(solution)/shard_map/ppermute | solution.py:665
  364.0 29.8 %collective-permute-start.34 = (bf16[256,768]{1,0:T(8,128)(2,1)S(1)}, bf16[256,768]{1,0:T(8,128)(2,1)S(1)}, u32[]{:S(2)}, u32[]{:S(2)}) collective-permute-start(bf16[256,768]{1,0:T(8,128)(2,1)S(1)} %copy-done.23), channel_id=1, source_target_pairs={{0,2},{1,3},{2,0},{3,1},{4,6},{5,7},{6,4},{7,5},{8,10},{9,11},{10,... | collective-permute-start | bytes 1179656 | tf_op jit(solution)/shard_map/ppermute | solution.py:665
  365.4 28.4 %collective-permute-start.35 = (bf16[256,768]{1,0:T(8,128)(2,1)S(1)}, bf16[256,768]{1,0:T(8,128)(2,1)S(1)}, u32[]{:S(2)}, u32[]{:S(2)}) collective-permute-start(bf16[256,768]{1,0:T(8,128)(2,1)S(1)} %copy-done.23), channel_id=1, source_target_pairs={{0,3},{1,0},{2,1},{3,2},{4,7},{5,4},{6,5},{7,6},{8,11},{9,8},{10,9... | collective-permute-start | bytes 1179656 | tf_op jit(solution)/shard_map/ppermute | solution.py:665
  368.3 4.4 %collective-permute-start.49 = (f32[16,768]{1,0:T(8,128)S(1)}, f32[16,768]{1,0:T(8,128)S(1)}, u32[]{:S(2)}, u32[]{:S(2)}) collective-permute-start(f32[16,768]{1,0:T(8,128)S(1)} %add.325), channel_id=1, source_target_pairs={{0,4},{4,0},{8,12},{12,8},{1,5},{5,1},{9,13},{13,9},{2,6},{6,2},{1... | collective-permute-start | bytes 147464 | tf_op jit(solution)/shard_map/ppermute | solution.py:663
  372.8 4.2 %collective-permute-start.50 = (f32[16,768]{1,0:T(8,128)S(1)}, f32[16,768]{1,0:T(8,128)S(1)}, u32[]{:S(2)}, u32[]{:S(2)}) collective-permute-start(f32[16,768]{1,0:T(8,128)S(1)} %add.326), channel_id=1, source_target_pairs={{0,8},{8,0},{4,12},{12,4},{1,9},{9,1},{5,13},{13,5},{2,10},{10,2},... | collective-permute-start | bytes 147464 | tf_op jit(solution)/shard_map/ppermute | solution.py:664
  (34 other events, 132.0 us)
Sparse Core Ops, SparseCore 0:
  206.8 96.0 all-gather.2

commit v9 on v8

--- a/solution.py
+++ b/solution.py
@@ -855,10 +855,9 @@
         )
         back_done = out[-1]
         *out, carried = out
-        dq, dkv = after(out[:n_tensor], wide_sends), out[n_tensor:]
+        dq, dkv = out[:n_tensor], out[n_tensor:]
         if grouped:
             dk_keep, dk_send, dv_keep, dv_send = dkv
-            dk_send, dv_send = after((dk_send, dv_send), wide_sends)
             r = along_x(dk_send).astype(f32)
             s = along_y(dv_send).astype(f32)
             r2 = along_y((dk_keep[1].astype(f32) + r[1]).astype(bf16)).astype(f32)

time: 410 us -> 415 us (1.012)
  waiting for transfers between devices: 162 us -> 179 us
  starting transfers between devices: 101 us -> 89.9 us
    ppermute x9, waiting for transfers between devices: 23.1 us -> 48.7 us  [body(): lax.ppermute(v, 'context', [(0, 1), (1, 0), (2, 3), (3, 2)])]
    ppermute x9, waiting for transfers between devices: 55.3 us -> 31.5 us  [body(): lax.ppermute(v, 'context', [(0, 2), (2, 0), (1, 3), (3, 1)])]
    ppermute x4, waiting for transfers between devices: 0.01 us -> 22.7 us  [scatter_line(): move = lambda a, perm: lax.ppermute(a.astype(bf16), 'tensor', perm)]
    ppermute x12, starting transfers between devices: 29.4 us -> 19.4 us  [body(): lax.ppermute(v, 'tensor', [(s, (s + d) % n_tensor) for s in range(n_tenso...]
    ppermute x4, starting transfers between devices: 5.45 us -> 14.5 us  [scatter_line(): move = lambda a, perm: lax.ppermute(a.astype(bf16), 'tensor', perm)]
    ppermute x9, starting transfers between devices: 12.1 us -> 7.83 us  [body(): lax.ppermute(v, 'context', [(0, 1), (1, 0), (2, 3), (3, 2)])]
    ppermute x9, starting transfers between devices: 24.3 us -> 20.1 us  [body(): lax.ppermute(v, 'context', [(0, 2), (2, 0), (1, 3), (3, 1)])]
    unnamed x100 -> x104, local copies, waits for them, and re-layouts: 9.17 us -> 10.6 us
  transfers between devices with their start and end apart: 52 -> 52, of which waited for: 27 -> 26; matrix products, arithmetic and copies ran while one was open for 11% -> 10% of each run, Pallas kernels for 9% -> 9%
where the time goes in v9:
time: 415 us; the launch traced here: 409 us
  waiting for transfers between devices  179 us (43%)
  starting transfers between devices  89.9 us (22%)
  Pallas kernels  70.5 us (17%)
  other arithmetic  29 us (7%)
  local copies, waits for them, and re-layouts  24 us (6%)
  between operations  15.1 us (4%)
    ppermute x9, waiting for transfers between devices, body(): lax.ppermute(v, 'context', [(0, 1), (1, 0), (2, 3), (3, 2)])  48.7 us
    ppermute x9, waiting for transfers between devices, body(): lax.ppermute(v, 'context', [(0, 2), (2, 0), (1, 3), (3, 1)])  31.5 us
    ppermute x6, waiting for transfers between devices, gather_begin(): move = lambda perm: lax.ppermute(v, 'tensor', perm)  30.9 us
    ppermute x6, starting transfers between devices, gather_begin(): move = lambda perm: lax.ppermute(v, 'tensor', perm)  24.8 us
    ppermute x12, waiting for transfers between devices, body(): lax.ppermute(v, 'tensor', [(s, (s + d) % n_tensor) for s in range(n_tenso...  23.3 us
    pallas_call x1, Pallas kernels, middle(): pl.pallas_call(functools.partial(middle_kernel, len(att), parts), grid_sp...  23.1 us
    ppermute x4, waiting for transfers between devices, scatter_line(): move = lambda a, perm: lax.ppermute(a.astype(bf16), 'tensor', perm)  22.7 us
    ppermute x9, starting transfers between devices, body(): lax.ppermute(v, 'context', [(0, 2), (2, 0), (1, 3), (3, 1)])  20.1 us
  transfers between devices with their start and end apart: 52, of which 26 were waited for; matrix products, arithmetic and copies ran while one was open for 10% of the time, Pallas kernels for 9%

profile of v9, /device:TPU:0, one launch (start us, length us, event | category | flops | bytes accessed | tf_op | source)
XLA Modules:
  0.0 408.9 jit_solution(1590341032416546405)
XLA Ops:
  10.3 4.1 %collective-permute-start.1 = (bf16[976,384]{1,0:T(8,128)(2,1)S(1)}, bf16[976,384]{1,0:T(8,128)(2,1)}, u32[]{:S(2)}, u32[]{:S(2)}) collective-permute-start(bf16[976,384]{1,0:T(8,128)(2,1)S(1)} %pad_maximum_fusion.4), channel_id=1, source_target_pairs={{0,2},{1,3},{2,0},{3,1},{4,6},{5,7},{6,4},{7,5},{8,10},{9,11},{10,... | collective-permute-start | bytes 2248712 | tf_op jit(solution)/shard_map/ppermute | solution.py:675
  14.4 4.4 %collective-permute-start.2 = (bf16[976,384]{1,0:T(8,128)(2,1)S(1)}, bf16[976,384]{1,0:T(8,128)(2,1)}, u32[]{:S(2)}, u32[]{:S(2)}) collective-permute-start(bf16[976,384]{1,0:T(8,128)(2,1)S(1)} %pad_maximum_fusion.4), channel_id=1, source_target_pairs={{0,1},{1,2},{2,3},{4,5},{5,6},{6,7},{8,9},{9,10},{10,11},{12,13},{... | collective-permute-start | bytes 2248712 | tf_op jit(solution)/shard_map/ppermute | solution.py:675
  23.0 6.3 %project.1 = (bf16[1024,768]{1,0:T(8,128)(2,1)}, bf16[192,1024]{1,0:T(8,128)(2,1)}, bf16[192,1024]{1,0:T(8,128)(2,1)}, bf16[192,1024]{1,0:T(8,128)(2,1)}) custom-call(s32[4]{0:T(128)} %pad_add_fusion.1.sc, bf16[1024,768]{1,0:T(8,128)(2,1)} %bitcast.127, bf16[384,576]{1,0:T(8,128)(2,1)} %copy-done.8, bf16[384,576]{1,0:T(8,128)(2,1)} %copy-done.39, ...), custom_call_target="tpu_custom_call" | custom-call | flops 8049999872 | bytes 1048576 | tf_op jit(solution)/shard_map/project/pallas_call | solution.py:90
  29.4 1.6 collective-permute-start.5
  30.9 1.5 collective-permute-start.4
  32.4 8.4 %collective-permute-done.5.refs_4_.refs_8_ = bf16[192,1024]{1,0:T(8,128)(2,1)S(1)} collective-permute-done((bf16[192,1024]{1,0:T(8,128)(2,1)}, bf16[192,1024]{1,0:T(8,128)(2,1)S(1)}, u32[]{:S(2)}, u32[]{:S(2)}) %collective-permute-start.5) | collective-permute-done | bytes 393248 | tf_op jit(solution)/shard_map/ppermute | solution.py:664
  42.1 6.0 %collective-permute-done.1 = bf16[976,384]{1,0:T(8,128)(2,1)} collective-permute-done((bf16[976,384]{1,0:T(8,128)(2,1)S(1)}, bf16[976,384]{1,0:T(8,128)(2,1)}, u32[]{:S(2)}, u32[]{:S(2)}) %collective-permute-start.1) | collective-permute-done | bytes 749600 | tf_op jit(solution)/shard_map/ppermute | solution.py:675
  48.2 5.4 %collective-permute-done.3 = bf16[976,384]{1,0:T(8,128)(2,1)} collective-permute-done((bf16[976,384]{1,0:T(8,128)(2,1)S(1)}, bf16[976,384]{1,0:T(8,128)(2,1)}, u32[]{:S(2)}, u32[]{:S(2)}) %collective-permute-start.3) | collective-permute-done | bytes 749600 | tf_op jit(solution)/shard_map/ppermute | solution.py:675
  53.5 1.6 collective-permute-start.6
  55.1 1.5 collective-permute-start.7
  57.8 3.8 fusion.63
  62.6 12.4 %collective-permute-start.13 = (bf16[768,384]{1,0:T(8,128)(2,1)}, bf16[768,384]{1,0:T(8,128)(2,1)}, u32[]{:S(2)}, u32[]{:S(2)}) collective-permute-start(bf16[768,384]{1,0:T(8,128)(2,1)} %param.20), channel_id=1, source_target_pairs={{0,2},{1,3},{2,0},{3,1},{4,6},{5,7},{6,4},{7,5},{8,10},{9,11},{10,... | collective-permute-start | bytes 1769480 | tf_op jit(solution)/shard_map/ppermute | solution.py:675
  77.2 9.5 %attend.1 = (f32[3,1024]{1,0:T(4,128)}, bf16[192,1024]{1,0:T(8,128)(2,1)}, bf16[192,256]{1,0:T(8,128)(2,1)}, bf16[192,256]{1,0:T(8,128)(2,1)}, bf16[192,256]{1,0:T(8,128)(2,1)}, /*index=5*/bf16[192,256]{1,0:T(8,128)(2,1)}) custom-call(s32[12]{0:T(128)} %concatenate.46.sc, bf16[192,1024]{1,0:T(8,128)(2,1)} %get-tuple-element.86.qt, ...), custom_call_target="tpu_custom_call" | custom-call | flops 23000000512 | bytes 1048576 | tf_op jit(solution)/shard_map/attend/pallas_call | solution.py:221
  87.1 7.4 %collective-permute-start.8 = (bf16[192,256]{1,0:T(8,128)(2,1)}, bf16[192,256]{1,0:T(8,128)(2,1)S(1)}, u32[]{:S(2)}, u32[]{:S(2)}) collective-permute-start(bf16[192,256]{1,0:T(8,128)(2,1)} %get-tuple-element.73), channel_id=1, source_target_pairs={{0,1},{1,2},{2,3},{3,0},{4,5},{5,6},{6,7},{7,4},{8,9},{9,10},{10,1... | collective-permute-start | bytes 294920 | tf_op jit(solution)/shard_map/ppermute | solution.py:665
  94.5 4.0 collective-permute-start.9
  98.5 6.9 %collective-permute-done.13 = bf16[768,384]{1,0:T(8,128)(2,1)} collective-permute-done((bf16[768,384]{1,0:T(8,128)(2,1)}, bf16[768,384]{1,0:T(8,128)(2,1)}, u32[]{:S(2)}, u32[]{:S(2)}) %collective-permute-start.13) | collective-permute-done | bytes 589856 | tf_op jit(solution)/shard_map/ppermute | solution.py:675
  105.4 1.3 collective-permute-start.15
  106.7 7.0 %collective-permute-done.10.refs_3_ = bf16[192,256]{1,0:T(8,128)(2,1)S(1)} collective-permute-done((bf16[192,256]{1,0:T(8,128)(2,1)}, bf16[192,256]{1,0:T(8,128)(2,1)S(1)}, u32[]{:S(2)}, u32[]{:S(2)}) %collective-permute-start.10) | collective-permute-done | bytes 98336 | tf_op jit(solution)/shard_map/ppermute | solution.py:665
  113.7 1.3 collective-permute-start.16
  115.1 1.5 collective-permute-start.14
  117.9 1.5 pad_maximum_fusion.refs_6_
  119.8 12.3 %collective-permute-done.16 = bf16[768,384]{1,0:T(8,128)(2,1)S(1)} collective-permute-done((bf16[768,384]{1,0:T(8,128)(2,1)}, bf16[768,384]{1,0:T(8,128)(2,1)S(1)}, u32[]{:S(2)}, u32[]{:S(2)}) %collective-permute-start.16) | collective-permute-done | bytes 589856 | tf_op jit(solution)/shard_map/ppermute | solution.py:675
  132.1 9.9 %collective-permute-done.14 = bf16[768,384]{1,0:T(8,128)(2,1)S(1)} collective-permute-done((bf16[768,384]{1,0:T(8,128)(2,1)}, bf16[768,384]{1,0:T(8,128)(2,1)S(1)}, u32[]{:S(2)}, u32[]{:S(2)}) %collective-permute-start.14) | collective-permute-done | bytes 589856 | tf_op jit(solution)/shard_map/ppermute | solution.py:688
  142.1 3.0 pad_maximum_fusion.1.refs_8_
  145.1 2.1 dynamic-slice_bitcast_fusion.2
  147.2 2.8 collective-permute-done.17.refs_9_
  150.0 23.1 %middle.1 = (bf16[256,768]{1,0:T(8,128)(2,1)}, f32[256,768]{1,0:T(8,128)}, f32[4,768]{1,0:T(4,128)}, f32[4,1,768]{2,1,0:T(1,128)}, bf16[192,256]{1,0:T(8,128)(2,...) custom-call(s32[4]{0:T(128)} %pad_add_fusion.1.sc, ...), custom_call_target="tpu_custom_call" | custom-call | flops 21849999360 | bytes 1048576 | tf_op jit(solution)/shard_map/middle/pallas_call | solution.py:465
  175.3 2.1 fusion.13.refs_10_
  177.4 4.9 %collective-permute-done.18.theirs = bf16[4,384,1792]{2,1,0:T(8,128)(2,1)S(1)} collective-permute-done((bf16[4,384,1792]{2,1,0:T(8,128)(2,1)}, bf16[4,384,1792]{2,1,0:T(8,128)(2,1)S(1)}, u32[]{:S(2)}, u32[]{:S(2)}) %collective-permute-start.18) | collective-permute-done | bytes 5505056 | tf_op jit(solution)/shard_map/ppermute | solution.py:662
  182.3 2.4 copy-done.35
  184.7 8.6 %fold.2 = (bf16[2,4,96,896]{3,2,1,0:T(8,128)(2,1)}, bf16[2,4,96,896]{3,2,1,0:T(8,128)(2,1)}, bf16[2,4,96,896]{3,2,1,0:T(8,128)(2,1)}, bf16[2,4,96,896]{3,2,1,0:T(8,128)(2,1)}) custom-call(s32[4]{0:T(128)} %pad_add_fusion.1.sc, bf16[4,384,1792]{2,1,0:T(8,128)(2,1)} %get-tuple-element.83.mine, bf16[4,384,1792]{2,1,0:T(8,128)(2,1)} %copy-done.35), custom_call_target="tpu_custom_call" | custom-call | flops 8049999872 | bytes 1048576 | tf_op jit(solution)/shard_map/fold/pallas_call | solution.py:587
  194.0 12.7 %attend_back.1 = (bf16[192,256]{1,0:T(8,128)(2,1)}, bf16[192,256]{1,0:T(8,128)(2,1)}, bf16[192,256]{1,0:T(8,128)(2,1)}, bf16[192,256]{1,0:T(8,128)(2,1)}, bf16[2...) custom-call(s32[12]{0:T(128)} %concatenate.46.sc, ...), custom_call_target="tpu_custom_call", output_to_operand_aliasing={{8}: (15, {})} | custom-call | flops 29899999232 | bytes 1048576 | tf_op jit(solution)/shard_map/attend_back/pallas_call | solution.py:327
  206.8 12.6 %collective-permute-start.24 = (bf16[2,192,1024]{2,1,0:T(8,128)(2,1)}, bf16[2,192,1024]{2,1,0:T(8,128)(2,1)S(1)}, u32[]{:S(2)}, u32[]{:S(2)}) collective-permute-start(bf16[2,192,1024]{2,1,0:T(8,128)(2,1)} %get-tuple-element.99), channel_id=1, source_target_pairs={{0,8},{8,0},{4,12},{12,4},{1,9},{9,1},{5,13},{13,5},{2,10},{10,2},... | collective-permute-start | bytes 2359304 | tf_op jit(solution)/shard_map/ppermute | solution.py:664
  219.5 2.0 collective-permute-start.38
  221.7 16.2 %collective-permute-done.24 = bf16[2,192,1024]{2,1,0:T(8,128)(2,1)S(1)} collective-permute-done((bf16[2,192,1024]{2,1,0:T(8,128)(2,1)}, bf16[2,192,1024]{2,1,0:T(8,128)(2,1)S(1)}, u32[]{:S(2)}, u32[]{:S(2)}) %collective-permute-start.24) | collective-permute-done | bytes 786464 | tf_op jit(solution)/shard_map/ppermute | solution.py:664
  238.3 1.7 collective-permute-done.22
  241.6 35.3 %collective-permute-done.25 = bf16[192,1024]{1,0:T(8,128)(2,1)S(1)} collective-permute-done((bf16[192,1024]{1,0:T(8,128)(2,1)S(1)}, bf16[192,1024]{1,0:T(8,128)(2,1)S(1)}, u32[]{:S(2)}, u32[]{:S(2)}) %collective-permute-start.25) | collective-permute-done | bytes 393248 | tf_op jit(solution)/shard_map/ppermute | solution.py:663
  277.3 1.6 convolution_convert_fusion
  283.0 1.6 copy-done.12
  286.2 4.2 %fold.3 = (bf16[2,1,96,384]{3,2,1,0:T(8,128)(2,1)}, bf16[2,1,96,384]{3,2,1,0:T(8,128)(2,1)}, bf16[2,1,96,256]{3,2,1,0:T(8,128)(2,1)}, bf16[2,1,96,256]{3,2,1,0:T(8,128)(2,1)}) custom-call(s32[4]{0:T(128)} %pad_add_fusion.1.sc, bf16[1,384,640]{2,1,0:T(8,128)(2,1)} %get-tuple-element.165.mine, bf16[1,384,640]{2,1,0:T(8,128)(2,1)} %copy-done.38), custom_call_target="tpu_custom_call" | custom-call | flops 2875000064 | bytes 1048576 | tf_op jit(solution)/shard_map/fold/pallas_call | solution.py:587
  291.0 1.7 collective-permute-start.39
  292.7 1.7 collective-permute-start.34
  294.5 1.9 collective-permute-done.36
  296.4 3.4 slice.195.refs_4_
  299.9 6.0 %collective-permute-done.34 = bf16[2,1,96,384]{3,2,1,0:T(8,128)(2,1)S(1)} collective-permute-done((bf16[2,1,96,384]{3,2,1,0:T(8,128)(2,1)S(1)}, bf16[2,1,96,384]{3,2,1,0:T(8,128)(2,1)S(1)}, u32[]{:S(2)}, u32[]{:S(2)}) %collective-permute-start.34) | collective-permute-done | bytes 147488 | tf_op jit(solution)/shard_map/ppermute | solution.py:663
  306.2 3.7 collective-permute-done.37
  311.8 1.6 fusion.3
  313.9 1.3 fusion.6
  316.2 1.6 collective-permute-done.35
  317.9 4.1 %collective-permute-start.44 = (bf16[96,1792]{1,0:T(8,128)(2,1)}, bf16[96,1792]{1,0:T(8,128)(2,1)}, u32[]{:S(2)}, u32[]{:S(2)}) collective-permute-start(bf16[96,1792]{1,0:T(8,128)(2,1)} %get-tuple-element.162), channel_id=1, source_target_pairs={{0,1},{3,2},{4,5},{7,6},{8,9},{11,10},{12,13},{15,14},{16,17},{19,... | collective-permute-start | bytes 1032200 | tf_op jit(solution)/shard_map/ppermute | solution.py:702
  323.1 7.0 %collective-permute-done.44 = bf16[96,1792]{1,0:T(8,128)(2,1)} collective-permute-done((bf16[96,1792]{1,0:T(8,128)(2,1)}, bf16[96,1792]{1,0:T(8,128)(2,1)}, u32[]{:S(2)}, u32[]{:S(2)}) %collective-permute-start.44) | collective-permute-done | bytes 344096 | tf_op jit(solution)/shard_map/ppermute | solution.py:702
  330.1 4.5 %collective-permute-start.42 = (bf16[96,1792]{1,0:T(8,128)(2,1)}, bf16[96,1792]{1,0:T(8,128)(2,1)S(1)}, u32[]{:S(2)}, u32[]{:S(2)}) collective-permute-start(bf16[96,1792]{1,0:T(8,128)(2,1)} %get-tuple-element.161), channel_id=1, source_target_pairs={{0,1},{1,2},{2,3},{4,5},{5,6},{6,7},{8,9},{9,10},{10,11},{12,13},{... | collective-permute-start | bytes 1032200 | tf_op jit(solution)/shard_map/ppermute | solution.py:702
  335.7 1.3 collective-permute-start.43
  337.0 4.5 %collective-permute-start.45 = (bf16[96,1792]{1,0:T(8,128)(2,1)S(1)}, bf16[96,1792]{1,0:T(8,128)(2,1)S(1)}, u32[]{:S(2)}, u32[]{:S(2)}) collective-permute-start(bf16[96,1792]{1,0:T(8,128)(2,1)S(1)} %fusion.33), channel_id=1, source_target_pairs={{0,2},{1,3},{2,0},{3,1},{4,6},{5,7},{6,4},{7,5},{8,10},{9,11},{10,... | collective-permute-start | bytes 1032200 | tf_op jit(solution)/shard_map/ppermute | solution.py:702
  341.5 6.1 %last.1 = (bf16[256,768]{1,0:T(8,128)(2,1)}, f32[16,768]{1,0:T(8,128)}) custom-call(s32[4]{0:T(128)} %pad_add_fusion.1.sc, bf16[576,256]{1,0:T(8,128)(2,1)} %pad_maximum_fusion.6.refs_0_, bf16[576,256]{1,0:T(8,128)(2,1)} %collective-permute-done.26.refs_1_, bf16[576,256]{1,0:T(8,128)(2,1)} %collective-permute-done.27.refs_2_, ...), custom_call_target="tpu_custom_call" | custom-call | flops 6899999744 | bytes 1048576 | tf_op jit(solution)/shard_map/last/pallas_call | solution.py:537
  347.6 15.7 %collective-permute-done.45 = bf16[96,1792]{1,0:T(8,128)(2,1)S(1)} collective-permute-done((bf16[96,1792]{1,0:T(8,128)(2,1)S(1)}, bf16[96,1792]{1,0:T(8,128)(2,1)S(1)}, u32[]{:S(2)}, u32[]{:S(2)}) %collective-permute-start.45) | collective-permute-done | bytes 344096 | tf_op jit(solution)/shard_map/ppermute | solution.py:702
  364.8 3.2 collective-permute-done.47
  368.8 1.6 slice.190
  370.6 3.7 collective-permute-start.33
  374.7 1.9 bitcast_convert_fusion
  376.6 1.9 collective-permute-done.49
  379.2 3.5 collective-permute-done.50
  384.4 15.9 %collective-permute-done.32 = bf16[256,768]{1,0:T(8,128)(2,1)S(1)} collective-permute-done((bf16[256,768]{1,0:T(8,128)(2,1)S(1)}, bf16[256,768]{1,0:T(8,128)(2,1)S(1)}, u32[]{:S(2)}, u32[]{:S(2)}) %collective-permute-start.32) | collective-permute-done | bytes 393248 | tf_op jit(solution)/shard_map/ppermute | solution.py:665
  400.4 1.7 copy-done.4
  (236 shorter events, 37.8 us)
Async XLA Ops:
  7.2 289.2 %all-gather.3.cloned.1.call-start = ((), (), s32[]{:S(2)}) async-start(), calls=%async_computation | async-start | bytes 4915200 | tf_op jit(solution)/shard_map/all_gather | solution.py:895
  10.2 19.1 %copy-start.6 = (bf16[976,384]{1,0:T(8,128)(2,1)}, bf16[976,384]{1,0:T(8,128)(2,1)S(1)}, u32[]{:S(2)}) copy-start(bf16[976,384]{1,0:T(8,128)(2,1)S(1)} %pad_maximum_fusion.4) | copy-start | bytes 2248708
  10.3 37.9 %collective-permute-start.1 = (bf16[976,384]{1,0:T(8,128)(2,1)S(1)}, bf16[976,384]{1,0:T(8,128)(2,1)}, u32[]{:S(2)}, u32[]{:S(2)}) collective-permute-start(bf16[976,384]{1,0:T(8,128)(2,1)S(1)} %pad_maximum_fusion.4), channel_id=1, source_target_pairs={{0,2},{1,3},{2,0},{3,1},{4,6},{5,7},{6,4},{7,5},{8,10},{9,11},{10,... | collective-permute-start | bytes 2248712 | tf_op jit(solution)/shard_map/ppermute | solution.py:675
  14.4 33.8 %collective-permute-start.2 = (bf16[976,384]{1,0:T(8,128)(2,1)S(1)}, bf16[976,384]{1,0:T(8,128)(2,1)}, u32[]{:S(2)}, u32[]{:S(2)}) collective-permute-start(bf16[976,384]{1,0:T(8,128)(2,1)S(1)} %pad_maximum_fusion.4), channel_id=1, source_target_pairs={{0,1},{1,2},{2,3},{4,5},{5,6},{6,7},{8,9},{9,10},{10,11},{12,13},{... | collective-permute-start | bytes 2248712 | tf_op jit(solution)/shard_map/ppermute | solution.py:675
  18.7 34.8 %collective-permute-start.3 = (bf16[976,384]{1,0:T(8,128)(2,1)S(1)}, bf16[976,384]{1,0:T(8,128)(2,1)}, u32[]{:S(2)}, u32[]{:S(2)}) collective-permute-start(bf16[976,384]{1,0:T(8,128)(2,1)S(1)} %pad_maximum_fusion.4), channel_id=1, source_target_pairs={{3,2},{2,1},{1,0},{7,6},{6,5},{5,4},{11,10},{10,9},{9,8},{15,14},{... | collective-permute-start | bytes 2248712 | tf_op jit(solution)/shard_map/ppermute | solution.py:675
  20.3 1.9 collective-permute-start
  29.4 11.4 %collective-permute-start.5 = (bf16[192,1024]{1,0:T(8,128)(2,1)}, bf16[192,1024]{1,0:T(8,128)(2,1)S(1)}, u32[]{:S(2)}, u32[]{:S(2)}) collective-permute-start(bf16[192,1024]{1,0:T(8,128)(2,1)} %get-tuple-element.69.refs_3_.refs_7_), channel_id=1, source_target_pairs={{0,8},{8,0},{4,12},{12,4},{1,9},{9,1},{5,13},{13,5},{2,10},{10,2},... | collective-permute-start | bytes 1179656 | tf_op jit(solution)/shard_map/ppermute | solution.py:664
  30.9 11.1 %collective-permute-start.4 = (bf16[192,1024]{1,0:T(8,128)(2,1)}, bf16[192,1024]{1,0:T(8,128)(2,1)S(1)}, u32[]{:S(2)}, u32[]{:S(2)}) collective-permute-start(bf16[192,1024]{1,0:T(8,128)(2,1)} %get-tuple-element.68.refs_0_.refs_4_), channel_id=1, source_target_pairs={{0,4},{4,0},{8,12},{12,8},{1,5},{5,1},{9,13},{13,9},{2,6},{6,2},{1... | collective-permute-start | bytes 1179656 | tf_op jit(solution)/shard_map/ppermute | solution.py:663
  40.8 15.8 %copy-start.28 = (s32[1,4096]{1,0:T(1,128)S(1)}, s32[1,4096]{1,0:T(1,128)}, u32[]{:S(2)}) copy-start(s32[1,4096]{1,0:T(1,128)} %param.16) | copy-start | bytes 49156
  53.5 22.7 %collective-permute-start.6 = (bf16[2,192,1024]{2,1,0:T(8,128)(2,1)S(1)}, bf16[2,192,1024]{2,1,0:T(8,128)(2,1)S(1)}, u32[]{:S(2)}, u32[]{:S(2)}) collective-permute-start(bf16[2,192,1024]{2,1,0:T(8,128)(2,1)S(1)} %pad_maximum_fusion.2), channel_id=1, source_target_pairs={{0,8},{8,0},{4,12},{12,4},{1,9},{9,1},{5,13},{13,5},{2,10},{10,2},... | collective-permute-start | bytes 2359304 | tf_op jit(solution)/shard_map/ppermute | solution.py:664
  55.1 21.2 %collective-permute-start.7 = (bf16[2,192,1024]{2,1,0:T(8,128)(2,1)S(1)}, bf16[2,192,1024]{2,1,0:T(8,128)(2,1)}, u32[]{:S(2)}, u32[]{:S(2)}) collective-permute-start(bf16[2,192,1024]{2,1,0:T(8,128)(2,1)S(1)} %pad_maximum_fusion.3), channel_id=1, source_target_pairs={{0,4},{4,0},{8,12},{12,8},{1,5},{5,1},{9,13},{13,9},{2,6},{6,2},{1... | collective-permute-start | bytes 2359304 | tf_op jit(solution)/shard_map/ppermute | solution.py:663
  62.6 42.8 %collective-permute-start.13 = (bf16[768,384]{1,0:T(8,128)(2,1)}, bf16[768,384]{1,0:T(8,128)(2,1)}, u32[]{:S(2)}, u32[]{:S(2)}) collective-permute-start(bf16[768,384]{1,0:T(8,128)(2,1)} %param.20), channel_id=1, source_target_pairs={{0,2},{1,3},{2,0},{3,1},{4,6},{5,7},{6,4},{7,5},{8,10},{9,11},{10,... | collective-permute-start | bytes 1769480 | tf_op jit(solution)/shard_map/ppermute | solution.py:675
  75.0 41.5 %collective-permute-start.11 = (bf16[976,384]{1,0:T(8,128)(2,1)}, bf16[976,384]{1,0:T(8,128)(2,1)S(1)}, u32[]{:S(2)}, u32[]{:S(2)}) collective-permute-start(bf16[976,384]{1,0:T(8,128)(2,1)} %collective-permute-done.1), channel_id=1, source_target_pairs={{2,3},{1,0},{6,7},{5,4},{10,11},{9,8},{14,15},{13,12},{18,19},{17,... | collective-permute-start | bytes 2248712 | tf_op jit(solution)/shard_map/ppermute | solution.py:688
  86.7 27.0 %collective-permute-start.10 = (bf16[192,256]{1,0:T(8,128)(2,1)}, bf16[192,256]{1,0:T(8,128)(2,1)S(1)}, u32[]{:S(2)}, u32[]{:S(2)}) collective-permute-start(bf16[192,256]{1,0:T(8,128)(2,1)} %get-tuple-element.75), channel_id=1, source_target_pairs={{0,3},{1,0},{2,1},{3,2},{4,7},{5,4},{6,5},{7,6},{8,11},{9,8},{10,9... | collective-permute-start | bytes 294920 | tf_op jit(solution)/shard_map/ppermute | solution.py:665
  87.1 27.9 %collective-permute-start.8 = (bf16[192,256]{1,0:T(8,128)(2,1)}, bf16[192,256]{1,0:T(8,128)(2,1)S(1)}, u32[]{:S(2)}, u32[]{:S(2)}) collective-permute-start(bf16[192,256]{1,0:T(8,128)(2,1)} %get-tuple-element.73), channel_id=1, source_target_pairs={{0,1},{1,2},{2,3},{3,0},{4,5},{5,6},{6,7},{7,4},{8,9},{9,10},{10,1... | collective-permute-start | bytes 294920 | tf_op jit(solution)/shard_map/ppermute | solution.py:665
  94.5 20.5 %collective-permute-start.9 = (bf16[192,256]{1,0:T(8,128)(2,1)}, bf16[192,256]{1,0:T(8,128)(2,1)S(1)}, u32[]{:S(2)}, u32[]{:S(2)}) collective-permute-start(bf16[192,256]{1,0:T(8,128)(2,1)} %get-tuple-element.74), channel_id=1, source_target_pairs={{0,2},{1,3},{2,0},{3,1},{4,6},{5,7},{6,4},{7,5},{8,10},{9,11},{10,... | collective-permute-start | bytes 294920 | tf_op jit(solution)/shard_map/ppermute | solution.py:665
  98.5 19.4 %copy-start.7 = (bf16[976,384]{1,0:T(8,128)(2,1)S(1)}, bf16[976,384]{1,0:T(8,128)(2,1)}, u32[]{:S(2)}) copy-start(bf16[976,384]{1,0:T(8,128)(2,1)} %copy-done.6) | copy-start | bytes 2248708
  105.4 14.4 %collective-permute-start.15 = (bf16[768,384]{1,0:T(8,128)(2,1)}, bf16[768,384]{1,0:T(8,128)(2,1)S(1)}, u32[]{:S(2)}, u32[]{:S(2)}) collective-permute-start(bf16[768,384]{1,0:T(8,128)(2,1)} %param.20), channel_id=1, source_target_pairs={{0,1},{1,2},{2,3},{4,5},{5,6},{6,7},{8,9},{9,10},{10,11},{12,13},{... | collective-permute-start | bytes 1769480 | tf_op jit(solution)/shard_map/ppermute | solution.py:675
  113.7 18.4 %collective-permute-start.16 = (bf16[768,384]{1,0:T(8,128)(2,1)}, bf16[768,384]{1,0:T(8,128)(2,1)S(1)}, u32[]{:S(2)}, u32[]{:S(2)}) collective-permute-start(bf16[768,384]{1,0:T(8,128)(2,1)} %param.20), channel_id=1, source_target_pairs={{3,2},{2,1},{1,0},{7,6},{6,5},{5,4},{11,10},{10,9},{9,8},{15,14},{... | collective-permute-start | bytes 1769480 | tf_op jit(solution)/shard_map/ppermute | solution.py:675
  115.1 26.9 %collective-permute-start.14 = (bf16[768,384]{1,0:T(8,128)(2,1)}, bf16[768,384]{1,0:T(8,128)(2,1)S(1)}, u32[]{:S(2)}, u32[]{:S(2)}) collective-permute-start(bf16[768,384]{1,0:T(8,128)(2,1)} %collective-permute-done.13), channel_id=1, source_target_pairs={{2,3},{1,0},{6,7},{5,4},{10,11},{9,8},{14,15},{13,12},{18,19},{17,... | collective-permute-start | bytes 1769480 | tf_op jit(solution)/shard_map/ppermute | solution.py:688
  119.4 25.7 %copy-start.5 = (bf16[4,976,384]{2,1,0:T(8,128)(2,1)}, bf16[4,976,384]{2,1,0:T(8,128)(2,1)S(1)}, u32[]{:S(2)}) copy-start(bf16[4,976,384]{2,1,0:T(8,128)(2,1)S(1)} %pad_maximum_fusion.refs_6_) | copy-start | bytes 8994820
  119.4 30.6 %collective-permute-start.12 = (bf16[4,976,384]{2,1,0:T(8,128)(2,1)S(1)}, bf16[4,976,384]{2,1,0:T(8,128)(2,1)}, u32[]{:S(2)}, u32[]{:S(2)}) collective-permute-start(bf16[4,976,384]{2,1,0:T(8,128)(2,1)S(1)} %pad_maximum_fusion.refs_6_), channel_id=1, source_target_pairs={{0,16},{16,0},{1,17},{17,1},{2,18},{18,2},{3,19},{19,3},{4,20},{20... | collective-permute-start | bytes 8994824 | tf_op jit(solution)/shard_map/ppermute | solution.py:662
  145.1 4.9 %collective-permute-start.17 = (bf16[4,768,384]{2,1,0:T(8,128)(2,1)}, bf16[4,768,384]{2,1,0:T(8,128)(2,1)}, u32[]{:S(2)}, u32[]{:S(2)}) collective-permute-start(bf16[4,768,384]{2,1,0:T(8,128)(2,1)} %pad_maximum_fusion.1.refs_8_), channel_id=1, source_target_pairs={{0,16},{16,0},{1,17},{17,1},{2,18},{18,2},{3,19},{19,3},{4,20},{20... | collective-permute-start | bytes 7077896 | tf_op jit(solution)/shard_map/ppermute | solution.py:662
  150.0 25.3 %copy-start.9 = (bf16[384,576]{1,0:T(8,128)(2,1)S(1)}, bf16[384,576]{1,0:T(8,128)(2,1)}, u32[]{:S(2)}) copy-start(bf16[384,576]{1,0:T(8,128)(2,1)} %copy-done.8) | copy-start | bytes 1327108
  173.1 9.2 %collective-permute-start.18 = (bf16[4,384,1792]{2,1,0:T(8,128)(2,1)}, bf16[4,384,1792]{2,1,0:T(8,128)(2,1)S(1)}, u32[]{:S(2)}, u32[]{:S(2)}) collective-permute-start(bf16[4,384,1792]{2,1,0:T(8,128)(2,1)} %get-tuple-element.84), channel_id=1, source_target_pairs={{0,16},{16,0},{1,17},{17,1},{2,18},{18,2},{3,19},{19,3},{4,20},{20... | collective-permute-start | bytes 16515080 | tf_op jit(solution)/shard_map/ppermute | solution.py:662
  173.3 20.0 %collective-permute-start.19 = (bf16[192,256]{1,0:T(8,128)(2,1)}, bf16[192,256]{1,0:T(8,128)(2,1)S(1)}, u32[]{:S(2)}, u32[]{:S(2)}) collective-permute-start(bf16[192,256]{1,0:T(8,128)(2,1)} %get-tuple-element.90), channel_id=1, source_target_pairs={{0,3},{1,0},{2,1},{3,2},{4,7},{5,4},{6,5},{7,6},{8,11},{9,8},{10,9... | collective-permute-start | bytes 294920 | tf_op jit(solution)/shard_map/ppermute | solution.py:665
  173.3 20.1 %collective-permute-start.20 = (bf16[192,256]{1,0:T(8,128)(2,1)}, bf16[192,256]{1,0:T(8,128)(2,1)S(1)}, u32[]{:S(2)}, u32[]{:S(2)}) collective-permute-start(bf16[192,256]{1,0:T(8,128)(2,1)} %get-tuple-element.91), channel_id=1, source_target_pairs={{0,2},{1,3},{2,0},{3,1},{4,6},{5,7},{6,4},{7,5},{8,10},{9,11},{10,... | collective-permute-start | bytes 294920 | tf_op jit(solution)/shard_map/ppermute | solution.py:665
  174.4 19.0 %collective-permute-start.21 = (bf16[192,256]{1,0:T(8,128)(2,1)}, bf16[192,256]{1,0:T(8,128)(2,1)S(1)}, u32[]{:S(2)}, u32[]{:S(2)}) collective-permute-start(bf16[192,256]{1,0:T(8,128)(2,1)} %get-tuple-element.92), channel_id=1, source_target_pairs={{0,1},{1,2},{2,3},{3,0},{4,5},{5,6},{6,7},{7,4},{8,9},{9,10},{10,1... | collective-permute-start | bytes 294920 | tf_op jit(solution)/shard_map/ppermute | solution.py:665
  194.0 25.5 %copy-start.36 = (bf16[2,4,96,896]{3,2,1,0:T(8,128)(2,1)S(1)}, bf16[2,4,96,896]{3,2,1,0:T(8,128)(2,1)}, u32[]{:S(2)}) copy-start(bf16[2,4,96,896]{3,2,1,0:T(8,128)(2,1)} %get-tuple-element.85) | copy-start | bytes 4128772
  206.7 14.9 %copy-start.16 = (bf16[192,256]{1,0:T(8,128)(2,1)S(1)}, bf16[192,256]{1,0:T(8,128)(2,1)}, u32[]{:S(2)}) copy-start(bf16[192,256]{1,0:T(8,128)(2,1)} %get-tuple-element.95) | copy-start | bytes 294916
  206.8 14.9 %copy-start.17 = (bf16[192,256]{1,0:T(8,128)(2,1)S(1)}, bf16[192,256]{1,0:T(8,128)(2,1)}, u32[]{:S(2)}) copy-start(bf16[192,256]{1,0:T(8,128)(2,1)} %get-tuple-element.100) | copy-start | bytes 294916
  206.8 31.1 %collective-permute-start.24 = (bf16[2,192,1024]{2,1,0:T(8,128)(2,1)}, bf16[2,192,1024]{2,1,0:T(8,128)(2,1)S(1)}, u32[]{:S(2)}, u32[]{:S(2)}) collective-permute-start(bf16[2,192,1024]{2,1,0:T(8,128)(2,1)} %get-tuple-element.99), channel_id=1, source_target_pairs={{0,8},{8,0},{4,12},{12,4},{1,9},{9,1},{5,13},{13,5},{2,10},{10,2},... | collective-permute-start | bytes 2359304 | tf_op jit(solution)/shard_map/ppermute | solution.py:664
  219.4 20.6 %collective-permute-start.22 = (bf16[2,192,1024]{2,1,0:T(8,128)(2,1)}, bf16[2,192,1024]{2,1,0:T(8,128)(2,1)S(1)}, u32[]{:S(2)}, u32[]{:S(2)}) collective-permute-start(bf16[2,192,1024]{2,1,0:T(8,128)(2,1)} %get-tuple-element.97), channel_id=1, source_target_pairs={{0,4},{4,0},{8,12},{12,8},{1,5},{5,1},{9,13},{13,9},{2,6},{6,2},{1... | collective-permute-start | bytes 2359304 | tf_op jit(solution)/shard_map/ppermute | solution.py:663
  219.5 65.7 %collective-permute-start.38 = (bf16[2,4,96,896]{3,2,1,0:T(8,128)(2,1)S(1)}, bf16[2,4,96,896]{3,2,1,0:T(8,128)(2,1)S(1)}, u32[]{:S(2)}, u32[]{:S(2)}) collective-permute-start(bf16[2,4,96,896]{3,2,1,0:T(8,128)(2,1)S(1)} %copy-done.36), channel_id=1, source_target_pairs={{0,4},{4,0},{8,12},{12,8},{1,5},{5,1},{9,13},{13,9},{2,6},{6,2},{1... | collective-permute-start | bytes 4128776 | tf_op jit(solution)/shard_map/ppermute | solution.py:663
  221.5 61.3 %collective-permute-start.40 = (bf16[2,4,96,896]{3,2,1,0:T(8,128)(2,1)}, bf16[2,4,96,896]{3,2,1,0:T(8,128)(2,1)S(1)}, u32[]{:S(2)}, u32[]{:S(2)}) collective-permute-start(bf16[2,4,96,896]{3,2,1,0:T(8,128)(2,1)} %get-tuple-element.116), channel_id=1, source_target_pairs={{0,8},{8,0},{4,12},{12,4},{1,9},{9,1},{5,13},{13,5},{2,10},{10,2},... | collective-permute-start | bytes 4128776 | tf_op jit(solution)/shard_map/ppermute | solution.py:664
  221.6 16.5 %copy-start.14 = (bf16[2,192,1024]{2,1,0:T(8,128)(2,1)S(1)}, bf16[2,192,1024]{2,1,0:T(8,128)(2,1)}, u32[]{:S(2)}) copy-start(bf16[2,192,1024]{2,1,0:T(8,128)(2,1)} %get-tuple-element.98) | copy-start | bytes 2359300
  238.2 38.7 %collective-permute-start.25 = (bf16[192,1024]{1,0:T(8,128)(2,1)S(1)}, bf16[192,1024]{1,0:T(8,128)(2,1)S(1)}, u32[]{:S(2)}, u32[]{:S(2)}) collective-permute-start(bf16[192,1024]{1,0:T(8,128)(2,1)S(1)} %fusion.36), channel_id=1, source_target_pairs={{0,4},{4,0},{8,12},{12,8},{1,5},{5,1},{9,13},{13,9},{2,6},{6,2},{1... | collective-permute-start | bytes 1179656 | tf_op jit(solution)/shard_map/ppermute | solution.py:663
  240.3 36.8 %collective-permute-start.23 = (bf16[192,1024]{1,0:T(8,128)(2,1)S(1)}, bf16[192,1024]{1,0:T(8,128)(2,1)S(1)}, u32[]{:S(2)}, u32[]{:S(2)}) collective-permute-start(bf16[192,1024]{1,0:T(8,128)(2,1)S(1)} %fusion.35), channel_id=1, source_target_pairs={{0,8},{8,0},{4,12},{12,4},{1,9},{9,1},{5,13},{13,5},{2,10},{10,2},... | collective-permute-start | bytes 1179656 | tf_op jit(solution)/shard_map/ppermute | solution.py:664
  241.6 35.7 %copy-start.47 = (bf16[1024,768]{1,0:T(8,128)(2,1)S(1)}, bf16[1024,768]{1,0:T(8,128)(2,1)}, u32[]{:S(2)}) copy-start(bf16[1024,768]{1,0:T(8,128)(2,1)} %get-tuple-element.104) | copy-start | bytes 4718596
  279.8 5.6 %collective-permute-start.30 = (bf16[1,384,640]{2,1,0:T(8,128)(2,1)S(1)}, bf16[1,384,640]{2,1,0:T(8,128)(2,1)S(1)}, u32[]{:S(2)}, u32[]{:S(2)}) collective-permute-start(bf16[1,384,640]{2,1,0:T(8,128)(2,1)S(1)} %get-tuple-element.164), channel_id=1, source_target_pairs={{0,16},{16,0},{1,17},{17,1},{2,18},{18,2},{3,19},{19,3},{4,20},{20... | collective-permute-start | bytes 1474568 | tf_op jit(solution)/shard_map/ppermute | solution.py:662
  280.6 55.0 %collective-permute-start.28 = (bf16[576,256]{1,0:T(8,128)(2,1)}, bf16[576,256]{1,0:T(8,128)(2,1)}, u32[]{:S(2)}, u32[]{:S(2)}) collective-permute-start(bf16[576,256]{1,0:T(8,128)(2,1)} %pad_maximum_fusion.9), channel_id=1, source_target_pairs={{0,3},{1,0},{2,1},{3,2},{4,7},{5,4},{6,5},{7,6},{8,11},{9,8},{10,9... | collective-permute-start | bytes 884744 | tf_op jit(solution)/shard_map/ppermute | solution.py:665
  284.8 26.0 %collective-permute-start.41 = (bf16[4,96,896]{2,1,0:T(8,128)(2,1)S(1)}, bf16[4,96,896]{2,1,0:T(8,128)(2,1)}, u32[]{:S(2)}, u32[]{:S(2)}) collective-permute-start(bf16[4,96,896]{2,1,0:T(8,128)(2,1)S(1)} %fusion.23), channel_id=1, source_target_pairs={{0,4},{4,0},{8,12},{12,8},{1,5},{5,1},{9,13},{13,9},{2,6},{6,2},{1... | collective-permute-start | bytes 2064392 | tf_op jit(solution)/shard_map/ppermute | solution.py:663
  290.5 5.9 %collective-permute-start.36 = (bf16[2,1,96,256]{3,2,1,0:T(8,128)(2,1)}, bf16[2,1,96,256]{3,2,1,0:T(8,128)(2,1)S(1)}, u32[]{:S(2)}, u32[]{:S(2)}) collective-permute-start(bf16[2,1,96,256]{3,2,1,0:T(8,128)(2,1)} %get-tuple-element.107), channel_id=1, source_target_pairs={{0,8},{8,0},{4,12},{12,4},{1,9},{9,1},{5,13},{13,5},{2,10},{10,2},... | collective-permute-start | bytes 294920 | tf_op jit(solution)/shard_map/ppermute | solution.py:664
  291.0 22.4 %collective-permute-start.39 = (bf16[4,96,896]{2,1,0:T(8,128)(2,1)S(1)}, bf16[4,96,896]{2,1,0:T(8,128)(2,1)}, u32[]{:S(2)}, u32[]{:S(2)}) collective-permute-start(bf16[4,96,896]{2,1,0:T(8,128)(2,1)S(1)} %fusion.22), channel_id=1, source_target_pairs={{0,8},{8,0},{4,12},{12,4},{1,9},{9,1},{5,13},{13,5},{2,10},{10,2},... | collective-permute-start | bytes 2064392 | tf_op jit(solution)/shard_map/ppermute | solution.py:664
  292.7 13.1 %collective-permute-start.34 = (bf16[2,1,96,384]{3,2,1,0:T(8,128)(2,1)S(1)}, bf16[2,1,96,384]{3,2,1,0:T(8,128)(2,1)S(1)}, u32[]{:S(2)}, u32[]{:S(2)}) collective-permute-start(bf16[2,1,96,384]{3,2,1,0:T(8,128)(2,1)S(1)} %copy-done.40), channel_id=1, source_target_pairs={{0,4},{4,0},{8,12},{12,8},{1,5},{5,1},{9,13},{13,9},{2,6},{6,2},{1... | collective-permute-start | bytes 442376 | tf_op jit(solution)/shard_map/ppermute | solution.py:663
  296.4 15.4 %copy-start.3 = (f32[2,4,96,896]{3,2,1,0:T(8,128)S(1)}, f32[2,4,96,896]{3,2,1,0:T(8,128)}, u32[]{:S(2)}) copy-start(f32[2,4,96,896]{3,2,1,0:T(8,128)} %copy-done.2) | copy-start | bytes 8257540
  299.8 41.6 %collective-permute-start.29 = (bf16[4,384,768]{2,1,0:T(8,128)(2,1)}, bf16[4,384,768]{2,1,0:T(8,128)(2,1)}, u32[]{:S(2)}, u32[]{:S(2)}) collective-permute-start(bf16[4,384,768]{2,1,0:T(8,128)(2,1)} %slice.195.refs_4_), channel_id=1, source_target_pairs={{0,16},{16,0},{1,17},{17,1},{2,18},{18,2},{3,19},{19,3},{4,20},{20... | collective-permute-start | bytes 7077896 | tf_op jit(solution)/shard_map/ppermute | solution.py:662
  305.9 4.1 %collective-permute-start.37 = (bf16[1,96,256]{2,1,0:T(8,128)(2,1)S(1)}, bf16[1,96,256]{2,1,0:T(8,128)(2,1)S(1)}, u32[]{:S(2)}, u32[]{:S(2)}) collective-permute-start(bf16[1,96,256]{2,1,0:T(8,128)(2,1)S(1)} %fusion.49), channel_id=1, source_target_pairs={{0,4},{4,0},{8,12},{12,8},{1,5},{5,1},{9,13},{13,9},{2,6},{6,2},{1... | collective-permute-start | bytes 147464 | tf_op jit(solution)/shard_map/ppermute | solution.py:663
  310.0 27.0 %collective-permute-start.27 = (bf16[576,256]{1,0:T(8,128)(2,1)}, bf16[576,256]{1,0:T(8,128)(2,1)}, u32[]{:S(2)}, u32[]{:S(2)}) collective-permute-start(bf16[576,256]{1,0:T(8,128)(2,1)} %pad_maximum_fusion.8), channel_id=1, source_target_pairs={{0,2},{1,3},{2,0},{3,1},{4,6},{5,7},{6,4},{7,5},{8,10},{9,11},{10,... | collective-permute-start | bytes 884744 | tf_op jit(solution)/shard_map/ppermute | solution.py:665
  310.9 30.6 %collective-permute-start.26 = (bf16[576,256]{1,0:T(8,128)(2,1)}, bf16[576,256]{1,0:T(8,128)(2,1)}, u32[]{:S(2)}, u32[]{:S(2)}) collective-permute-start(bf16[576,256]{1,0:T(8,128)(2,1)} %pad_maximum_fusion.7), channel_id=1, source_target_pairs={{0,1},{1,2},{2,3},{3,0},{4,5},{5,6},{6,7},{7,4},{8,9},{9,10},{10,1... | collective-permute-start | bytes 884744 | tf_op jit(solution)/shard_map/ppermute | solution.py:665
  313.4 4.4 %collective-permute-start.35 = (bf16[1,96,384]{2,1,0:T(8,128)(2,1)S(1)}, bf16[1,96,384]{2,1,0:T(8,128)(2,1)S(1)}, u32[]{:S(2)}, u32[]{:S(2)}) collective-permute-start(bf16[1,96,384]{2,1,0:T(8,128)(2,1)S(1)} %fusion.48), channel_id=1, source_target_pairs={{0,8},{8,0},{4,12},{12,4},{1,9},{9,1},{5,13},{13,5},{2,10},{10,2},... | collective-permute-start | bytes 221192 | tf_op jit(solution)/shard_map/ppermute | solution.py:664
  317.9 12.2 %collective-permute-start.44 = (bf16[96,1792]{1,0:T(8,128)(2,1)}, bf16[96,1792]{1,0:T(8,128)(2,1)}, u32[]{:S(2)}, u32[]{:S(2)}) collective-permute-start(bf16[96,1792]{1,0:T(8,128)(2,1)} %get-tuple-element.162), channel_id=1, source_target_pairs={{0,1},{3,2},{4,5},{7,6},{8,9},{11,10},{12,13},{15,14},{16,17},{19,... | collective-permute-start | bytes 1032200 | tf_op jit(solution)/shard_map/ppermute | solution.py:702
  330.1 17.5 %collective-permute-start.42 = (bf16[96,1792]{1,0:T(8,128)(2,1)}, bf16[96,1792]{1,0:T(8,128)(2,1)S(1)}, u32[]{:S(2)}, u32[]{:S(2)}) collective-permute-start(bf16[96,1792]{1,0:T(8,128)(2,1)} %get-tuple-element.161), channel_id=1, source_target_pairs={{0,1},{1,2},{2,3},{4,5},{5,6},{6,7},{8,9},{9,10},{10,11},{12,13},{... | collective-permute-start | bytes 1032200 | tf_op jit(solution)/shard_map/ppermute | solution.py:702
  335.7 11.9 %collective-permute-start.43 = (bf16[96,1792]{1,0:T(8,128)(2,1)S(1)}, bf16[96,1792]{1,0:T(8,128)(2,1)S(1)}, u32[]{:S(2)}, u32[]{:S(2)}) collective-permute-start(bf16[96,1792]{1,0:T(8,128)(2,1)S(1)} %copy-done.24), channel_id=1, source_target_pairs={{3,2},{2,1},{1,0},{7,6},{6,5},{5,4},{11,10},{10,9},{9,8},{15,14},{... | collective-permute-start | bytes 1032200 | tf_op jit(solution)/shard_map/ppermute | solution.py:702
  337.0 26.3 %collective-permute-start.45 = (bf16[96,1792]{1,0:T(8,128)(2,1)S(1)}, bf16[96,1792]{1,0:T(8,128)(2,1)S(1)}, u32[]{:S(2)}, u32[]{:S(2)}) collective-permute-start(bf16[96,1792]{1,0:T(8,128)(2,1)S(1)} %fusion.33), channel_id=1, source_target_pairs={{0,2},{1,3},{2,0},{3,1},{4,6},{5,7},{6,4},{7,5},{8,10},{9,11},{10,... | collective-permute-start | bytes 1032200 | tf_op jit(solution)/shard_map/ppermute | solution.py:702
  347.5 16.3 %copy-start.27 = (f32[16,768]{1,0:T(8,128)S(1)}, f32[16,768]{1,0:T(8,128)}, u32[]{:S(2)}) copy-start(f32[16,768]{1,0:T(8,128)} %get-tuple-element.117) | copy-start | bytes 147460
  347.5 16.3 %collective-permute-start.46 = (f32[16,768]{1,0:T(8,128)}, f32[16,768]{1,0:T(8,128)S(1)}, u32[]{:S(2)}, u32[]{:S(2)}) collective-permute-start(f32[16,768]{1,0:T(8,128)} %get-tuple-element.117), channel_id=1, source_target_pairs={{0,2},{2,0},{1,3},{3,1},{4,6},{6,4},{5,7},{7,5},{8,10},{10,8},{9,1... | collective-permute-start | bytes 147464 | tf_op jit(solution)/shard_map/ppermute | solution.py:917
  363.9 4.2 %collective-permute-start.47 = (f32[16,768]{1,0:T(8,128)S(1)}, f32[16,768]{1,0:T(8,128)S(1)}, u32[]{:S(2)}, u32[]{:S(2)}) collective-permute-start(f32[16,768]{1,0:T(8,128)S(1)} %add.323), channel_id=1, source_target_pairs={{0,1},{1,0},{2,3},{3,2},{4,5},{5,4},{6,7},{7,6},{8,9},{9,8},{10,11... | collective-permute-start | bytes 147464 | tf_op jit(solution)/shard_map/ppermute | solution.py:918
  368.0 6.3 %collective-permute-start.48 = (f32[16,768]{1,0:T(8,128)S(1)}, f32[16,768]{1,0:T(8,128)S(1)}, u32[]{:S(2)}, u32[]{:S(2)}) collective-permute-start(f32[16,768]{1,0:T(8,128)S(1)} %add.324), channel_id=1, source_target_pairs={{0,16},{16,0},{1,17},{17,1},{2,18},{18,2},{3,19},{19,3},{4,20},{20... | collective-permute-start | bytes 147464 | tf_op jit(solution)/shard_map/ppermute | solution.py:662
  370.4 13.9 %collective-permute-start.31 = (bf16[256,768]{1,0:T(8,128)(2,1)S(1)}, bf16[256,768]{1,0:T(8,128)(2,1)S(1)}, u32[]{:S(2)}, u32[]{:S(2)}) collective-permute-start(bf16[256,768]{1,0:T(8,128)(2,1)S(1)} %copy-done.23), channel_id=1, source_target_pairs={{0,1},{1,2},{2,3},{3,0},{4,5},{5,6},{6,7},{7,4},{8,9},{9,10},{10,1... | collective-permute-start | bytes 1179656 | tf_op jit(solution)/shard_map/ppermute | solution.py:665
  370.5 29.8 %collective-permute-start.32 = (bf16[256,768]{1,0:T(8,128)(2,1)S(1)}, bf16[256,768]{1,0:T(8,128)(2,1)S(1)}, u32[]{:S(2)}, u32[]{:S(2)}) collective-permute-start(bf16[256,768]{1,0:T(8,128)(2,1)S(1)} %copy-done.23), channel_id=1, source_target_pairs={{0,2},{1,3},{2,0},{3,1},{4,6},{5,7},{6,4},{7,5},{8,10},{9,11},{10,... | collective-permute-start | bytes 1179656 | tf_op jit(solution)/shard_map/ppermute | solution.py:665
  370.6 29.8 %collective-permute-start.33 = (bf16[256,768]{1,0:T(8,128)(2,1)S(1)}, bf16[256,768]{1,0:T(8,128)(2,1)S(1)}, u32[]{:S(2)}, u32[]{:S(2)}) collective-permute-start(bf16[256,768]{1,0:T(8,128)(2,1)S(1)} %copy-done.23), channel_id=1, source_target_pairs={{0,3},{1,0},{2,1},{3,2},{4,7},{5,4},{6,5},{7,6},{8,11},{9,8},{10,9... | collective-permute-start | bytes 1179656 | tf_op jit(solution)/shard_map/ppermute | solution.py:665
  374.3 4.2 %collective-permute-start.49 = (f32[16,768]{1,0:T(8,128)S(1)}, f32[16,768]{1,0:T(8,128)S(1)}, u32[]{:S(2)}, u32[]{:S(2)}) collective-permute-start(f32[16,768]{1,0:T(8,128)S(1)} %add.325), channel_id=1, source_target_pairs={{0,4},{4,0},{8,12},{12,8},{1,5},{5,1},{9,13},{13,9},{2,6},{6,2},{1... | collective-permute-start | bytes 147464 | tf_op jit(solution)/shard_map/ppermute | solution.py:663
  378.5 4.2 %collective-permute-start.50 = (f32[16,768]{1,0:T(8,128)S(1)}, f32[16,768]{1,0:T(8,128)S(1)}, u32[]{:S(2)}, u32[]{:S(2)}) collective-permute-start(f32[16,768]{1,0:T(8,128)S(1)} %add.326), channel_id=1, source_target_pairs={{0,8},{8,0},{4,12},{12,4},{1,9},{9,1},{5,13},{13,5},{2,10},{10,2},... | collective-permute-start | bytes 147464 | tf_op jit(solution)/shard_map/ppermute | solution.py:664
  (36 other events, 186.4 us)
Sparse Core Ops, SparseCore 0:
  206.9 88.9 all-gather.2
